TPU v7x, 128 devices: a whole 4x4x4 slice. The times are simulated.
128 devices in a mesh: img: 32 (over x, y, core), tile: 4 (over z).
Axes of the slice: x: 4, y: 4, z: 4, core: 2. Of those that a mesh axis runs over, the one named last changes fastest.
Arguments:
- features: bfloat16 [512, 64, 16, 768], P('img', None, 'tile'), may hold values from -6 to 6
- partner_ids: int32 [512], replicated, may hold values from 0 to 511, as said below
- depth_planes: float32 [64], replicated, may hold values from 0.5 to 4
- cam_height: float32 [512], P('img'), may hold values from 2 to 4
- ray_down: float32 [512, 16, 512], P('img', 'tile'), may hold values from 0.3 to 0.9
- depth_index: int32 [512, 16, 512], P('img', 'tile'), may hold values from 0 to 63
- cell_index: int32 [512, 16, 512], P('img', 'tile'), may hold values from 0 to 127
- block_list: int32 [32, 4, 4, 128], P('img', 'tile'), may hold values from 0 to 255, as said below
- block_slot: int32 [32, 4, 4, 128], P('img', 'tile'), may hold values from 0 to 511
- block_count: int32 [32, 4, 4], P('img', 'tile'), may hold values from 0 to 128, as said below
Outputs:
- mean_range_per_sample: float32 [512, 16, 512], P('img', 'tile')
- terrain_height_grid: float32 [2048, 128], P(('img', 'tile'))
Inputs may be any that keep to these rules, and one draw needn't show every extreme that they name: `partner_ids`: image g lies on index g // 16 of img; the partners of the 16 images of one index of img include at most 1 images held by any one index of img, and exactly 1 from some. `block_list`: for each device and owner, entries below block_count are ids of that device's blocks; each block of a device is listed exactly once over its owners; entries at or past the count are 0. `block_count`: a device's counts sum to 256; every device has an owner with exactly 128.
All inputs are finite; a program needn't handle non-finite values.
Results may differ from a plain program's by a relative error of at most 0.0003.
Values may be sent and summed in bfloat16 or wider, within the bound.
No kernel may reach another device: no remote copies, remote signals or barrier semaphores. Data moves between devices by JAX's collectives and lax.ppermute only.
A program may use at most 192 MiB of HBM per device.

v0:
```python
import jax
import jax.numpy as jnp
from jax import lax
from jax.sharding import PartitionSpec as P

NDEPTH = 64
CELLS = 128
PATCH_DEV = 16


def with_halo(cells, sides, width):
    for axis, dim in sides:
        count = lax.axis_size(axis)
        ends = count - 1
        head = lax.slice_in_dim(cells, 0, width, axis=dim)
        tail = lax.slice_in_dim(cells, cells.shape[dim] - width, cells.shape[dim], axis=dim)
        cells = jnp.concatenate(
            [
                lax.ppermute(tail, axis, [(i, (i + 1) % count) for i in range(ends)]),
                cells,
                lax.ppermute(head, axis, [((i + 1) % count, i) for i in range(ends)]),
            ],
            axis=dim,
        )
    return cells


def window(values, out_width):
    across = (
        values[..., :, 0:out_width]
        + values[..., :, 1 : out_width + 1]
        + values[..., :, 2 : out_width + 2]
    )
    return across[..., 0:-2, :] + across[..., 1:-1, :] + across[..., 2:, :]


def diagonals(stats, out_width):
    groups, count_of_rows, length = stats.shape
    span = out_width + NDEPTH
    trimmed = stats[:, :, :span]
    spread = jnp.broadcast_to(trimmed[:, :, None, :], (groups, count_of_rows, NDEPTH, span))
    flat = jnp.pad(
        spread.reshape(groups, count_of_rows, NDEPTH * span), ((0, 0), (0, 0), (0, NDEPTH))
    )
    skewed = flat.reshape(groups, count_of_rows, NDEPTH, span + 1)[:, :, :, :out_width]
    return jnp.transpose(skewed, (0, 2, 1, 3))


def sweep(own_ext, other_ext, planes, selected_image):
    channels, count_of_rows, full_width = own_ext.shape
    out_width = full_width - 256
    col_blocks = full_width // 128 - 1
    own_cols = own_ext[:, :, : col_blocks * 128].reshape(channels, count_of_rows, col_blocks, 128)
    other_split = other_ext.reshape(channels, count_of_rows, col_blocks + 1, 128)
    other_cols = jnp.concatenate([other_split[:, :, :-1], other_split[:, :, 1:]], axis=3)
    products = jnp.einsum(
        "crkx,crky->rkxy", own_cols, other_cols, preferred_element_type=jnp.float32
    )
    flattened = jnp.pad(
        products.reshape(count_of_rows, col_blocks, 128 * 256), ((0, 0), (0, 0), (0, 128))
    )
    band_limited = flattened.reshape(count_of_rows, col_blocks, 128, 257)[:, :, :, :NDEPTH]
    band_limited = jnp.transpose(band_limited, (3, 0, 1, 2)).reshape(
        NDEPTH, count_of_rows, col_blocks * 128
    )
    cross_sum = window(band_limited, out_width)
    own_f = own_ext.astype(jnp.float32)
    other_f = other_ext.astype(jnp.float32)
    own_sum = window(jnp.sum(own_f, 0), out_width)
    own_squared_sum = window(jnp.sum(own_f * own_f, 0), out_width)
    other_stats = window(
        jnp.stack([jnp.sum(other_f, 0), jnp.sum(other_f * other_f, 0)]), full_width - 2
    )
    shifted = diagonals(other_stats, out_width)
    other_sum = shifted[0]
    other_sq = shifted[1]
    entries = 9.0 * channels
    mean_own = own_sum / entries
    var_own = own_squared_sum / entries - mean_own * mean_own
    mean_other = other_sum / entries
    var_other = other_sq / entries - mean_other * mean_other
    correlation = (cross_sum / entries - mean_own * mean_other) / jnp.sqrt(
        (var_own + 1e-05) * (var_other + 1e-05)
    )
    weights_exp = jnp.exp(24.0 * correlation)
    likelihood = weights_exp / jnp.sum(weights_exp, 0)
    depth_out = jnp.sum(likelihood * planes[:, None, None], 0)
    matched = jnp.arange(NDEPTH, dtype=jnp.int32)[:, None, None] == selected_image[None]
    confidence = jnp.sum(jnp.where(matched, likelihood, jnp.float32(0.0)), 0)
    plane_at = jnp.sum(jnp.where(matched, planes[:, None, None], jnp.float32(0.0)), 0)
    return (depth_out, confidence, plane_at)


def on_device(
    features,
    partner_ids,
    depth_planes,
    cam_height,
    ray_down,
    depth_index,
    cell_index,
    block_list,
    block_slot,
    block_count,
):
    group_count = lax.axis_size("img")
    my_group = lax.axis_index("img")
    img_dev = features.shape[0]
    cap_slots = -(-img_dev // group_count)
    table = partner_ids.reshape(group_count, img_dev)
    source_of = table // img_dev
    local_idx = table % img_dev
    same_src = source_of[:, :, None] == source_of[:, None, :]
    earlier = jnp.arange(img_dev)[None, :] < jnp.arange(img_dev)[:, None]
    slot_rank = jnp.sum((same_src & earlier[None]).astype(jnp.int32), axis=2)
    matched = (source_of == my_group)[:, :, None] & (
        slot_rank[:, :, None] == jnp.arange(cap_slots)[None, None, :]
    )
    chosen_img = jnp.sum(jnp.where(matched, local_idx[:, :, None], 0), axis=1)
    filled = jnp.any(matched, axis=1)
    own_ext = with_halo(features, (("tile", 2),), 1)
    send_buf = jnp.where(
        filled[:, :, None, None, None], features[chosen_img], jnp.zeros((), features.dtype)
    )
    received = lax.all_to_all(send_buf, "img", split_axis=0, concat_axis=0, tiled=True)
    received = received.reshape((group_count * cap_slots,) + received.shape[2:])
    my_source = lax.dynamic_index_in_dim(source_of, my_group, 0, False)
    my_rank = lax.dynamic_index_in_dim(slot_rank, my_group, 0, False)
    partner_feat = received[my_source * cap_slots + my_rank]
    partner_ext = with_halo(partner_feat, (("tile", 2),), 1)

    def per_image(items):
        return sweep(items[0], items[1], depth_planes, items[2])

    mean_range_per_sample, confidence, plane_at = lax.map(
        per_image, (own_ext, partner_ext, depth_index)
    )
    point_elevation = cam_height[:, None, None] - ray_down * plane_at
    blk_dev = confidence.size // 128
    weighted = (confidence * point_elevation).reshape(-1)
    plain = confidence.reshape(-1)
    segment = (
        jnp.arange(blk_dev, dtype=jnp.int32)[:, None] * CELLS + cell_index.reshape(blk_dev, 128)
    ).reshape(-1)
    block_num = jax.ops.segment_sum(weighted, segment, num_segments=blk_dev * CELLS).reshape(
        blk_dev, CELLS
    )
    block_den = jax.ops.segment_sum(plain, segment, num_segments=blk_dev * CELLS).reshape(
        blk_dev, CELLS
    )
    lists = block_list[0, 0]
    slot_ids = block_slot[0, 0]
    counts = block_count[0, 0]
    usable = jnp.arange(lists.shape[1], dtype=jnp.int32)[None, :] < counts[:, None]
    send_num = jnp.where(usable[:, :, None], block_num[lists], jnp.float32(0.0))
    send_den = jnp.where(usable[:, :, None], block_den[lists], jnp.float32(0.0))
    safe_slots = jnp.where(usable, slot_ids, 0)
    got_num, got_den, got_slots = (
        lax.all_to_all(send_num, "tile", split_axis=0, concat_axis=0, tiled=True),
        lax.all_to_all(send_den, "tile", split_axis=0, concat_axis=0, tiled=True),
        lax.all_to_all(safe_slots, "tile", split_axis=0, concat_axis=0, tiled=True),
    )
    total_rows = group_count * PATCH_DEV
    dense_num = (
        jnp.zeros((total_rows, CELLS), jnp.float32)
        .at[got_slots.reshape(-1)]
        .add(got_num.reshape(-1, CELLS))
    )
    full_weight_totals = (
        jnp.zeros((total_rows, CELLS), jnp.float32)
        .at[got_slots.reshape(-1)]
        .add(got_den.reshape(-1, CELLS))
    )
    terrain_weighted_heights, terrain_weight_totals = (
        lax.psum_scatter(dense_num, "img", scatter_dimension=0, tiled=True),
        lax.psum_scatter(full_weight_totals, "img", scatter_dimension=0, tiled=True),
    )
    terrain_height_grid = terrain_weighted_heights / (terrain_weight_totals + 1.0)
    return (mean_range_per_sample, terrain_height_grid)


def solution(mesh):
    return jax.shard_map(
        on_device,
        mesh=mesh,
        in_specs=(
            P("img", None, "tile", None),
            P(),
            P(),
            P("img"),
            P("img", "tile", None),
            P("img", "tile", None),
            P("img", "tile", None),
            P("img", "tile", None, None),
            P("img", "tile", None, None),
            P("img", "tile", None),
        ),
        out_specs=(P("img", "tile", None), P(("img", "tile"), None)),
        check_vma=False,
    )
```

profile of v0, /device:TPU:1, one launch (start us, length us, event | category | flops | bytes accessed | tf_op | source)
XLA Modules:
  0.0 1568.9 jit_solution(16517791272315847679)
XLA Ops:
  9.1 15.6 gather_fusion
  24.7 11.7 fusion.25
  36.4 8.8 all-to-all-start
  59.0 160.8 %all-to-all-done = bf16[32,1,64,4,768]{4,3,2,1,0:T(4,128)(2,1)} async-done(((bf16[32,1,64,4,768]{4,3,2,1,0:T(4,128)(2,1)}), bf16[32,1,64,4,768]{4,3,2,1,0:T(4,128)(2,1)}, u32[]{:S(2)}, u32[]{:S(2)}) %all-to-all-start) | async-done | bytes 12582944 | tf_op jit(solution)/shard_map/all_to_all | solution.py:125
  219.8 11.8 copy.98
  231.6 8.2 gather_fusion.1
  250.4 5.5 all-to-all-start.1
  257.1 8.3 pad_maximum_fusion.2
  265.4 14.1 collective-permute-done.2
  279.5 5.0 collective-permute-done.3
  284.5 6.2 pad_maximum_fusion.3
  290.7 619.0 %while.16 = (s32[]{:T(128)}, f32[16,4,512]{2,1,0:T(4,128)}, f32[16,4,512]{2,1,0:T(4,128)}, f32[16,4,512]{2,1,0:T(4,128)}, bf16[16,64,6,768]{3,1,2,0:T(8,128)(2,1...) while((s32[]{:T(128)}, f32[16,4,512]{2,1,0:T(4,128)}, ...), condition=%wide.region_12.13_spmd, body=%wide.region_3.12_spmd.sunk | while | flops 133365704 | bytes 59209624 | solution.py:135
  301.9 4.9 reshape.582
  306.8 5.2 pad.82
  311.9 8.4 reshape.583
  345.5 5.2 pad.82
  350.6 8.4 reshape.583
  379.2 4.9 reshape.582
  384.2 5.2 pad.82
  389.3 8.4 reshape.583
  417.9 4.9 reshape.582
  422.8 5.2 pad.82
  428.0 8.4 reshape.583
  456.6 4.9 reshape.582
  461.5 5.2 pad.82
  466.7 8.4 reshape.583
  495.3 4.9 reshape.582
  500.2 5.2 pad.82
  505.4 8.4 reshape.583
  534.0 4.9 reshape.582
  538.9 5.2 pad.82
  544.1 8.4 reshape.583
  572.7 4.9 reshape.582
  577.6 5.2 pad.82
  582.8 8.4 reshape.583
  611.4 4.9 reshape.582
  616.3 5.2 pad.82
  621.5 8.4 reshape.583
  650.1 4.9 reshape.582
  655.0 5.2 pad.82
  660.2 8.4 reshape.583
  688.8 4.9 reshape.582
  693.7 5.2 pad.82
  698.9 8.4 reshape.583
  727.4 4.9 reshape.582
  732.4 5.2 pad.82
  737.5 8.4 reshape.583
  766.1 4.9 reshape.582
  771.1 5.2 pad.82
  776.2 8.4 reshape.583
  804.8 4.9 reshape.582
  809.7 5.2 pad.82
  814.9 8.4 reshape.583
  843.5 4.9 reshape.582
  848.4 5.2 pad.82
  853.6 8.4 reshape.583
  887.1 5.2 pad.82
  892.3 8.4 reshape.583
  911.9 226.9 %scatter_custom_fusion = f32[32768]{0:T(1024)S(1)} fusion(s32[32768]{0:T(1024)} %bitcast.137, f32[32768]{0:T(1024)S(1)} %bitcast.140, f32[]{:T(128)} %constant.112.clone.1), kind=kCustom, calls=%fused_computation.88 | custom fusion | flops 32768 | bytes 131584 | tf_op jit(solution)/shard_map/scatter-add | solution.py:145
  1138.8 226.7 %scatter_custom_fusion.2 = f32[32768]{0:T(1024)S(1)} fusion(s32[32768]{0:T(1024)} %bitcast.138, f32[32768]{0:T(1024)S(1)} %bitcast.139, f32[]{:T(128)} %constant.112.clone.1), kind=kCustom, calls=%fused_computation.86 | custom fusion | flops 32768 | bytes 131584 | tf_op jit(solution)/shard_map/scatter-add | solution.py:148
  1372.0 5.5 all-to-all-done.3
  1381.4 7.9 all_to_all.21
  1393.2 87.9 %reduce-scatter.5.cloned.1.call-done = f32[16,128]{1,0:T(8,128)} async-done(((f32[512,128]{1,0:T(8,128)}), f32[16,128]{1,0:T(8,128)}) %reduce-scatter.5.cloned.1.call-update) | async-done | bytes 8208 | tf_op jit(solution)/shard_map/reduce_scatter | solution.py:176
  1481.1 79.7 %reduce-scatter.3.cloned.1.call-done = f32[16,128]{1,0:T(8,128)} async-done(((f32[512,128]{1,0:T(8,128)}), f32[16,128]{1,0:T(8,128)}) %reduce-scatter.3.cloned.1.call-update) | async-done | bytes 8208 | tf_op jit(solution)/shard_map/reduce_scatter | solution.py:175
  (485 shorter events, 376.2 us)
Async XLA Ops:
  36.4 183.4 %all-to-all-start = ((bf16[32,1,64,4,768]{4,3,2,1,0:T(4,128)(2,1)}), bf16[32,1,64,4,768]{4,3,2,1,0:T(4,128)(2,1)}, u32[]{:S(2)}, u32[]{:S(2)}) async-start(bf16[32,1,64,4,768]{4,3,2,1,0:T(4,128)(2,1)} %fusion.25), calls=%async_computation | async-start | bytes 25165824 | tf_op jit(solution)/shard_map/all_to_all | solution.py:125
  49.3 2.7 copy-start
  53.8 203.2 %collective-permute-start = (bf16[16,64,1,768]{3,1,2,0:T(8,128)(2,1)}, bf16[16,64,1,768]{3,1,2,0:T(8,128)(2,1)S(1)}, u32[]{:S(2)}, u32[]{:S(2)}) collective-permute-start(bf16[16,64,1,768]{3,1,2,0:T(8,128)(2,1)} %get-tuple-element.147), channel_id=1, source_target_pairs={{0,1},{1,2},{2,3},{4,5},{5,6},{6,7},{8,9},{9,10},{10,11},{12,13},{... | collective-permute-start | bytes 4718600 | tf_op jit(solution)/shard_map/ppermute | solution.py:19
  57.5 199.6 %collective-permute-start.1 = (bf16[16,64,1,768]{3,1,2,0:T(8,128)(2,1)}, bf16[16,64,1,768]{3,1,2,0:T(8,128)(2,1)S(1)}, u32[]{:S(2)}, u32[]{:S(2)}) collective-permute-start(bf16[16,64,1,768]{3,1,2,0:T(8,128)(2,1)} %get-tuple-element.148), channel_id=1, source_target_pairs={{1,0},{2,1},{3,2},{5,4},{6,5},{7,6},{9,8},{10,9},{11,10},{13,12},{... | collective-permute-start | bytes 4718600 | tf_op jit(solution)/shard_map/ppermute | solution.py:21
  239.8 9.9 copy-start.2
  239.8 9.9 copy-start.5
  239.8 16.1 %copy-start.1 = (s32[16,4,512]{2,1,0:T(4,128)S(1)}, s32[16,4,512]{2,1,0:T(4,128)}, u32[]{:S(2)}) copy-start(s32[16,4,512]{2,1,0:T(4,128)} %param.18) | copy-start | bytes 393220
  239.8 17.1 %copy-start.3 = (s32[1,1,4,128]{3,2,1,0:T(4,128)S(1)}, s32[1,1,4,128]{3,2,1,0:T(4,128)}, u32[]{:S(2)}) copy-start(s32[1,1,4,128]{3,2,1,0:T(4,128)} %param.19) | copy-start | bytes 6148
  243.8 35.8 %collective-permute-start.2 = (bf16[16,64,1,768]{3,1,2,0:T(8,128)(2,1)}, bf16[16,64,1,768]{3,1,2,0:T(8,128)(2,1)}, u32[]{:S(2)}, u32[]{:S(2)}) collective-permute-start(bf16[16,64,1,768]{3,1,2,0:T(8,128)(2,1)} %get-tuple-element.145), channel_id=1, source_target_pairs={{0,1},{1,2},{2,3},{4,5},{5,6},{6,7},{8,9},{9,10},{10,11},{12,13},{... | collective-permute-start | bytes 4718600 | tf_op jit(solution)/shard_map/ppermute | solution.py:19
  248.5 36.0 %collective-permute-start.3 = (bf16[16,64,1,768]{3,1,2,0:T(8,128)(2,1)}, bf16[16,64,1,768]{3,1,2,0:T(8,128)(2,1)}, u32[]{:S(2)}, u32[]{:S(2)}) collective-permute-start(bf16[16,64,1,768]{3,1,2,0:T(8,128)(2,1)} %get-tuple-element.146), channel_id=1, source_target_pairs={{1,0},{2,1},{3,2},{5,4},{6,5},{7,6},{9,8},{10,9},{11,10},{13,12},{... | collective-permute-start | bytes 4718600 | tf_op jit(solution)/shard_map/ppermute | solution.py:21
  250.4 1118.0 %all-to-all-start.1 = ((s32[4,1,128]{2,1,0:T(1,128)}), s32[4,1,128]{2,1,0:T(1,128)S(1)}, u32[]{:S(2)}, u32[]{:S(2)}) async-start(s32[4,1,128]{2,1,0:T(1,128)} %compare_select_fusion.1), calls=%async_computation.1 | async-start | bytes 4096 | tf_op jit(solution)/shard_map/all_to_all | solution.py:161
  257.0 27.5 %slice-start = ((s8[6291456]{0:T(1024)(128)(4,1)}), s8[4194304]{0:T(1024)(128)(4,1)S(1)}, s32[]{:S(2)}) async-start(s8[6291456]{0:T(1024)(128)(4,1)} %bitcast.124), calls=%async_computation.8 | async-start | bytes 8388608
  257.1 27.5 %slice-start.1 = ((s8[6291456]{0:T(1024)(128)(4,1)}), s8[2097152]{0:T(1024)(128)(4,1)S(1)}, s32[]{:S(2)}) async-start(s8[6291456]{0:T(1024)(128)(4,1)} %bitcast.124), calls=%async_computation.9 | async-start | bytes 4194304
  290.7 619.1 %copy-start.4 = (f32[16]{0:T(128)S(1)}, f32[16]{0:T(128)}, u32[]{:S(2)}) copy-start(f32[16]{0:T(128)} %param.15) | copy-start | bytes 196
  1368.5 8.9 all-to-all-start.3
  1371.9 109.2 %reduce-scatter.5.cloned.1.call-start = ((), (), s32[]{:S(2)}) async-start(), calls=%async_computation.7 | async-start | bytes 270336 | tf_op jit(solution)/shard_map/reduce_scatter | solution.py:176
  1381.3 179.4 %reduce-scatter.3.cloned.1.call-start = ((), (), s32[]{:S(2)}) async-start(), calls=%async_computation.6 | async-start | bytes 270336 | tf_op jit(solution)/shard_map/reduce_scatter | solution.py:175
Sparse Core Ops, SparseCore 0:
  1381.5 99.5 reduce-scatter.4
  1484.5 76.1 reduce-scatter.2
where the time goes:
time: 1580 us; the launch traced here: 1570 us
  other arithmetic  611 us (39%)
  local copies, waits for them, and re-layouts  509 us (32%)
  waiting for transfers between devices  353 us (22%)
  matrix products  43.2 us (3%)
  starting transfers between devices  28.6 us (2%)
    scatter-add x1, other arithmetic, on_device(): jax.ops.segment_sum(weighted, segment, num_segments=blk_dev * CELLS)  227 us
    scatter-add x1, other arithmetic, on_device(): jax.ops.segment_sum(plain, segment, num_segments=blk_dev * CELLS)  227 us
    all_to_all x1, waiting for transfers between devices, on_device(): lax.all_to_all(send_buf, 'img', split_axis=0, concat_axis=0, tiled=True)  161 us
    reshape x16, local copies, waits for them, and re-layouts, sweep(): flattened.reshape(count_of_rows, col_blocks, 128, 257)[:, :, :, :NDEPTH]  134 us
    reduce_scatter x1, waiting for transfers between devices, on_device(): lax.psum_scatter(full_weight_totals, 'img', scatter_dimension=0, tiled=True)  87.9 us
    pad x16, local copies, waits for them, and re-layouts, sweep(): jnp.pad(products.reshape(count_of_rows, col_blocks, 128 * 256), ((0, 0),...  82.7 us
    reduce_scatter x1, waiting for transfers between devices, on_device(): lax.psum_scatter(dense_num, 'img', scatter_dimension=0, tiled=True)  79.7 us
    reshape x16, local copies, waits for them, and re-layouts, sweep(): products.reshape(count_of_rows, col_blocks, 128 * 256)  78.8 us
  transfers between devices with their start and end apart: 9, of which 6 were waited for; matrix products, arithmetic and copies ran while one was open for 72% of the time, Pallas kernels for 0%

commit v1 on v0

v1 whole, which is shorter than its diff:
```python
import math

import numpy as np
import jax
import jax.numpy as jnp
from jax import lax
from jax.experimental import pallas as pl
from jax.experimental.pallas import tpu as pltpu
from jax.sharding import PartitionSpec as P

NDEPTH = 64
CELLS = 128
PATCH_DEV = 16
STEPS = 4
WIN = 144
LOG2E = math.log2(math.e)
BF = jnp.bfloat16
F32 = jnp.float32
NT = (((1,), (1,)), ((), ()))


def dot(a, b):
    return jnp.dot(a, b, preferred_element_type=F32)


def dot_nt(a, b):
    return lax.dot_general(a, b, NT, preferred_element_type=F32)


def table_patterns():
    pat = np.zeros((128, 12, 128), np.float32)
    for half in range(2):
        lanes = slice(64 * half, 64 * half + 64)
        for y in range(4):
            for q in range(2):
                for s in range(3):
                    pat[half * 32 + s * 8 + q * 4 + y, y * 3 + q, lanes] = 1.0
            pat[half * 32 + 24 + y, y * 3 + 2, lanes] = 1.0
    return jnp.asarray(pat.reshape(128, 12 * 128), BF)


def row_masks():
    y = np.arange(16)[:, None]
    k = np.arange(256)[None, :] % 4
    return jnp.asarray((np.abs(k - y) <= 1) & (y < 4), BF)


def flips():
    m = np.zeros((128, 128), np.float32)
    for i in range(128):
        m[i, i // 64 * 64 + 63 - i % 64] = 1.0
    return jnp.asarray(m, BF)


def reversal():
    m = np.zeros((WIN, 256), np.float32)
    for i in range(WIN):
        m[i, WIN - 1 - i] = 1.0
    return jnp.asarray(m, BF)


def edge_constants():
    sel = np.zeros((128, 256), np.float32)
    for c in range(64):
        sel[c, 4 * c] = 1.0
        sel[64 + c, 4 * c + 3] = 1.0
    stat = np.zeros((16, 256), np.float32)
    for y in range(4):
        stat[y, y::4] = 1.0
        stat[12 + y, y::4] = 1.0
    return jnp.asarray(sel, BF), jnp.asarray(stat, BF)


def split2(a):
    high = a.astype(BF)
    return high, (a - high.astype(F32)).astype(BF)


def boxed_stats(stats, up, down):
    upf = up.astype(F32)
    downf = down.astype(F32)
    sums = [jnp.sum(upf, 0, keepdims=True)] + [stats[y : y + 1] for y in range(4)]
    sums.append(jnp.sum(downf, 0, keepdims=True))
    sqs = [jnp.sum(upf * upf, 0, keepdims=True)] + [stats[4 + y : 5 + y] for y in range(4)]
    sqs.append(jnp.sum(downf * downf, 0, keepdims=True))
    tall = jnp.concatenate(
        [v[y] + v[y + 1] + v[y + 2] for v in (sums, sqs) for y in range(4)], axis=0
    )
    boxed = (tall + pltpu.roll(tall, 255, 1) + pltpu.roll(tall, 254, 1)) * (1.0 / 576.0)
    mean = boxed[0:4]
    return mean, lax.rsqrt(boxed[4:8] - mean * mean + 1e-5)


def pick_kernel(blocks, idx_ref, strip_ref, out_ref):
    for j in range(blocks):
        out_ref[0, j] = strip_ref[0, :, :, 128 * j : 128 * j + 128]


def pick(idx, features, first, blocks):
    count = idx.shape[0]
    images, channels, rows, _ = features.shape

    def kernel(*refs):
        pick_kernel(blocks, *refs)

    out = pl.pallas_call(
        kernel,
        grid_spec=pltpu.PrefetchScalarGridSpec(
            num_scalar_prefetch=1,
            grid=(count,),
            in_specs=[
                pl.BlockSpec(
                    (1, channels, rows, 128 * blocks), lambda s, r: (r[s], 0, 0, first // blocks)
                )
            ],
            out_specs=pl.BlockSpec((1, blocks, channels, rows, 128), lambda s, r: (s, 0, 0, 0, 0)),
        ),
        out_shape=jax.ShapeDtypeStruct((count, blocks, channels, rows, 128), BF),
        cost_estimate=pl.CostEstimate(
            flops=0, bytes_accessed=count * blocks * 131072, transcendentals=0
        ),
        name="pick",
    )(idx, features)
    return out.reshape(count, blocks, channels * rows, 128)


def edge_kernel(slot_ref, block_ref, sel_ref, stat_ref, head_ref, tail_ref, stats_ref):
    for j in range(block_ref.shape[1]):
        block = block_ref[0, j]
        rows = dot(sel_ref[...], block).astype(BF)
        head_ref[0, j] = rows[0:64]
        tail_ref[0, j] = rows[64:128]
        value = block.astype(F32)
        high, low = split2(value * value)
        stats_ref[0, j] = (
            dot(stat_ref[0:8], block) + dot(stat_ref[8:16], high) + dot(stat_ref[8:16], low)
        )


def edges(slot, recv):
    images = slot.shape[0]
    blocks = recv.shape[1]
    sel, stat = edge_constants()
    return pl.pallas_call(
        edge_kernel,
        grid_spec=pltpu.PrefetchScalarGridSpec(
            num_scalar_prefetch=1,
            grid=(images,),
            in_specs=[
                pl.BlockSpec((1, blocks, 256, 128), lambda k, s: (s[k], 0, 0, 0)),
                pl.BlockSpec((128, 256), lambda k, s: (0, 0)),
                pl.BlockSpec((16, 256), lambda k, s: (0, 0)),
            ],
            out_specs=[
                pl.BlockSpec((1, blocks, 64, 128), lambda k, s: (k, 0, 0, 0)),
                pl.BlockSpec((1, blocks, 64, 128), lambda k, s: (k, 0, 0, 0)),
                pl.BlockSpec((1, blocks, 8, 128), lambda k, s: (k, 0, 0, 0)),
            ],
        ),
        out_shape=[
            jax.ShapeDtypeStruct((images, blocks, 64, 128), BF),
            jax.ShapeDtypeStruct((images, blocks, 64, 128), BF),
            jax.ShapeDtypeStruct((images, blocks, 8, 128), F32),
        ],
        cost_estimate=pl.CostEstimate(
            flops=images * blocks * 20_000_000, bytes_accessed=images * blocks * 100_000,
            transcendentals=0,
        ),
        name="edges",
    )(slot, recv, sel, stat)


def prepare_kernel(
    own_ref, up_ref, down_ref, stat_ref, index_ref, rev_ref, flip_ref, own_out, edge_out, table_out
):
    mean_inv = 24.0 * LOG2E
    for n in range(STEPS):
        block = jnp.concatenate([own_ref[0, n], own_ref[0, n + 1]], axis=1)
        up = jnp.concatenate([up_ref[0, n], up_ref[0, n + 1]], axis=1)
        down = jnp.concatenate([down_ref[0, n], down_ref[0, n + 1]], axis=1)
        own_out[0, n] = dot_nt(rev_ref[...], block).astype(BF)
        edge_out[0, n] = dot_nt(rev_ref[...], jnp.concatenate([up, down], axis=0)).astype(BF)
        stats = jnp.concatenate([stat_ref[0, n], stat_ref[0, n + 1]], axis=1)
        mean, inv = boxed_stats(stats, up, down)
        scaled = inv * mean_inv
        both = jnp.concatenate([scaled * (1.0 / 576.0), scaled * mean], axis=0)[:, :128]
        high = both.astype(BF).astype(F32)
        mid = (both - high).astype(BF).astype(F32)
        index = index_ref[0, :, 128 * n : 128 * n + 128].astype(F32)
        rows = jnp.concatenate(
            [high, mid, both - high - mid, index, jnp.zeros((4, 128), F32)], axis=0
        ).astype(BF)
        blank = jnp.zeros((64, 64), F32)
        left = dot_nt(flip_ref[0:64, :], rows)
        right = dot_nt(flip_ref[64:128, :], rows)
        table_out[0, n] = jnp.concatenate([left, right, blank], axis=1).astype(BF)


def prepare(own, up, down, stats, depth_index):
    images, blocks = own.shape[0], own.shape[1]
    return pl.pallas_call(
        prepare_kernel,
        grid=(images,),
        in_specs=[
            pl.BlockSpec((1, blocks, 256, 128), lambda k: (k, 0, 0, 0)),
            pl.BlockSpec((1, blocks, 64, 128), lambda k: (k, 0, 0, 0)),
            pl.BlockSpec((1, blocks, 64, 128), lambda k: (k, 0, 0, 0)),
            pl.BlockSpec((1, blocks, 8, 128), lambda k: (k, 0, 0, 0)),
            pl.BlockSpec((1, 4, 512), lambda k: (k, 0, 0)),
            pl.BlockSpec((WIN, 256), lambda k: (0, 0)),
            pl.BlockSpec((128, 128), lambda k: (0, 0)),
        ],
        out_specs=[
            pl.BlockSpec((1, STEPS, WIN, 256), lambda k: (k, 0, 0, 0)),
            pl.BlockSpec((1, STEPS, WIN, 128), lambda k: (k, 0, 0, 0)),
            pl.BlockSpec((1, STEPS, 64, 128), lambda k: (k, 0, 0, 0)),
        ],
        out_shape=[
            jax.ShapeDtypeStruct((images, STEPS, WIN, 256), BF),
            jax.ShapeDtypeStruct((images, STEPS, WIN, 128), BF),
            jax.ShapeDtypeStruct((images, STEPS, 64, 128), BF),
        ],
        cost_estimate=pl.CostEstimate(
            flops=images * STEPS * 40_000_000, bytes_accessed=images * 1_000_000, transcendentals=0
        ),
        name="prepare",
    )(own, up, down, stats, depth_index, reversal(), flips())


def sweep_kernel(
    slot_ref, own_ref, oh_ref, o0_ref, o1_ref, u0_ref, u1_ref, d0_ref, d1_ref, s0_ref, s1_ref,
    sl_ref, pat_ref, mask_ref, w2_ref, flip_ref, elev_ref, cell_ref, mean_ref, rows_ref, skew,
):
    rhs = jnp.concatenate([o0_ref[0, 0], o1_ref[0, 0]], axis=1)
    up = jnp.concatenate([u0_ref[0, 0], u1_ref[0, 0]], axis=1)
    down = jnp.concatenate([d0_ref[0, 0], d1_ref[0, 0]], axis=1)
    own = own_ref[0, 0]
    own_edge = oh_ref[0, 0]
    stats = jnp.concatenate([s0_ref[0, 0], s1_ref[0, 0]], axis=1)

    mean_b, inv_b = boxed_stats(stats, up, down)

    column = 63 - lax.broadcasted_iota(jnp.int32, (64, 128), 0)
    lane = lax.broadcasted_iota(jnp.int32, (64, 128), 1)
    wrapped = lane < column
    first = lane < column + 64
    column8 = 7 - lax.broadcasted_iota(jnp.int32, (8, 128), 0)
    lane8 = lax.broadcasted_iota(jnp.int32, (8, 128), 1)
    hyp = (lane % 64).astype(F32)

    table = dot(sl_ref[0, 0], pat_ref[...])

    soft = []
    chosen = []
    for y in range(4):
        p = dot(own * mask_ref[y : y + 1, :], rhs)
        if y == 0:
            p = p + dot(own_edge[:, 0:64], up)
        if y == 3:
            p = p + dot(own_edge[:, 64:128], down)
        z = jnp.where(wrapped, p[16:80, 128:], jnp.where(first, p[80:144, :128], p[16:80, :128]))
        z8 = jnp.where(
            lane8 < column8,
            p[72:80, 128:],
            jnp.where(lane8 < column8 + 64, p[8:16, 128:], p[72:80, :128]),
        )
        skew[y, 0:8, :] = pltpu.roll(z8, 57, 1, stride=1, stride_axis=0)
        skew[y, 8:72, :] = pltpu.roll(z, 65, 1, stride=1, stride_axis=0)
        cross = skew[y, 8:72, :] + skew[y, 7:71, :] + skew[y, 6:70, :]
        mb = pltpu.roll(
            jnp.where(wrapped, mean_b[y : y + 1, 128:], mean_b[y : y + 1, :128]),
            65, 1, stride=1, stride_axis=0,
        )
        rb = pltpu.roll(
            jnp.where(wrapped, inv_b[y : y + 1, 128:], inv_b[y : y + 1, :128]),
            65, 1, stride=1, stride_axis=0,
        )
        a1 = table[:, (3 * y) * 128 : (3 * y + 1) * 128]
        a2 = table[:, (3 * y + 1) * 128 : (3 * y + 2) * 128]
        at = table[:, (3 * y + 2) * 128 : (3 * y + 3) * 128]
        weight = jnp.exp2((cross * a1 - a2 * mb) * rb)
        picked = jnp.where(at == hyp, weight, 0.0)
        for value, out in ((weight, soft), (picked, chosen)):
            high = value.astype(BF)
            low = (value - high.astype(F32)).astype(BF)
            out.append(jnp.concatenate([high, low], axis=1))
    soft = jnp.concatenate(soft, axis=0)
    chosen = jnp.concatenate(chosen, axis=0)
    w2 = w2_ref[...]
    r = lax.dot_general(w2, soft, NT, preferred_element_type=F32)
    rc = lax.dot_general(w2, chosen, NT, preferred_element_type=F32)
    inv = 1.0 / r[0:2]
    depth = (r[2:4] + r[4:6] + r[6:8]) * inv
    conf = rc[0:2] * inv
    both = jnp.concatenate([depth, conf], axis=0)
    high = both.astype(BF).astype(F32)
    mid = (both - high).astype(BF).astype(F32)
    pieces = jnp.concatenate([high, mid, both - high - mid, jnp.zeros((4, 256), F32)], axis=0)
    pieces = jnp.concatenate([pieces[:, :128], pieces[:, 128:]], axis=0).astype(BF)
    flipped = dot(pieces, flip_ref[...])
    both = jnp.concatenate([flipped[0:16], flipped[16:32]], axis=1)
    both = both[0:4] + both[4:8] + both[8:12]
    lane1 = lax.broadcasted_iota(jnp.int32, (1, 128), 1)
    left = lane1 < 64
    cell_iota = lax.broadcasted_iota(jnp.int32, (128, 128), 0)
    for y in range(4):
        part = both[:, 128 * (y // 2) : 128 * (y // 2) + 128]
        turned = pltpu.roll(part, 64, 1)
        if y % 2 == 0:
            lo, hi = part, turned
        else:
            lo, hi = turned, part
        mean_ref[0, y : y + 1, :] = jnp.where(left, lo[0:1], hi[1:2])
        c = jnp.where(left, lo[2:3], hi[3:4])
        num = c * elev_ref[0, y : y + 1, :]
        pair = jnp.concatenate([num, c], axis=0)
        pair_hi = pair.astype(BF).astype(F32)
        vals = jnp.concatenate([pair_hi, pair - pair_hi, jnp.zeros((4, 128), F32)], axis=0)
        hot = jnp.where(cell_iota == cell_ref[0, y : y + 1, :], 1.0, 0.0).astype(BF)
        binned = lax.dot_general(vals.astype(BF), hot, NT, preferred_element_type=F32)
        got = binned[0:2] + binned[2:4]
        rows_ref[0, 0, y : y + 1, 0:128] = got[0:1]
        rows_ref[0, 0, y : y + 1, 128:256] = got[1:2]


def sweep_steps(first_step, steps, slot, ownT, ohT, o0, o1, up, down, stats, sl, pat, masks, w2, flip, elev, cell, o1_by_slot):
    images = ownT.shape[0]
    st = first_step
    in_specs = [
        pl.BlockSpec((1, 1, 144, 256), lambda n, k, s: (k, n + st, 0, 0)),
        pl.BlockSpec((1, 1, 144, 128), lambda n, k, s: (k, n + st, 0, 0)),
        pl.BlockSpec((1, 1, 256, 128), lambda n, k, s: (s[k], n + st, 0, 0)),
        pl.BlockSpec((1, 1, 256, 128), (lambda n, k, s: (s[k], n + st + 1, 0, 0)) if o1_by_slot else (lambda n, k, s: (s[k], 0, 0, 0))),
    ]
    u0, u1 = up
    d0, d1 = down
    s0, s1 = stats
    near = lambda n, k, s: (k, n + st, 0, 0)
    far = (lambda n, k, s: (k, n + st + 1, 0, 0)) if o1_by_slot else (lambda n, k, s: (k, 0, 0, 0))
    in_specs += [
        pl.BlockSpec((1, 1, 64, 128), near), pl.BlockSpec((1, 1, 64, 128), far),
        pl.BlockSpec((1, 1, 64, 128), near), pl.BlockSpec((1, 1, 64, 128), far),
        pl.BlockSpec((1, 1, 8, 128), near), pl.BlockSpec((1, 1, 8, 128), far),
        pl.BlockSpec((1, 1, 64, 128), near),
        pl.BlockSpec((128, 1536), lambda n, k, s: (0, 0)),
        pl.BlockSpec((16, 256), lambda n, k, s: (0, 0)),
        pl.BlockSpec((8, 256), lambda n, k, s: (0, 0)),
        pl.BlockSpec((128, 128), lambda n, k, s: (0, 0)),
        pl.BlockSpec((1, 4, 128), lambda n, k, s: (k, 0, n + st)),
        pl.BlockSpec((1, 4, 128), lambda n, k, s: (k, 0, n + st)),
    ]
    return pl.pallas_call(
        sweep_kernel,
        grid_spec=pltpu.PrefetchScalarGridSpec(
            num_scalar_prefetch=1,
            grid=(steps, images),
            in_specs=in_specs,
            out_specs=[
                pl.BlockSpec((1, 4, 128), lambda n, k, s: (k, 0, n)),
                pl.BlockSpec((1, 1, 4, 256), lambda n, k, s: (n, k, 0, 0)),
            ],
            scratch_shapes=[pltpu.VMEM((4, 72, 128), F32)],
        ),
        out_shape=[
            jax.ShapeDtypeStruct((images, 4, steps * 128), F32),
            jax.ShapeDtypeStruct((steps, images, 4, 256), F32),
        ],
        compiler_params=pltpu.CompilerParams(vmem_limit_bytes=32 * 1024 * 1024),
        cost_estimate=pl.CostEstimate(flops=steps * images * 200_000_000, bytes_accessed=steps * images * 400_000, transcendentals=0),
        name="sweep",
    )(slot, ownT, ohT, o0, o1, u0, u1, d0, d1, s0, s1, sl, pat, masks, w2, flip, elev, cell)


def depth_weights(planes):
    high = lax.reduce_precision(planes, 8, 7)
    mid = lax.reduce_precision(planes - high, 8, 7)
    zero = jnp.zeros_like(planes)
    rows = []
    for v in (jnp.ones_like(planes), high, mid, planes - high - mid):
        rows.append(jnp.concatenate([v, zero]))
        rows.append(jnp.concatenate([zero, v]))
    w = jnp.stack(rows)
    return jnp.concatenate([w, w], axis=1).astype(BF)


def collect_kernel(list_ref, count_ref, rows_ref, out_ref):
    owners = out_ref.shape[0]
    for o in range(owners):

        def move(e, carry):
            out_ref[o, pl.ds(e, 1), :] = rows_ref[pl.ds(list_ref[o, e], 1), :]
            return carry

        lax.fori_loop(0, count_ref[o], move, 0)


def collect(row_list, counts, rows):
    owners, cap = row_list.shape
    return pl.pallas_call(
        collect_kernel,
        grid_spec=pltpu.PrefetchScalarGridSpec(
            num_scalar_prefetch=2,
            grid=(1,),
            in_specs=[pl.BlockSpec(rows.shape, lambda i, a, b: (0, 0))],
            out_specs=pl.BlockSpec((owners, cap, 2 * CELLS), lambda i, a, b: (0, 0, 0)),
        ),
        out_shape=jax.ShapeDtypeStruct((owners, cap, 2 * CELLS), F32),
        name="collect",
    )(row_list, counts, rows)


def place_kernel(slot_ref, count_ref, got_ref, out_ref):
    out_ref[...] = jnp.zeros_like(out_ref)
    for t in range(got_ref.shape[0]):

        def add(e, carry):
            at = pl.ds(slot_ref[t, e], 1)
            out_ref[at, :] = out_ref[at, :] + got_ref[t, pl.ds(e, 1), :]
            return carry

        lax.fori_loop(0, count_ref[t], add, 0)


def place(slots, counts, got, total):
    return pl.pallas_call(
        place_kernel,
        grid_spec=pltpu.PrefetchScalarGridSpec(
            num_scalar_prefetch=2,
            grid=(1,),
            in_specs=[pl.BlockSpec(got.shape, lambda i, a, b: (0, 0, 0))],
            out_specs=pl.BlockSpec((total, 2 * CELLS), lambda i, a, b: (0, 0)),
        ),
        out_shape=jax.ShapeDtypeStruct((total, 2 * CELLS), F32),
        name="place",
    )(slots, counts, got)


def neighbour_rows(head, tail):
    count = lax.axis_size("tile")
    above = lax.ppermute(tail, "tile", [(i, i + 1) for i in range(count - 1)])
    below = lax.ppermute(head, "tile", [(i + 1, i) for i in range(count - 1)])
    return above, below


def on_device(
    features, partner_ids, depth_planes, cam_height, ray_down, depth_index, cell_index,
    block_list, block_slot, block_count,
):
    group_count = lax.axis_size("img")
    owners = lax.axis_size("tile")
    my_group = lax.axis_index("img")
    my_tile = lax.axis_index("tile")
    images = features.shape[0]
    table = partner_ids.reshape(group_count, images)
    source_of = table // images
    chosen = jnp.sum(jnp.where(source_of == my_group, table % images, 0), axis=1)
    slot = lax.dynamic_index_in_dim(source_of, my_group, 0, False)

    def exchange(a):
        return lax.all_to_all(a, "img", split_axis=0, concat_axis=0, tiled=True)

    main = exchange(pick(chosen, features, 0, 4))
    last = exchange(pick(chosen, features, 4, 1))

    every = jnp.arange(images, dtype=jnp.int32)
    own = jnp.concatenate([pick(every, features, 0, 4), pick(every, features, 4, 1)], axis=1)
    own_head, own_tail, own_stats = edges(every, own)
    own_up, own_down = neighbour_rows(own_head, own_tail)
    own_turned, edge_turned, own_table = prepare(own, own_up, own_down, own_stats, depth_index)

    hyp = jnp.arange(NDEPTH, dtype=jnp.int32)[:, None, None, None]
    plane_at = jnp.sum(
        jnp.where(hyp == depth_index[None], depth_planes[:, None, None, None], 0.0), 0
    )
    elevation = cam_height[:, None, None] - ray_down * plane_at

    meta = jnp.concatenate(
        [block_slot[0, 0], jnp.broadcast_to(block_count[0, 0][:, None], (owners, 128))], axis=1
    )
    metas = [lax.dynamic_slice_in_dim(meta, my_tile, 1, 0)]
    for s in range(1, owners):
        mine = lax.dynamic_slice_in_dim(meta, (my_tile + s) % owners, 1, 0)
        metas.append(lax.ppermute(mine, "tile", [(i, (i + s) % owners) for i in range(owners)]))
    metas = jnp.concatenate(metas, axis=0)
    metas = jnp.take(metas, (my_tile - jnp.arange(owners)) % owners, axis=0)

    w2 = depth_weights(depth_planes)
    pat, masks, flip = table_patterns(), row_masks(), flips()

    head, tail, stats = edges(slot, main)
    up, down = neighbour_rows(head, tail)
    common = (own_table, pat, masks, w2, flip, elevation, cell_index)
    mean_a, rows_a = sweep_steps(
        0, 3, slot, own_turned, edge_turned, main, main, (up, up), (down, down), (stats, stats),
        *common, True,
    )
    head_l, tail_l, stats_l = edges(slot, last)
    up_l, down_l = neighbour_rows(head_l, tail_l)
    mean_b, rows_b = sweep_steps(
        3, 1, slot, own_turned, edge_turned, main, last, (up, up_l), (down, down_l),
        (stats, stats_l), *common, False,
    )
    mean_range = jnp.concatenate([mean_a, mean_b], axis=2)
    rows = jnp.concatenate([rows_a, rows_b], axis=0).reshape(-1, 2 * CELLS)

    lists = block_list[0, 0]
    blocks_per_step = rows.shape[0] // STEPS
    send = collect(lists % STEPS * blocks_per_step + lists // STEPS, block_count[0, 0], rows)
    got = lax.all_to_all(send, "tile", split_axis=0, concat_axis=0, tiled=True)
    dense = place(metas[:, :128], metas[:, 128], got, group_count * PATCH_DEV)
    parts = exchange(dense.reshape(group_count, PATCH_DEV, 2 * CELLS))
    total = jnp.sum(parts, axis=0)
    return mean_range, total[:, :CELLS] / (total[:, CELLS:] + 1.0)


def solution(mesh):
    return jax.shard_map(
        on_device,
        mesh=mesh,
        in_specs=(
            P("img", None, "tile", None),
            P(),
            P(),
            P("img"),
            P("img", "tile", None),
            P("img", "tile", None),
            P("img", "tile", None),
            P("img", "tile", None, None),
            P("img", "tile", None, None),
            P("img", "tile", None),
        ),
        out_specs=(P("img", "tile", None), P(("img", "tile"), None)),
        check_vma=False,
    )
```

time: 1580 us -> 344 us (0.22)
  other arithmetic: 611 us -> 11.9 us
  local copies, waits for them, and re-layouts: 509 us -> 15.9 us
  waiting for transfers between devices: 353 us -> 55.8 us
  Pallas kernels: 0 us -> 185 us
  matrix products: 43.2 us -> 0 us
  starting transfers between devices: 28.6 us -> 68.9 us
    scatter-add x4 -> x0, other arithmetic: 461 us -> none  [the longest x1 227 us: on_device(): jax.ops.segment_sum(weighted, segment, num_segments=blk_dev * CELLS)]
    reshape x101 -> x2, local copies, waits for them, and re-layouts: 268 us -> 1.56 us  [the longest x1 0.81 us: on_device(): rows = jnp.concatenate([rows_a, rows_b], axis=0).reshape(-1, 2 * CELLS)]
    pallas_call x0 -> x12, Pallas kernels: none -> 185 us  [the longest x2 67.5 us: sweep_steps(): pl.pallas_call(sweep_kernel, grid_spec=pltpu.PrefetchScalarGridSpec(num_s...]
    reduce_scatter x2 -> x0, waiting for transfers between devices: 168 us -> none  [the longest x1 87.9 us: on_device(): lax.psum_scatter(full_weight_totals, 'img', scatter_dimension=0, tiled=True)]
    all_to_all x3 -> x4, waiting for transfers between devices: 166 us -> 55.8 us  [the longest x3 52.1 us: exchange(): return lax.all_to_all(a, 'img', split_axis=0, concat_axis=0, tiled=True)]
    pad x32 -> x0, local copies, waits for them, and re-layouts: 86 us -> none  [the longest x16 82.7 us: sweep(): jnp.pad(products.reshape(count_of_rows, col_blocks, 128 * 256), ((0, 0),...]
    transpose x48 -> x0, local copies, waits for them, and re-layouts: 62.9 us -> none  [the longest x32 45.3 us: sweep(): jnp.transpose(band_limited, (3, 0, 1, 2))]
    reduce_sum x34 -> x3, other arithmetic: 51.4 us -> 1.65 us  [the longest x1 0.96 us: on_device(): jnp.sum(jnp.where(hyp == depth_index[None], depth_planes[:, None, None, N...]
  transfers between devices with their start and end apart: 9 -> 13, of which waited for: 6 -> 3; matrix products, arithmetic and copies ran while one was open for 72% -> 5% of each run, Pallas kernels for 0% -> 47%
where the time goes in v1:
time: 344 us; the launch traced here: 338 us
  Pallas kernels  185 us (54%)
  starting transfers between devices  68.9 us (20%)
  waiting for transfers between devices  55.8 us (16%)
  local copies, waits for them, and re-layouts  15.9 us (5%)
  other arithmetic  11.9 us (3%)
    pallas_call x2, Pallas kernels, sweep_steps(): pl.pallas_call(sweep_kernel, grid_spec=pltpu.PrefetchScalarGridSpec(num_s...  67.5 us
    pallas_call x4, Pallas kernels, pick(): pl.pallas_call(kernel, grid_spec=pltpu.PrefetchScalarGridSpec(num_scalar_...  56.2 us
    all_to_all x3, waiting for transfers between devices, exchange(): return lax.all_to_all(a, 'img', split_axis=0, concat_axis=0, tiled=True)  52.1 us
    all_to_all x3, starting transfers between devices, exchange(): return lax.all_to_all(a, 'img', split_axis=0, concat_axis=0, tiled=True)  40.5 us
    pallas_call x3, Pallas kernels, edges(): pl.pallas_call(edge_kernel, grid_spec=pltpu.PrefetchScalarGridSpec(num_sc...  35.9 us
    pallas_call x1, Pallas kernels, prepare(): pl.pallas_call(prepare_kernel, grid=(images,), in_specs=[pl.BlockSpec((1,...  15.6 us
    ppermute x3, starting transfers between devices, neighbour_rows(): above = lax.ppermute(tail, 'tile', [(i, i + 1) for i in range(count - 1)])  10.2 us
    unnamed x49, local copies, waits for them, and re-layouts  10.1 us
  transfers between devices with their start and end apart: 13, of which 3 were waited for; matrix products, arithmetic and copies ran while one was open for 5% of the time, Pallas kernels for 47%

profile of v1, /device:TPU:1, one launch (start us, length us, event | category | flops | bytes accessed | tf_op | source)
XLA Modules:
  0.0 338.4 jit_solution(13407696094924620814)
XLA Ops:
  0.6 0.8 reshape.83
  1.4 0.6 fusion.2
  2.0 19.3 %pick.6 = bf16[32,4,64,4,128]{4,3,2,1,0:T(4,128)(2,1)} custom-call(s32[32]{0:T(128)} %get-tuple-element.34.refs_0_, bf16[16,64,4,768]{3,2,1,0:T(4,128)(2,1)} %refs_1_.7), custom_call_target="tpu_custom_call" | custom-call | bytes 16777216 | tf_op jit(solution)/shard_map/pick/pallas_call | solution.py:106
  21.3 9.4 %all-to-all-start = ((bf16[32,4,256,128]{3,2,1,0:T(8,128)(2,1)}), bf16[32,4,256,128]{3,2,1,0:T(8,128)(2,1)}, u32[]{:S(2)}, u32[]{:S(2)}) async-start(bf16[32,4,256,128]{3,2,1,0:T(8,128)(2,1)} %bitcast.39), calls=%async_computation | async-start | bytes 16777216 | tf_op jit(solution)/shard_map/all_to_all | solution.py:460
  30.7 0.5 iota.18.refs_0_
  31.2 9.5 %pick.5 = bf16[16,1,64,4,128]{4,3,2,1,0:T(4,128)(2,1)} custom-call(s32[16]{0:T(128)} %iota.18.refs_0_, bf16[16,64,4,768]{3,2,1,0:T(4,128)(2,1)} %refs_1_.7), custom_call_target="tpu_custom_call" | custom-call | bytes 2097152 | tf_op jit(solution)/shard_map/pick/pallas_call | solution.py:106
  40.7 0.5 iota.17.refs_0_
  41.2 11.5 %pick.4 = bf16[16,4,64,4,128]{4,3,2,1,0:T(4,128)(2,1)} custom-call(s32[16]{0:T(128)} %iota.17.refs_0_, bf16[16,64,4,768]{3,2,1,0:T(4,128)(2,1)} %refs_1_.7), custom_call_target="tpu_custom_call" | custom-call | bytes 8388608 | tf_op jit(solution)/shard_map/pick/pallas_call | solution.py:106
  52.7 5.0 %pad_maximum_fusion.block_ref.own_ref = bf16[16,5,256,128]{3,2,1,0:T(8,128)(2,1)} fusion(bf16[16,1,256,128]{3,2,1,0:T(8,128)(2,1)S(1)} %bitcast.42, bf16[16,4,256,128]{3,2,1,0:T(8,128)(2,1)} %bitcast.40), kind=kLoop, calls=%fused_computation.3 | loop fusion | flops 2621440 | bytes 10485760 | tf_op jit(solution)/shard_map/concatenate | solution.py:466
  57.7 0.5 iota.19.slot_ref
  58.2 13.1 %edges.3 = (bf16[16,5,64,128]{3,2,1,0:T(8,128)(2,1)}, bf16[16,5,64,128]{3,2,1,0:T(8,128)(2,1)}, f32[16,5,8,128]{3,2,1,0:T(8,128)}) custom-call(s32[16]{0:T(128)} %iota.19.slot_ref, bf16[16,5,256,128]{3,2,1,0:T(8,128)(2,1)} %pad_maximum_fusion.block_ref.own_ref, bf16[128,256]{1,0:T(8,128)(2,1)} %constant.130.clone.sel_ref, ...), custom_call_target="tpu_custom_call" | custom-call | flops 1600000000 | bytes 8000000 | tf_op jit(solution)/shard_map/edges/pallas_call | solution.py:144
  71.3 4.7 %collective-permute-start = (bf16[16,5,64,128]{3,2,1,0:T(8,128)(2,1)}, bf16[16,5,64,128]{3,2,1,0:T(8,128)(2,1)}, u32[]{:S(2)}, u32[]{:S(2)}) collective-permute-start(bf16[16,5,64,128]{3,2,1,0:T(8,128)(2,1)} %get-tuple-element.18), channel_id=1, source_target_pairs={{0,1},{1,2},{2,3},{4,5},{5,6},{6,7},{8,9},{9,10},{10,11},{12,13},{... | collective-permute-start | bytes 3932168 | tf_op jit(solution)/shard_map/ppermute | solution.py:440
  76.0 1.3 collective-permute-start.1
  77.3 0.1 broadcast_in_dim.40
  77.4 0.6 fusion.12
  78.0 4.1 %collective-permute-start.8 = (s32[1,256]{1,0:T(1,128)}, s32[1,256]{1,0:T(1,128)}, u32[]{:S(2)}, u32[]{:S(2)}) collective-permute-start(s32[1,256]{1,0:T(1,128)} %get-tuple-element.39), channel_id=1, source_target_pairs={{0,3},{1,0},{2,1},{3,2},{4,7},{5,4},{6,5},{7,6},{8,11},{9,8},{10,9... | collective-permute-start | bytes 3080 | tf_op jit(solution)/shard_map/ppermute | solution.py:483
  82.1 15.9 %pick.7 = bf16[32,1,64,4,128]{4,3,2,1,0:T(4,128)(2,1)} custom-call(s32[32]{0:T(128)} %get-tuple-element.34.refs_0_, bf16[16,64,4,768]{3,2,1,0:T(4,128)(2,1)} %refs_1_.7), custom_call_target="tpu_custom_call" | custom-call | bytes 4194304 | tf_op jit(solution)/shard_map/pick/pallas_call | solution.py:106
  98.1 41.2 %all-to-all-done.block_ref.o0_ref.o1_ref = bf16[32,4,256,128]{3,2,1,0:T(8,128)(2,1)} async-done(((bf16[32,4,256,128]{3,2,1,0:T(8,128)(2,1)}), bf16[32,4,256,128]{3,2,1,0:T(8,128)(2,1)}, u32[]{:S(2)}, u32[]{:S(2)}) %all-to-all-start) | async-done | bytes 8388640 | tf_op jit(solution)/shard_map/all_to_all | solution.py:460
  139.2 21.4 %all-to-all-start.1 = ((bf16[32,1,256,128]{3,2,1,0:T(8,128)(2,1)}), bf16[32,1,256,128]{3,2,1,0:T(8,128)(2,1)S(1)}, u32[]{:S(2)}, u32[]{:S(2)}) async-start(bf16[32,1,256,128]{3,2,1,0:T(8,128)(2,1)} %bitcast.41), calls=%async_computation.1 | async-start | bytes 4194304 | tf_op jit(solution)/shard_map/all_to_all | solution.py:460
  160.7 0.0 copy-start.16
  160.7 0.0 copy-start.19
  160.7 0.0 copy-start.21
  160.8 0.1 pad_bitcast_fusion.4
  160.8 0.1 pad_bitcast_fusion
  161.0 0.5 fusion.17.slot_ref
  161.5 0.6 pad_clamp_fusion
  162.1 12.4 %edges.4 = (bf16[16,4,64,128]{3,2,1,0:T(8,128)(2,1)}, bf16[16,4,64,128]{3,2,1,0:T(8,128)(2,1)}, f32[16,4,8,128]{3,2,1,0:T(8,128)}) custom-call(s32[16]{0:T(128)} %fusion.17.slot_ref, bf16[32,4,256,128]{3,2,1,0:T(8,128)(2,1)} %all-to-all-done.block_ref.o0_ref.o1_ref, bf16[128,256]{1,0:T(8,128)(2,1)} %constant.130.clone.sel_ref, ...), custom_call_target="tpu_custom_call" | custom-call | flops 1280000000 | bytes 6400000 | tf_op jit(solution)/shard_map/edges/pallas_call | solution.py:144
  174.5 3.6 %collective-permute-start.2 = (bf16[16,4,64,128]{3,2,1,0:T(8,128)(2,1)}, bf16[16,4,64,128]{3,2,1,0:T(8,128)(2,1)S(1)}, u32[]{:S(2)}, u32[]{:S(2)}) collective-permute-start(bf16[16,4,64,128]{3,2,1,0:T(8,128)(2,1)} %get-tuple-element.23), channel_id=1, source_target_pairs={{0,1},{1,2},{2,3},{4,5},{5,6},{6,7},{8,9},{9,10},{10,11},{12,13},{... | collective-permute-start | bytes 3145736 | tf_op jit(solution)/shard_map/ppermute | solution.py:440
  178.1 1.3 collective-permute-start.3
  179.4 0.6 compare_and_fusion
  180.1 0.6 fusion.7.list_ref
  180.6 1.0 select_reduce_fusion
  181.6 0.1 fusion.elev_ref
  181.7 4.1 %collective-permute-start.7 = (s32[1,256]{1,0:T(1,128)}, s32[1,256]{1,0:T(1,128)}, u32[]{:S(2)}, u32[]{:S(2)}) collective-permute-start(s32[1,256]{1,0:T(1,128)} %get-tuple-element.38), channel_id=1, source_target_pairs={{0,2},{1,3},{2,0},{3,1},{4,6},{5,7},{6,4},{7,5},{8,10},{9,11},{10,... | collective-permute-start | bytes 3080 | tf_op jit(solution)/shard_map/ppermute | solution.py:483
  185.8 1.7 collective-permute-start.6
  187.5 15.6 %prepare.1 = (bf16[16,4,144,256]{3,2,1,0:T(8,128)(2,1)}, bf16[16,4,144,128]{3,2,1,0:T(8,128)(2,1)}, bf16[16,4,64,128]{3,2,1,0:T(8,128)(2,1)}) custom-call(bf16[16,5,256,128]{3,2,1,0:T(8,128)(2,1)} %pad_maximum_fusion.block_ref.own_ref, bf16[16,5,64,128]{3,2,1,0:T(8,128)(2,1)} %collective-permute-done.up_ref, ...), custom_call_target="tpu_custom_call" | custom-call | flops 2560000000 | bytes 16000000 | tf_op jit(solution)/shard_map/prepare/pallas_call | solution.py:201
  203.1 1.3 copy-done
  204.4 10.4 %edges.5 = (bf16[16,1,64,128]{3,2,1,0:T(8,128)(2,1)}, bf16[16,1,64,128]{3,2,1,0:T(8,128)(2,1)}, f32[16,1,8,128]{3,2,1,0:T(8,128)}) custom-call(s32[16]{0:T(128)} %fusion.17.slot_ref, bf16[32,1,256,128]{3,2,1,0:T(8,128)(2,1)} %copy-done, bf16[128,256]{1,0:T(8,128)(2,1)} %constant.130.clone.sel_ref, bf16[16,256]{1,0:T(8,128)(2,1)} %constant.131.clone.stat_ref), custom_call_target="tpu_custom_call" | custom-call | flops 320000000 | bytes 1600000 | tf_op jit(solution)/shard_map/edges/pallas_call | solution.py:144
  214.8 1.9 collective-permute-start.4
  216.8 1.3 collective-permute-start.5
  218.1 2.3 copy-done.2
  220.4 1.7 copy-done.3
  222.1 1.2 copy-done.4
  223.3 1.0 copy-done.5
  224.3 0.9 copy-done.8
  225.2 0.8 copy-done.10
  226.0 50.1 %sweep.2 = (f32[16,4,384]{2,1,0:T(4,128)S(1)}, f32[3,16,4,256]{3,2,1,0:T(4,128)S(1)}) custom-call(s32[16]{0:T(128)S(1)} %copy-done.12, bf16[16,4,144,256]{3,2,1,0:T(8,128)(2,1)S(1)} %copy-done.2, bf16[16,4,144,128]{3,2,1,0:T(8,128)(2,1)S(1)} %copy-done.3, bf16[32,4,256,128]{3,2,1,0:T(8,128)(2,1)} %all-to-all-done.block_ref.o0_ref.o1_ref, ...), custom_call_target="tpu_custom_call" | custom-call | flops 9600000000 | bytes 19200000 | tf_op jit(solution)/shard_map/sweep/pallas_call | solution.py:352
  276.2 17.4 %sweep.3 = (f32[16,4,128]{2,1,0:T(4,128)S(1)}, f32[1,16,4,256]{3,2,1,0:T(4,128)S(1)}) custom-call(s32[16]{0:T(128)S(1)} %copy-done.12, bf16[16,4,144,256]{3,2,1,0:T(8,128)(2,1)S(1)} %copy-done.2, bf16[16,4,144,128]{3,2,1,0:T(8,128)(2,1)S(1)} %copy-done.3, bf16[32,4,256,128]{3,2,1,0:T(8,128)(2,1)} %all-to-all-done.block_ref.o0_ref.o1_ref, ...), custom_call_target="tpu_custom_call" | custom-call | flops 3200000000 | bytes 6400000 | tf_op jit(solution)/shard_map/sweep/pallas_call | solution.py:352
  293.6 0.1 pad_maximum_fusion.1
  293.7 0.8 reshape.88.rows_ref
  294.5 4.3 %collect.1 = f32[4,128,256]{2,1,0:T(8,128)} custom-call(s32[4,128]{1,0:T(4,128)} %fusion.7.list_ref, s32[4]{0:T(128)} %bitcast.45, f32[256,256]{1,0:T(8,128)} %reshape.88.rows_ref), custom_call_target="tpu_custom_call" | custom-call | tf_op jit(solution)/shard_map/collect/pallas_call | solution.py:399
  298.8 4.5 %all-to-all-start.2 = ((f32[4,128,256]{2,1,0:T(8,128)}), f32[4,128,256]{2,1,0:T(8,128)S(1)}, u32[]{:S(2)}, u32[]{:S(2)}) async-start(f32[4,128,256]{2,1,0:T(8,128)} %collect.1), calls=%async_computation.2 | async-start | bytes 1048576 | tf_op jit(solution)/shard_map/all_to_all | solution.py:509
  303.3 0.7 pad_add_fusion
  304.0 0.7 gather_fusion
  304.7 0.7 broadcast_select_fusion
  305.5 0.6 slice.18.slot_ref
  306.1 0.6 slice_reduce_fusion.count_ref
  306.7 3.7 %all-to-all-done.2.got_ref = f32[4,128,256]{2,1,0:T(8,128)S(1)} async-done(((f32[4,128,256]{2,1,0:T(8,128)}), f32[4,128,256]{2,1,0:T(8,128)S(1)}, u32[]{:S(2)}, u32[]{:S(2)}) %all-to-all-start.2) | async-done | bytes 524320 | tf_op jit(solution)/shard_map/all_to_all | solution.py:509
  310.3 0.8 copy-done.14
  311.1 5.4 %place.1 = f32[512,256]{1,0:T(8,128)} custom-call(s32[4,128]{1,0:T(4,128)} %slice.18.slot_ref, s32[4]{0:T(128)} %slice_reduce_fusion.count_ref, f32[4,128,256]{2,1,0:T(8,128)} %copy-done.14), custom_call_target="tpu_custom_call" | custom-call | tf_op jit(solution)/shard_map/place/pallas_call | solution.py:425
  316.5 9.6 %all-to-all-start.3 = ((f32[32,16,256]{2,1,0:T(8,128)}), f32[32,16,256]{2,1,0:T(8,128)S(1)}, u32[]{:S(2)}, u32[]{:S(2)}) async-start(f32[32,16,256]{2,1,0:T(8,128)} %bitcast.43), calls=%async_computation.3 | async-start | bytes 1048576 | tf_op jit(solution)/shard_map/all_to_all | solution.py:460
  326.2 0.7 pad_maximum_fusion.2
  326.9 10.9 %all-to-all-done.3 = f32[32,16,256]{2,1,0:T(8,128)S(1)} async-done(((f32[32,16,256]{2,1,0:T(8,128)}), f32[32,16,256]{2,1,0:T(8,128)S(1)}, u32[]{:S(2)}, u32[]{:S(2)}) %all-to-all-start.3) | async-done | bytes 524320 | tf_op jit(solution)/shard_map/all_to_all | solution.py:460
  337.8 0.6 fusion.5
  (53 shorter events, 0.2 us)
Async XLA Ops:
  21.3 118.0 %all-to-all-start = ((bf16[32,4,256,128]{3,2,1,0:T(8,128)(2,1)}), bf16[32,4,256,128]{3,2,1,0:T(8,128)(2,1)}, u32[]{:S(2)}, u32[]{:S(2)}) async-start(bf16[32,4,256,128]{3,2,1,0:T(8,128)(2,1)} %bitcast.39), calls=%async_computation | async-start | bytes 16777216 | tf_op jit(solution)/shard_map/all_to_all | solution.py:460
  41.2 11.5 %copy-start.13 = (bf16[16,1,64,4,128]{4,3,2,1,0:T(4,128)(2,1)S(1)}, bf16[16,1,64,4,128]{4,3,2,1,0:T(4,128)(2,1)}, u32[]{:S(2)}) copy-start(bf16[16,1,64,4,128]{4,3,2,1,0:T(4,128)(2,1)} %pick.5) | copy-start | bytes 3145732
  57.7 19.6 %copy-start.20 = (s32[1,1,4]{2,1,0:T(1,128)S(1)}, s32[1,1,4]{2,1,0:T(1,128)}, u32[]{:S(2)}) copy-start(s32[1,1,4]{2,1,0:T(1,128)} %param.30) | copy-start | bytes 52
  57.7 19.7 %copy-start.18 = (s32[1,1,4,128]{3,2,1,0:T(4,128)S(1)}, s32[1,1,4,128]{3,2,1,0:T(4,128)}, u32[]{:S(2)}) copy-start(s32[1,1,4,128]{3,2,1,0:T(4,128)} %param.29) | copy-start | bytes 6148
  71.3 110.4 %collective-permute-start = (bf16[16,5,64,128]{3,2,1,0:T(8,128)(2,1)}, bf16[16,5,64,128]{3,2,1,0:T(8,128)(2,1)}, u32[]{:S(2)}, u32[]{:S(2)}) collective-permute-start(bf16[16,5,64,128]{3,2,1,0:T(8,128)(2,1)} %get-tuple-element.18), channel_id=1, source_target_pairs={{0,1},{1,2},{2,3},{4,5},{5,6},{6,7},{8,9},{9,10},{10,11},{12,13},{... | collective-permute-start | bytes 3932168 | tf_op jit(solution)/shard_map/ppermute | solution.py:440
  76.0 109.8 %collective-permute-start.1 = (bf16[16,5,64,128]{3,2,1,0:T(8,128)(2,1)}, bf16[16,5,64,128]{3,2,1,0:T(8,128)(2,1)}, u32[]{:S(2)}, u32[]{:S(2)}) collective-permute-start(bf16[16,5,64,128]{3,2,1,0:T(8,128)(2,1)} %get-tuple-element.19), channel_id=1, source_target_pairs={{1,0},{2,1},{3,2},{5,4},{6,5},{7,6},{9,8},{10,9},{11,10},{13,12},{... | collective-permute-start | bytes 3932168 | tf_op jit(solution)/shard_map/ppermute | solution.py:441
  78.0 82.7 %copy-start.17 = (f32[64]{0:T(128)S(1)}, f32[64]{0:T(128)}, u32[]{:S(2)}) copy-start(f32[64]{0:T(128)} %param.23) | copy-start | bytes 772
  78.0 82.9 %copy-start.22 = (bf16[1,128]{1,0:T(2,128)(2,1)S(1)}, bf16[1,128]{1,0:T(2,128)(2,1)}, u32[]{:S(2)}) copy-start(bf16[1,128]{1,0:T(2,128)(2,1)} %constant.220) | copy-start | bytes 772
  78.0 82.9 %copy-start.23 = (bf16[1,128]{1,0:T(2,128)(2,1)S(1)}, bf16[1,128]{1,0:T(2,128)(2,1)}, u32[]{:S(2)}) copy-start(bf16[1,128]{1,0:T(2,128)(2,1)} %constant.221) | copy-start | bytes 772
  78.0 225.3 %collective-permute-start.8 = (s32[1,256]{1,0:T(1,128)}, s32[1,256]{1,0:T(1,128)}, u32[]{:S(2)}, u32[]{:S(2)}) collective-permute-start(s32[1,256]{1,0:T(1,128)} %get-tuple-element.39), channel_id=1, source_target_pairs={{0,3},{1,0},{2,1},{3,2},{4,7},{5,4},{6,5},{7,6},{8,11},{9,8},{10,9... | collective-permute-start | bytes 3080 | tf_op jit(solution)/shard_map/ppermute | solution.py:483
  139.2 63.8 %all-to-all-start.1 = ((bf16[32,1,256,128]{3,2,1,0:T(8,128)(2,1)}), bf16[32,1,256,128]{3,2,1,0:T(8,128)(2,1)S(1)}, u32[]{:S(2)}, u32[]{:S(2)}) async-start(bf16[32,1,256,128]{3,2,1,0:T(8,128)(2,1)} %bitcast.41), calls=%async_computation.1 | async-start | bytes 4194304 | tf_op jit(solution)/shard_map/all_to_all | solution.py:460
  160.7 19.3 %copy-start.16 = (s32[16,4,512]{2,1,0:T(4,128)S(1)}, s32[16,4,512]{2,1,0:T(4,128)}, u32[]{:S(2)}) copy-start(s32[16,4,512]{2,1,0:T(4,128)} %index_ref.1) | copy-start | bytes 393220
  160.7 19.4 %copy-start.19 = (s32[1,1,4,128]{3,2,1,0:T(4,128)S(1)}, s32[1,1,4,128]{3,2,1,0:T(4,128)}, u32[]{:S(2)}) copy-start(s32[1,1,4,128]{3,2,1,0:T(4,128)} %param.28) | copy-start | bytes 6148
  160.7 20.9 %copy-start.15 = (f32[16,4,512]{2,1,0:T(4,128)S(1)}, f32[16,4,512]{2,1,0:T(4,128)}, u32[]{:S(2)}) copy-start(f32[16,4,512]{2,1,0:T(4,128)} %param.25) | copy-start | bytes 393220
  160.7 20.9 %copy-start.21 = (f32[16]{0:T(128)S(1)}, f32[16]{0:T(128)}, u32[]{:S(2)}) copy-start(f32[16]{0:T(128)} %param.24) | copy-start | bytes 196
  174.5 40.3 %collective-permute-start.2 = (bf16[16,4,64,128]{3,2,1,0:T(8,128)(2,1)}, bf16[16,4,64,128]{3,2,1,0:T(8,128)(2,1)S(1)}, u32[]{:S(2)}, u32[]{:S(2)}) collective-permute-start(bf16[16,4,64,128]{3,2,1,0:T(8,128)(2,1)} %get-tuple-element.23), channel_id=1, source_target_pairs={{0,1},{1,2},{2,3},{4,5},{5,6},{6,7},{8,9},{9,10},{10,11},{12,13},{... | collective-permute-start | bytes 3145736 | tf_op jit(solution)/shard_map/ppermute | solution.py:440
  178.1 38.7 %collective-permute-start.3 = (bf16[16,4,64,128]{3,2,1,0:T(8,128)(2,1)}, bf16[16,4,64,128]{3,2,1,0:T(8,128)(2,1)}, u32[]{:S(2)}, u32[]{:S(2)}) collective-permute-start(bf16[16,4,64,128]{3,2,1,0:T(8,128)(2,1)} %get-tuple-element.24), channel_id=1, source_target_pairs={{1,0},{2,1},{3,2},{5,4},{6,5},{7,6},{9,8},{10,9},{11,10},{13,12},{... | collective-permute-start | bytes 3145736 | tf_op jit(solution)/shard_map/ppermute | solution.py:441
  181.7 121.6 %collective-permute-start.7 = (s32[1,256]{1,0:T(1,128)}, s32[1,256]{1,0:T(1,128)}, u32[]{:S(2)}, u32[]{:S(2)}) collective-permute-start(s32[1,256]{1,0:T(1,128)} %get-tuple-element.38), channel_id=1, source_target_pairs={{0,2},{1,3},{2,0},{3,1},{4,6},{5,7},{6,4},{7,5},{8,10},{9,11},{10,... | collective-permute-start | bytes 3080 | tf_op jit(solution)/shard_map/ppermute | solution.py:483
  185.8 117.5 %collective-permute-start.6 = (s32[1,256]{1,0:T(1,128)}, s32[1,256]{1,0:T(1,128)}, u32[]{:S(2)}, u32[]{:S(2)}) collective-permute-start(s32[1,256]{1,0:T(1,128)} %get-tuple-element.37), channel_id=1, source_target_pairs={{0,1},{1,2},{2,3},{3,0},{4,5},{5,6},{6,7},{7,4},{8,9},{9,10},{10,1... | collective-permute-start | bytes 3080 | tf_op jit(solution)/shard_map/ppermute | solution.py:483
  187.5 30.6 %copy-start.7 = (f32[16,4,8,128]{3,2,1,0:T(8,128)S(1)}, f32[16,4,8,128]{3,2,1,0:T(8,128)}, u32[]{:S(2)}) copy-start(f32[16,4,8,128]{3,2,1,0:T(8,128)} %get-tuple-element.25.s0_ref.s1_ref) | copy-start | bytes 786436
  187.5 30.6 %copy-start.11 = (bf16[16,256]{1,0:T(8,128)(2,1)S(1)}, bf16[16,256]{1,0:T(8,128)(2,1)}, u32[]{:S(2)}) copy-start(bf16[16,256]{1,0:T(8,128)(2,1)} %constant.135.clone.mask_ref) | copy-start | bytes 24580
  187.5 30.6 %copy-start.12 = (s32[16]{0:T(128)S(1)}, s32[16]{0:T(128)}, u32[]{:S(2)}) copy-start(s32[16]{0:T(128)} %fusion.17.slot_ref) | copy-start | bytes 196
  203.1 1.3 copy-start
  214.8 61.3 %collective-permute-start.4 = (bf16[16,1,64,128]{3,2,1,0:T(8,128)(2,1)}, bf16[16,1,64,128]{3,2,1,0:T(8,128)(2,1)S(1)}, u32[]{:S(2)}, u32[]{:S(2)}) collective-permute-start(bf16[16,1,64,128]{3,2,1,0:T(8,128)(2,1)} %get-tuple-element.28), channel_id=1, source_target_pairs={{0,1},{1,2},{2,3},{4,5},{5,6},{6,7},{8,9},{9,10},{10,11},{12,13},{... | collective-permute-start | bytes 786440 | tf_op jit(solution)/shard_map/ppermute | solution.py:440
  216.8 59.4 %collective-permute-start.5 = (bf16[16,1,64,128]{3,2,1,0:T(8,128)(2,1)}, bf16[16,1,64,128]{3,2,1,0:T(8,128)(2,1)S(1)}, u32[]{:S(2)}, u32[]{:S(2)}) collective-permute-start(bf16[16,1,64,128]{3,2,1,0:T(8,128)(2,1)} %get-tuple-element.29), channel_id=1, source_target_pairs={{1,0},{2,1},{3,2},{5,4},{6,5},{7,6},{9,8},{10,9},{11,10},{13,12},{... | collective-permute-start | bytes 786440 | tf_op jit(solution)/shard_map/ppermute | solution.py:441
  218.1 2.3 copy-start.2
  220.4 1.7 copy-start.3
  222.1 1.2 copy-start.4
  223.3 1.0 copy-start.5
  224.3 0.9 copy-start.8
  225.2 0.8 copy-start.10
  226.0 50.2 %copy-start.1 = (bf16[32,1,256,128]{3,2,1,0:T(8,128)(2,1)S(1)}, bf16[32,1,256,128]{3,2,1,0:T(8,128)(2,1)}, u32[]{:S(2)}) copy-start(bf16[32,1,256,128]{3,2,1,0:T(8,128)(2,1)} %copy-done) | copy-start | bytes 6291460
  226.0 50.2 %copy-start.6 = (bf16[128,1536]{1,0:T(8,128)(2,1)S(1)}, bf16[128,1536]{1,0:T(8,128)(2,1)}, u32[]{:S(2)}) copy-start(bf16[128,1536]{1,0:T(8,128)(2,1)} %constant.134.clone.pat_ref) | copy-start | bytes 1179652
  226.0 50.2 %copy-start.9 = (f32[16,1,8,128]{3,2,1,0:T(8,128)S(1)}, f32[16,1,8,128]{3,2,1,0:T(8,128)}, u32[]{:S(2)}) copy-start(f32[16,1,8,128]{3,2,1,0:T(8,128)} %get-tuple-element.30.s1_ref) | copy-start | bytes 196612
  298.8 11.5 %all-to-all-start.2 = ((f32[4,128,256]{2,1,0:T(8,128)}), f32[4,128,256]{2,1,0:T(8,128)S(1)}, u32[]{:S(2)}, u32[]{:S(2)}) async-start(f32[4,128,256]{2,1,0:T(8,128)} %collect.1), calls=%async_computation.2 | async-start | bytes 1048576 | tf_op jit(solution)/shard_map/all_to_all | solution.py:509
  310.3 0.8 copy-start.14
  316.5 21.3 %all-to-all-start.3 = ((f32[32,16,256]{2,1,0:T(8,128)}), f32[32,16,256]{2,1,0:T(8,128)S(1)}, u32[]{:S(2)}, u32[]{:S(2)}) async-start(f32[32,16,256]{2,1,0:T(8,128)} %bitcast.43), calls=%async_computation.3 | async-start | bytes 1048576 | tf_op jit(solution)/shard_map/all_to_all | solution.py:460

commit v2 on v1

v2 whole, which is shorter than its diff:
```python
import math

import numpy as np
import jax
import jax.numpy as jnp
from jax import lax
from jax.experimental import pallas as pl
from jax.experimental.pallas import tpu as pltpu
from jax.sharding import PartitionSpec as P

NDEPTH = 64
CELLS = 128
PATCH_DEV = 16
STEPS = 4
WIN = 144
LOG2E = math.log2(math.e)
BF = jnp.bfloat16
F32 = jnp.float32
NT = (((1,), (1,)), ((), ()))
PARAMS = pltpu.CompilerParams(vmem_limit_bytes=60 * 1024 * 1024)


def dot(a, b):
    return jnp.dot(a, b, preferred_element_type=F32)


def dot_nt(a, b):
    return lax.dot_general(a, b, NT, preferred_element_type=F32)


def table_patterns():
    pat = np.zeros((128, 12, 128), np.float32)
    for half in range(2):
        lanes = slice(64 * half, 64 * half + 64)
        for y in range(4):
            for q in range(2):
                for s in range(3):
                    pat[half * 32 + s * 8 + q * 4 + y, y * 3 + q, lanes] = 1.0
            pat[half * 32 + 24 + y, y * 3 + 2, lanes] = 1.0
    return jnp.asarray(pat.reshape(128, 12 * 128), BF)


def row_masks():
    y = np.arange(16)[:, None]
    k = np.arange(256)[None, :] % 4
    return jnp.asarray((np.abs(k - y) <= 1) & (y < 4), BF)


def flips():
    m = np.zeros((128, 128), np.float32)
    for i in range(128):
        m[i, i // 64 * 64 + 63 - i % 64] = 1.0
    return jnp.asarray(m, BF)


def reversal():
    m = np.zeros((WIN, 256), np.float32)
    for i in range(WIN):
        m[i, WIN - 1 - i] = 1.0
    return jnp.asarray(m, BF)


def edge_constants():
    sel = np.zeros((128, 256), np.float32)
    for c in range(64):
        sel[c, 4 * c] = 1.0
        sel[64 + c, 4 * c + 3] = 1.0
    stat = np.zeros((16, 256), np.float32)
    for y in range(4):
        stat[y, y::4] = 1.0
        stat[12 + y, y::4] = 1.0
    return jnp.asarray(sel, BF), jnp.asarray(stat, BF)


def split2(a):
    high = a.astype(BF)
    return high, (a - high.astype(F32)).astype(BF)


def boxed_stats(stats, up, down):
    upf = up.astype(F32)
    downf = down.astype(F32)
    sums = [jnp.sum(upf, 0, keepdims=True)] + [stats[y : y + 1] for y in range(4)]
    sums.append(jnp.sum(downf, 0, keepdims=True))
    sqs = [jnp.sum(upf * upf, 0, keepdims=True)] + [stats[4 + y : 5 + y] for y in range(4)]
    sqs.append(jnp.sum(downf * downf, 0, keepdims=True))
    tall = jnp.concatenate(
        [v[y] + v[y + 1] + v[y + 2] for v in (sums, sqs) for y in range(4)], axis=0
    )
    boxed = (tall + pltpu.roll(tall, 255, 1) + pltpu.roll(tall, 254, 1)) * (1.0 / 576.0)
    mean = boxed[0:4]
    return mean, lax.rsqrt(boxed[4:8] - mean * mean + 1e-5)


DEPTH = 8
PART = 4
PACKED = 136


def pick(idx, features, blocks):
    count = idx.shape[0]
    _, channels, rows, _ = features.shape
    ahead = DEPTH // 2

    def kernel(idx_ref, features_ref, out_ref, strips, in_sem, out_sem):
        def read(s):
            return pltpu.make_async_copy(
                features_ref.at[idx_ref[s], :, :, pl.ds(0, 128 * blocks)],
                strips.at[s % DEPTH],
                in_sem.at[s % DEPTH],
            )

        def write(s, j):
            return pltpu.make_async_copy(
                strips.at[s % DEPTH, :, :, pl.ds(128 * j, 128)],
                out_ref.at[s, j],
                out_sem.at[s % DEPTH, j],
            )

        for s in range(DEPTH):
            read(s).start()
        for s in range(count):
            read(s).wait()
            for j in range(blocks):
                write(s, j).start()
            later = s + ahead
            if DEPTH <= later < count:
                for j in range(blocks):
                    write(later - DEPTH, j).wait()
                read(later).start()
        for s in range(count - DEPTH, count):
            for j in range(blocks):
                write(s, j).wait()

    out = pl.pallas_call(
        kernel,
        grid_spec=pltpu.PrefetchScalarGridSpec(
            num_scalar_prefetch=1,
            grid=(1,),
            in_specs=[pl.BlockSpec(memory_space=pl.ANY)],
            out_specs=pl.BlockSpec(memory_space=pl.ANY),
            scratch_shapes=[
                pltpu.VMEM((DEPTH, channels, rows, 128 * blocks), BF),
                pltpu.SemaphoreType.DMA((DEPTH,)),
                pltpu.SemaphoreType.DMA((DEPTH, blocks)),
            ],
        ),
        out_shape=jax.ShapeDtypeStruct((count, blocks, channels, rows, 128), BF),
        compiler_params=PARAMS,
        cost_estimate=pl.CostEstimate(
            flops=0, bytes_accessed=count * blocks * 131072, transcendentals=0
        ),
        name="pick",
    )(idx, features)
    return out.reshape(count, blocks, channels * rows, 128)


def pack_constants():
    spread = np.zeros((128, 256), np.float32)
    for i in range(64):
        spread[i, i] = 1.0
        spread[64 + i, 128 + i] = 1.0
    column = np.zeros((8, 128), np.float32)
    column[0, 64] = 1.0
    into = np.zeros((256, 128), np.float32)
    into[:, 64] = 1.0
    return tuple(jnp.asarray(m, BF) for m in (spread, column, into, np.eye(256)))


def pack_kernel(idx_ref, *refs):
    blocks, (spread_ref, column_ref, out_ref) = refs[:PART], refs[PART:]
    for g in range(PART):
        block = blocks[g][0, 0]
        out_ref[g, 0:128, :] = (
            dot_nt(block[0:128], spread_ref[:, 0:128]) + dot_nt(block[128:256], spread_ref[:, 128:])
        ).astype(BF)
        line = dot_nt(column_ref[...], block)
        out_ref[g, 128:136, :] = jnp.concatenate(
            [line[0:1, 0:128], line[0:1, 128:256], jnp.zeros((6, 128), F32)], axis=0
        ).astype(BF)


def pack(idx, own):
    count = idx.shape[0]
    spread, column, _, _ = pack_constants()

    def chosen(g):
        return lambda k, s: (s[PART * k + g], STEPS, 0, 0)

    return pl.pallas_call(
        pack_kernel,
        grid_spec=pltpu.PrefetchScalarGridSpec(
            num_scalar_prefetch=1,
            grid=(count // PART,),
            in_specs=[pl.BlockSpec((1, 1, 256, 128), chosen(g)) for g in range(PART)]
            + [
                pl.BlockSpec((128, 256), lambda k, s: (0, 0)),
                pl.BlockSpec((8, 128), lambda k, s: (0, 0)),
            ],
            out_specs=pl.BlockSpec((PART, PACKED, 128), lambda k, s: (k, 0, 0)),
        ),
        out_shape=jax.ShapeDtypeStruct((count, PACKED, 128), BF),
        compiler_params=PARAMS,
        name="pack",
    )(idx, *[own] * PART, spread, column)


def block_edges(block, sel_ref, stat_ref):
    rows = dot(sel_ref[...], block).astype(BF)
    value = block.astype(F32)
    high, low = split2(value * value)
    stats = dot(stat_ref[0:8], block) + dot(stat_ref[8:16], high) + dot(stat_ref[8:16], low)
    return rows[0:64], rows[64:128], stats


def edge_kernel(slot_ref, *refs):
    blocks, (sel_ref, stat_ref, head_ref, tail_ref, stats_ref) = refs[:PART], refs[PART:]
    for g in range(PART):
        for j in range(stats_ref.shape[1]):
            head, tail, stats = block_edges(blocks[g][0, j], sel_ref, stat_ref)
            head_ref[g, j] = head
            tail_ref[g, j] = tail
            stats_ref[g, j] = stats


def unpack_kernel(slot_ref, *refs):
    packed = refs[:PART]
    (
        spread_ref, into_ref, eye_ref, sel_ref, stat_ref, head_ref, tail_ref, stats_ref, block_ref,
    ) = refs[PART:]
    for g in range(PART):
        wide = dot(packed[g][0, 0:128, :], spread_ref[...])
        line = packed[g][0, 128:136, :]
        line = jnp.concatenate([line[0:1], line[1:2]], axis=1)
        column = dot(eye_ref[...] * line, into_ref[...])
        block = jnp.concatenate([wide[:, :128], wide[:, 128:]], axis=0) + column
        block = block.astype(BF)
        block_ref[g, 0] = block
        head, tail, stats = block_edges(block, sel_ref, stat_ref)
        head_ref[g, 0] = head
        tail_ref[g, 0] = tail
        stats_ref[g, 0] = stats


def edge_outputs(images, blocks):
    specs = [
        pl.BlockSpec((PART, blocks, 64, 128), lambda k, s: (k, 0, 0, 0)),
        pl.BlockSpec((PART, blocks, 64, 128), lambda k, s: (k, 0, 0, 0)),
        pl.BlockSpec((PART, blocks, 8, 128), lambda k, s: (k, 0, 0, 0)),
    ]
    shapes = [
        jax.ShapeDtypeStruct((images, blocks, 64, 128), BF),
        jax.ShapeDtypeStruct((images, blocks, 64, 128), BF),
        jax.ShapeDtypeStruct((images, blocks, 8, 128), F32),
    ]
    return specs, shapes


def whole_spec(a):
    return pl.BlockSpec(a.shape, lambda k, s: (0,) * a.ndim)


def edges(slot, recv):
    images, blocks = slot.shape[0], recv.shape[1]
    constants = edge_constants()
    specs, shapes = edge_outputs(images, blocks)

    def by_slot(g):
        return lambda k, s: (s[PART * k + g], 0, 0, 0)

    return pl.pallas_call(
        edge_kernel,
        grid_spec=pltpu.PrefetchScalarGridSpec(
            num_scalar_prefetch=1,
            grid=(images // PART,),
            in_specs=[pl.BlockSpec((1, blocks, 256, 128), by_slot(g)) for g in range(PART)]
            + [whole_spec(a) for a in constants],
            out_specs=specs,
        ),
        out_shape=shapes,
        cost_estimate=pl.CostEstimate(
            flops=images * blocks * 20_000_000, bytes_accessed=images * blocks * 100_000,
            transcendentals=0,
        ),
        compiler_params=PARAMS,
        name="edges",
    )(slot, *[recv] * PART, *constants)


def unpack(slot, packed):
    images = slot.shape[0]
    spread, _, into, eye = pack_constants()
    constants = (spread, into, eye) + edge_constants()
    specs, shapes = edge_outputs(images, 1)

    def by_slot(g):
        return lambda k, s: (s[PART * k + g], 0, 0)

    return pl.pallas_call(
        unpack_kernel,
        grid_spec=pltpu.PrefetchScalarGridSpec(
            num_scalar_prefetch=1,
            grid=(images // PART,),
            in_specs=[pl.BlockSpec((1, PACKED, 128), by_slot(g)) for g in range(PART)]
            + [whole_spec(a) for a in constants],
            out_specs=specs + [pl.BlockSpec((PART, 1, 256, 128), lambda k, s: (k, 0, 0, 0))],
        ),
        out_shape=shapes + [jax.ShapeDtypeStruct((images, 1, 256, 128), BF)],
        compiler_params=PARAMS,
        name="unpack",
    )(slot, *[packed] * PART, *constants)


def prepare_kernel(
    own_ref, up_ref, down_ref, stat_ref, index_ref, rev_ref, flip_ref, own_out, edge_out, table_out
):
    mean_inv = 24.0 * LOG2E
    for n in range(STEPS):
        block = jnp.concatenate([own_ref[0, n], own_ref[0, n + 1]], axis=1)
        up = jnp.concatenate([up_ref[0, n], up_ref[0, n + 1]], axis=1)
        down = jnp.concatenate([down_ref[0, n], down_ref[0, n + 1]], axis=1)
        own_out[0, n] = dot_nt(rev_ref[...], block).astype(BF)
        edge_out[0, n] = dot_nt(rev_ref[...], jnp.concatenate([up, down], axis=0)).astype(BF)
        stats = jnp.concatenate([stat_ref[0, n], stat_ref[0, n + 1]], axis=1)
        mean, inv = boxed_stats(stats, up, down)
        scaled = inv * mean_inv
        both = jnp.concatenate([scaled * (1.0 / 576.0), scaled * mean], axis=0)[:, :128]
        high = both.astype(BF).astype(F32)
        mid = (both - high).astype(BF).astype(F32)
        index = index_ref[0, :, 128 * n : 128 * n + 128].astype(F32)
        rows = jnp.concatenate(
            [high, mid, both - high - mid, index, jnp.zeros((4, 128), F32)], axis=0
        ).astype(BF)
        blank = jnp.zeros((64, 64), F32)
        left = dot_nt(flip_ref[0:64, :], rows)
        right = dot_nt(flip_ref[64:128, :], rows)
        table_out[0, n] = jnp.concatenate([left, right, blank], axis=1).astype(BF)


def prepare(own, up, down, stats, depth_index):
    images, blocks = own.shape[0], own.shape[1]
    return pl.pallas_call(
        prepare_kernel,
        grid=(images,),
        in_specs=[
            pl.BlockSpec((1, blocks, 256, 128), lambda k: (k, 0, 0, 0)),
            pl.BlockSpec((1, blocks, 64, 128), lambda k: (k, 0, 0, 0)),
            pl.BlockSpec((1, blocks, 64, 128), lambda k: (k, 0, 0, 0)),
            pl.BlockSpec((1, blocks, 8, 128), lambda k: (k, 0, 0, 0)),
            pl.BlockSpec((1, 4, 512), lambda k: (k, 0, 0)),
            pl.BlockSpec((WIN, 256), lambda k: (0, 0)),
            pl.BlockSpec((128, 128), lambda k: (0, 0)),
        ],
        out_specs=[
            pl.BlockSpec((1, STEPS, WIN, 256), lambda k: (k, 0, 0, 0)),
            pl.BlockSpec((1, STEPS, WIN, 128), lambda k: (k, 0, 0, 0)),
            pl.BlockSpec((1, STEPS, 64, 128), lambda k: (k, 0, 0, 0)),
        ],
        out_shape=[
            jax.ShapeDtypeStruct((images, STEPS, WIN, 256), BF),
            jax.ShapeDtypeStruct((images, STEPS, WIN, 128), BF),
            jax.ShapeDtypeStruct((images, STEPS, 64, 128), BF),
        ],
        cost_estimate=pl.CostEstimate(
            flops=images * STEPS * 40_000_000, bytes_accessed=images * 1_000_000, transcendentals=0
        ),
        compiler_params=PARAMS,
        name="prepare",
    )(own, up, down, stats, depth_index, reversal(), flips())


GROUP = 8


def skewed(left, right, column, lane, shift):
    return pltpu.roll(jnp.where(lane < column, right, left), shift, 1, stride=1, stride_axis=0)


def sweep_kernel(slot_ref, *refs):
    near_refs, far_refs = refs[:GROUP], refs[GROUP : 2 * GROUP]
    (
        own_ref, edge_ref, u0_ref, u1_ref, d0_ref, d1_ref, s0_ref, s1_ref, table_ref, pat_ref,
        mask_ref, w2_ref, flip_ref, elev_ref, cell_ref, mean_ref, rows_ref, skew,
    ) = refs[2 * GROUP :]
    column = 63 - lax.broadcasted_iota(jnp.int32, (64, 128), 0)
    lane = lax.broadcasted_iota(jnp.int32, (64, 128), 1)
    wrapped = lane < column
    first = lane < column + 64
    column8 = 7 - lax.broadcasted_iota(jnp.int32, (8, 128), 0)
    lane8 = lax.broadcasted_iota(jnp.int32, (8, 128), 1)
    hyp = (lane % 64).astype(F32)
    tables = dot(table_ref[:, 0].reshape(GROUP * 64, 128), pat_ref[...])

    soft = []
    chosen = []
    for g in range(GROUP):
        rhs = jnp.concatenate([near_refs[g][0, 0], far_refs[g][0, 0]], axis=1)
        up = jnp.concatenate([u0_ref[g, 0], u1_ref[g, 0]], axis=1)
        down = jnp.concatenate([d0_ref[g, 0], d1_ref[g, 0]], axis=1)
        stats = jnp.concatenate([s0_ref[g, 0], s1_ref[g, 0]], axis=1)
        mean_b, inv_b = boxed_stats(stats, up, down)
        own = own_ref[g, 0]
        masked = jnp.concatenate([own * mask_ref[y : y + 1, :] for y in range(4)], axis=0)
        product = dot(masked, rhs)
        above = dot(edge_ref[g, 0][:, 0:64], up)
        below = dot(edge_ref[g, 0][:, 64:128], down)
        for y in range(4):
            p = product[WIN * y : WIN * y + WIN]
            if y == 0:
                p = p + above
            if y == 3:
                p = p + below
            z = jnp.where(
                wrapped, p[16:80, 128:], jnp.where(first, p[80:144, :128], p[16:80, :128])
            )
            z8 = jnp.where(
                lane8 < column8,
                p[72:80, 128:],
                jnp.where(lane8 < column8 + 64, p[8:16, 128:], p[72:80, :128]),
            )
            at = 4 * g + y
            skew[at, 0:8, :] = pltpu.roll(z8, 57, 1, stride=1, stride_axis=0)
            skew[at, 8:72, :] = pltpu.roll(z, 65, 1, stride=1, stride_axis=0)
            cross = skew[at, 8:72, :] + skew[at, 7:71, :] + skew[at, 6:70, :]
            mb = skewed(mean_b[y : y + 1, :128], mean_b[y : y + 1, 128:], column, lane, 65)
            rb = skewed(inv_b[y : y + 1, :128], inv_b[y : y + 1, 128:], column, lane, 65)
            a1, a2, index = (
                tables[64 * g : 64 * g + 64, (3 * y + q) * 128 : (3 * y + q + 1) * 128]
                for q in range(3)
            )
            weight = jnp.exp2((cross * a1 - a2 * mb) * rb)
            picked = jnp.where(index == hyp, weight, 0.0)
            soft.append(jnp.concatenate(split2(weight), axis=1))
            chosen.append(jnp.concatenate(split2(picked), axis=1))
    soft = jnp.concatenate(soft, axis=0)
    chosen = jnp.concatenate(chosen, axis=0)
    r = dot_nt(w2_ref[...], soft)
    rc = dot_nt(w2_ref[...], chosen)
    inv = 1.0 / r[0:2]
    both = jnp.concatenate([(r[2:4] + r[4:6] + r[6:8]) * inv, rc[0:2] * inv], axis=0)
    both = jnp.concatenate([both[:, 128 * v : 128 * v + 128] for v in range(2 * GROUP)], axis=0)
    high = both.astype(BF)
    rest = both - high.astype(F32)
    mid = rest.astype(BF)
    low = (rest - mid.astype(F32)).astype(BF)
    both = dot(jnp.concatenate([high, mid, low], axis=0), flip_ref[...])
    both = both[0 : 8 * GROUP] + both[8 * GROUP : 16 * GROUP] + both[16 * GROUP : 24 * GROUP]
    turned = pltpu.roll(both, 64, 1)
    left = lax.broadcasted_iota(jnp.int32, (1, 128), 1) < 64
    cell_iota = lax.broadcasted_iota(jnp.int32, (128, 128), 0)
    for g in range(GROUP):
        for y in range(4):
            at = (2 * g + y // 2) * 4
            lo, hi = (both, turned) if y % 2 == 0 else (turned, both)
            mean_ref[g, y : y + 1, :] = jnp.where(left, lo[at : at + 1], hi[at + 1 : at + 2])
            c = jnp.where(left, lo[at + 2 : at + 3], hi[at + 3 : at + 4])
            pair = jnp.concatenate([c * elev_ref[g, y : y + 1, :], c], axis=0)
            pair_hi = pair.astype(BF).astype(F32)
            vals = jnp.concatenate([pair_hi, pair - pair_hi, jnp.zeros((4, 128), F32)], axis=0)
            hot = jnp.where(cell_iota == cell_ref[g, y : y + 1, :], 1.0, 0.0).astype(BF)
            binned = dot_nt(vals.astype(BF), hot)
            got = binned[0:2] + binned[2:4]
            at = 4 * g + y
            rows_ref[0, at : at + 1, 0:128] = got[0:1]
            rows_ref[0, at : at + 1, 128:256] = got[1:2]


def sweep_steps(
    first, steps, slot, own, edge, main, far_blocks, up, down, stats, table, pat, masks, w2, flip,
    elev, cell, far_in_main,
):
    images = own.shape[0]

    def slot_near(g):
        return lambda n, k, s: (s[GROUP * k + g], n + first, 0, 0)

    def slot_far(g):
        if far_in_main:
            return lambda n, k, s: (s[GROUP * k + g], n + first + 1, 0, 0)
        return lambda n, k, s: (GROUP * k + g, 0, 0, 0)

    def near(n, k, s):
        return (k, n + first, 0, 0)

    def far(n, k, s):
        return (k, n + first + 1, 0, 0) if far_in_main else (k, 0, 0, 0)

    def whole(n, k, s):
        return (0, 0)

    def pixels(n, k, s):
        return (k, 0, n + first)

    in_specs = [pl.BlockSpec((1, 1, 256, 128), slot_near(g)) for g in range(GROUP)]
    in_specs += [pl.BlockSpec((1, 1, 256, 128), slot_far(g)) for g in range(GROUP)]
    in_specs += [
        pl.BlockSpec((GROUP, 1, WIN, 256), near),
        pl.BlockSpec((GROUP, 1, WIN, 128), near),
        pl.BlockSpec((GROUP, 1, 64, 128), near),
        pl.BlockSpec((GROUP, 1, 64, 128), far),
        pl.BlockSpec((GROUP, 1, 64, 128), near),
        pl.BlockSpec((GROUP, 1, 64, 128), far),
        pl.BlockSpec((GROUP, 1, 8, 128), near),
        pl.BlockSpec((GROUP, 1, 8, 128), far),
        pl.BlockSpec((GROUP, 1, 64, 128), near),
        pl.BlockSpec((128, 1536), whole),
        pl.BlockSpec((16, 256), whole),
        pl.BlockSpec((8, 256), whole),
        pl.BlockSpec((128, 128), whole),
        pl.BlockSpec((GROUP, 4, 128), pixels),
        pl.BlockSpec((GROUP, 4, 128), pixels),
    ]
    return pl.pallas_call(
        sweep_kernel,
        grid_spec=pltpu.PrefetchScalarGridSpec(
            num_scalar_prefetch=1,
            grid=(steps, images // GROUP),
            in_specs=in_specs,
            out_specs=[
                pl.BlockSpec((GROUP, 4, 128), lambda n, k, s: (k, 0, n)),
                pl.BlockSpec((1, 4 * GROUP, 256), lambda n, k, s: (n, k, 0)),
            ],
            scratch_shapes=[pltpu.VMEM((4 * GROUP, 72, 128), F32)],
        ),
        out_shape=[
            jax.ShapeDtypeStruct((images, 4, steps * 128), F32),
            jax.ShapeDtypeStruct((steps, images * 4, 256), F32),
        ],
        compiler_params=PARAMS,
        cost_estimate=pl.CostEstimate(
            flops=steps * images * 200_000_000, bytes_accessed=steps * images * 400_000,
            transcendentals=0,
        ),
        name="sweep",
    )(
        slot, *[main] * GROUP, *[far_blocks] * GROUP, own, edge, up[0], up[1], down[0], down[1],
        stats[0], stats[1], table, pat, masks, w2, flip, elev, cell,
    )


def depth_weights(planes):
    high = lax.reduce_precision(planes, 8, 7)
    mid = lax.reduce_precision(planes - high, 8, 7)
    zero = jnp.zeros_like(planes)
    rows = []
    for v in (jnp.ones_like(planes), high, mid, planes - high - mid):
        rows.append(jnp.concatenate([v, zero]))
        rows.append(jnp.concatenate([zero, v]))
    w = jnp.stack(rows)
    return jnp.concatenate([w, w], axis=1).astype(BF)


def collect_kernel(list_ref, count_ref, a_ref, b_ref, c_ref, out_ref, rows):
    at = 0
    for part in (a_ref, b_ref, c_ref):
        for n in range(part.shape[0]):
            rows[at : at + part.shape[1], :] = part[n]
            at += part.shape[1]
    for o in range(out_ref.shape[0]):

        def move(step, carry):
            for i in range(8):
                e = step * 8 + i
                out_ref[o, pl.ds(e, 1), :] = rows[pl.ds(list_ref[o, e], 1), :]
            return carry

        lax.fori_loop(0, (count_ref[o] + 7) // 8, move, 0)


def collect(row_list, counts, parts):
    owners, cap = row_list.shape
    total = sum(p.shape[0] * p.shape[1] for p in parts)
    return pl.pallas_call(
        collect_kernel,
        grid_spec=pltpu.PrefetchScalarGridSpec(
            num_scalar_prefetch=2,
            grid=(1,),
            in_specs=[pl.BlockSpec(p.shape, lambda i, a, b: (0, 0, 0)) for p in parts],
            out_specs=pl.BlockSpec((owners, cap, 2 * CELLS), lambda i, a, b: (0, 0, 0)),
            scratch_shapes=[pltpu.VMEM((total, 2 * CELLS), F32)],
        ),
        out_shape=jax.ShapeDtypeStruct((owners, cap, 2 * CELLS), F32),
        compiler_params=PARAMS,
        name="collect",
    )(row_list, counts, *parts)


def place_kernel(slot_ref, count_ref, got_ref, out_ref):
    out_ref[...] = jnp.zeros_like(out_ref)
    for t in range(got_ref.shape[0]):
        count = count_ref[t]

        def add(step, carry):
            for i in range(8):
                e = step * 8 + i
                at = pl.ds(slot_ref[t, e], 1)
                row = jnp.where(e < count, got_ref[t, pl.ds(e, 1), :], 0.0)
                out_ref[at, :] = out_ref[at, :] + row
            return carry

        lax.fori_loop(0, (count + 7) // 8, add, 0)


def place(slots, counts, got, total):
    return pl.pallas_call(
        place_kernel,
        grid_spec=pltpu.PrefetchScalarGridSpec(
            num_scalar_prefetch=2,
            grid=(1,),
            in_specs=[pl.BlockSpec(got.shape, lambda i, a, b: (0, 0, 0))],
            out_specs=pl.BlockSpec((total, 2 * CELLS), lambda i, a, b: (0, 0)),
        ),
        out_shape=jax.ShapeDtypeStruct((total, 2 * CELLS), F32),
        compiler_params=PARAMS,
        name="place",
    )(slots, counts, got)


def neighbour_rows(head, tail):
    count = lax.axis_size("tile")
    above = lax.ppermute(tail, "tile", [(i, i + 1) for i in range(count - 1)])
    below = lax.ppermute(head, "tile", [(i + 1, i) for i in range(count - 1)])
    return above, below


def on_device(
    features, partner_ids, depth_planes, cam_height, ray_down, depth_index, cell_index,
    block_list, block_slot, block_count,
):
    group_count = lax.axis_size("img")
    owners = lax.axis_size("tile")
    my_group = lax.axis_index("img")
    my_tile = lax.axis_index("tile")
    images = features.shape[0]
    table = partner_ids.reshape(group_count, images)
    source_of = table // images
    chosen = jnp.sum(jnp.where(source_of == my_group, table % images, 0), axis=1)
    slot = lax.dynamic_index_in_dim(source_of, my_group, 0, False)

    def exchange(a):
        return lax.all_to_all(a, "img", split_axis=0, concat_axis=0, tiled=True)

    main = exchange(pick(chosen, features, STEPS))

    every = jnp.arange(images, dtype=jnp.int32)
    own = pick(every, features, STEPS + 1)
    own_head, own_tail, own_stats = edges(every, own)
    own_up, own_down = neighbour_rows(own_head, own_tail)
    own_turned, edge_turned, own_table = prepare(own, own_up, own_down, own_stats, depth_index)
    packed = pack(chosen, own)

    hyp = jnp.arange(NDEPTH, dtype=jnp.int32)[:, None, None, None]
    plane_at = jnp.sum(
        jnp.where(hyp == depth_index[None], depth_planes[:, None, None, None], 0.0), 0
    )
    elevation = cam_height[:, None, None] - ray_down * plane_at

    meta = jnp.concatenate(
        [block_slot[0, 0], jnp.broadcast_to(block_count[0, 0][:, None], (owners, 128))], axis=1
    )
    metas = [lax.dynamic_slice_in_dim(meta, my_tile, 1, 0)]
    for s in range(1, owners):
        mine = lax.dynamic_slice_in_dim(meta, (my_tile + s) % owners, 1, 0)
        metas.append(lax.ppermute(mine, "tile", [(i, (i + s) % owners) for i in range(owners)]))
    metas = jnp.concatenate(metas, axis=0)
    metas = jnp.take(metas, (my_tile - jnp.arange(owners)) % owners, axis=0)

    w2 = depth_weights(depth_planes)
    pat, masks, flip = table_patterns(), row_masks(), flips()

    last = exchange(packed)
    main, _, own_turned, edge_turned, own_table, elevation, metas, w2 = lax.optimization_barrier(
        (main, packed, own_turned, edge_turned, own_table, elevation, metas, w2)
    )
    head, tail, stats = edges(slot, main)
    up, down = neighbour_rows(head, tail)
    common = (own_table, pat, masks, w2, flip, elevation, cell_index)

    def inner(first, steps):
        return sweep_steps(
            first, steps, slot, own_turned, edge_turned, main, main, (up, up), (down, down),
            (stats, stats), *common, True,
        )

    mean_a, rows_a = inner(0, 2)
    last, mean_a = lax.optimization_barrier((last, mean_a))
    head_l, tail_l, stats_l, far = unpack(slot, last)
    up_l, down_l = neighbour_rows(head_l, tail_l)
    mean_b, rows_b = inner(2, 1)
    mean_c, rows_c = sweep_steps(
        3, 1, slot, own_turned, edge_turned, main, far, (up, up_l), (down, down_l),
        (stats, stats_l), *common, False,
    )
    mean_range = jnp.concatenate([mean_a, mean_b, mean_c], axis=2)

    lists = block_list[0, 0]
    row_list = lists % STEPS * rows_c.shape[1] + lists // STEPS
    send = collect(row_list, block_count[0, 0], (rows_a, rows_b, rows_c))
    got = lax.all_to_all(send, "tile", split_axis=0, concat_axis=0, tiled=True)
    dense = place(metas[:, :128], metas[:, 128], got, group_count * PATCH_DEV)
    parts = exchange(dense.reshape(group_count, PATCH_DEV, 2 * CELLS))
    total = jnp.sum(parts, axis=0)
    return mean_range, total[:, :CELLS] / (total[:, CELLS:] + 1.0)


def solution(mesh):
    return jax.shard_map(
        on_device,
        mesh=mesh,
        in_specs=(
            P("img", None, "tile", None),
            P(),
            P(),
            P("img"),
            P("img", "tile", None),
            P("img", "tile", None),
            P("img", "tile", None),
            P("img", "tile", None, None),
            P("img", "tile", None, None),
            P("img", "tile", None),
        ),
        out_specs=(P("img", "tile", None), P(("img", "tile"), None)),
        check_vma=False,
    )
```

time: 344 us -> 279 us (0.81); the launches traced: 338 us -> 277 us
  Pallas kernels: 185 us -> 107 us
  waiting for transfers between devices: 55.8 us -> 71 us
  starting transfers between devices: 68.9 us -> 82.6 us
  other arithmetic: 11.9 us -> 5.82 us
  local copies, waits for them, and re-layouts: 15.9 us -> 9.84 us
    pallas_call x4 -> x2, Pallas kernels: 56.2 us -> 17.4 us  [pick(): pl.pallas_call(kernel, grid_spec=pltpu.PrefetchScalarGridSpec(num_scalar_...]
    pallas_call x2 -> x3, Pallas kernels: 67.5 us -> 37.5 us  [sweep_steps(): pl.pallas_call(sweep_kernel, grid_spec=pltpu.PrefetchScalarGridSpec(num_s...]
    pallas_call x3 -> x2, Pallas kernels: 35.9 us -> 14.6 us  [edges(): pl.pallas_call(edge_kernel, grid_spec=pltpu.PrefetchScalarGridSpec(num_sc...]
    all_to_all x3, starting transfers between devices: 40.5 us -> 56.7 us  [exchange(): return lax.all_to_all(a, 'img', split_axis=0, concat_axis=0, tiled=True)]
    ppermute x3, waiting for transfers between devices: 0.01 us -> 15.4 us  [on_device(): lax.ppermute(mine, 'tile', [(i, (i + s) % owners) for i in range(owners)])]
    pallas_call x0 -> x2, Pallas kernels: none -> 14.6 us  [the longest x1 7.36 us: unpack(): pl.pallas_call(unpack_kernel, grid_spec=pltpu.PrefetchScalarGridSpec(num_...]
    ppermute x3, starting transfers between devices: 9.89 us -> 4.94 us  [on_device(): lax.ppermute(mine, 'tile', [(i, (i + s) % owners) for i in range(owners)])]
    unnamed x49 -> x39, local copies, waits for them, and re-layouts: 10.1 us -> 5.49 us
  transfers between devices with their start and end apart: 13 -> 13, of which waited for: 3 -> 4; matrix products, arithmetic and copies ran while one was open for 5% -> 3% of each run, Pallas kernels for 47% -> 23%
where the time goes in v2:
time: 279 us; the launch traced here: 277 us
  Pallas kernels  107 us (38%)
  starting transfers between devices  82.6 us (30%)
  waiting for transfers between devices  71 us (25%)
  local copies, waits for them, and re-layouts  9.84 us (4%)
  other arithmetic  5.82 us (2%)
    all_to_all x3, starting transfers between devices, exchange(): return lax.all_to_all(a, 'img', split_axis=0, concat_axis=0, tiled=True)  56.7 us
    all_to_all x3, waiting for transfers between devices, exchange(): return lax.all_to_all(a, 'img', split_axis=0, concat_axis=0, tiled=True)  49.9 us
    pallas_call x3, Pallas kernels, sweep_steps(): pl.pallas_call(sweep_kernel, grid_spec=pltpu.PrefetchScalarGridSpec(num_s...  37.5 us
    pallas_call x2, Pallas kernels, pick(): pl.pallas_call(kernel, grid_spec=pltpu.PrefetchScalarGridSpec(num_scalar_...  17.4 us
    pallas_call x1, Pallas kernels, prepare(): pl.pallas_call(prepare_kernel, grid=(images,), in_specs=[pl.BlockSpec((1,...  15.5 us
    ppermute x3, waiting for transfers between devices, on_device(): lax.ppermute(mine, 'tile', [(i, (i + s) % owners) for i in range(owners)])  15.4 us
    pallas_call x2, Pallas kernels, edges(): pl.pallas_call(edge_kernel, grid_spec=pltpu.PrefetchScalarGridSpec(num_sc...  14.6 us
    ppermute x3, starting transfers between devices, neighbour_rows(): above = lax.ppermute(tail, 'tile', [(i, i + 1) for i in range(count - 1)])  11.5 us
  transfers between devices with their start and end apart: 13, of which 4 were waited for; matrix products, arithmetic and copies ran while one was open for 3% of the time, Pallas kernels for 23%

profile of v2, /device:TPU:1, one launch (start us, length us, event | category | flops | bytes accessed | tf_op | source)
XLA Modules:
  0.0 277.3 jit_solution(5128358951252347059)
XLA Ops:
  0.6 0.8 reshape.74
  1.4 0.7 fusion.2
  2.1 10.9 %pick.3 = bf16[32,4,64,4,128]{4,3,2,1,0:T(4,128)(2,1)} custom-call(s32[32]{0:T(128)} %get-tuple-element.58.idx_ref, bf16[16,64,4,768]{3,2,1,0:T(4,128)(2,1)} %features_ref.3), custom_call_target="tpu_custom_call" | custom-call | bytes 16777216 | tf_op jit(solution)/shard_map/pick/pallas_call | solution.py:135
  13.0 8.6 %all-to-all-start.1 = ((bf16[32,4,256,128]{3,2,1,0:T(8,128)(2,1)}), bf16[32,4,256,128]{3,2,1,0:T(8,128)(2,1)}, u32[]{:S(2)}, u32[]{:S(2)}) async-start(bf16[32,4,256,128]{3,2,1,0:T(8,128)(2,1)} %bitcast.46), calls=%async_computation.1 | async-start | bytes 16777216 | tf_op jit(solution)/shard_map/all_to_all | solution.py:641
  21.6 0.5 iota.15.idx_ref
  22.1 6.5 %pick.2 = bf16[16,5,64,4,128]{4,3,2,1,0:T(4,128)(2,1)} custom-call(s32[16]{0:T(128)} %iota.15.idx_ref, bf16[16,64,4,768]{3,2,1,0:T(4,128)(2,1)} %features_ref.3), custom_call_target="tpu_custom_call" | custom-call | bytes 10485760 | tf_op jit(solution)/shard_map/pick/pallas_call | solution.py:135
  28.7 0.5 iota.16.slot_ref
  29.2 0.0 copy-start.15
  29.2 0.0 copy-start.16
  29.2 0.0 copy-start.6
  29.3 0.0 copy-start.14
  29.3 7.7 %edges.2 = (bf16[16,5,64,128]{3,2,1,0:T(8,128)(2,1)}, bf16[16,5,64,128]{3,2,1,0:T(8,128)(2,1)}, f32[16,5,8,128]{3,2,1,0:T(8,128)}) custom-call(s32[16]{0:T(128)} %iota.16.slot_ref, bf16[16,5,256,128]{3,2,1,0:T(8,128)(2,1)} %bitcast.37, bf16[16,5,256,128]{3,2,1,0:T(8,128)(2,1)} %bitcast.38, bf16[16,5,256,128]{3,2,1,0:T(8,128)(2,1)} %bitcast.39, ...), custom_call_target="tpu_custom_call" | custom-call | flops 1600000000 | bytes 8000000 | tf_op jit(solution)/shard_map/edges/pallas_call | solution.py:271
  37.0 3.6 %collective-permute-start = (bf16[16,5,64,128]{3,2,1,0:T(8,128)(2,1)}, bf16[16,5,64,128]{3,2,1,0:T(8,128)(2,1)S(1)}, u32[]{:S(2)}, u32[]{:S(2)}) collective-permute-start(bf16[16,5,64,128]{3,2,1,0:T(8,128)(2,1)} %get-tuple-element.30), channel_id=1, source_target_pairs={{0,1},{1,2},{2,3},{4,5},{5,6},{6,7},{8,9},{9,10},{10,11},{12,13},{... | collective-permute-start | bytes 3932168 | tf_op jit(solution)/shard_map/ppermute | solution.py:621
  40.6 1.3 collective-permute-start.1
  42.0 0.1 broadcast_in_dim.40
  42.0 4.3 %collective-permute-start.4 = (s32[1,256]{1,0:T(1,128)S(1)}, s32[1,256]{1,0:T(1,128)S(1)}, u32[]{:S(2)}, u32[]{:S(2)}) collective-permute-start(s32[1,256]{1,0:T(1,128)S(1)} %get-tuple-element.63), channel_id=1, source_target_pairs={{0,3},{1,0},{2,1},{3,2},{4,7},{5,4},{6,5},{7,6},{8,11},{9,8},{10,9... | collective-permute-start | bytes 3080 | tf_op jit(solution)/shard_map/ppermute | solution.py:664
  46.3 0.0 collective-permute-start.3
  46.3 0.7 collective-permute-start.2
  47.1 0.1 pad_bitcast_fusion.4
  47.1 0.1 pad_bitcast_fusion
  47.3 0.6 pad_maximum_fusion.1.refs_27_
  47.9 1.0 select_reduce_fusion
  48.9 0.8 fusion.refs_29_
  49.6 0.5 fusion.17.slot_ref
  50.2 7.2 %pack.1 = bf16[32,136,128]{2,1,0:T(8,128)(2,1)} custom-call(s32[32]{0:T(128)} %get-tuple-element.58.idx_ref, bf16[16,5,256,128]{3,2,1,0:T(8,128)(2,1)} %bitcast.41, bf16[16,5,256,128]{3,2,1,0:T(8,128)(2,1)} %bitcast.42, bf16[16,5,256,128]{3,2,1,0:T(8,128)(2,1)} %bitcast.43, bf16[16,5,256,128]{3,2,1,0:T(8,128)(2,1)} %bitcast.44, ...), custom_call_target="tpu_custom_call" | custom-call | tf_op jit(solution)/shard_map/pack/pallas_call | solution.py:190
  57.4 15.4 %collective-permute-done.4 = s32[1,256]{1,0:T(1,128)S(1)} collective-permute-done((s32[1,256]{1,0:T(1,128)S(1)}, s32[1,256]{1,0:T(1,128)S(1)}, u32[]{:S(2)}, u32[]{:S(2)}) %collective-permute-start.4) | collective-permute-done | bytes 1056 | tf_op jit(solution)/shard_map/ppermute | solution.py:664
  72.8 0.0 collective-permute-done.3
  72.8 0.6 gather_fusion
  73.4 0.1 broadcast_select_fusion
  73.5 0.0 collective-permute-done.up_ref
  73.5 0.0 collective-permute-done.1.down_ref
  73.5 1.1 copy-done.17
  74.6 0.4 copy-done.18
  74.9 15.5 %prepare.1 = (bf16[16,4,144,256]{3,2,1,0:T(8,128)(2,1)}, bf16[16,4,144,128]{3,2,1,0:T(8,128)(2,1)}, bf16[16,4,64,128]{3,2,1,0:T(8,128)(2,1)}) custom-call(bf16[16,5,256,128]{3,2,1,0:T(8,128)(2,1)} %bitcast.45, bf16[16,5,64,128]{3,2,1,0:T(8,128)(2,1)} %copy-done.17, bf16[16,5,64,128]{3,2,1,0:T(8,128)(2,1)} %copy-done.18, ...), custom_call_target="tpu_custom_call" | custom-call | flops 2560000000 | bytes 16000000 | tf_op jit(solution)/shard_map/prepare/pallas_call | solution.py:342
  90.4 39.8 %all-to-all-done.1.refs_0_.refs_1_.refs_2_.refs_3_.refs_4_.refs_5_.refs_6_.refs_7_.refs_8_.refs_9_.refs_10_.refs_11_.refs_12_.refs_13_.refs_14_.refs_15_ = bf16[32,4,256,128]{3,2,1,0:T(8,128)(2,1)} async-done(((bf16[32,4,256,128]{3,2,1,0:T(8,128)(2,1)}), bf16[32,4,256,128]{3,2,1,0:T(8,128)(2,1)}, u32[]{:S(2)}, u32[]{:S(2)}) %all-to-all-start.1) | async-done | bytes 8388640 | tf_op jit(solution)/shard_map/all_to_all | solution.py:641
  130.2 6.9 %edges.3 = (bf16[16,4,64,128]{3,2,1,0:T(8,128)(2,1)}, bf16[16,4,64,128]{3,2,1,0:T(8,128)(2,1)}, f32[16,4,8,128]{3,2,1,0:T(8,128)}) custom-call(s32[16]{0:T(128)} %fusion.17.slot_ref, ...), custom_call_target="tpu_custom_call" | custom-call | flops 1280000000 | bytes 6400000 | tf_op jit(solution)/shard_map/edges/pallas_call | solution.py:271
  137.0 3.6 %collective-permute-start.5 = (bf16[16,4,64,128]{3,2,1,0:T(8,128)(2,1)}, bf16[16,4,64,128]{3,2,1,0:T(8,128)(2,1)S(1)}, u32[]{:S(2)}, u32[]{:S(2)}) collective-permute-start(bf16[16,4,64,128]{3,2,1,0:T(8,128)(2,1)} %get-tuple-element.39), channel_id=1, source_target_pairs={{0,1},{1,2},{2,3},{4,5},{5,6},{6,7},{8,9},{9,10},{10,11},{12,13},{... | collective-permute-start | bytes 3145736 | tf_op jit(solution)/shard_map/ppermute | solution.py:621
  140.6 1.3 collective-permute-start.6
  141.9 21.7 %all-to-all-start = ((bf16[32,136,128]{2,1,0:T(8,128)(2,1)}), bf16[32,136,128]{2,1,0:T(8,128)(2,1)S(1)}, u32[]{:S(2)}, u32[]{:S(2)}) async-start(bf16[32,136,128]{2,1,0:T(8,128)(2,1)} %pack.1), calls=%async_computation | async-start | bytes 2228224 | tf_op jit(solution)/shard_map/all_to_all | solution.py:641
  163.7 0.5 fusion.7.list_ref
  164.2 1.0 copy-done.1
  165.2 0.3 copy-done.2
  165.6 17.3 %sweep.3 = (f32[16,4,256]{2,1,0:T(4,128)}, f32[2,64,256]{2,1,0:T(8,128)}) custom-call(s32[16]{0:T(128)} %fusion.17.slot_ref, bf16[32,4,256,128]{3,2,1,0:T(8,128)(2,1)} %all-to-all-done.1.refs_0_.refs_1_.refs_2_.refs_3_.refs_4_.refs_5_.refs_6_.refs_7_.refs_8_.refs_9_.refs_10_.refs_11_.refs_12_.refs_13_.refs_14_.refs_15_, ...), custom_call_target="tpu_custom_call" | custom-call | flops 6400000000 | bytes 12800000 | tf_op jit(solution)/shard_map/sweep/pallas_call | solution.py:513
  182.8 0.0 all-to-all-done.refs_0_.refs_1_.refs_2_.refs_3_
  182.9 1.0 copy-done
  183.9 7.4 %unpack.1 = (bf16[16,1,64,128]{3,2,1,0:T(8,128)(2,1)}, bf16[16,1,64,128]{3,2,1,0:T(8,128)(2,1)}, f32[16,1,8,128]{3,2,1,0:T(8,128)}, bf16[16,1,256,128]{3,2,1,0:T(8,128)(2,1)}) custom-call(s32[16]{0:T(128)} %fusion.17.slot_ref, bf16[32,136,128]{2,1,0:T(8,128)(2,1)} %copy-done, bf16[32,136,128]{2,1,0:T(8,128)(2,1)} %copy-done, bf16[32,136,128]{2,1,0:T(8,128)(2,1)} %copy-done, ...), custom_call_target="tpu_custom_call" | custom-call | tf_op jit(solution)/shard_map/unpack/pallas_call | solution.py:299
  191.2 4.3 %collective-permute-start.7 = (bf16[16,1,64,128]{3,2,1,0:T(8,128)(2,1)}, bf16[16,1,64,128]{3,2,1,0:T(8,128)(2,1)S(1)}, u32[]{:S(2)}, u32[]{:S(2)}) collective-permute-start(bf16[16,1,64,128]{3,2,1,0:T(8,128)(2,1)} %get-tuple-element.50), channel_id=1, source_target_pairs={{0,1},{1,2},{2,3},{4,5},{5,6},{6,7},{8,9},{9,10},{10,11},{12,13},{... | collective-permute-start | bytes 786440 | tf_op jit(solution)/shard_map/ppermute | solution.py:621
  195.5 1.5 collective-permute-start.8
  197.0 10.1 %sweep.4 = (f32[16,4,128]{2,1,0:T(4,128)}, f32[1,64,256]{2,1,0:T(8,128)}) custom-call(s32[16]{0:T(128)} %fusion.17.slot_ref, bf16[32,4,256,128]{3,2,1,0:T(8,128)(2,1)} %all-to-all-done.1.refs_0_.refs_1_.refs_2_.refs_3_.refs_4_.refs_5_.refs_6_.refs_7_.refs_8_.refs_9_.refs_10_.refs_11_.refs_12_.refs_13_.refs_14_.refs_15_, ...), custom_call_target="tpu_custom_call" | custom-call | flops 3200000000 | bytes 6400000 | tf_op jit(solution)/shard_map/sweep/pallas_call | solution.py:513
  207.1 0.0 collective-permute-done.7.refs_19_
  207.2 0.7 copy-done.4
  207.8 0.1 copy-done.5
  207.9 10.1 %sweep.5 = (f32[16,4,128]{2,1,0:T(4,128)}, f32[1,64,256]{2,1,0:T(8,128)}) custom-call(s32[16]{0:T(128)} %fusion.17.slot_ref, bf16[32,4,256,128]{3,2,1,0:T(8,128)(2,1)} %all-to-all-done.1.refs_0_.refs_1_.refs_2_.refs_3_.refs_4_.refs_5_.refs_6_.refs_7_.refs_8_.refs_9_.refs_10_.refs_11_.refs_12_.refs_13_.refs_14_.refs_15_, ...), custom_call_target="tpu_custom_call" | custom-call | flops 3200000000 | bytes 6400000 | tf_op jit(solution)/shard_map/sweep/pallas_call | solution.py:513
  218.1 3.7 %collect.1 = f32[4,128,256]{2,1,0:T(8,128)} custom-call(s32[4,128]{1,0:T(4,128)} %fusion.7.list_ref, s32[4]{0:T(128)} %bitcast.49, f32[2,64,256]{2,1,0:T(8,128)} %get-tuple-element.55.a_ref, f32[1,64,256]{2,1,0:T(8,128)} %get-tuple-element.56.b_ref, f32[1,64,256]{2,1,0:T(8,128)} %get-tuple-element.57.c_ref), custom_call_target="tpu_custom_call" | custom-call | tf_op jit(solution)/shard_map/collect/pallas_call | solution.py:573
  221.8 5.5 %all-to-all-start.2 = ((f32[4,128,256]{2,1,0:T(8,128)}), f32[4,128,256]{2,1,0:T(8,128)S(1)}, u32[]{:S(2)}, u32[]{:S(2)}) async-start(f32[4,128,256]{2,1,0:T(8,128)} %collect.1), calls=%async_computation.2 | async-start | bytes 1048576 | tf_op jit(solution)/shard_map/all_to_all | solution.py:699
  227.3 0.6 slice.12.slot_ref
  227.9 0.6 slice_reduce_fusion.count_ref
  228.5 5.7 %all-to-all-done.2.got_ref = f32[4,128,256]{2,1,0:T(8,128)S(1)} async-done(((f32[4,128,256]{2,1,0:T(8,128)}), f32[4,128,256]{2,1,0:T(8,128)S(1)}, u32[]{:S(2)}, u32[]{:S(2)}) %all-to-all-start.2) | async-done | bytes 524320 | tf_op jit(solution)/shard_map/all_to_all | solution.py:699
  234.2 0.8 copy-done.3
  235.0 3.7 %place.1 = f32[512,256]{1,0:T(8,128)} custom-call(s32[4,128]{1,0:T(4,128)} %slice.12.slot_ref, s32[4]{0:T(128)} %slice_reduce_fusion.count_ref, f32[4,128,256]{2,1,0:T(8,128)} %copy-done.3), custom_call_target="tpu_custom_call" | custom-call | tf_op jit(solution)/shard_map/place/pallas_call | solution.py:605
  238.7 26.3 %all-to-all-start.3 = ((f32[32,16,256]{2,1,0:T(8,128)}), f32[32,16,256]{2,1,0:T(8,128)S(1)}, u32[]{:S(2)}, u32[]{:S(2)}) async-start(f32[32,16,256]{2,1,0:T(8,128)} %bitcast.47), calls=%async_computation.3 | async-start | bytes 1048576 | tf_op jit(solution)/shard_map/all_to_all | solution.py:641
  265.1 1.4 pad_maximum_fusion
  266.5 10.2 %all-to-all-done.3 = f32[32,16,256]{2,1,0:T(8,128)S(1)} async-done(((f32[32,16,256]{2,1,0:T(8,128)}), f32[32,16,256]{2,1,0:T(8,128)S(1)}, u32[]{:S(2)}, u32[]{:S(2)}) %all-to-all-start.3) | async-done | bytes 524320 | tf_op jit(solution)/shard_map/all_to_all | solution.py:641
  276.7 0.6 fusion.5
  (39 shorter events, 0.3 us)
Async XLA Ops:
  13.0 117.2 %all-to-all-start.1 = ((bf16[32,4,256,128]{3,2,1,0:T(8,128)(2,1)}), bf16[32,4,256,128]{3,2,1,0:T(8,128)(2,1)}, u32[]{:S(2)}, u32[]{:S(2)}) async-start(bf16[32,4,256,128]{3,2,1,0:T(8,128)(2,1)} %bitcast.46), calls=%async_computation.1 | async-start | bytes 16777216 | tf_op jit(solution)/shard_map/all_to_all | solution.py:641
  29.2 12.7 %copy-start.13 = (s32[1,1,4]{2,1,0:T(1,128)S(1)}, s32[1,1,4]{2,1,0:T(1,128)}, u32[]{:S(2)}) copy-start(s32[1,1,4]{2,1,0:T(1,128)} %param.35) | copy-start | bytes 52
  29.2 12.8 %copy-start.11 = (s32[1,1,4,128]{3,2,1,0:T(4,128)S(1)}, s32[1,1,4,128]{3,2,1,0:T(4,128)}, u32[]{:S(2)}) copy-start(s32[1,1,4,128]{3,2,1,0:T(4,128)} %param.34) | copy-start | bytes 6148
  29.2 17.8 %copy-start.7 = (s32[16,4,512]{2,1,0:T(4,128)S(1)}, s32[16,4,512]{2,1,0:T(4,128)}, u32[]{:S(2)}) copy-start(s32[16,4,512]{2,1,0:T(4,128)} %index_ref.1) | copy-start | bytes 393220
  29.2 17.8 %copy-start.10 = (f32[64]{0:T(128)S(1)}, f32[64]{0:T(128)}, u32[]{:S(2)}) copy-start(f32[64]{0:T(128)} %param.28) | copy-start | bytes 772
  29.2 18.0 %copy-start.15 = (bf16[1,128]{1,0:T(2,128)(2,1)S(1)}, bf16[1,128]{1,0:T(2,128)(2,1)}, u32[]{:S(2)}) copy-start(bf16[1,128]{1,0:T(2,128)(2,1)} %constant.228) | copy-start | bytes 772
  29.2 18.0 %copy-start.16 = (bf16[1,128]{1,0:T(2,128)(2,1)S(1)}, bf16[1,128]{1,0:T(2,128)(2,1)}, u32[]{:S(2)}) copy-start(bf16[1,128]{1,0:T(2,128)(2,1)} %constant.229) | copy-start | bytes 772
  29.2 19.6 %copy-start.6 = (f32[16,4,512]{2,1,0:T(4,128)S(1)}, f32[16,4,512]{2,1,0:T(4,128)}, u32[]{:S(2)}) copy-start(f32[16,4,512]{2,1,0:T(4,128)} %param.30) | copy-start | bytes 393220
  29.3 19.6 %copy-start.14 = (f32[16]{0:T(128)S(1)}, f32[16]{0:T(128)}, u32[]{:S(2)}) copy-start(f32[16]{0:T(128)} %param.29) | copy-start | bytes 196
  37.0 36.5 %collective-permute-start = (bf16[16,5,64,128]{3,2,1,0:T(8,128)(2,1)}, bf16[16,5,64,128]{3,2,1,0:T(8,128)(2,1)S(1)}, u32[]{:S(2)}, u32[]{:S(2)}) collective-permute-start(bf16[16,5,64,128]{3,2,1,0:T(8,128)(2,1)} %get-tuple-element.30), channel_id=1, source_target_pairs={{0,1},{1,2},{2,3},{4,5},{5,6},{6,7},{8,9},{9,10},{10,11},{12,13},{... | collective-permute-start | bytes 3932168 | tf_op jit(solution)/shard_map/ppermute | solution.py:621
  40.6 32.9 %collective-permute-start.1 = (bf16[16,5,64,128]{3,2,1,0:T(8,128)(2,1)}, bf16[16,5,64,128]{3,2,1,0:T(8,128)(2,1)S(1)}, u32[]{:S(2)}, u32[]{:S(2)}) collective-permute-start(bf16[16,5,64,128]{3,2,1,0:T(8,128)(2,1)} %get-tuple-element.31), channel_id=1, source_target_pairs={{1,0},{2,1},{3,2},{5,4},{6,5},{7,6},{9,8},{10,9},{11,10},{13,12},{... | collective-permute-start | bytes 3932168 | tf_op jit(solution)/shard_map/ppermute | solution.py:622
  42.0 30.7 %collective-permute-start.4 = (s32[1,256]{1,0:T(1,128)S(1)}, s32[1,256]{1,0:T(1,128)S(1)}, u32[]{:S(2)}, u32[]{:S(2)}) collective-permute-start(s32[1,256]{1,0:T(1,128)S(1)} %get-tuple-element.63), channel_id=1, source_target_pairs={{0,3},{1,0},{2,1},{3,2},{4,7},{5,4},{6,5},{7,6},{8,11},{9,8},{10,9... | collective-permute-start | bytes 3080 | tf_op jit(solution)/shard_map/ppermute | solution.py:664
  46.3 26.5 %collective-permute-start.3 = (s32[1,256]{1,0:T(1,128)S(1)}, s32[1,256]{1,0:T(1,128)S(1)}, u32[]{:S(2)}, u32[]{:S(2)}) collective-permute-start(s32[1,256]{1,0:T(1,128)S(1)} %get-tuple-element.62), channel_id=1, source_target_pairs={{0,2},{1,3},{2,0},{3,1},{4,6},{5,7},{6,4},{7,5},{8,10},{9,11},{10,... | collective-permute-start | bytes 3080 | tf_op jit(solution)/shard_map/ppermute | solution.py:664
  46.3 26.5 %collective-permute-start.2 = (s32[1,256]{1,0:T(1,128)S(1)}, s32[1,256]{1,0:T(1,128)S(1)}, u32[]{:S(2)}, u32[]{:S(2)}) collective-permute-start(s32[1,256]{1,0:T(1,128)S(1)} %get-tuple-element.61), channel_id=1, source_target_pairs={{0,1},{1,2},{2,3},{3,0},{4,5},{5,6},{6,7},{7,4},{8,9},{9,10},{10,1... | collective-permute-start | bytes 3080 | tf_op jit(solution)/shard_map/ppermute | solution.py:664
  73.5 1.1 copy-start.17
  73.5 1.5 copy-start.18
  130.2 33.5 %copy-start.12 = (s32[1,1,4,128]{3,2,1,0:T(4,128)S(1)}, s32[1,1,4,128]{3,2,1,0:T(4,128)}, u32[]{:S(2)}) copy-start(s32[1,1,4,128]{3,2,1,0:T(4,128)} %param.33) | copy-start | bytes 6148
  137.0 27.2 %collective-permute-start.5 = (bf16[16,4,64,128]{3,2,1,0:T(8,128)(2,1)}, bf16[16,4,64,128]{3,2,1,0:T(8,128)(2,1)S(1)}, u32[]{:S(2)}, u32[]{:S(2)}) collective-permute-start(bf16[16,4,64,128]{3,2,1,0:T(8,128)(2,1)} %get-tuple-element.39), channel_id=1, source_target_pairs={{0,1},{1,2},{2,3},{4,5},{5,6},{6,7},{8,9},{9,10},{10,11},{12,13},{... | collective-permute-start | bytes 3145736 | tf_op jit(solution)/shard_map/ppermute | solution.py:621
  140.6 23.6 %collective-permute-start.6 = (bf16[16,4,64,128]{3,2,1,0:T(8,128)(2,1)}, bf16[16,4,64,128]{3,2,1,0:T(8,128)(2,1)S(1)}, u32[]{:S(2)}, u32[]{:S(2)}) collective-permute-start(bf16[16,4,64,128]{3,2,1,0:T(8,128)(2,1)} %get-tuple-element.40), channel_id=1, source_target_pairs={{1,0},{2,1},{3,2},{5,4},{6,5},{7,6},{9,8},{10,9},{11,10},{13,12},{... | collective-permute-start | bytes 3145736 | tf_op jit(solution)/shard_map/ppermute | solution.py:622
  141.9 40.9 %all-to-all-start = ((bf16[32,136,128]{2,1,0:T(8,128)(2,1)}), bf16[32,136,128]{2,1,0:T(8,128)(2,1)S(1)}, u32[]{:S(2)}, u32[]{:S(2)}) async-start(bf16[32,136,128]{2,1,0:T(8,128)(2,1)} %pack.1), calls=%async_computation | async-start | bytes 2228224 | tf_op jit(solution)/shard_map/all_to_all | solution.py:641
  164.2 1.0 copy-start.1
  164.2 1.3 copy-start.2
  182.9 1.0 copy-start
  191.2 15.9 %collective-permute-start.7 = (bf16[16,1,64,128]{3,2,1,0:T(8,128)(2,1)}, bf16[16,1,64,128]{3,2,1,0:T(8,128)(2,1)S(1)}, u32[]{:S(2)}, u32[]{:S(2)}) collective-permute-start(bf16[16,1,64,128]{3,2,1,0:T(8,128)(2,1)} %get-tuple-element.50), channel_id=1, source_target_pairs={{0,1},{1,2},{2,3},{4,5},{5,6},{6,7},{8,9},{9,10},{10,11},{12,13},{... | collective-permute-start | bytes 786440 | tf_op jit(solution)/shard_map/ppermute | solution.py:621
  195.5 11.6 %collective-permute-start.8 = (bf16[16,1,64,128]{3,2,1,0:T(8,128)(2,1)}, bf16[16,1,64,128]{3,2,1,0:T(8,128)(2,1)S(1)}, u32[]{:S(2)}, u32[]{:S(2)}) collective-permute-start(bf16[16,1,64,128]{3,2,1,0:T(8,128)(2,1)} %get-tuple-element.51), channel_id=1, source_target_pairs={{1,0},{2,1},{3,2},{5,4},{6,5},{7,6},{9,8},{10,9},{11,10},{13,12},{... | collective-permute-start | bytes 786440 | tf_op jit(solution)/shard_map/ppermute | solution.py:622
  207.1 0.7 copy-start.4
  207.1 0.8 copy-start.5
  207.9 57.1 %copy-start.8 = (f32[16,4,256]{2,1,0:T(4,128)S(1)}, f32[16,4,256]{2,1,0:T(4,128)}, u32[]{:S(2)}) copy-start(f32[16,4,256]{2,1,0:T(4,128)} %get-tuple-element.46) | copy-start | bytes 196612
  207.9 57.1 %copy-start.9 = (f32[16,4,128]{2,1,0:T(4,128)S(1)}, f32[16,4,128]{2,1,0:T(4,128)}, u32[]{:S(2)}) copy-start(f32[16,4,128]{2,1,0:T(4,128)} %get-tuple-element.47) | copy-start | bytes 98308
  221.8 12.4 %all-to-all-start.2 = ((f32[4,128,256]{2,1,0:T(8,128)}), f32[4,128,256]{2,1,0:T(8,128)S(1)}, u32[]{:S(2)}, u32[]{:S(2)}) async-start(f32[4,128,256]{2,1,0:T(8,128)} %collect.1), calls=%async_computation.2 | async-start | bytes 1048576 | tf_op jit(solution)/shard_map/all_to_all | solution.py:699
  234.2 0.8 copy-start.3
  238.7 38.0 %all-to-all-start.3 = ((f32[32,16,256]{2,1,0:T(8,128)}), f32[32,16,256]{2,1,0:T(8,128)S(1)}, u32[]{:S(2)}, u32[]{:S(2)}) async-start(f32[32,16,256]{2,1,0:T(8,128)} %bitcast.47), calls=%async_computation.3 | async-start | bytes 1048576 | tf_op jit(solution)/shard_map/all_to_all | solution.py:641

commit v3 on v2

--- a/solution.py
+++ b/solution.py
@@ -1,3 +1,4 @@
+import functools
 import math
 
 import numpy as np
@@ -28,16 +29,16 @@
     return lax.dot_general(a, b, NT, preferred_element_type=F32)
 
 
-def table_patterns():
-    pat = np.zeros((128, 12, 128), np.float32)
+def table_patterns(ys):
+    pat = np.zeros((128, 3 * len(ys), 128), np.float32)
     for half in range(2):
         lanes = slice(64 * half, 64 * half + 64)
-        for y in range(4):
+        for i, y in enumerate(ys):
             for q in range(2):
                 for s in range(3):
-                    pat[half * 32 + s * 8 + q * 4 + y, y * 3 + q, lanes] = 1.0
-            pat[half * 32 + 24 + y, y * 3 + 2, lanes] = 1.0
-    return jnp.asarray(pat.reshape(128, 12 * 128), BF)
+                    pat[half * 32 + s * 8 + q * 4 + y, i * 3 + q, lanes] = 1.0
+            pat[half * 32 + 24 + y, i * 3 + 2, lanes] = 1.0
+    return jnp.asarray(pat.reshape(128, -1), BF)
 
 
 def row_masks():
@@ -78,12 +79,13 @@
 
 
 def boxed_stats(stats, up, down):
-    upf = up.astype(F32)
-    downf = down.astype(F32)
-    sums = [jnp.sum(upf, 0, keepdims=True)] + [stats[y : y + 1] for y in range(4)]
-    sums.append(jnp.sum(downf, 0, keepdims=True))
-    sqs = [jnp.sum(upf * upf, 0, keepdims=True)] + [stats[4 + y : 5 + y] for y in range(4)]
-    sqs.append(jnp.sum(downf * downf, 0, keepdims=True))
+    blank = jnp.zeros((1, 256), F32)
+    sums = [blank] + [stats[y : y + 1] for y in range(4)] + [blank]
+    sqs = [blank] + [stats[4 + y : 5 + y] for y in range(4)] + [blank]
+    if up is not None:
+        for at, halo in ((0, up.astype(F32)), (5, down.astype(F32))):
+            sums[at] = jnp.sum(halo, 0, keepdims=True)
+            sqs[at] = jnp.sum(halo * halo, 0, keepdims=True)
     tall = jnp.concatenate(
         [v[y] + v[y + 1] + v[y + 2] for v in (sums, sqs) for y in range(4)], axis=0
     )
@@ -95,6 +97,7 @@
 DEPTH = 8
 PART = 4
 PACKED = 136
+FIRST = 3
 
 
 def pick(idx, features, blocks):
@@ -168,14 +171,16 @@
 
 
 def pack_kernel(idx_ref, *refs):
-    blocks, (spread_ref, column_ref, out_ref) = refs[:PART], refs[PART:]
+    whole, part = refs[:PART], refs[PART : 2 * PART]
+    spread_ref, column_ref, out_ref = refs[2 * PART :]
     for g in range(PART):
-        block = blocks[g][0, 0]
-        out_ref[g, 0:128, :] = (
+        out_ref[g, 0:256, :] = whole[g][0, 0]
+        block = part[g][0, 0]
+        out_ref[g, 256:384, :] = (
             dot_nt(block[0:128], spread_ref[:, 0:128]) + dot_nt(block[128:256], spread_ref[:, 128:])
         ).astype(BF)
         line = dot_nt(column_ref[...], block)
-        out_ref[g, 128:136, :] = jnp.concatenate(
+        out_ref[g, 384:392, :] = jnp.concatenate(
             [line[0:1, 0:128], line[0:1, 128:256], jnp.zeros((6, 128), F32)], axis=0
         ).astype(BF)
 
@@ -184,25 +189,29 @@
     count = idx.shape[0]
     spread, column, _, _ = pack_constants()
 
-    def chosen(g):
-        return lambda k, s: (s[PART * k + g], STEPS, 0, 0)
+    def chosen(g, j):
+        return lambda k, s: (s[PART * k + g], j, 0, 0)
 
     return pl.pallas_call(
         pack_kernel,
         grid_spec=pltpu.PrefetchScalarGridSpec(
             num_scalar_prefetch=1,
             grid=(count // PART,),
-            in_specs=[pl.BlockSpec((1, 1, 256, 128), chosen(g)) for g in range(PART)]
+            in_specs=[
+                pl.BlockSpec((1, 1, 256, 128), chosen(g, j))
+                for j in (FIRST, FIRST + 1)
+                for g in range(PART)
+            ]
             + [
                 pl.BlockSpec((128, 256), lambda k, s: (0, 0)),
                 pl.BlockSpec((8, 128), lambda k, s: (0, 0)),
             ],
-            out_specs=pl.BlockSpec((PART, PACKED, 128), lambda k, s: (k, 0, 0)),
-        ),
-        out_shape=jax.ShapeDtypeStruct((count, PACKED, 128), BF),
+            out_specs=pl.BlockSpec((PART, 256 + PACKED, 128), lambda k, s: (k, 0, 0)),
+        ),
+        out_shape=jax.ShapeDtypeStruct((count, 256 + PACKED, 128), BF),
         compiler_params=PARAMS,
         name="pack",
-    )(idx, *[own] * PART, spread, column)
+    )(idx, *[own] * (2 * PART), spread, column)
 
 
 def block_edges(block, sel_ref, stat_ref):
@@ -224,22 +233,24 @@
 
 
 def unpack_kernel(slot_ref, *refs):
-    packed = refs[:PART]
+    packed, before = refs[:PART], refs[PART : 2 * PART]
     (
         spread_ref, into_ref, eye_ref, sel_ref, stat_ref, head_ref, tail_ref, stats_ref, block_ref,
-    ) = refs[PART:]
+    ) = refs[2 * PART :]
     for g in range(PART):
-        wide = dot(packed[g][0, 0:128, :], spread_ref[...])
-        line = packed[g][0, 128:136, :]
+        wide = dot(packed[g][0, 256:384, :], spread_ref[...])
+        line = packed[g][0, 384:392, :]
         line = jnp.concatenate([line[0:1], line[1:2]], axis=1)
         column = dot(eye_ref[...] * line, into_ref[...])
         block = jnp.concatenate([wide[:, :128], wide[:, 128:]], axis=0) + column
-        block = block.astype(BF)
-        block_ref[g, 0] = block
-        head, tail, stats = block_edges(block, sel_ref, stat_ref)
-        head_ref[g, 0] = head
-        tail_ref[g, 0] = tail
-        stats_ref[g, 0] = stats
+        blocks = (packed[g][0, 0:256, :], block.astype(BF))
+        block_ref[g, 0] = before[g][0, 0]
+        for j in range(2):
+            block_ref[g, j + 1] = blocks[j]
+            head, tail, stats = block_edges(blocks[j], sel_ref, stat_ref)
+            head_ref[g, j] = head
+            tail_ref[g, j] = tail
+            stats_ref[g, j] = stats
 
 
 def edge_outputs(images, blocks):
@@ -287,28 +298,32 @@
     )(slot, *[recv] * PART, *constants)
 
 
-def unpack(slot, packed):
+def unpack(slot, packed, main):
     images = slot.shape[0]
     spread, _, into, eye = pack_constants()
     constants = (spread, into, eye) + edge_constants()
-    specs, shapes = edge_outputs(images, 1)
+    specs, shapes = edge_outputs(images, 2)
 
     def by_slot(g):
         return lambda k, s: (s[PART * k + g], 0, 0)
+
+    def before(g):
+        return lambda k, s: (s[PART * k + g], FIRST - 1, 0, 0)
 
     return pl.pallas_call(
         unpack_kernel,
         grid_spec=pltpu.PrefetchScalarGridSpec(
             num_scalar_prefetch=1,
             grid=(images // PART,),
-            in_specs=[pl.BlockSpec((1, PACKED, 128), by_slot(g)) for g in range(PART)]
+            in_specs=[pl.BlockSpec((1, 256 + PACKED, 128), by_slot(g)) for g in range(PART)]
+            + [pl.BlockSpec((1, 1, 256, 128), before(g)) for g in range(PART)]
             + [whole_spec(a) for a in constants],
-            out_specs=specs + [pl.BlockSpec((PART, 1, 256, 128), lambda k, s: (k, 0, 0, 0))],
-        ),
-        out_shape=shapes + [jax.ShapeDtypeStruct((images, 1, 256, 128), BF)],
+            out_specs=specs + [pl.BlockSpec((PART, 3, 256, 128), lambda k, s: (k, 0, 0, 0))],
+        ),
+        out_shape=shapes + [jax.ShapeDtypeStruct((images, 3, 256, 128), BF)],
         compiler_params=PARAMS,
         name="unpack",
-    )(slot, *[packed] * PART, *constants)
+    )(slot, *[packed] * PART, *[main] * PART, *constants)
 
 
 def prepare_kernel(
@@ -369,19 +384,42 @@
     )(own, up, down, stats, depth_index, reversal(), flips())
 
 
-GROUP = 8
-
-
 def skewed(left, right, column, lane, shift):
     return pltpu.roll(jnp.where(lane < column, right, left), shift, 1, stride=1, stride_axis=0)
 
 
-def sweep_kernel(slot_ref, *refs):
-    near_refs, far_refs = refs[:GROUP], refs[GROUP : 2 * GROUP]
-    (
-        own_ref, edge_ref, u0_ref, u1_ref, d0_ref, d1_ref, s0_ref, s1_ref, table_ref, pat_ref,
-        mask_ref, w2_ref, flip_ref, elev_ref, cell_ref, mean_ref, rows_ref, skew,
-    ) = refs[2 * GROUP :]
+def sweep_kernel(group, ys, halo, late, *refs):
+    refs = list(refs[1:])
+
+    def take(count):
+        out = refs[:count]
+        del refs[:count]
+        return out
+
+    count = len(ys)
+    near_refs, far_refs = take(group), take(group)
+    own_ref, table_ref, pat_ref, mask_ref, w2_ref, flip_ref, elev_ref, cell_ref = take(8)
+
+    def pair(g):
+        if late:
+            early, before, after = ref_sets[0]
+            first = jnp.where(pl.program_id(0) == 0, early[g, 0].astype(F32), before[g, 0].astype(F32))
+            return jnp.concatenate([first.astype(early.dtype), after[g, 0]], axis=1)
+        before, after = ref_sets[0]
+        return jnp.concatenate([before[g, 0], after[g, 0]], axis=1)
+
+    width = 3 if late else 2
+    stat_refs = take(width)
+    up_refs = take(width) if halo else None
+    down_refs = take(width) if halo else None
+    edge_ref = take(1)[0] if halo else None
+    mean_ref, rows_ref, skew = refs
+
+    def joined(set_refs, g):
+        ref_sets[0] = set_refs
+        return pair(g)
+
+    ref_sets = [None]
     column = 63 - lax.broadcasted_iota(jnp.int32, (64, 128), 0)
     lane = lax.broadcasted_iota(jnp.int32, (64, 128), 1)
     wrapped = lane < column
@@ -389,23 +427,26 @@
     column8 = 7 - lax.broadcasted_iota(jnp.int32, (8, 128), 0)
     lane8 = lax.broadcasted_iota(jnp.int32, (8, 128), 1)
     hyp = (lane % 64).astype(F32)
-    tables = dot(table_ref[:, 0].reshape(GROUP * 64, 128), pat_ref[...])
+    tables = dot(table_ref[:, 0].reshape(group * 64, 128), pat_ref[...])
 
     soft = []
     chosen = []
-    for g in range(GROUP):
+    for g in range(group):
         rhs = jnp.concatenate([near_refs[g][0, 0], far_refs[g][0, 0]], axis=1)
-        up = jnp.concatenate([u0_ref[g, 0], u1_ref[g, 0]], axis=1)
-        down = jnp.concatenate([d0_ref[g, 0], d1_ref[g, 0]], axis=1)
-        stats = jnp.concatenate([s0_ref[g, 0], s1_ref[g, 0]], axis=1)
+        stats = joined(stat_refs, g)
+        if halo:
+            up = joined(up_refs, g)
+            down = joined(down_refs, g)
+            above = dot(edge_ref[g, 0][:, 0:64], up)
+            below = dot(edge_ref[g, 0][:, 64:128], down)
+        else:
+            up = down = None
         mean_b, inv_b = boxed_stats(stats, up, down)
         own = own_ref[g, 0]
-        masked = jnp.concatenate([own * mask_ref[y : y + 1, :] for y in range(4)], axis=0)
+        masked = jnp.concatenate([own * mask_ref[y : y + 1, :] for y in ys], axis=0)
         product = dot(masked, rhs)
-        above = dot(edge_ref[g, 0][:, 0:64], up)
-        below = dot(edge_ref[g, 0][:, 64:128], down)
-        for y in range(4):
-            p = product[WIN * y : WIN * y + WIN]
+        for i, y in enumerate(ys):
+            p = product[WIN * i : WIN * i + WIN]
             if y == 0:
                 p = p + above
             if y == 3:
@@ -418,14 +459,14 @@
                 p[72:80, 128:],
                 jnp.where(lane8 < column8 + 64, p[8:16, 128:], p[72:80, :128]),
             )
-            at = 4 * g + y
+            at = count * g + i
             skew[at, 0:8, :] = pltpu.roll(z8, 57, 1, stride=1, stride_axis=0)
             skew[at, 8:72, :] = pltpu.roll(z, 65, 1, stride=1, stride_axis=0)
             cross = skew[at, 8:72, :] + skew[at, 7:71, :] + skew[at, 6:70, :]
             mb = skewed(mean_b[y : y + 1, :128], mean_b[y : y + 1, 128:], column, lane, 65)
             rb = skewed(inv_b[y : y + 1, :128], inv_b[y : y + 1, 128:], column, lane, 65)
             a1, a2, index = (
-                tables[64 * g : 64 * g + 64, (3 * y + q) * 128 : (3 * y + q + 1) * 128]
+                tables[64 * g : 64 * g + 64, (3 * i + q) * 128 : (3 * i + q + 1) * 128]
                 for q in range(3)
             )
             weight = jnp.exp2((cross * a1 - a2 * mb) * rb)
@@ -438,104 +479,112 @@
     rc = dot_nt(w2_ref[...], chosen)
     inv = 1.0 / r[0:2]
     both = jnp.concatenate([(r[2:4] + r[4:6] + r[6:8]) * inv, rc[0:2] * inv], axis=0)
-    both = jnp.concatenate([both[:, 128 * v : 128 * v + 128] for v in range(2 * GROUP)], axis=0)
+    pieces = group * count // 2
+    both = jnp.concatenate([both[:, 128 * v : 128 * v + 128] for v in range(pieces)], axis=0)
     high = both.astype(BF)
     rest = both - high.astype(F32)
     mid = rest.astype(BF)
     low = (rest - mid.astype(F32)).astype(BF)
     both = dot(jnp.concatenate([high, mid, low], axis=0), flip_ref[...])
-    both = both[0 : 8 * GROUP] + both[8 * GROUP : 16 * GROUP] + both[16 * GROUP : 24 * GROUP]
+    both = both[0 : 4 * pieces] + both[4 * pieces : 8 * pieces] + both[8 * pieces :]
     turned = pltpu.roll(both, 64, 1)
     left = lax.broadcasted_iota(jnp.int32, (1, 128), 1) < 64
     cell_iota = lax.broadcasted_iota(jnp.int32, (128, 128), 0)
-    for g in range(GROUP):
-        for y in range(4):
-            at = (2 * g + y // 2) * 4
-            lo, hi = (both, turned) if y % 2 == 0 else (turned, both)
-            mean_ref[g, y : y + 1, :] = jnp.where(left, lo[at : at + 1], hi[at + 1 : at + 2])
+    for g in range(group):
+        for i, y in enumerate(ys):
+            at = (count * g + i) // 2 * 4
+            lo, hi = (both, turned) if i % 2 == 0 else (turned, both)
+            mean_ref[g, i : i + 1, :] = jnp.where(left, lo[at : at + 1], hi[at + 1 : at + 2])
             c = jnp.where(left, lo[at + 2 : at + 3], hi[at + 3 : at + 4])
-            pair = jnp.concatenate([c * elev_ref[g, y : y + 1, :], c], axis=0)
-            pair_hi = pair.astype(BF).astype(F32)
-            vals = jnp.concatenate([pair_hi, pair - pair_hi, jnp.zeros((4, 128), F32)], axis=0)
+            values = jnp.concatenate([c * elev_ref[g, y : y + 1, :], c], axis=0)
+            value_hi = values.astype(BF).astype(F32)
+            values = jnp.concatenate([value_hi, values - value_hi, jnp.zeros((4, 128), F32)], axis=0)
             hot = jnp.where(cell_iota == cell_ref[g, y : y + 1, :], 1.0, 0.0).astype(BF)
-            binned = dot_nt(vals.astype(BF), hot)
+            binned = dot_nt(values.astype(BF), hot)
             got = binned[0:2] + binned[2:4]
-            at = 4 * g + y
+            at = count * g + i
             rows_ref[0, at : at + 1, 0:128] = got[0:1]
             rows_ref[0, at : at + 1, 128:256] = got[1:2]
 
 
 def sweep_steps(
-    first, steps, slot, own, edge, main, far_blocks, up, down, stats, table, pat, masks, w2, flip,
-    elev, cell, far_in_main,
+    first, steps, ys, group, slot, blocks, stats, ups, downs, own, edge, table, w2, elev, cell, late
 ):
     images = own.shape[0]
-
-    def slot_near(g):
-        return lambda n, k, s: (s[GROUP * k + g], n + first, 0, 0)
-
-    def slot_far(g):
-        if far_in_main:
-            return lambda n, k, s: (s[GROUP * k + g], n + first + 1, 0, 0)
-        return lambda n, k, s: (GROUP * k + g, 0, 0, 0)
+    halo = ups is not None
+    count = len(ys)
+
+    def slot_block(g, j):
+        return lambda n, k, s: (s[group * k + g], n + first + j, 0, 0)
+
+    def compact_block(g, j):
+        return lambda n, k, s: (group * k + g, n + j, 0, 0)
+
+    block_at = compact_block if late else slot_block
 
     def near(n, k, s):
         return (k, n + first, 0, 0)
 
-    def far(n, k, s):
-        return (k, n + first + 1, 0, 0) if far_in_main else (k, 0, 0, 0)
-
     def whole(n, k, s):
         return (0, 0)
 
     def pixels(n, k, s):
         return (k, 0, n + first)
 
-    in_specs = [pl.BlockSpec((1, 1, 256, 128), slot_near(g)) for g in range(GROUP)]
-    in_specs += [pl.BlockSpec((1, 1, 256, 128), slot_far(g)) for g in range(GROUP)]
+    def pair_specs(rows):
+        if late:
+            maps = (
+                lambda n, k, s: (k, FIRST - 1, 0, 0),
+                lambda n, k, s: (k, 0, 0, 0),
+                lambda n, k, s: (k, n, 0, 0),
+            )
+        else:
+            maps = (near, lambda n, k, s: (k, n + first + 1, 0, 0))
+        return [pl.BlockSpec((group, 1, rows, 128), m) for m in maps]
+
+    def pair_args(arrays):
+        return [arrays[0], arrays[1], arrays[1]] if late else [arrays[0], arrays[0]]
+
+    in_specs = [pl.BlockSpec((1, 1, 256, 128), block_at(g, j)) for j in range(2) for g in range(group)]
     in_specs += [
-        pl.BlockSpec((GROUP, 1, WIN, 256), near),
-        pl.BlockSpec((GROUP, 1, WIN, 128), near),
-        pl.BlockSpec((GROUP, 1, 64, 128), near),
-        pl.BlockSpec((GROUP, 1, 64, 128), far),
-        pl.BlockSpec((GROUP, 1, 64, 128), near),
-        pl.BlockSpec((GROUP, 1, 64, 128), far),
-        pl.BlockSpec((GROUP, 1, 8, 128), near),
-        pl.BlockSpec((GROUP, 1, 8, 128), far),
-        pl.BlockSpec((GROUP, 1, 64, 128), near),
-        pl.BlockSpec((128, 1536), whole),
+        pl.BlockSpec((group, 1, WIN, 256), near),
+        pl.BlockSpec((group, 1, 64, 128), near),
+        pl.BlockSpec((128, 3 * 128 * count), whole),
         pl.BlockSpec((16, 256), whole),
         pl.BlockSpec((8, 256), whole),
         pl.BlockSpec((128, 128), whole),
-        pl.BlockSpec((GROUP, 4, 128), pixels),
-        pl.BlockSpec((GROUP, 4, 128), pixels),
-    ]
+        pl.BlockSpec((group, 4, 128), pixels),
+        pl.BlockSpec((group, 4, 128), pixels),
+    ] + pair_specs(8)
+    args = [blocks] * (2 * group) + [
+        own, table, table_patterns(ys), row_masks(), w2, flips(), elev, cell,
+    ] + pair_args(stats)
+    if halo:
+        in_specs += pair_specs(64) + pair_specs(64) + [pl.BlockSpec((group, 1, WIN, 128), near)]
+        args += pair_args(ups) + pair_args(downs) + [edge]
+    work = steps * images * count // 4
     return pl.pallas_call(
-        sweep_kernel,
+        functools.partial(sweep_kernel, group, ys, halo, late),
         grid_spec=pltpu.PrefetchScalarGridSpec(
             num_scalar_prefetch=1,
-            grid=(steps, images // GROUP),
+            grid=(steps, images // group),
             in_specs=in_specs,
             out_specs=[
-                pl.BlockSpec((GROUP, 4, 128), lambda n, k, s: (k, 0, n)),
-                pl.BlockSpec((1, 4 * GROUP, 256), lambda n, k, s: (n, k, 0)),
+                pl.BlockSpec((group, count, 128), lambda n, k, s: (k, 0, n)),
+                pl.BlockSpec((1, count * group, 256), lambda n, k, s: (n, k, 0)),
             ],
-            scratch_shapes=[pltpu.VMEM((4 * GROUP, 72, 128), F32)],
+            scratch_shapes=[pltpu.VMEM((count * group, 72, 128), F32)],
         ),
         out_shape=[
-            jax.ShapeDtypeStruct((images, 4, steps * 128), F32),
-            jax.ShapeDtypeStruct((steps, images * 4, 256), F32),
+            jax.ShapeDtypeStruct((images, count, steps * 128), F32),
+            jax.ShapeDtypeStruct((steps, images * count, 256), F32),
         ],
         compiler_params=PARAMS,
         cost_estimate=pl.CostEstimate(
-            flops=steps * images * 200_000_000, bytes_accessed=steps * images * 400_000,
-            transcendentals=0,
+            flops=work * 200_000_000, bytes_accessed=work * 400_000, transcendentals=0
         ),
         name="sweep",
-    )(
-        slot, *[main] * GROUP, *[far_blocks] * GROUP, own, edge, up[0], up[1], down[0], down[1],
-        stats[0], stats[1], table, pat, masks, w2, flip, elev, cell,
-    )
+    )(slot, *args)
 
 
 def depth_weights(planes):
@@ -640,7 +689,7 @@
     def exchange(a):
         return lax.all_to_all(a, "img", split_axis=0, concat_axis=0, tiled=True)
 
-    main = exchange(pick(chosen, features, STEPS))
+    main = exchange(pick(chosen, features, FIRST))
 
     every = jnp.arange(images, dtype=jnp.int32)
     own = pick(every, features, STEPS + 1)
@@ -666,35 +715,36 @@
     metas = jnp.take(metas, (my_tile - jnp.arange(owners)) % owners, axis=0)
 
     w2 = depth_weights(depth_planes)
-    pat, masks, flip = table_patterns(), row_masks(), flips()
-
+
+    packed, own_turned, edge_turned, own_table, elevation, metas, w2 = lax.optimization_barrier(
+        (packed, own_turned, edge_turned, own_table, elevation, metas, w2)
+    )
     last = exchange(packed)
-    main, _, own_turned, edge_turned, own_table, elevation, metas, w2 = lax.optimization_barrier(
-        (main, packed, own_turned, edge_turned, own_table, elevation, metas, w2)
-    )
     head, tail, stats = edges(slot, main)
     up, down = neighbour_rows(head, tail)
-    common = (own_table, pat, masks, w2, flip, elevation, cell_index)
-
-    def inner(first, steps):
-        return sweep_steps(
-            first, steps, slot, own_turned, edge_turned, main, main, (up, up), (down, down),
-            (stats, stats), *common, True,
-        )
-
-    mean_a, rows_a = inner(0, 2)
+    shared = (own_turned, edge_turned, own_table, w2, elevation, cell_index)
+    mean_a, rows_a = sweep_steps(
+        0, 2, (0, 1, 2, 3), 8, slot, main, (stats,), (up,), (down,), *shared, False
+    )
     last, mean_a = lax.optimization_barrier((last, mean_a))
-    head_l, tail_l, stats_l, far = unpack(slot, last)
+    head_l, tail_l, stats_l, late = unpack(slot, last, main)
     up_l, down_l = neighbour_rows(head_l, tail_l)
-    mean_b, rows_b = inner(2, 1)
+    both = (stats, stats_l)
+    mean_b, rows_b = sweep_steps(2, 2, (1, 2), 8, slot, late, both, None, None, *shared, True)
     mean_c, rows_c = sweep_steps(
-        3, 1, slot, own_turned, edge_turned, main, far, (up, up_l), (down, down_l),
-        (stats, stats_l), *common, False,
+        2, 2, (0, 3), 8, slot, late, both, (up, up_l), (down, down_l), *shared, True
     )
-    mean_range = jnp.concatenate([mean_a, mean_b, mean_c], axis=2)
+    mean_bc = jnp.concatenate([mean_c[:, 0:1], mean_b, mean_c[:, 1:2]], axis=1)
+    mean_range = jnp.concatenate([mean_a, mean_bc], axis=2)
 
     lists = block_list[0, 0]
-    row_list = lists % STEPS * rows_c.shape[1] + lists // STEPS
+    n, r, k = lists % STEPS, lists // STEPS % 4, lists // (4 * STEPS)
+    half = (n - 2) * 2 * images + 2 * k
+    row_list = jnp.where(
+        n < 2,
+        n * 4 * images + 4 * k + r,
+        jnp.where((r == 1) | (r == 2), 8 * images + half + r - 1, 12 * images + half + r // 3),
+    )
     send = collect(row_list, block_count[0, 0], (rows_a, rows_b, rows_c))
     got = lax.all_to_all(send, "tile", split_axis=0, concat_axis=0, tiled=True)
     dense = place(metas[:, :128], metas[:, 128], got, group_count * PATCH_DEV)

time: 279 us -> 249 us (0.89)
  starting transfers between devices: 82.6 us -> 58.7 us
  waiting for transfers between devices: 71 us -> 60.7 us
  Pallas kernels: 107 us -> 111 us
    all_to_all x3, waiting for transfers between devices: 49.9 us -> 16.5 us  [exchange(): return lax.all_to_all(a, 'img', split_axis=0, concat_axis=0, tiled=True)]
    ppermute x3, waiting for transfers between devices: 0.01 us -> 29 us  [neighbour_rows(): above = lax.ppermute(tail, 'tile', [(i, i + 1) for i in range(count - 1)])]
    all_to_all x3, starting transfers between devices: 56.7 us -> 34 us  [exchange(): return lax.all_to_all(a, 'img', split_axis=0, concat_axis=0, tiled=True)]
    ppermute x3, waiting for transfers between devices: 15.4 us -> 0.01 us  [on_device(): lax.ppermute(mine, 'tile', [(i, (i + s) % owners) for i in range(owners)])]
    ppermute x3, waiting for transfers between devices: 0.01 us -> 9.34 us  [neighbour_rows(): below = lax.ppermute(head, 'tile', [(i + 1, i) for i in range(count - 1)])]
    pallas_call x3, Pallas kernels: 37.5 us -> 41.4 us  [sweep_steps(): pl.pallas_call(functools.partial(sweep_kernel, group, ys, halo, late), gr...]
  transfers between devices with their start and end apart: 13 -> 13, of which waited for: 4 -> 8; matrix products, arithmetic and copies ran while one was open for 3% -> 3% of each run, Pallas kernels for 23% -> 29%
where the time goes in v3:
time: 249 us; the launch traced here: 246 us
  Pallas kernels  111 us (45%)
  waiting for transfers between devices  60.7 us (24%)
  starting transfers between devices  58.7 us (24%)
  local copies, waits for them, and re-layouts  9.74 us (4%)
  other arithmetic  5.09 us (2%)
    pallas_call x3, Pallas kernels, sweep_steps(): pl.pallas_call(functools.partial(sweep_kernel, group, ys, halo, late), gr...  41.4 us
    all_to_all x3, starting transfers between devices, exchange(): return lax.all_to_all(a, 'img', split_axis=0, concat_axis=0, tiled=True)  34 us
    ppermute x3, waiting for transfers between devices, neighbour_rows(): above = lax.ppermute(tail, 'tile', [(i, i + 1) for i in range(count - 1)])  29 us
    pallas_call x2, Pallas kernels, pick(): pl.pallas_call(kernel, grid_spec=pltpu.PrefetchScalarGridSpec(num_scalar_...  16.7 us
    all_to_all x3, waiting for transfers between devices, exchange(): return lax.all_to_all(a, 'img', split_axis=0, concat_axis=0, tiled=True)  16.5 us
    pallas_call x1, Pallas kernels, prepare(): pl.pallas_call(prepare_kernel, grid=(images,), in_specs=[pl.BlockSpec((1,...  15.4 us
    pallas_call x2, Pallas kernels, edges(): pl.pallas_call(edge_kernel, grid_spec=pltpu.PrefetchScalarGridSpec(num_sc...  13.8 us
    ppermute x3, starting transfers between devices, neighbour_rows(): above = lax.ppermute(tail, 'tile', [(i, i + 1) for i in range(count - 1)])  9.84 us
  transfers between devices with their start and end apart: 13, of which 8 were waited for; matrix products, arithmetic and copies ran while one was open for 3% of the time, Pallas kernels for 29%

profile of v3, /device:TPU:1, one launch (start us, length us, event | category | flops | bytes accessed | tf_op | source)
XLA Modules:
  0.0 246.3 jit_solution(10800767394470331136)
XLA Ops:
  0.6 0.8 reshape.74
  1.4 0.6 fusion.2
  2.0 10.2 %pick.3 = bf16[32,3,64,4,128]{4,3,2,1,0:T(4,128)(2,1)} custom-call(s32[32]{0:T(128)} %get-tuple-element.60.idx_ref, bf16[16,64,4,768]{3,2,1,0:T(4,128)(2,1)} %features_ref.3), custom_call_target="tpu_custom_call" | custom-call | bytes 12582912 | tf_op jit(solution)/shard_map/pick/pallas_call | solution.py:138
  12.2 0.0 copy-start.11
  12.2 0.0 copy-start.9
  12.3 8.6 %all-to-all-start.1 = ((bf16[32,3,256,128]{3,2,1,0:T(8,128)(2,1)}), bf16[32,3,256,128]{3,2,1,0:T(8,128)(2,1)}, u32[]{:S(2)}, u32[]{:S(2)}) async-start(bf16[32,3,256,128]{3,2,1,0:T(8,128)(2,1)} %bitcast.50), calls=%async_computation.1 | async-start | bytes 12582912 | tf_op jit(solution)/shard_map/all_to_all | solution.py:690
  21.0 0.1 broadcast_in_dim.40
  21.1 1.7 collective-permute-start.2
  22.8 3.3 %collective-permute-start.3 = (s32[1,256]{1,0:T(1,128)S(1)}, s32[1,256]{1,0:T(1,128)S(1)}, u32[]{:S(2)}, u32[]{:S(2)}) collective-permute-start(s32[1,256]{1,0:T(1,128)S(1)} %get-tuple-element.64), channel_id=1, source_target_pairs={{0,2},{1,3},{2,0},{3,1},{4,6},{5,7},{6,4},{7,5},{8,10},{9,11},{10,... | collective-permute-start | bytes 3080 | tf_op jit(solution)/shard_map/ppermute | solution.py:713
  26.1 0.7 collective-permute-start.4
  26.8 0.5 iota.15.idx_ref
  27.3 6.6 %pick.2 = bf16[16,5,64,4,128]{4,3,2,1,0:T(4,128)(2,1)} custom-call(s32[16]{0:T(128)} %iota.15.idx_ref, bf16[16,64,4,768]{3,2,1,0:T(4,128)(2,1)} %features_ref.3), custom_call_target="tpu_custom_call" | custom-call | bytes 10485760 | tf_op jit(solution)/shard_map/pick/pallas_call | solution.py:138
  33.9 0.5 iota.16.slot_ref
  34.4 0.0 copy-start.4
  34.4 0.0 copy-start.12
  34.4 7.7 %edges.2 = (bf16[16,5,64,128]{3,2,1,0:T(8,128)(2,1)}, bf16[16,5,64,128]{3,2,1,0:T(8,128)(2,1)}, f32[16,5,8,128]{3,2,1,0:T(8,128)}) custom-call(s32[16]{0:T(128)} %iota.16.slot_ref, bf16[16,5,256,128]{3,2,1,0:T(8,128)(2,1)} %bitcast.37, bf16[16,5,256,128]{3,2,1,0:T(8,128)(2,1)} %bitcast.38, bf16[16,5,256,128]{3,2,1,0:T(8,128)(2,1)} %bitcast.39, ...), custom_call_target="tpu_custom_call" | custom-call | flops 1600000000 | bytes 8000000 | tf_op jit(solution)/shard_map/edges/pallas_call | solution.py:282
  42.1 2.7 %collective-permute-start = (bf16[16,5,64,128]{3,2,1,0:T(8,128)(2,1)}, bf16[16,5,64,128]{3,2,1,0:T(8,128)(2,1)S(1)}, u32[]{:S(2)}, u32[]{:S(2)}) collective-permute-start(bf16[16,5,64,128]{3,2,1,0:T(8,128)(2,1)} %get-tuple-element.30), channel_id=1, source_target_pairs={{0,1},{1,2},{2,3},{4,5},{5,6},{6,7},{8,9},{9,10},{10,11},{12,13},{... | collective-permute-start | bytes 3932168 | tf_op jit(solution)/shard_map/ppermute | solution.py:670
  44.9 1.3 collective-permute-start.1
  46.2 0.1 pad_bitcast_fusion.4
  46.3 0.1 pad_bitcast_fusion
  46.5 0.6 pad_maximum_fusion.refs_21_
  47.1 1.0 select_reduce_fusion
  48.0 0.7 fusion.refs_23_
  48.8 8.4 %pack.1 = bf16[32,392,128]{2,1,0:T(8,128)(2,1)} custom-call(s32[32]{0:T(128)} %get-tuple-element.60.idx_ref, bf16[16,5,256,128]{3,2,1,0:T(8,128)(2,1)} %bitcast.41, bf16[16,5,256,128]{3,2,1,0:T(8,128)(2,1)} %bitcast.42, bf16[16,5,256,128]{3,2,1,0:T(8,128)(2,1)} %bitcast.43, bf16[16,5,256,128]{3,2,1,0:T(8,128)(2,1)} %bitcast.44, ...), custom_call_target="tpu_custom_call" | custom-call | tf_op jit(solution)/shard_map/pack/pallas_call | solution.py:195
  57.2 0.0 collective-permute-done.2
  57.2 0.0 collective-permute-done.3
  57.2 0.0 collective-permute-done.4
  57.2 0.6 gather_fusion
  57.8 0.1 broadcast_select_fusion
  57.9 14.1 %collective-permute-done.up_ref = bf16[16,5,64,128]{3,2,1,0:T(8,128)(2,1)S(1)} collective-permute-done((bf16[16,5,64,128]{3,2,1,0:T(8,128)(2,1)}, bf16[16,5,64,128]{3,2,1,0:T(8,128)(2,1)S(1)}, u32[]{:S(2)}, u32[]{:S(2)}) %collective-permute-start) | collective-permute-done | bytes 1310752 | tf_op jit(solution)/shard_map/ppermute | solution.py:670
  72.0 3.9 %collective-permute-done.1.down_ref = bf16[16,5,64,128]{3,2,1,0:T(8,128)(2,1)S(1)} collective-permute-done((bf16[16,5,64,128]{3,2,1,0:T(8,128)(2,1)}, bf16[16,5,64,128]{3,2,1,0:T(8,128)(2,1)S(1)}, u32[]{:S(2)}, u32[]{:S(2)}) %collective-permute-start.1) | collective-permute-done | bytes 1310752 | tf_op jit(solution)/shard_map/ppermute | solution.py:671
  75.9 1.1 copy-done.16
  77.0 15.4 %prepare.1 = (bf16[16,4,144,256]{3,2,1,0:T(8,128)(2,1)}, bf16[16,4,144,128]{3,2,1,0:T(8,128)(2,1)}, bf16[16,4,64,128]{3,2,1,0:T(8,128)(2,1)}) custom-call(bf16[16,5,256,128]{3,2,1,0:T(8,128)(2,1)} %bitcast.49, bf16[16,5,64,128]{3,2,1,0:T(8,128)(2,1)} %copy-done.15, bf16[16,5,64,128]{3,2,1,0:T(8,128)(2,1)} %copy-done.16, ...), custom_call_target="tpu_custom_call" | custom-call | flops 2560000000 | bytes 16000000 | tf_op jit(solution)/shard_map/prepare/pallas_call | solution.py:357
  92.4 6.5 %all-to-all-done.1.refs_0_.refs_1_.refs_2_.refs_3_.refs_4_.refs_5_.refs_6_.refs_7_.refs_8_.refs_9_.refs_10_.refs_11_.refs_12_.refs_13_.refs_14_.refs_15_.refs_16_ = bf16[32,3,256,128]{3,2,1,0:T(8,128)(2,1)} async-done(((bf16[32,3,256,128]{3,2,1,0:T(8,128)(2,1)}), bf16[32,3,256,128]{3,2,1,0:T(8,128)(2,1)}, u32[]{:S(2)}, u32[]{:S(2)}) %all-to-all-start.1) | async-done | bytes 6291488 | tf_op jit(solution)/shard_map/all_to_all | solution.py:690
  98.9 14.5 %all-to-all-start = ((bf16[32,392,128]{2,1,0:T(8,128)(2,1)}), bf16[32,392,128]{2,1,0:T(8,128)(2,1)S(1)}, u32[]{:S(2)}, u32[]{:S(2)}) async-start(bf16[32,392,128]{2,1,0:T(8,128)(2,1)} %pack.1), calls=%async_computation | async-start | bytes 6422528 | tf_op jit(solution)/shard_map/all_to_all | solution.py:690
  113.4 0.6 fusion.20.slot_ref.refs_0_
  114.0 6.1 %edges.3 = (bf16[16,3,64,128]{3,2,1,0:T(8,128)(2,1)}, bf16[16,3,64,128]{3,2,1,0:T(8,128)(2,1)}, f32[16,3,8,128]{3,2,1,0:T(8,128)}) custom-call(s32[16]{0:T(128)} %fusion.20.slot_ref.refs_0_, ...), custom_call_target="tpu_custom_call" | custom-call | flops 960000000 | bytes 4800000 | tf_op jit(solution)/shard_map/edges/pallas_call | solution.py:282
  120.0 4.4 %collective-permute-start.5 = (bf16[16,3,64,128]{3,2,1,0:T(8,128)(2,1)}, bf16[16,3,64,128]{3,2,1,0:T(8,128)(2,1)}, u32[]{:S(2)}, u32[]{:S(2)}) collective-permute-start(bf16[16,3,64,128]{3,2,1,0:T(8,128)(2,1)} %get-tuple-element.42), channel_id=1, source_target_pairs={{0,1},{1,2},{2,3},{4,5},{5,6},{6,7},{8,9},{9,10},{10,11},{12,13},{... | collective-permute-start | bytes 2359304 | tf_op jit(solution)/shard_map/ppermute | solution.py:670
  124.5 1.3 collective-permute-start.6
  125.8 14.8 %collective-permute-done.5.refs_27_.refs_28_ = bf16[16,3,64,128]{3,2,1,0:T(8,128)(2,1)} collective-permute-done((bf16[16,3,64,128]{3,2,1,0:T(8,128)(2,1)}, bf16[16,3,64,128]{3,2,1,0:T(8,128)(2,1)}, u32[]{:S(2)}, u32[]{:S(2)}) %collective-permute-start.5) | collective-permute-done | bytes 786464 | tf_op jit(solution)/shard_map/ppermute | solution.py:670
  140.6 4.7 %collective-permute-done.6.refs_29_.refs_30_.refs_31_ = bf16[16,3,64,128]{3,2,1,0:T(8,128)(2,1)} collective-permute-done((bf16[16,3,64,128]{3,2,1,0:T(8,128)(2,1)}, bf16[16,3,64,128]{3,2,1,0:T(8,128)(2,1)}, u32[]{:S(2)}, u32[]{:S(2)}) %collective-permute-start.6) | collective-permute-done | bytes 786464 | tf_op jit(solution)/shard_map/ppermute | solution.py:671
  145.3 17.3 %sweep.3 = (f32[16,4,256]{2,1,0:T(4,128)}, f32[2,64,256]{2,1,0:T(8,128)}) custom-call(s32[16]{0:T(128)} %fusion.20.slot_ref.refs_0_, bf16[32,3,256,128]{3,2,1,0:T(8,128)(2,1)} %all-to-all-done.1.refs_0_.refs_1_.refs_2_.refs_3_.refs_4_.refs_5_.refs_6_.refs_7_.refs_8_.refs_9_.refs_10_.refs_11_.refs_12_.refs_13_.refs_14_.refs_15_.refs_16_, ...), custom_call_target="tpu_custom_call" | custom-call | flops 6400000000 | bytes 12800000 | tf_op jit(solution)/shard_map/sweep/pallas_call | solution.py:566
  162.6 1.7 copy-done
  164.3 8.0 %unpack.1 = (bf16[16,2,64,128]{3,2,1,0:T(8,128)(2,1)}, bf16[16,2,64,128]{3,2,1,0:T(8,128)(2,1)}, f32[16,2,8,128]{3,2,1,0:T(8,128)}, bf16[16,3,256,128]{3,2,1,0:T(8,128)(2,1)}) custom-call(s32[16]{0:T(128)} %fusion.20.slot_ref.refs_0_, bf16[32,392,128]{2,1,0:T(8,128)(2,1)} %copy-done, bf16[32,392,128]{2,1,0:T(8,128)(2,1)} %copy-done, ...), custom_call_target="tpu_custom_call" | custom-call | tf_op jit(solution)/shard_map/unpack/pallas_call | solution.py:313
  172.3 2.7 %collective-permute-start.7 = (bf16[16,2,64,128]{3,2,1,0:T(8,128)(2,1)}, bf16[16,2,64,128]{3,2,1,0:T(8,128)(2,1)S(1)}, u32[]{:S(2)}, u32[]{:S(2)}) collective-permute-start(bf16[16,2,64,128]{3,2,1,0:T(8,128)(2,1)} %get-tuple-element.50), channel_id=1, source_target_pairs={{0,1},{1,2},{2,3},{4,5},{5,6},{6,7},{8,9},{9,10},{10,11},{12,13},{... | collective-permute-start | bytes 1572872 | tf_op jit(solution)/shard_map/ppermute | solution.py:670
  175.0 1.5 collective-permute-start.8
  176.5 0.6 fusion.8.list_ref
  177.1 11.0 %sweep.5 = (f32[16,2,256]{2,1,0:T(2,128)}, f32[2,32,256]{2,1,0:T(8,128)}) custom-call(s32[16]{0:T(128)} %fusion.20.slot_ref.refs_0_, bf16[16,3,256,128]{3,2,1,0:T(8,128)(2,1)} %get-tuple-element.48.refs_1_.refs_2_.refs_3_.refs_4_.refs_5_.refs_6_.refs_7_.refs_8_.refs_9_.refs_10_.refs_11_.refs_12_.refs_13_.refs_14_.refs_15_.refs_16_, ...), custom_call_target="tpu_custom_call" | custom-call | flops 3200000000 | bytes 6400000 | tf_op jit(solution)/shard_map/sweep/pallas_call | solution.py:566
  188.1 0.7 collective-permute-done.8.refs_32_.refs_33_
  188.9 0.0 copy-done.1
  188.9 0.8 copy-done.2
  189.7 13.1 %sweep.4 = (f32[16,2,256]{2,1,0:T(2,128)}, f32[2,32,256]{2,1,0:T(8,128)}) custom-call(s32[16]{0:T(128)} %fusion.20.slot_ref.refs_0_, bf16[16,3,256,128]{3,2,1,0:T(8,128)(2,1)} %get-tuple-element.48.refs_1_.refs_2_.refs_3_.refs_4_.refs_5_.refs_6_.refs_7_.refs_8_.refs_9_.refs_10_.refs_11_.refs_12_.refs_13_.refs_14_.refs_15_.refs_16_, ...), custom_call_target="tpu_custom_call" | custom-call | flops 3200000000 | bytes 6400000 | tf_op jit(solution)/shard_map/sweep/pallas_call | solution.py:566
  202.9 3.7 %collect.1 = f32[4,128,256]{2,1,0:T(8,128)} custom-call(s32[4,128]{1,0:T(4,128)} %fusion.8.list_ref, s32[4]{0:T(128)} %bitcast.53, f32[2,64,256]{2,1,0:T(8,128)} %get-tuple-element.55.a_ref, f32[2,32,256]{2,1,0:T(8,128)} %get-tuple-element.56.b_ref, f32[2,32,256]{2,1,0:T(8,128)} %get-tuple-element.57.c_ref), custom_call_target="tpu_custom_call" | custom-call | tf_op jit(solution)/shard_map/collect/pallas_call | solution.py:622
  206.5 5.0 %all-to-all-start.2 = ((f32[4,128,256]{2,1,0:T(8,128)}), f32[4,128,256]{2,1,0:T(8,128)S(1)}, u32[]{:S(2)}, u32[]{:S(2)}) async-start(f32[4,128,256]{2,1,0:T(8,128)} %collect.1), calls=%async_computation.2 | async-start | bytes 1048576 | tf_op jit(solution)/shard_map/all_to_all | solution.py:749
  211.5 0.6 slice.20.slot_ref
  212.1 0.6 slice_reduce_fusion.count_ref
  212.7 5.9 %all-to-all-done.2.got_ref = f32[4,128,256]{2,1,0:T(8,128)S(1)} async-done(((f32[4,128,256]{2,1,0:T(8,128)}), f32[4,128,256]{2,1,0:T(8,128)S(1)}, u32[]{:S(2)}, u32[]{:S(2)}) %all-to-all-start.2) | async-done | bytes 524320 | tf_op jit(solution)/shard_map/all_to_all | solution.py:749
  218.7 0.8 copy-done.3
  219.5 3.7 %place.1 = f32[512,256]{1,0:T(8,128)} custom-call(s32[4,128]{1,0:T(4,128)} %slice.20.slot_ref, s32[4]{0:T(128)} %slice_reduce_fusion.count_ref, f32[4,128,256]{2,1,0:T(8,128)} %copy-done.3), custom_call_target="tpu_custom_call" | custom-call | tf_op jit(solution)/shard_map/place/pallas_call | solution.py:654
  223.1 10.9 %all-to-all-start.3 = ((f32[32,16,256]{2,1,0:T(8,128)}), f32[32,16,256]{2,1,0:T(8,128)S(1)}, u32[]{:S(2)}, u32[]{:S(2)}) async-start(f32[32,16,256]{2,1,0:T(8,128)} %bitcast.51), calls=%async_computation.3 | async-start | bytes 1048576 | tf_op jit(solution)/shard_map/all_to_all | solution.py:690
  234.0 0.9 fusion.22
  234.9 0.7 maximum_maximum_fusion
  235.6 10.0 %all-to-all-done.3 = f32[32,16,256]{2,1,0:T(8,128)S(1)} async-done(((f32[32,16,256]{2,1,0:T(8,128)}), f32[32,16,256]{2,1,0:T(8,128)S(1)}, u32[]{:S(2)}, u32[]{:S(2)}) %all-to-all-start.3) | async-done | bytes 524320 | tf_op jit(solution)/shard_map/all_to_all | solution.py:690
  245.7 0.6 fusion.5
  (36 shorter events, 0.2 us)
Async XLA Ops:
  12.2 8.7 %copy-start.11 = (s32[1,1,4]{2,1,0:T(1,128)S(1)}, s32[1,1,4]{2,1,0:T(1,128)}, u32[]{:S(2)}) copy-start(s32[1,1,4]{2,1,0:T(1,128)} %param.41) | copy-start | bytes 52
  12.2 8.8 %copy-start.9 = (s32[1,1,4,128]{3,2,1,0:T(4,128)S(1)}, s32[1,1,4,128]{3,2,1,0:T(4,128)}, u32[]{:S(2)}) copy-start(s32[1,1,4,128]{3,2,1,0:T(4,128)} %param.40) | copy-start | bytes 6148
  12.3 86.6 %all-to-all-start.1 = ((bf16[32,3,256,128]{3,2,1,0:T(8,128)(2,1)}), bf16[32,3,256,128]{3,2,1,0:T(8,128)(2,1)}, u32[]{:S(2)}, u32[]{:S(2)}) async-start(bf16[32,3,256,128]{3,2,1,0:T(8,128)(2,1)} %bitcast.50), calls=%async_computation.1 | async-start | bytes 12582912 | tf_op jit(solution)/shard_map/all_to_all | solution.py:690
  21.1 36.1 %collective-permute-start.2 = (s32[1,256]{1,0:T(1,128)S(1)}, s32[1,256]{1,0:T(1,128)S(1)}, u32[]{:S(2)}, u32[]{:S(2)}) collective-permute-start(s32[1,256]{1,0:T(1,128)S(1)} %get-tuple-element.63), channel_id=1, source_target_pairs={{0,1},{1,2},{2,3},{3,0},{4,5},{5,6},{6,7},{7,4},{8,9},{9,10},{10,1... | collective-permute-start | bytes 3080 | tf_op jit(solution)/shard_map/ppermute | solution.py:713
  22.8 34.4 %collective-permute-start.3 = (s32[1,256]{1,0:T(1,128)S(1)}, s32[1,256]{1,0:T(1,128)S(1)}, u32[]{:S(2)}, u32[]{:S(2)}) collective-permute-start(s32[1,256]{1,0:T(1,128)S(1)} %get-tuple-element.64), channel_id=1, source_target_pairs={{0,2},{1,3},{2,0},{3,1},{4,6},{5,7},{6,4},{7,5},{8,10},{9,11},{10,... | collective-permute-start | bytes 3080 | tf_op jit(solution)/shard_map/ppermute | solution.py:713
  26.1 31.1 %collective-permute-start.4 = (s32[1,256]{1,0:T(1,128)S(1)}, s32[1,256]{1,0:T(1,128)S(1)}, u32[]{:S(2)}, u32[]{:S(2)}) collective-permute-start(s32[1,256]{1,0:T(1,128)S(1)} %get-tuple-element.65), channel_id=1, source_target_pairs={{0,3},{1,0},{2,1},{3,2},{4,7},{5,4},{6,5},{7,6},{8,11},{9,8},{10,9... | collective-permute-start | bytes 3080 | tf_op jit(solution)/shard_map/ppermute | solution.py:713
  34.4 11.8 %copy-start.5 = (s32[16,4,512]{2,1,0:T(4,128)S(1)}, s32[16,4,512]{2,1,0:T(4,128)}, u32[]{:S(2)}) copy-start(s32[16,4,512]{2,1,0:T(4,128)} %index_ref.1) | copy-start | bytes 393220
  34.4 11.8 %copy-start.8 = (f32[64]{0:T(128)S(1)}, f32[64]{0:T(128)}, u32[]{:S(2)}) copy-start(f32[64]{0:T(128)} %param.34) | copy-start | bytes 772
  34.4 12.0 %copy-start.13 = (bf16[1,128]{1,0:T(2,128)(2,1)S(1)}, bf16[1,128]{1,0:T(2,128)(2,1)}, u32[]{:S(2)}) copy-start(bf16[1,128]{1,0:T(2,128)(2,1)} %constant.274) | copy-start | bytes 772
  34.4 12.0 %copy-start.14 = (bf16[1,128]{1,0:T(2,128)(2,1)S(1)}, bf16[1,128]{1,0:T(2,128)(2,1)}, u32[]{:S(2)}) copy-start(bf16[1,128]{1,0:T(2,128)(2,1)} %constant.275) | copy-start | bytes 772
  34.4 13.6 %copy-start.4 = (f32[16,4,512]{2,1,0:T(4,128)S(1)}, f32[16,4,512]{2,1,0:T(4,128)}, u32[]{:S(2)}) copy-start(f32[16,4,512]{2,1,0:T(4,128)} %param.36) | copy-start | bytes 393220
  34.4 13.6 %copy-start.12 = (f32[16]{0:T(128)S(1)}, f32[16]{0:T(128)}, u32[]{:S(2)}) copy-start(f32[16]{0:T(128)} %param.35) | copy-start | bytes 196
  42.1 29.9 %collective-permute-start = (bf16[16,5,64,128]{3,2,1,0:T(8,128)(2,1)}, bf16[16,5,64,128]{3,2,1,0:T(8,128)(2,1)S(1)}, u32[]{:S(2)}, u32[]{:S(2)}) collective-permute-start(bf16[16,5,64,128]{3,2,1,0:T(8,128)(2,1)} %get-tuple-element.30), channel_id=1, source_target_pairs={{0,1},{1,2},{2,3},{4,5},{5,6},{6,7},{8,9},{9,10},{10,11},{12,13},{... | collective-permute-start | bytes 3932168 | tf_op jit(solution)/shard_map/ppermute | solution.py:670
  44.9 31.1 %collective-permute-start.1 = (bf16[16,5,64,128]{3,2,1,0:T(8,128)(2,1)}, bf16[16,5,64,128]{3,2,1,0:T(8,128)(2,1)S(1)}, u32[]{:S(2)}, u32[]{:S(2)}) collective-permute-start(bf16[16,5,64,128]{3,2,1,0:T(8,128)(2,1)} %get-tuple-element.31), channel_id=1, source_target_pairs={{1,0},{2,1},{3,2},{5,4},{6,5},{7,6},{9,8},{10,9},{11,10},{13,12},{... | collective-permute-start | bytes 3932168 | tf_op jit(solution)/shard_map/ppermute | solution.py:671
  72.0 3.9 %copy-start.15 = (bf16[16,5,64,128]{3,2,1,0:T(8,128)(2,1)}, bf16[16,5,64,128]{3,2,1,0:T(8,128)(2,1)S(1)}, u32[]{:S(2)}) copy-start(bf16[16,5,64,128]{3,2,1,0:T(8,128)(2,1)S(1)} %collective-permute-done.up_ref) | copy-start | bytes 3932164
  75.9 1.1 copy-start.16
  98.9 63.7 %all-to-all-start = ((bf16[32,392,128]{2,1,0:T(8,128)(2,1)}), bf16[32,392,128]{2,1,0:T(8,128)(2,1)S(1)}, u32[]{:S(2)}, u32[]{:S(2)}) async-start(bf16[32,392,128]{2,1,0:T(8,128)(2,1)} %pack.1), calls=%async_computation | async-start | bytes 6422528 | tf_op jit(solution)/shard_map/all_to_all | solution.py:690
  120.0 20.5 %collective-permute-start.5 = (bf16[16,3,64,128]{3,2,1,0:T(8,128)(2,1)}, bf16[16,3,64,128]{3,2,1,0:T(8,128)(2,1)}, u32[]{:S(2)}, u32[]{:S(2)}) collective-permute-start(bf16[16,3,64,128]{3,2,1,0:T(8,128)(2,1)} %get-tuple-element.42), channel_id=1, source_target_pairs={{0,1},{1,2},{2,3},{4,5},{5,6},{6,7},{8,9},{9,10},{10,11},{12,13},{... | collective-permute-start | bytes 2359304 | tf_op jit(solution)/shard_map/ppermute | solution.py:670
  124.5 20.8 %collective-permute-start.6 = (bf16[16,3,64,128]{3,2,1,0:T(8,128)(2,1)}, bf16[16,3,64,128]{3,2,1,0:T(8,128)(2,1)}, u32[]{:S(2)}, u32[]{:S(2)}) collective-permute-start(bf16[16,3,64,128]{3,2,1,0:T(8,128)(2,1)} %get-tuple-element.43), channel_id=1, source_target_pairs={{1,0},{2,1},{3,2},{5,4},{6,5},{7,6},{9,8},{10,9},{11,10},{13,12},{... | collective-permute-start | bytes 2359304 | tf_op jit(solution)/shard_map/ppermute | solution.py:671
  162.6 1.7 copy-start
  164.3 12.2 %copy-start.10 = (s32[1,1,4,128]{3,2,1,0:T(4,128)S(1)}, s32[1,1,4,128]{3,2,1,0:T(4,128)}, u32[]{:S(2)}) copy-start(s32[1,1,4,128]{3,2,1,0:T(4,128)} %param.39) | copy-start | bytes 6148
  172.3 15.8 %collective-permute-start.7 = (bf16[16,2,64,128]{3,2,1,0:T(8,128)(2,1)}, bf16[16,2,64,128]{3,2,1,0:T(8,128)(2,1)S(1)}, u32[]{:S(2)}, u32[]{:S(2)}) collective-permute-start(bf16[16,2,64,128]{3,2,1,0:T(8,128)(2,1)} %get-tuple-element.50), channel_id=1, source_target_pairs={{0,1},{1,2},{2,3},{4,5},{5,6},{6,7},{8,9},{9,10},{10,11},{12,13},{... | collective-permute-start | bytes 1572872 | tf_op jit(solution)/shard_map/ppermute | solution.py:670
  175.0 13.9 %collective-permute-start.8 = (bf16[16,2,64,128]{3,2,1,0:T(8,128)(2,1)}, bf16[16,2,64,128]{3,2,1,0:T(8,128)(2,1)S(1)}, u32[]{:S(2)}, u32[]{:S(2)}) collective-permute-start(bf16[16,2,64,128]{3,2,1,0:T(8,128)(2,1)} %get-tuple-element.51), channel_id=1, source_target_pairs={{1,0},{2,1},{3,2},{5,4},{6,5},{7,6},{9,8},{10,9},{11,10},{13,12},{... | collective-permute-start | bytes 1572872 | tf_op jit(solution)/shard_map/ppermute | solution.py:671
  188.1 46.8 %copy-start.6 = (f32[16,4,256]{2,1,0:T(4,128)S(1)}, f32[16,4,256]{2,1,0:T(4,128)}, u32[]{:S(2)}) copy-start(f32[16,4,256]{2,1,0:T(4,128)} %get-tuple-element.46) | copy-start | bytes 196612
  188.1 46.8 %copy-start.7 = (f32[16,2,256]{2,1,0:T(2,128)S(1)}, f32[16,2,256]{2,1,0:T(2,128)}, u32[]{:S(2)}) copy-start(f32[16,2,256]{2,1,0:T(2,128)} %get-tuple-element.53) | copy-start | bytes 98308
  188.1 0.8 copy-start.1
  188.9 0.8 copy-start.2
  206.5 12.1 %all-to-all-start.2 = ((f32[4,128,256]{2,1,0:T(8,128)}), f32[4,128,256]{2,1,0:T(8,128)S(1)}, u32[]{:S(2)}, u32[]{:S(2)}) async-start(f32[4,128,256]{2,1,0:T(8,128)} %collect.1), calls=%async_computation.2 | async-start | bytes 1048576 | tf_op jit(solution)/shard_map/all_to_all | solution.py:749
  218.7 0.8 copy-start.3
  223.1 22.5 %all-to-all-start.3 = ((f32[32,16,256]{2,1,0:T(8,128)}), f32[32,16,256]{2,1,0:T(8,128)S(1)}, u32[]{:S(2)}, u32[]{:S(2)}) async-start(f32[32,16,256]{2,1,0:T(8,128)} %bitcast.51), calls=%async_computation.3 | async-start | bytes 1048576 | tf_op jit(solution)/shard_map/all_to_all | solution.py:690

commit v4 on v3

--- a/solution.py
+++ b/solution.py
@@ -94,44 +94,34 @@
     return mean, lax.rsqrt(boxed[4:8] - mean * mean + 1e-5)
 
 
-DEPTH = 8
-PART = 4
+PART = 8
 PACKED = 136
 FIRST = 3
 
 
 def pick(idx, features, blocks):
     count = idx.shape[0]
-    _, channels, rows, _ = features.shape
-    ahead = DEPTH // 2
+    images, channels, rows, _ = features.shape
 
     def kernel(idx_ref, features_ref, out_ref, strips, in_sem, out_sem):
-        def read(s):
+        def read(k):
             return pltpu.make_async_copy(
-                features_ref.at[idx_ref[s], :, :, pl.ds(0, 128 * blocks)],
-                strips.at[s % DEPTH],
-                in_sem.at[s % DEPTH],
+                features_ref.at[k, :, :, pl.ds(0, 128 * blocks)], strips.at[k], in_sem.at[k]
             )
 
         def write(s, j):
             return pltpu.make_async_copy(
-                strips.at[s % DEPTH, :, :, pl.ds(128 * j, 128)],
-                out_ref.at[s, j],
-                out_sem.at[s % DEPTH, j],
+                strips.at[idx_ref[s], :, :, pl.ds(128 * j, 128)], out_ref.at[s, j], out_sem.at[s, j]
             )
 
-        for s in range(DEPTH):
-            read(s).start()
+        for k in range(images):
+            read(k).start()
+        for k in range(images):
+            read(k).wait()
         for s in range(count):
-            read(s).wait()
             for j in range(blocks):
                 write(s, j).start()
-            later = s + ahead
-            if DEPTH <= later < count:
-                for j in range(blocks):
-                    write(later - DEPTH, j).wait()
-                read(later).start()
-        for s in range(count - DEPTH, count):
+        for s in range(count):
             for j in range(blocks):
                 write(s, j).wait()
 
@@ -143,9 +133,9 @@
             in_specs=[pl.BlockSpec(memory_space=pl.ANY)],
             out_specs=pl.BlockSpec(memory_space=pl.ANY),
             scratch_shapes=[
-                pltpu.VMEM((DEPTH, channels, rows, 128 * blocks), BF),
-                pltpu.SemaphoreType.DMA((DEPTH,)),
-                pltpu.SemaphoreType.DMA((DEPTH, blocks)),
+                pltpu.VMEM((images, channels, rows, 128 * blocks), BF),
+                pltpu.SemaphoreType.DMA((images,)),
+                pltpu.SemaphoreType.DMA((count, blocks)),
             ],
         ),
         out_shape=jax.ShapeDtypeStruct((count, blocks, channels, rows, 128), BF),
@@ -223,8 +213,10 @@
 
 
 def edge_kernel(slot_ref, *refs):
-    blocks, (sel_ref, stat_ref, head_ref, tail_ref, stats_ref) = refs[:PART], refs[PART:]
+    blocks, (sel_ref, stat_ref, head_ref, tail_ref, stats_ref, *kept) = refs[:PART], refs[PART:]
     for g in range(PART):
+        if kept:
+            kept[0][g, 0] = blocks[g][0, blocks[g].shape[1] - 1]
         for j in range(stats_ref.shape[1]):
             head, tail, stats = block_edges(blocks[g][0, j], sel_ref, stat_ref)
             head_ref[g, j] = head
@@ -233,10 +225,10 @@
 
 
 def unpack_kernel(slot_ref, *refs):
-    packed, before = refs[:PART], refs[PART : 2 * PART]
+    packed = refs[:PART]
     (
         spread_ref, into_ref, eye_ref, sel_ref, stat_ref, head_ref, tail_ref, stats_ref, block_ref,
-    ) = refs[2 * PART :]
+    ) = refs[PART:]
     for g in range(PART):
         wide = dot(packed[g][0, 256:384, :], spread_ref[...])
         line = packed[g][0, 384:392, :]
@@ -244,9 +236,8 @@
         column = dot(eye_ref[...] * line, into_ref[...])
         block = jnp.concatenate([wide[:, :128], wide[:, 128:]], axis=0) + column
         blocks = (packed[g][0, 0:256, :], block.astype(BF))
-        block_ref[g, 0] = before[g][0, 0]
         for j in range(2):
-            block_ref[g, j + 1] = blocks[j]
+            block_ref[g, j] = blocks[j]
             head, tail, stats = block_edges(blocks[j], sel_ref, stat_ref)
             head_ref[g, j] = head
             tail_ref[g, j] = tail
@@ -271,10 +262,13 @@
     return pl.BlockSpec(a.shape, lambda k, s: (0,) * a.ndim)
 
 
-def edges(slot, recv):
+def edges(slot, recv, keep_last):
     images, blocks = slot.shape[0], recv.shape[1]
     constants = edge_constants()
     specs, shapes = edge_outputs(images, blocks)
+    if keep_last:
+        specs = specs + [pl.BlockSpec((PART, 1, 256, 128), lambda k, s: (k, 0, 0, 0))]
+        shapes = shapes + [jax.ShapeDtypeStruct((images, 1, 256, 128), BF)]
 
     def by_slot(g):
         return lambda k, s: (s[PART * k + g], 0, 0, 0)
@@ -298,7 +292,7 @@
     )(slot, *[recv] * PART, *constants)
 
 
-def unpack(slot, packed, main):
+def unpack(slot, packed):
     images = slot.shape[0]
     spread, _, into, eye = pack_constants()
     constants = (spread, into, eye) + edge_constants()
@@ -306,9 +300,6 @@
 
     def by_slot(g):
         return lambda k, s: (s[PART * k + g], 0, 0)
-
-    def before(g):
-        return lambda k, s: (s[PART * k + g], FIRST - 1, 0, 0)
 
     return pl.pallas_call(
         unpack_kernel,
@@ -316,14 +307,13 @@
             num_scalar_prefetch=1,
             grid=(images // PART,),
             in_specs=[pl.BlockSpec((1, 256 + PACKED, 128), by_slot(g)) for g in range(PART)]
-            + [pl.BlockSpec((1, 1, 256, 128), before(g)) for g in range(PART)]
             + [whole_spec(a) for a in constants],
-            out_specs=specs + [pl.BlockSpec((PART, 3, 256, 128), lambda k, s: (k, 0, 0, 0))],
-        ),
-        out_shape=shapes + [jax.ShapeDtypeStruct((images, 3, 256, 128), BF)],
+            out_specs=specs + [pl.BlockSpec((PART, 2, 256, 128), lambda k, s: (k, 0, 0, 0))],
+        ),
+        out_shape=shapes + [jax.ShapeDtypeStruct((images, 2, 256, 128), BF)],
         compiler_params=PARAMS,
         name="unpack",
-    )(slot, *[packed] * PART, *[main] * PART, *constants)
+    )(slot, *[packed] * PART, *constants)
 
 
 def prepare_kernel(
@@ -397,16 +387,16 @@
         return out
 
     count = len(ys)
-    near_refs, far_refs = take(group), take(group)
+    block_refs = take(3) if late else (take(group), take(group))
     own_ref, table_ref, pat_ref, mask_ref, w2_ref, flip_ref, elev_ref, cell_ref = take(8)
 
-    def pair(g):
+    def joined(three, g):
         if late:
-            early, before, after = ref_sets[0]
-            first = jnp.where(pl.program_id(0) == 0, early[g, 0].astype(F32), before[g, 0].astype(F32))
-            return jnp.concatenate([first.astype(early.dtype), after[g, 0]], axis=1)
-        before, after = ref_sets[0]
-        return jnp.concatenate([before[g, 0], after[g, 0]], axis=1)
+            early, before, after = three
+            near = jnp.where(pl.program_id(0) == 0, early[g, 0], before[g, 0])
+        else:
+            near, after = three[0][g, 0], three[1]
+        return jnp.concatenate([near, after[g, 0]], axis=1)
 
     width = 3 if late else 2
     stat_refs = take(width)
@@ -415,11 +405,6 @@
     edge_ref = take(1)[0] if halo else None
     mean_ref, rows_ref, skew = refs
 
-    def joined(set_refs, g):
-        ref_sets[0] = set_refs
-        return pair(g)
-
-    ref_sets = [None]
     column = 63 - lax.broadcasted_iota(jnp.int32, (64, 128), 0)
     lane = lax.broadcasted_iota(jnp.int32, (64, 128), 1)
     wrapped = lane < column
@@ -432,7 +417,10 @@
     soft = []
     chosen = []
     for g in range(group):
-        rhs = jnp.concatenate([near_refs[g][0, 0], far_refs[g][0, 0]], axis=1)
+        if late:
+            rhs = joined(block_refs, g)
+        else:
+            rhs = jnp.concatenate([block_refs[0][g][0, 0], block_refs[1][g][0, 0]], axis=1)
         stats = joined(stat_refs, g)
         if halo:
             up = joined(up_refs, g)
@@ -517,11 +505,6 @@
     def slot_block(g, j):
         return lambda n, k, s: (s[group * k + g], n + first + j, 0, 0)
 
-    def compact_block(g, j):
-        return lambda n, k, s: (group * k + g, n + j, 0, 0)
-
-    block_at = compact_block if late else slot_block
-
     def near(n, k, s):
         return (k, n + first, 0, 0)
 
@@ -531,10 +514,10 @@
     def pixels(n, k, s):
         return (k, 0, n + first)
 
-    def pair_specs(rows):
+    def pair_specs(rows, kept=FIRST - 1):
         if late:
             maps = (
-                lambda n, k, s: (k, FIRST - 1, 0, 0),
+                lambda n, k, s: (k, kept, 0, 0),
                 lambda n, k, s: (k, 0, 0, 0),
                 lambda n, k, s: (k, n, 0, 0),
             )
@@ -545,7 +528,14 @@
     def pair_args(arrays):
         return [arrays[0], arrays[1], arrays[1]] if late else [arrays[0], arrays[0]]
 
-    in_specs = [pl.BlockSpec((1, 1, 256, 128), block_at(g, j)) for j in range(2) for g in range(group)]
+    if late:
+        in_specs = pair_specs(256, 0)
+        args = pair_args(blocks)
+    else:
+        in_specs = [
+            pl.BlockSpec((1, 1, 256, 128), slot_block(g, j)) for j in range(2) for g in range(group)
+        ]
+        args = [blocks] * (2 * group)
     in_specs += [
         pl.BlockSpec((group, 1, WIN, 256), near),
         pl.BlockSpec((group, 1, 64, 128), near),
@@ -556,7 +546,7 @@
         pl.BlockSpec((group, 4, 128), pixels),
         pl.BlockSpec((group, 4, 128), pixels),
     ] + pair_specs(8)
-    args = [blocks] * (2 * group) + [
+    args += [
         own, table, table_patterns(ys), row_masks(), w2, flips(), elev, cell,
     ] + pair_args(stats)
     if halo:
@@ -599,9 +589,9 @@
     return jnp.concatenate([w, w], axis=1).astype(BF)
 
 
-def collect_kernel(list_ref, count_ref, a_ref, b_ref, c_ref, out_ref, rows):
+def collect_kernel(list_ref, count_ref, a_ref, b_ref, c_ref, d_ref, out_ref, rows):
     at = 0
-    for part in (a_ref, b_ref, c_ref):
+    for part in (a_ref, b_ref, c_ref, d_ref):
         for n in range(part.shape[0]):
             rows[at : at + part.shape[1], :] = part[n]
             at += part.shape[1]
@@ -693,7 +683,7 @@
 
     every = jnp.arange(images, dtype=jnp.int32)
     own = pick(every, features, STEPS + 1)
-    own_head, own_tail, own_stats = edges(every, own)
+    own_head, own_tail, own_stats = edges(every, own, False)
     own_up, own_down = neighbour_rows(own_head, own_tail)
     own_turned, edge_turned, own_table = prepare(own, own_up, own_down, own_stats, depth_index)
     packed = pack(chosen, own)
@@ -720,32 +710,32 @@
         (packed, own_turned, edge_turned, own_table, elevation, metas, w2)
     )
     last = exchange(packed)
-    head, tail, stats = edges(slot, main)
+    head, tail, stats, early = edges(slot, main, True)
     up, down = neighbour_rows(head, tail)
     shared = (own_turned, edge_turned, own_table, w2, elevation, cell_index)
-    mean_a, rows_a = sweep_steps(
-        0, 2, (0, 1, 2, 3), 8, slot, main, (stats,), (up,), (down,), *shared, False
+    shared = (own_turned, edge_turned, own_table, w2, elevation, cell_index)
+    inner, outer = (1, 2), (0, 3)
+    one = (stats,)
+    mean_i, rows_i = sweep_steps(0, 2, inner, 16, slot, main, one, None, None, *shared, False)
+    up, down, mean_i = lax.optimization_barrier((up, down, mean_i))
+    mean_o, rows_o = sweep_steps(0, 2, outer, 16, slot, main, one, (up,), (down,), *shared, False)
+    last, mean_o = lax.optimization_barrier((last, mean_o))
+    head_l, tail_l, stats_l, late = unpack(slot, last)
+    up_l, down_l = neighbour_rows(head_l, tail_l)
+    blocks, both = (early, late), (stats, stats_l)
+    mean_il, rows_il = sweep_steps(2, 2, inner, 16, slot, blocks, both, None, None, *shared, True)
+    mean_ol, rows_ol = sweep_steps(
+        2, 2, outer, 16, slot, blocks, both, (up, up_l), (down, down_l), *shared, True
     )
-    last, mean_a = lax.optimization_barrier((last, mean_a))
-    head_l, tail_l, stats_l, late = unpack(slot, last, main)
-    up_l, down_l = neighbour_rows(head_l, tail_l)
-    both = (stats, stats_l)
-    mean_b, rows_b = sweep_steps(2, 2, (1, 2), 8, slot, late, both, None, None, *shared, True)
-    mean_c, rows_c = sweep_steps(
-        2, 2, (0, 3), 8, slot, late, both, (up, up_l), (down, down_l), *shared, True
-    )
-    mean_bc = jnp.concatenate([mean_c[:, 0:1], mean_b, mean_c[:, 1:2]], axis=1)
-    mean_range = jnp.concatenate([mean_a, mean_bc], axis=2)
+    mean_i = jnp.concatenate([mean_i, mean_il], axis=2)
+    mean_o = jnp.concatenate([mean_o, mean_ol], axis=2)
+    mean_range = jnp.concatenate([mean_o[:, 0:1], mean_i, mean_o[:, 1:2]], axis=1)
 
     lists = block_list[0, 0]
     n, r, k = lists % STEPS, lists // STEPS % 4, lists // (4 * STEPS)
-    half = (n - 2) * 2 * images + 2 * k
-    row_list = jnp.where(
-        n < 2,
-        n * 4 * images + 4 * k + r,
-        jnp.where((r == 1) | (r == 2), 8 * images + half + r - 1, 12 * images + half + r // 3),
-    )
-    send = collect(row_list, block_count[0, 0], (rows_a, rows_b, rows_c))
+    inside = (r == 1) | (r == 2)
+    row_list = 2 * images * n + 2 * k + jnp.where(inside, r - 1, 8 * images + r // 3)
+    send = collect(row_list, block_count[0, 0], (rows_i, rows_il, rows_o, rows_ol))
     got = lax.all_to_all(send, "tile", split_axis=0, concat_axis=0, tiled=True)
     dense = place(metas[:, :128], metas[:, 128], got, group_count * PATCH_DEV)
     parts = exchange(dense.reshape(group_count, PATCH_DEV, 2 * CELLS))

time: 249 us -> 235 us (0.944)
  waiting for transfers between devices: 60.7 us -> 52.8 us
  Pallas kernels: 111 us -> 108 us
    ppermute x3, waiting for transfers between devices: 29 us -> 19.4 us  [neighbour_rows(): above = lax.ppermute(tail, 'tile', [(i, i + 1) for i in range(count - 1)])]
    pallas_call x2, Pallas kernels: 16.7 us -> 12.4 us  [pick(): pl.pallas_call(kernel, grid_spec=pltpu.PrefetchScalarGridSpec(num_scalar_...]
    pallas_call x3 -> x4, Pallas kernels: 41.4 us -> 43.2 us  [sweep_steps(): pl.pallas_call(functools.partial(sweep_kernel, group, ys, halo, late), gr...]
  transfers between devices with their start and end apart: 13 -> 13, of which waited for: 8 -> 8; matrix products, arithmetic and copies ran while one was open for 3% -> 4% of each run, Pallas kernels for 29% -> 32%
where the time goes in v4:
time: 235 us; the launch traced here: 233 us
  Pallas kernels  108 us (46%)
  starting transfers between devices  56.3 us (24%)
  waiting for transfers between devices  52.8 us (22%)
  local copies, waits for them, and re-layouts  9.63 us (4%)
  other arithmetic  5.74 us (2%)
    pallas_call x4, Pallas kernels, sweep_steps(): pl.pallas_call(functools.partial(sweep_kernel, group, ys, halo, late), gr...  43.2 us
    all_to_all x3, starting transfers between devices, exchange(): return lax.all_to_all(a, 'img', split_axis=0, concat_axis=0, tiled=True)  32.9 us
    ppermute x3, waiting for transfers between devices, neighbour_rows(): above = lax.ppermute(tail, 'tile', [(i, i + 1) for i in range(count - 1)])  19.4 us
    all_to_all x3, waiting for transfers between devices, exchange(): return lax.all_to_all(a, 'img', split_axis=0, concat_axis=0, tiled=True)  16.9 us
    pallas_call x1, Pallas kernels, prepare(): pl.pallas_call(prepare_kernel, grid=(images,), in_specs=[pl.BlockSpec((1,...  15.4 us
    pallas_call x2, Pallas kernels, edges(): pl.pallas_call(edge_kernel, grid_spec=pltpu.PrefetchScalarGridSpec(num_sc...  13.5 us
    pallas_call x2, Pallas kernels, pick(): pl.pallas_call(kernel, grid_spec=pltpu.PrefetchScalarGridSpec(num_scalar_...  12.4 us
    ppermute x3, waiting for transfers between devices, neighbour_rows(): below = lax.ppermute(head, 'tile', [(i + 1, i) for i in range(count - 1)])  10.8 us
  transfers between devices with their start and end apart: 13, of which 8 were waited for; matrix products, arithmetic and copies ran while one was open for 4% of the time, Pallas kernels for 32%

profile of v4, /device:TPU:1, one launch (start us, length us, event | category | flops | bytes accessed | tf_op | source)
XLA Modules:
  0.0 233.1 jit_solution(14819896770909374334)
XLA Ops:
  0.6 0.8 reshape.74
  1.4 0.7 add_select_fusion.1
  2.1 6.2 %pick.3 = bf16[32,3,64,4,128]{4,3,2,1,0:T(4,128)(2,1)} custom-call(s32[32]{0:T(128)} %get-tuple-element.73.idx_ref, bf16[16,64,4,768]{3,2,1,0:T(4,128)(2,1)} %features_ref.3), custom_call_target="tpu_custom_call" | custom-call | bytes 12582912 | tf_op jit(solution)/shard_map/pick/pallas_call | solution.py:128
  8.3 0.0 copy-start.13
  8.3 0.0 copy-start.11
  8.4 8.6 %all-to-all-start.1 = ((bf16[32,3,256,128]{3,2,1,0:T(8,128)(2,1)}), bf16[32,3,256,128]{3,2,1,0:T(8,128)(2,1)}, u32[]{:S(2)}, u32[]{:S(2)}) async-start(bf16[32,3,256,128]{3,2,1,0:T(8,128)(2,1)} %bitcast.62), calls=%async_computation.1 | async-start | bytes 12582912 | tf_op jit(solution)/shard_map/all_to_all | solution.py:680
  17.1 0.1 broadcast_in_dim.40
  17.2 1.7 collective-permute-start.2
  18.9 3.3 %collective-permute-start.3 = (s32[1,256]{1,0:T(1,128)S(1)}, s32[1,256]{1,0:T(1,128)S(1)}, u32[]{:S(2)}, u32[]{:S(2)}) collective-permute-start(s32[1,256]{1,0:T(1,128)S(1)} %get-tuple-element.76), channel_id=1, source_target_pairs={{0,2},{1,3},{2,0},{3,1},{4,6},{5,7},{6,4},{7,5},{8,10},{9,11},{10,... | collective-permute-start | bytes 3080 | tf_op jit(solution)/shard_map/ppermute | solution.py:703
  22.2 0.7 collective-permute-start.4
  22.9 0.5 iota.15.idx_ref
  23.4 6.2 %pick.2 = bf16[16,5,64,4,128]{4,3,2,1,0:T(4,128)(2,1)} custom-call(s32[16]{0:T(128)} %iota.15.idx_ref, bf16[16,64,4,768]{3,2,1,0:T(4,128)(2,1)} %features_ref.3), custom_call_target="tpu_custom_call" | custom-call | bytes 10485760 | tf_op jit(solution)/shard_map/pick/pallas_call | solution.py:128
  29.7 0.5 iota.16.slot_ref
  30.2 0.0 copy-start.4
  30.2 0.0 copy-start.14
  30.2 7.6 %edges.2 = (bf16[16,5,64,128]{3,2,1,0:T(8,128)(2,1)}, bf16[16,5,64,128]{3,2,1,0:T(8,128)(2,1)}, f32[16,5,8,128]{3,2,1,0:T(8,128)}) custom-call(s32[16]{0:T(128)} %iota.16.slot_ref, bf16[16,5,256,128]{3,2,1,0:T(8,128)(2,1)} %bitcast.37, bf16[16,5,256,128]{3,2,1,0:T(8,128)(2,1)} %bitcast.38, bf16[16,5,256,128]{3,2,1,0:T(8,128)(2,1)} %bitcast.39, ...), custom_call_target="tpu_custom_call" | custom-call | flops 1600000000 | bytes 8000000 | tf_op jit(solution)/shard_map/edges/pallas_call | solution.py:276
  37.8 2.7 %collective-permute-start = (bf16[16,5,64,128]{3,2,1,0:T(8,128)(2,1)}, bf16[16,5,64,128]{3,2,1,0:T(8,128)(2,1)S(1)}, u32[]{:S(2)}, u32[]{:S(2)}) collective-permute-start(bf16[16,5,64,128]{3,2,1,0:T(8,128)(2,1)} %get-tuple-element.36), channel_id=1, source_target_pairs={{0,1},{1,2},{2,3},{4,5},{5,6},{6,7},{8,9},{9,10},{10,11},{12,13},{... | collective-permute-start | bytes 3932168 | tf_op jit(solution)/shard_map/ppermute | solution.py:660
  40.6 1.3 collective-permute-start.1
  42.0 0.1 pad_bitcast_fusion.4
  42.0 0.1 pad_bitcast_fusion
  42.2 0.6 pad_maximum_fusion.1.refs_37_.refs_8_
  42.8 1.0 select_reduce_fusion
  43.8 0.8 fusion.refs_39_.refs_10_
  44.5 7.1 %pack.1 = bf16[32,392,128]{2,1,0:T(8,128)(2,1)} custom-call(s32[32]{0:T(128)} %get-tuple-element.73.idx_ref, bf16[16,5,256,128]{3,2,1,0:T(8,128)(2,1)} %bitcast.49, bf16[16,5,256,128]{3,2,1,0:T(8,128)(2,1)} %bitcast.46, bf16[16,5,256,128]{3,2,1,0:T(8,128)(2,1)} %bitcast.47, bf16[16,5,256,128]{3,2,1,0:T(8,128)(2,1)} %bitcast.48, ...), custom_call_target="tpu_custom_call" | custom-call | tf_op jit(solution)/shard_map/pack/pallas_call | solution.py:185
  51.6 0.0 collective-permute-done.2
  51.7 0.0 collective-permute-done.4
  51.7 0.6 gather_fusion
  52.3 0.7 broadcast_select_fusion
  52.9 14.8 %collective-permute-done.up_ref = bf16[16,5,64,128]{3,2,1,0:T(8,128)(2,1)S(1)} collective-permute-done((bf16[16,5,64,128]{3,2,1,0:T(8,128)(2,1)}, bf16[16,5,64,128]{3,2,1,0:T(8,128)(2,1)S(1)}, u32[]{:S(2)}, u32[]{:S(2)}) %collective-permute-start) | collective-permute-done | bytes 1310752 | tf_op jit(solution)/shard_map/ppermute | solution.py:660
  67.7 3.9 %collective-permute-done.1.down_ref = bf16[16,5,64,128]{3,2,1,0:T(8,128)(2,1)S(1)} collective-permute-done((bf16[16,5,64,128]{3,2,1,0:T(8,128)(2,1)}, bf16[16,5,64,128]{3,2,1,0:T(8,128)(2,1)S(1)}, u32[]{:S(2)}, u32[]{:S(2)}) %collective-permute-start.1) | collective-permute-done | bytes 1310752 | tf_op jit(solution)/shard_map/ppermute | solution.py:661
  71.6 1.0 copy-done.18
  72.7 15.4 %prepare.1 = (bf16[16,4,144,256]{3,2,1,0:T(8,128)(2,1)}, bf16[16,4,144,128]{3,2,1,0:T(8,128)(2,1)}, bf16[16,4,64,128]{3,2,1,0:T(8,128)(2,1)}) custom-call(bf16[16,5,256,128]{3,2,1,0:T(8,128)(2,1)} %bitcast.61, bf16[16,5,64,128]{3,2,1,0:T(8,128)(2,1)} %copy-done.17, bf16[16,5,64,128]{3,2,1,0:T(8,128)(2,1)} %copy-done.18, ...), custom_call_target="tpu_custom_call" | custom-call | flops 2560000000 | bytes 16000000 | tf_op jit(solution)/shard_map/prepare/pallas_call | solution.py:347
  88.1 6.9 %all-to-all-done.1.refs_0_.refs_1_.refs_2_.refs_3_.refs_4_.refs_5_.refs_6_.refs_7_.refs_8_.refs_9_.refs_10_.refs_11_.refs_12_.refs_13_.refs_14_.refs_15_.refs_16_.refs_17_.refs_18_.refs_19_.refs_20_.refs_21_.refs_22_.refs_23_.refs_24_.refs_25_.refs_26_.refs_27_.refs_28_.refs_29_.refs_30_.refs_31_.refs_32_ = bf16[32,3,256,128]{3,2,1,0:T(8,128)(2,1)} async-done(((bf16[32,3,256,128]{3,2,1,0:T(8,128)(2,1)}), ...) | async-done | bytes 6291488 | tf_op jit(solution)/shard_map/all_to_all | solution.py:680
  95.0 14.5 %all-to-all-start = ((bf16[32,392,128]{2,1,0:T(8,128)(2,1)}), bf16[32,392,128]{2,1,0:T(8,128)(2,1)S(1)}, u32[]{:S(2)}, u32[]{:S(2)}) async-start(bf16[32,392,128]{2,1,0:T(8,128)(2,1)} %pack.1), calls=%async_computation | async-start | bytes 6422528 | tf_op jit(solution)/shard_map/all_to_all | solution.py:680
  109.5 0.5 fusion.21.slot_ref.refs_0_
  110.1 5.8 %edges.3 = (bf16[16,3,64,128]{3,2,1,0:T(8,128)(2,1)}, bf16[16,3,64,128]{3,2,1,0:T(8,128)(2,1)}, f32[16,3,8,128]{3,2,1,0:T(8,128)}, bf16[16,1,256,128]{3,2,1,0:T(8,128)(2,1)}) custom-call(s32[16]{0:T(128)} %fusion.21.slot_ref.refs_0_, ...), custom_call_target="tpu_custom_call" | custom-call | flops 960000000 | bytes 4800000 | tf_op jit(solution)/shard_map/edges/pallas_call | solution.py:276
  115.9 4.5 %collective-permute-start.5 = (bf16[16,3,64,128]{3,2,1,0:T(8,128)(2,1)}, bf16[16,3,64,128]{3,2,1,0:T(8,128)(2,1)}, u32[]{:S(2)}, u32[]{:S(2)}) collective-permute-start(bf16[16,3,64,128]{3,2,1,0:T(8,128)(2,1)} %get-tuple-element.48), channel_id=1, source_target_pairs={{0,1},{1,2},{2,3},{4,5},{5,6},{6,7},{8,9},{9,10},{10,11},{12,13},{... | collective-permute-start | bytes 2359304 | tf_op jit(solution)/shard_map/ppermute | solution.py:660
  120.4 1.5 collective-permute-start.6
  121.9 10.0 %sweep.4 = (f32[16,2,256]{2,1,0:T(2,128)}, f32[2,32,256]{2,1,0:T(8,128)}) custom-call(s32[16]{0:T(128)} %fusion.21.slot_ref.refs_0_, ...), custom_call_target="tpu_custom_call" | custom-call | flops 3200000000 | bytes 6400000 | tf_op jit(solution)/shard_map/sweep/pallas_call | solution.py:556
  131.9 4.6 %collective-permute-done.5.refs_43_.refs_44_.refs_15_ = bf16[16,3,64,128]{3,2,1,0:T(8,128)(2,1)} collective-permute-done((bf16[16,3,64,128]{3,2,1,0:T(8,128)(2,1)}, bf16[16,3,64,128]{3,2,1,0:T(8,128)(2,1)}, u32[]{:S(2)}, u32[]{:S(2)}) %collective-permute-start.5) | collective-permute-done | bytes 786464 | tf_op jit(solution)/shard_map/ppermute | solution.py:660
  136.4 4.7 %collective-permute-done.6.refs_45_.refs_46_.refs_18_ = bf16[16,3,64,128]{3,2,1,0:T(8,128)(2,1)} collective-permute-done((bf16[16,3,64,128]{3,2,1,0:T(8,128)(2,1)}, bf16[16,3,64,128]{3,2,1,0:T(8,128)(2,1)}, u32[]{:S(2)}, u32[]{:S(2)}) %collective-permute-start.6) | collective-permute-done | bytes 786464 | tf_op jit(solution)/shard_map/ppermute | solution.py:661
  141.2 11.9 %sweep.5 = (f32[16,2,256]{2,1,0:T(2,128)}, f32[2,32,256]{2,1,0:T(8,128)}) custom-call(s32[16]{0:T(128)} %fusion.21.slot_ref.refs_0_, ...), custom_call_target="tpu_custom_call" | custom-call | flops 3200000000 | bytes 6400000 | tf_op jit(solution)/shard_map/sweep/pallas_call | solution.py:556
  153.1 1.7 copy-done
  154.8 7.6 %unpack.1 = (bf16[16,2,64,128]{3,2,1,0:T(8,128)(2,1)}, bf16[16,2,64,128]{3,2,1,0:T(8,128)(2,1)}, f32[16,2,8,128]{3,2,1,0:T(8,128)}, bf16[16,2,256,128]{3,2,1,0:T(8,128)(2,1)}) custom-call(s32[16]{0:T(128)} %fusion.21.slot_ref.refs_0_, bf16[32,392,128]{2,1,0:T(8,128)(2,1)} %copy-done, bf16[32,392,128]{2,1,0:T(8,128)(2,1)} %copy-done, ...), custom_call_target="tpu_custom_call" | custom-call | tf_op jit(solution)/shard_map/unpack/pallas_call | solution.py:304
  162.4 2.6 %collective-permute-start.7 = (bf16[16,2,64,128]{3,2,1,0:T(8,128)(2,1)}, bf16[16,2,64,128]{3,2,1,0:T(8,128)(2,1)S(1)}, u32[]{:S(2)}, u32[]{:S(2)}) collective-permute-start(bf16[16,2,64,128]{3,2,1,0:T(8,128)(2,1)} %get-tuple-element.60), channel_id=1, source_target_pairs={{0,1},{1,2},{2,3},{4,5},{5,6},{6,7},{8,9},{9,10},{10,11},{12,13},{... | collective-permute-start | bytes 1572872 | tf_op jit(solution)/shard_map/ppermute | solution.py:660
  165.0 1.5 collective-permute-start.8
  166.5 0.6 fusion.8.list_ref
  167.1 9.6 %sweep.7 = (f32[16,2,256]{2,1,0:T(2,128)}, f32[2,32,256]{2,1,0:T(8,128)}) custom-call(s32[16]{0:T(128)} %fusion.21.slot_ref.refs_0_, bf16[16,1,256,128]{3,2,1,0:T(8,128)(2,1)} %get-tuple-element.56.refs_1_, bf16[16,2,256,128]{3,2,1,0:T(8,128)(2,1)} %get-tuple-element.58.refs_2_.refs_3_, bf16[16,2,256,128]{3,2,1,0:T(8,128)(2,1)} %get-tuple-element.58.refs_2_.refs_3_, ...), custom_call_target="tpu_custom_call" | custom-call | flops 3200000000 | bytes 6400000 | tf_op jit(solution)/shard_map/sweep/pallas_call | solution.py:556
  176.8 2.1 collective-permute-done.8.refs_19_.refs_20_
  178.9 0.8 copy-done.2
  179.7 11.8 %sweep.6 = (f32[16,2,256]{2,1,0:T(2,128)}, f32[2,32,256]{2,1,0:T(8,128)}) custom-call(s32[16]{0:T(128)} %fusion.21.slot_ref.refs_0_, bf16[16,1,256,128]{3,2,1,0:T(8,128)(2,1)} %get-tuple-element.56.refs_1_, bf16[16,2,256,128]{3,2,1,0:T(8,128)(2,1)} %get-tuple-element.58.refs_2_.refs_3_, bf16[16,2,256,128]{3,2,1,0:T(8,128)(2,1)} %get-tuple-element.58.refs_2_.refs_3_, ...), custom_call_target="tpu_custom_call" | custom-call | flops 3200000000 | bytes 6400000 | tf_op jit(solution)/shard_map/sweep/pallas_call | solution.py:556
  191.5 3.7 %collect.1 = f32[4,128,256]{2,1,0:T(8,128)} custom-call(s32[4,128]{1,0:T(4,128)} %fusion.8.list_ref, s32[4]{0:T(128)} %bitcast.65, f32[2,32,256]{2,1,0:T(8,128)} %get-tuple-element.66.a_ref, f32[2,32,256]{2,1,0:T(8,128)} %get-tuple-element.67.b_ref, f32[2,32,256]{2,1,0:T(8,128)} %get-tuple-element.68.c_ref, f32[2,32,256]{2,1,0:T(8,128)} %get-tuple-element.69.d_ref), custom_call_target="tpu_custom_call" | custom-call | tf_op jit(solution)/shard_map/collect/pallas_call | solution.py:612
  195.2 3.6 %all-to-all-start.2 = ((f32[4,128,256]{2,1,0:T(8,128)}), f32[4,128,256]{2,1,0:T(8,128)S(1)}, u32[]{:S(2)}, u32[]{:S(2)}) async-start(f32[4,128,256]{2,1,0:T(8,128)} %collect.1), calls=%async_computation.2 | async-start | bytes 1048576 | tf_op jit(solution)/shard_map/all_to_all | solution.py:739
  198.8 0.6 slice.20.slot_ref
  199.3 0.6 slice_reduce_fusion.count_ref
  200.0 5.8 %all-to-all-done.2.got_ref = f32[4,128,256]{2,1,0:T(8,128)S(1)} async-done(((f32[4,128,256]{2,1,0:T(8,128)}), f32[4,128,256]{2,1,0:T(8,128)S(1)}, u32[]{:S(2)}, u32[]{:S(2)}) %all-to-all-start.2) | async-done | bytes 524320 | tf_op jit(solution)/shard_map/all_to_all | solution.py:739
  205.7 0.8 copy-done.3
  206.5 4.6 %place.1 = f32[512,256]{1,0:T(8,128)} custom-call(s32[4,128]{1,0:T(4,128)} %slice.20.slot_ref, s32[4]{0:T(128)} %slice_reduce_fusion.count_ref, f32[4,128,256]{2,1,0:T(8,128)} %copy-done.3), custom_call_target="tpu_custom_call" | custom-call | tf_op jit(solution)/shard_map/place/pallas_call | solution.py:644
  211.1 9.7 %all-to-all-start.3 = ((f32[32,16,256]{2,1,0:T(8,128)}), f32[32,16,256]{2,1,0:T(8,128)S(1)}, u32[]{:S(2)}, u32[]{:S(2)}) async-start(f32[32,16,256]{2,1,0:T(8,128)} %bitcast.63), calls=%async_computation.3 | async-start | bytes 1048576 | tf_op jit(solution)/shard_map/all_to_all | solution.py:680
  220.9 0.8 constant_dynamic-update-slice_fusion
  221.6 0.1 fusion.23
  221.7 0.7 pad_maximum_fusion
  222.4 10.0 %all-to-all-done.3 = f32[32,16,256]{2,1,0:T(8,128)S(1)} async-done(((f32[32,16,256]{2,1,0:T(8,128)}), f32[32,16,256]{2,1,0:T(8,128)S(1)}, u32[]{:S(2)}, u32[]{:S(2)}) %all-to-all-start.3) | async-done | bytes 524320 | tf_op jit(solution)/shard_map/all_to_all | solution.py:680
  232.5 0.6 fusion.5
  (43 shorter events, 0.3 us)
Async XLA Ops:
  8.3 8.7 %copy-start.13 = (s32[1,1,4]{2,1,0:T(1,128)S(1)}, s32[1,1,4]{2,1,0:T(1,128)}, u32[]{:S(2)}) copy-start(s32[1,1,4]{2,1,0:T(1,128)} %param.44) | copy-start | bytes 52
  8.3 8.8 %copy-start.11 = (s32[1,1,4,128]{3,2,1,0:T(4,128)S(1)}, s32[1,1,4,128]{3,2,1,0:T(4,128)}, u32[]{:S(2)}) copy-start(s32[1,1,4,128]{3,2,1,0:T(4,128)} %param.43) | copy-start | bytes 6148
  8.4 86.6 %all-to-all-start.1 = ((bf16[32,3,256,128]{3,2,1,0:T(8,128)(2,1)}), bf16[32,3,256,128]{3,2,1,0:T(8,128)(2,1)}, u32[]{:S(2)}, u32[]{:S(2)}) async-start(bf16[32,3,256,128]{3,2,1,0:T(8,128)(2,1)} %bitcast.62), calls=%async_computation.1 | async-start | bytes 12582912 | tf_op jit(solution)/shard_map/all_to_all | solution.py:680
  17.2 34.5 %collective-permute-start.2 = (s32[1,256]{1,0:T(1,128)S(1)}, s32[1,256]{1,0:T(1,128)S(1)}, u32[]{:S(2)}, u32[]{:S(2)}) collective-permute-start(s32[1,256]{1,0:T(1,128)S(1)} %get-tuple-element.75), channel_id=1, source_target_pairs={{0,1},{1,2},{2,3},{3,0},{4,5},{5,6},{6,7},{7,4},{8,9},{9,10},{10,1... | collective-permute-start | bytes 3080 | tf_op jit(solution)/shard_map/ppermute | solution.py:703
  18.9 32.8 %collective-permute-start.3 = (s32[1,256]{1,0:T(1,128)S(1)}, s32[1,256]{1,0:T(1,128)S(1)}, u32[]{:S(2)}, u32[]{:S(2)}) collective-permute-start(s32[1,256]{1,0:T(1,128)S(1)} %get-tuple-element.76), channel_id=1, source_target_pairs={{0,2},{1,3},{2,0},{3,1},{4,6},{5,7},{6,4},{7,5},{8,10},{9,11},{10,... | collective-permute-start | bytes 3080 | tf_op jit(solution)/shard_map/ppermute | solution.py:703
  22.2 29.5 %collective-permute-start.4 = (s32[1,256]{1,0:T(1,128)S(1)}, s32[1,256]{1,0:T(1,128)S(1)}, u32[]{:S(2)}, u32[]{:S(2)}) collective-permute-start(s32[1,256]{1,0:T(1,128)S(1)} %get-tuple-element.77), channel_id=1, source_target_pairs={{0,3},{1,0},{2,1},{3,2},{4,7},{5,4},{6,5},{7,6},{8,11},{9,8},{10,9... | collective-permute-start | bytes 3080 | tf_op jit(solution)/shard_map/ppermute | solution.py:703
  30.2 11.7 %copy-start.5 = (s32[16,4,512]{2,1,0:T(4,128)S(1)}, s32[16,4,512]{2,1,0:T(4,128)}, u32[]{:S(2)}) copy-start(s32[16,4,512]{2,1,0:T(4,128)} %index_ref.1) | copy-start | bytes 393220
  30.2 11.8 %copy-start.10 = (f32[64]{0:T(128)S(1)}, f32[64]{0:T(128)}, u32[]{:S(2)}) copy-start(f32[64]{0:T(128)} %param.37) | copy-start | bytes 772
  30.2 11.9 %copy-start.15 = (bf16[1,128]{1,0:T(2,128)(2,1)S(1)}, bf16[1,128]{1,0:T(2,128)(2,1)}, u32[]{:S(2)}) copy-start(bf16[1,128]{1,0:T(2,128)(2,1)} %constant.268) | copy-start | bytes 772
  30.2 11.9 %copy-start.16 = (bf16[1,128]{1,0:T(2,128)(2,1)S(1)}, bf16[1,128]{1,0:T(2,128)(2,1)}, u32[]{:S(2)}) copy-start(bf16[1,128]{1,0:T(2,128)(2,1)} %constant.269) | copy-start | bytes 772
  30.2 13.6 %copy-start.4 = (f32[16,4,512]{2,1,0:T(4,128)S(1)}, f32[16,4,512]{2,1,0:T(4,128)}, u32[]{:S(2)}) copy-start(f32[16,4,512]{2,1,0:T(4,128)} %param.39) | copy-start | bytes 393220
  30.2 13.6 %copy-start.14 = (f32[16]{0:T(128)S(1)}, f32[16]{0:T(128)}, u32[]{:S(2)}) copy-start(f32[16]{0:T(128)} %param.38) | copy-start | bytes 196
  37.8 29.9 %collective-permute-start = (bf16[16,5,64,128]{3,2,1,0:T(8,128)(2,1)}, bf16[16,5,64,128]{3,2,1,0:T(8,128)(2,1)S(1)}, u32[]{:S(2)}, u32[]{:S(2)}) collective-permute-start(bf16[16,5,64,128]{3,2,1,0:T(8,128)(2,1)} %get-tuple-element.36), channel_id=1, source_target_pairs={{0,1},{1,2},{2,3},{4,5},{5,6},{6,7},{8,9},{9,10},{10,11},{12,13},{... | collective-permute-start | bytes 3932168 | tf_op jit(solution)/shard_map/ppermute | solution.py:660
  40.6 31.1 %collective-permute-start.1 = (bf16[16,5,64,128]{3,2,1,0:T(8,128)(2,1)}, bf16[16,5,64,128]{3,2,1,0:T(8,128)(2,1)S(1)}, u32[]{:S(2)}, u32[]{:S(2)}) collective-permute-start(bf16[16,5,64,128]{3,2,1,0:T(8,128)(2,1)} %get-tuple-element.37), channel_id=1, source_target_pairs={{1,0},{2,1},{3,2},{5,4},{6,5},{7,6},{9,8},{10,9},{11,10},{13,12},{... | collective-permute-start | bytes 3932168 | tf_op jit(solution)/shard_map/ppermute | solution.py:661
  67.7 3.9 %copy-start.17 = (bf16[16,5,64,128]{3,2,1,0:T(8,128)(2,1)}, bf16[16,5,64,128]{3,2,1,0:T(8,128)(2,1)S(1)}, u32[]{:S(2)}) copy-start(bf16[16,5,64,128]{3,2,1,0:T(8,128)(2,1)S(1)} %collective-permute-done.up_ref) | copy-start | bytes 3932164
  71.6 1.0 copy-start.18
  95.0 58.1 %all-to-all-start = ((bf16[32,392,128]{2,1,0:T(8,128)(2,1)}), bf16[32,392,128]{2,1,0:T(8,128)(2,1)S(1)}, u32[]{:S(2)}, u32[]{:S(2)}) async-start(bf16[32,392,128]{2,1,0:T(8,128)(2,1)} %pack.1), calls=%async_computation | async-start | bytes 6422528 | tf_op jit(solution)/shard_map/all_to_all | solution.py:680
  115.9 20.6 %collective-permute-start.5 = (bf16[16,3,64,128]{3,2,1,0:T(8,128)(2,1)}, bf16[16,3,64,128]{3,2,1,0:T(8,128)(2,1)}, u32[]{:S(2)}, u32[]{:S(2)}) collective-permute-start(bf16[16,3,64,128]{3,2,1,0:T(8,128)(2,1)} %get-tuple-element.48), channel_id=1, source_target_pairs={{0,1},{1,2},{2,3},{4,5},{5,6},{6,7},{8,9},{9,10},{10,11},{12,13},{... | collective-permute-start | bytes 2359304 | tf_op jit(solution)/shard_map/ppermute | solution.py:660
  120.4 20.8 %collective-permute-start.6 = (bf16[16,3,64,128]{3,2,1,0:T(8,128)(2,1)}, bf16[16,3,64,128]{3,2,1,0:T(8,128)(2,1)}, u32[]{:S(2)}, u32[]{:S(2)}) collective-permute-start(bf16[16,3,64,128]{3,2,1,0:T(8,128)(2,1)} %get-tuple-element.49), channel_id=1, source_target_pairs={{1,0},{2,1},{3,2},{5,4},{6,5},{7,6},{9,8},{10,9},{11,10},{13,12},{... | collective-permute-start | bytes 2359304 | tf_op jit(solution)/shard_map/ppermute | solution.py:661
  153.1 1.7 copy-start
  154.8 11.8 %copy-start.12 = (s32[1,1,4,128]{3,2,1,0:T(4,128)S(1)}, s32[1,1,4,128]{3,2,1,0:T(4,128)}, u32[]{:S(2)}) copy-start(s32[1,1,4,128]{3,2,1,0:T(4,128)} %param.42) | copy-start | bytes 6148
  162.4 14.4 %collective-permute-start.7 = (bf16[16,2,64,128]{3,2,1,0:T(8,128)(2,1)}, bf16[16,2,64,128]{3,2,1,0:T(8,128)(2,1)S(1)}, u32[]{:S(2)}, u32[]{:S(2)}) collective-permute-start(bf16[16,2,64,128]{3,2,1,0:T(8,128)(2,1)} %get-tuple-element.60), channel_id=1, source_target_pairs={{0,1},{1,2},{2,3},{4,5},{5,6},{6,7},{8,9},{9,10},{10,11},{12,13},{... | collective-permute-start | bytes 1572872 | tf_op jit(solution)/shard_map/ppermute | solution.py:660
  165.0 13.9 %collective-permute-start.8 = (bf16[16,2,64,128]{3,2,1,0:T(8,128)(2,1)}, bf16[16,2,64,128]{3,2,1,0:T(8,128)(2,1)S(1)}, u32[]{:S(2)}, u32[]{:S(2)}) collective-permute-start(bf16[16,2,64,128]{3,2,1,0:T(8,128)(2,1)} %get-tuple-element.61), channel_id=1, source_target_pairs={{1,0},{2,1},{3,2},{5,4},{6,5},{7,6},{9,8},{10,9},{11,10},{13,12},{... | collective-permute-start | bytes 1572872 | tf_op jit(solution)/shard_map/ppermute | solution.py:661
  176.7 22.1 %copy-start.9 = (s32[4,256]{1,0:T(4,128)S(1)}, s32[4,256]{1,0:T(4,128)}, u32[]{:S(2)}) copy-start(s32[4,256]{1,0:T(4,128)} %broadcast_select_fusion) | copy-start | bytes 12292
  176.7 44.1 %copy-start.6 = (f32[16,2,256]{2,1,0:T(2,128)S(1)}, f32[16,2,256]{2,1,0:T(2,128)}, u32[]{:S(2)}) copy-start(f32[16,2,256]{2,1,0:T(2,128)} %get-tuple-element.55) | copy-start | bytes 98308
  176.7 45.0 %copy-start.7 = (f32[16,2,256]{2,1,0:T(2,128)S(1)}, f32[16,2,256]{2,1,0:T(2,128)}, u32[]{:S(2)}) copy-start(f32[16,2,256]{2,1,0:T(2,128)} %get-tuple-element.63) | copy-start | bytes 98308
  176.7 45.0 %copy-start.8 = (f32[16,2,256]{2,1,0:T(2,128)S(1)}, f32[16,2,256]{2,1,0:T(2,128)}, u32[]{:S(2)}) copy-start(f32[16,2,256]{2,1,0:T(2,128)} %get-tuple-element.64) | copy-start | bytes 98308
  176.8 2.1 copy-start.1
  178.9 0.8 copy-start.2
  195.2 10.5 %all-to-all-start.2 = ((f32[4,128,256]{2,1,0:T(8,128)}), f32[4,128,256]{2,1,0:T(8,128)S(1)}, u32[]{:S(2)}, u32[]{:S(2)}) async-start(f32[4,128,256]{2,1,0:T(8,128)} %collect.1), calls=%async_computation.2 | async-start | bytes 1048576 | tf_op jit(solution)/shard_map/all_to_all | solution.py:739
  205.7 0.8 copy-start.3
  211.1 21.3 %all-to-all-start.3 = ((f32[32,16,256]{2,1,0:T(8,128)}), f32[32,16,256]{2,1,0:T(8,128)S(1)}, u32[]{:S(2)}, u32[]{:S(2)}) async-start(f32[32,16,256]{2,1,0:T(8,128)} %bitcast.63), calls=%async_computation.3 | async-start | bytes 1048576 | tf_op jit(solution)/shard_map/all_to_all | solution.py:680

commit v5 on v4

--- a/solution.py
+++ b/solution.py
@@ -19,6 +19,7 @@
 F32 = jnp.float32
 NT = (((1,), (1,)), ((), ()))
 PARAMS = pltpu.CompilerParams(vmem_limit_bytes=60 * 1024 * 1024)
+SMALL = pltpu.CompilerParams(vmem_limit_bytes=24 * 1024 * 1024)
 
 
 def dot(a, b):
@@ -66,11 +67,7 @@
     for c in range(64):
         sel[c, 4 * c] = 1.0
         sel[64 + c, 4 * c + 3] = 1.0
-    stat = np.zeros((16, 256), np.float32)
-    for y in range(4):
-        stat[y, y::4] = 1.0
-        stat[12 + y, y::4] = 1.0
-    return jnp.asarray(sel, BF), jnp.asarray(stat, BF)
+    return (jnp.asarray(sel, BF),)
 
 
 def split2(a):
@@ -204,21 +201,22 @@
     )(idx, *[own] * (2 * PART), spread, column)
 
 
-def block_edges(block, sel_ref, stat_ref):
+def block_edges(block, sel_ref):
     rows = dot(sel_ref[...], block).astype(BF)
-    value = block.astype(F32)
-    high, low = split2(value * value)
-    stats = dot(stat_ref[0:8], block) + dot(stat_ref[8:16], high) + dot(stat_ref[8:16], low)
+    value = block.astype(F32).reshape(32, 8, 128)
+    total = jnp.sum(value, 0)
+    square = jnp.sum(value * value, 0)
+    stats = jnp.concatenate([total[0:4] + total[4:8], square[0:4] + square[4:8]], axis=0)
     return rows[0:64], rows[64:128], stats
 
 
 def edge_kernel(slot_ref, *refs):
-    blocks, (sel_ref, stat_ref, head_ref, tail_ref, stats_ref, *kept) = refs[:PART], refs[PART:]
+    blocks, (sel_ref, head_ref, tail_ref, stats_ref, *kept) = refs[:PART], refs[PART:]
     for g in range(PART):
         if kept:
             kept[0][g, 0] = blocks[g][0, blocks[g].shape[1] - 1]
         for j in range(stats_ref.shape[1]):
-            head, tail, stats = block_edges(blocks[g][0, j], sel_ref, stat_ref)
+            head, tail, stats = block_edges(blocks[g][0, j], sel_ref)
             head_ref[g, j] = head
             tail_ref[g, j] = tail
             stats_ref[g, j] = stats
@@ -227,7 +225,7 @@
 def unpack_kernel(slot_ref, *refs):
     packed = refs[:PART]
     (
-        spread_ref, into_ref, eye_ref, sel_ref, stat_ref, head_ref, tail_ref, stats_ref, block_ref,
+        spread_ref, into_ref, eye_ref, sel_ref, head_ref, tail_ref, stats_ref, block_ref,
     ) = refs[PART:]
     for g in range(PART):
         wide = dot(packed[g][0, 256:384, :], spread_ref[...])
@@ -238,7 +236,7 @@
         blocks = (packed[g][0, 0:256, :], block.astype(BF))
         for j in range(2):
             block_ref[g, j] = blocks[j]
-            head, tail, stats = block_edges(blocks[j], sel_ref, stat_ref)
+            head, tail, stats = block_edges(blocks[j], sel_ref)
             head_ref[g, j] = head
             tail_ref[g, j] = tail
             stats_ref[g, j] = stats
@@ -311,19 +309,22 @@
             out_specs=specs + [pl.BlockSpec((PART, 2, 256, 128), lambda k, s: (k, 0, 0, 0))],
         ),
         out_shape=shapes + [jax.ShapeDtypeStruct((images, 2, 256, 128), BF)],
-        compiler_params=PARAMS,
+        compiler_params=SMALL,
         name="unpack",
     )(slot, *[packed] * PART, *constants)
 
 
 def prepare_kernel(
-    own_ref, up_ref, down_ref, stat_ref, index_ref, rev_ref, flip_ref, own_out, edge_out, table_out
+    own_ref, up_ref, up_last_ref, down_ref, down_last_ref, stat_ref, index_ref, rev_ref, flip_ref, own_out, edge_out, table_out
 ):
     mean_inv = 24.0 * LOG2E
     for n in range(STEPS):
         block = jnp.concatenate([own_ref[0, n], own_ref[0, n + 1]], axis=1)
-        up = jnp.concatenate([up_ref[0, n], up_ref[0, n + 1]], axis=1)
-        down = jnp.concatenate([down_ref[0, n], down_ref[0, n + 1]], axis=1)
+        final = n + 1 == STEPS
+        up = jnp.concatenate([up_ref[0, n], up_last_ref[0] if final else up_ref[0, n + 1]], axis=1)
+        down = jnp.concatenate(
+            [down_ref[0, n], down_last_ref[0] if final else down_ref[0, n + 1]], axis=1
+        )
         own_out[0, n] = dot_nt(rev_ref[...], block).astype(BF)
         edge_out[0, n] = dot_nt(rev_ref[...], jnp.concatenate([up, down], axis=0)).astype(BF)
         stats = jnp.concatenate([stat_ref[0, n], stat_ref[0, n + 1]], axis=1)
@@ -342,15 +343,17 @@
         table_out[0, n] = jnp.concatenate([left, right, blank], axis=1).astype(BF)
 
 
-def prepare(own, up, down, stats, depth_index):
+def prepare(own, up, up_last, down, down_last, stats, depth_index):
     images, blocks = own.shape[0], own.shape[1]
     return pl.pallas_call(
         prepare_kernel,
         grid=(images,),
         in_specs=[
             pl.BlockSpec((1, blocks, 256, 128), lambda k: (k, 0, 0, 0)),
-            pl.BlockSpec((1, blocks, 64, 128), lambda k: (k, 0, 0, 0)),
-            pl.BlockSpec((1, blocks, 64, 128), lambda k: (k, 0, 0, 0)),
+            pl.BlockSpec((1, STEPS, 64, 128), lambda k: (k, 0, 0, 0)),
+            pl.BlockSpec((1, 64, 128), lambda k: (k, 0, 0)),
+            pl.BlockSpec((1, STEPS, 64, 128), lambda k: (k, 0, 0, 0)),
+            pl.BlockSpec((1, 64, 128), lambda k: (k, 0, 0)),
             pl.BlockSpec((1, blocks, 8, 128), lambda k: (k, 0, 0, 0)),
             pl.BlockSpec((1, 4, 512), lambda k: (k, 0, 0)),
             pl.BlockSpec((WIN, 256), lambda k: (0, 0)),
@@ -371,7 +374,7 @@
         ),
         compiler_params=PARAMS,
         name="prepare",
-    )(own, up, down, stats, depth_index, reversal(), flips())
+    )(own, up, up_last, down, down_last, stats, depth_index, reversal(), flips())
 
 
 def skewed(left, right, column, lane, shift):
@@ -619,7 +622,7 @@
             scratch_shapes=[pltpu.VMEM((total, 2 * CELLS), F32)],
         ),
         out_shape=jax.ShapeDtypeStruct((owners, cap, 2 * CELLS), F32),
-        compiler_params=PARAMS,
+        compiler_params=SMALL,
         name="collect",
     )(row_list, counts, *parts)
 
@@ -650,7 +653,7 @@
             out_specs=pl.BlockSpec((total, 2 * CELLS), lambda i, a, b: (0, 0)),
         ),
         out_shape=jax.ShapeDtypeStruct((total, 2 * CELLS), F32),
-        compiler_params=PARAMS,
+        compiler_params=SMALL,
         name="place",
     )(slots, counts, got)
 
@@ -684,8 +687,15 @@
     every = jnp.arange(images, dtype=jnp.int32)
     own = pick(every, features, STEPS + 1)
     own_head, own_tail, own_stats = edges(every, own, False)
-    own_up, own_down = neighbour_rows(own_head, own_tail)
-    own_turned, edge_turned, own_table = prepare(own, own_up, own_down, own_stats, depth_index)
+    own_up, own_down = neighbour_rows(own_head[:, :STEPS], own_tail[:, :STEPS])
+    ends = [jnp.transpose(v[:, STEPS, :, :2], (0, 2, 1)).reshape(images, -1) for v in (own_head, own_tail)]
+    ends = [v.reshape(images, 2, -1) for v in neighbour_rows(*ends)]
+    up_last, down_last = (
+        jnp.pad(jnp.transpose(v, (0, 2, 1)), ((0, 0), (0, 0), (0, 126))) for v in ends
+    )
+    own_turned, edge_turned, own_table = prepare(
+        own, own_up, up_last, own_down, down_last, own_stats, depth_index
+    )
     packed = pack(chosen, own)
 
     hyp = jnp.arange(NDEPTH, dtype=jnp.int32)[:, None, None, None]

time: 235 us -> 230 us (0.979)
  waiting for transfers between devices: 52.8 us -> 41.3 us
  starting transfers between devices: 56.3 us -> 64 us
  Pallas kernels: 108 us -> 102 us
  local copies, waits for them, and re-layouts: 9.63 us -> 15.2 us
    ppermute x3 -> x4, waiting for transfers between devices: 19.4 us -> 4.61 us  [neighbour_rows(): above = lax.ppermute(tail, 'tile', [(i, i + 1) for i in range(count - 1)])]
    ppermute x3 -> x4, starting transfers between devices: 9.86 us -> 16.4 us  [neighbour_rows(): above = lax.ppermute(tail, 'tile', [(i, i + 1) for i in range(count - 1)])]
    slice x0 -> x2, local copies, waits for them, and re-layouts: none -> 2.68 us  [on_device(): own_up, own_down = neighbour_rows(own_head[:, :STEPS], own_tail[:, :STEPS])]
    all_to_all x3, waiting for transfers between devices: 16.9 us -> 19.4 us  [exchange(): return lax.all_to_all(a, 'img', split_axis=0, concat_axis=0, tiled=True)]
    pallas_call x1, Pallas kernels: 7.61 us -> 5.23 us  [unpack(): pl.pallas_call(unpack_kernel, grid_spec=pltpu.PrefetchScalarGridSpec(num_...]
    ppermute x3 -> x4, starting transfers between devices: 4.27 us -> 5.32 us  [neighbour_rows(): below = lax.ppermute(head, 'tile', [(i + 1, i) for i in range(count - 1)])]
    ppermute x3 -> x4, waiting for transfers between devices: 10.8 us -> 10.5 us  [neighbour_rows(): below = lax.ppermute(head, 'tile', [(i + 1, i) for i in range(count - 1)])]
  transfers between devices with their start and end apart: 13 -> 15, of which waited for: 8 -> 6; matrix products, arithmetic and copies ran while one was open for 4% -> 6% of each run, Pallas kernels for 32% -> 31%
where the time goes in v5:
time: 230 us; the launch traced here: 228 us
  Pallas kernels  102 us (44%)
  starting transfers between devices  64 us (28%)
  waiting for transfers between devices  41.3 us (18%)
  local copies, waits for them, and re-layouts  15.2 us (7%)
  other arithmetic  5.15 us (2%)
    pallas_call x4, Pallas kernels, sweep_steps(): pl.pallas_call(functools.partial(sweep_kernel, group, ys, halo, late), gr...  43.5 us
    all_to_all x3, starting transfers between devices, exchange(): return lax.all_to_all(a, 'img', split_axis=0, concat_axis=0, tiled=True)  32.9 us
    all_to_all x3, waiting for transfers between devices, exchange(): return lax.all_to_all(a, 'img', split_axis=0, concat_axis=0, tiled=True)  19.4 us
    ppermute x4, starting transfers between devices, neighbour_rows(): above = lax.ppermute(tail, 'tile', [(i, i + 1) for i in range(count - 1)])  16.4 us
    pallas_call x1, Pallas kernels, prepare(): pl.pallas_call(prepare_kernel, grid=(images,), in_specs=[pl.BlockSpec((1,...  15.5 us
    pallas_call x2, Pallas kernels, pick(): pl.pallas_call(kernel, grid_spec=pltpu.PrefetchScalarGridSpec(num_scalar_...  12.5 us
    pallas_call x2, Pallas kernels, edges(): pl.pallas_call(edge_kernel, grid_spec=pltpu.PrefetchScalarGridSpec(num_sc...  11.3 us
    ppermute x4, waiting for transfers between devices, neighbour_rows(): below = lax.ppermute(head, 'tile', [(i + 1, i) for i in range(count - 1)])  10.5 us
  transfers between devices with their start and end apart: 15, of which 6 were waited for; matrix products, arithmetic and copies ran while one was open for 6% of the time, Pallas kernels for 31%

profile of v5, /device:TPU:1, one launch (start us, length us, event | category | flops | bytes accessed | tf_op | source)
XLA Modules:
  0.0 228.4 jit_solution(14616938897994291273)
XLA Ops:
  0.6 0.8 reshape.86
  1.4 0.7 add_select_fusion.1
  2.0 6.3 %pick.3 = bf16[32,3,64,4,128]{4,3,2,1,0:T(4,128)(2,1)} custom-call(s32[32]{0:T(128)} %get-tuple-element.73.idx_ref, bf16[16,64,4,768]{3,2,1,0:T(4,128)(2,1)} %features_ref.3), custom_call_target="tpu_custom_call" | custom-call | bytes 12582912 | tf_op jit(solution)/shard_map/pick/pallas_call | solution.py:125
  8.3 8.6 %all-to-all-start.1 = ((bf16[32,3,256,128]{3,2,1,0:T(8,128)(2,1)}), bf16[32,3,256,128]{3,2,1,0:T(8,128)(2,1)}, u32[]{:S(2)}, u32[]{:S(2)}) async-start(bf16[32,3,256,128]{3,2,1,0:T(8,128)(2,1)} %bitcast.74), calls=%async_computation.1 | async-start | bytes 12582912 | tf_op jit(solution)/shard_map/all_to_all | solution.py:683
  17.2 1.7 collective-permute-start.4
  18.9 3.3 %collective-permute-start.5 = (s32[1,256]{1,0:T(1,128)S(1)}, s32[1,256]{1,0:T(1,128)S(1)}, u32[]{:S(2)}, u32[]{:S(2)}) collective-permute-start(s32[1,256]{1,0:T(1,128)S(1)} %get-tuple-element.76), channel_id=1, source_target_pairs={{0,2},{1,3},{2,0},{3,1},{4,6},{5,7},{6,4},{7,5},{8,10},{9,11},{10,... | collective-permute-start | bytes 3080 | tf_op jit(solution)/shard_map/ppermute | solution.py:713
  22.2 0.7 collective-permute-start.6
  22.9 0.5 iota.15.idx_ref
  23.4 6.3 %pick.2 = bf16[16,5,64,4,128]{4,3,2,1,0:T(4,128)(2,1)} custom-call(s32[16]{0:T(128)} %iota.15.idx_ref, bf16[16,64,4,768]{3,2,1,0:T(4,128)(2,1)} %features_ref.3), custom_call_target="tpu_custom_call" | custom-call | bytes 10485760 | tf_op jit(solution)/shard_map/pick/pallas_call | solution.py:125
  29.7 0.5 iota.16.slot_ref
  30.2 6.3 %edges.2 = (bf16[16,5,64,128]{3,2,1,0:T(8,128)(2,1)}, bf16[16,5,64,128]{3,2,1,0:T(8,128)(2,1)}, f32[16,5,8,128]{3,2,1,0:T(8,128)}) custom-call(s32[16]{0:T(128)} %iota.16.slot_ref, bf16[16,5,256,128]{3,2,1,0:T(8,128)(2,1)} %bitcast.49, bf16[16,5,256,128]{3,2,1,0:T(8,128)(2,1)} %bitcast.50, bf16[16,5,256,128]{3,2,1,0:T(8,128)(2,1)} %bitcast.51, ...), custom_call_target="tpu_custom_call" | custom-call | flops 1600000000 | bytes 8000000 | tf_op jit(solution)/shard_map/edges/pallas_call | solution.py:274
  36.6 1.4 slice.30
  37.9 3.6 %collective-permute-start = (bf16[16,4,64,128]{3,2,1,0:T(8,128)(2,1)S(1)}, bf16[16,4,64,128]{3,2,1,0:T(8,128)(2,1)}, u32[]{:S(2)}, u32[]{:S(2)}) collective-permute-start(bf16[16,4,64,128]{3,2,1,0:T(8,128)(2,1)S(1)} %slice.30), channel_id=1, source_target_pairs={{0,1},{1,2},{2,3},{4,5},{5,6},{6,7},{8,9},{9,10},{10,11},{12,13},{... | collective-permute-start | bytes 3145736 | tf_op jit(solution)/shard_map/ppermute | solution.py:663
  41.5 1.3 slice.32
  42.9 1.3 collective-permute-start.2
  44.4 1.0 select_reduce_fusion
  45.4 0.6 pad_maximum_fusion.1.refs_37_.refs_8_
  46.0 0.8 fusion.refs_39_.refs_10_
  46.8 1.1 slice_bitcast_fusion
  47.9 0.2 copy.38
  48.1 0.1 reshape.88
  48.2 0.2 copy.40
  48.3 0.1 reshape.90
  48.4 7.2 %pack.1 = bf16[32,392,128]{2,1,0:T(8,128)(2,1)} custom-call(s32[32]{0:T(128)} %get-tuple-element.73.idx_ref, bf16[16,5,256,128]{3,2,1,0:T(8,128)(2,1)} %bitcast.61, bf16[16,5,256,128]{3,2,1,0:T(8,128)(2,1)} %bitcast.58, bf16[16,5,256,128]{3,2,1,0:T(8,128)(2,1)} %bitcast.59, bf16[16,5,256,128]{3,2,1,0:T(8,128)(2,1)} %bitcast.60, ...), custom_call_target="tpu_custom_call" | custom-call | tf_op jit(solution)/shard_map/pack/pallas_call | solution.py:182
  55.6 4.0 %collective-permute-start.1 = (bf16[16,128]{1,0:T(8,128)(2,1)S(1)}, bf16[16,128]{1,0:T(8,128)(2,1)S(1)}, u32[]{:S(2)}, u32[]{:S(2)}) collective-permute-start(bf16[16,128]{1,0:T(8,128)(2,1)S(1)} %reshape.88), channel_id=1, source_target_pairs={{0,1},{1,2},{2,3},{4,5},{5,6},{6,7},{8,9},{9,10},{10,11},{12,13},{... | collective-permute-start | bytes 12296 | tf_op jit(solution)/shard_map/ppermute | solution.py:663
  59.6 1.3 collective-permute-start.3
  60.9 0.6 gather_fusion
  61.5 0.7 broadcast_select_fusion
  62.2 0.2 copy.39
  62.5 5.7 %collective-permute-done.3 = bf16[16,128]{1,0:T(8,128)(2,1)S(1)} collective-permute-done((bf16[16,128]{1,0:T(8,128)(2,1)S(1)}, bf16[16,128]{1,0:T(8,128)(2,1)S(1)}, u32[]{:S(2)}, u32[]{:S(2)}) %collective-permute-start.3) | collective-permute-done | bytes 4128 | tf_op jit(solution)/shard_map/ppermute | solution.py:664
  68.3 0.2 copy.41
  68.5 0.8 pad.13.up_last_ref
  69.3 0.8 pad.14.down_last_ref
  70.1 15.5 %prepare.1 = (bf16[16,4,144,256]{3,2,1,0:T(8,128)(2,1)}, bf16[16,4,144,128]{3,2,1,0:T(8,128)(2,1)}, bf16[16,4,64,128]{3,2,1,0:T(8,128)(2,1)}) custom-call(bf16[16,5,256,128]{3,2,1,0:T(8,128)(2,1)} %bitcast.73, bf16[16,4,64,128]{3,2,1,0:T(8,128)(2,1)} %collective-permute-done.up_ref, bf16[16,64,128]{2,1,0:T(8,128)(2,1)} %pad.13.up_last_ref, ...), custom_call_target="tpu_custom_call" | custom-call | flops 2560000000 | bytes 16000000 | tf_op jit(solution)/shard_map/prepare/pallas_call | solution.py:348
  85.5 9.4 %all-to-all-done.1.refs_0_.refs_1_.refs_2_.refs_3_.refs_4_.refs_5_.refs_6_.refs_7_.refs_8_.refs_9_.refs_10_.refs_11_.refs_12_.refs_13_.refs_14_.refs_15_.refs_16_.refs_17_.refs_18_.refs_19_.refs_20_.refs_21_.refs_22_.refs_23_.refs_24_.refs_25_.refs_26_.refs_27_.refs_28_.refs_29_.refs_30_.refs_31_.refs_32_ = bf16[32,3,256,128]{3,2,1,0:T(8,128)(2,1)} async-done(((bf16[32,3,256,128]{3,2,1,0:T(8,128)(2,1)}), ...) | async-done | bytes 6291488 | tf_op jit(solution)/shard_map/all_to_all | solution.py:683
  95.0 14.5 %all-to-all-start = ((bf16[32,392,128]{2,1,0:T(8,128)(2,1)}), bf16[32,392,128]{2,1,0:T(8,128)(2,1)S(1)}, u32[]{:S(2)}, u32[]{:S(2)}) async-start(bf16[32,392,128]{2,1,0:T(8,128)(2,1)} %pack.1), calls=%async_computation | async-start | bytes 6422528 | tf_op jit(solution)/shard_map/all_to_all | solution.py:683
  109.5 0.6 fusion.21.slot_ref.refs_0_
  110.1 5.0 %edges.3 = (bf16[16,3,64,128]{3,2,1,0:T(8,128)(2,1)}, bf16[16,3,64,128]{3,2,1,0:T(8,128)(2,1)}, f32[16,3,8,128]{3,2,1,0:T(8,128)}, bf16[16,1,256,128]{3,2,1,0:T(8,128)(2,1)}) custom-call(s32[16]{0:T(128)} %fusion.21.slot_ref.refs_0_, ...), custom_call_target="tpu_custom_call" | custom-call | flops 960000000 | bytes 4800000 | tf_op jit(solution)/shard_map/edges/pallas_call | solution.py:274
  115.1 4.5 %collective-permute-start.7 = (bf16[16,3,64,128]{3,2,1,0:T(8,128)(2,1)}, bf16[16,3,64,128]{3,2,1,0:T(8,128)(2,1)}, u32[]{:S(2)}, u32[]{:S(2)}) collective-permute-start(bf16[16,3,64,128]{3,2,1,0:T(8,128)(2,1)} %get-tuple-element.48), channel_id=1, source_target_pairs={{0,1},{1,2},{2,3},{4,5},{5,6},{6,7},{8,9},{9,10},{10,11},{12,13},{... | collective-permute-start | bytes 2359304 | tf_op jit(solution)/shard_map/ppermute | solution.py:663
  119.6 1.5 collective-permute-start.8
  121.1 10.0 %sweep.4 = (f32[16,2,256]{2,1,0:T(2,128)}, f32[2,32,256]{2,1,0:T(8,128)}) custom-call(s32[16]{0:T(128)} %fusion.21.slot_ref.refs_0_, ...), custom_call_target="tpu_custom_call" | custom-call | flops 3200000000 | bytes 6400000 | tf_op jit(solution)/shard_map/sweep/pallas_call | solution.py:559
  131.0 4.6 %collective-permute-done.7.refs_43_.refs_44_.refs_15_ = bf16[16,3,64,128]{3,2,1,0:T(8,128)(2,1)} collective-permute-done((bf16[16,3,64,128]{3,2,1,0:T(8,128)(2,1)}, bf16[16,3,64,128]{3,2,1,0:T(8,128)(2,1)}, u32[]{:S(2)}, u32[]{:S(2)}) %collective-permute-start.7) | collective-permute-done | bytes 786464 | tf_op jit(solution)/shard_map/ppermute | solution.py:663
  135.6 4.7 %collective-permute-done.8.refs_45_.refs_46_.refs_18_ = bf16[16,3,64,128]{3,2,1,0:T(8,128)(2,1)} collective-permute-done((bf16[16,3,64,128]{3,2,1,0:T(8,128)(2,1)}, bf16[16,3,64,128]{3,2,1,0:T(8,128)(2,1)}, u32[]{:S(2)}, u32[]{:S(2)}) %collective-permute-start.8) | collective-permute-done | bytes 786464 | tf_op jit(solution)/shard_map/ppermute | solution.py:664
  140.4 12.1 %sweep.5 = (f32[16,2,256]{2,1,0:T(2,128)}, f32[2,32,256]{2,1,0:T(8,128)}) custom-call(s32[16]{0:T(128)} %fusion.21.slot_ref.refs_0_, ...), custom_call_target="tpu_custom_call" | custom-call | flops 3200000000 | bytes 6400000 | tf_op jit(solution)/shard_map/sweep/pallas_call | solution.py:559
  152.6 5.2 %unpack.1 = (bf16[16,2,64,128]{3,2,1,0:T(8,128)(2,1)}, bf16[16,2,64,128]{3,2,1,0:T(8,128)(2,1)}, f32[16,2,8,128]{3,2,1,0:T(8,128)S(1)}, bf16[16,2,256,128]{3,2,1,0:T(8,128)(2,1)S(1)}) custom-call(s32[16]{0:T(128)S(1)} %copy-done.10, bf16[32,392,128]{2,1,0:T(8,128)(2,1)S(1)} %all-to-all-done.refs_0_.refs_1_.refs_2_.refs_3_.refs_4_.refs_5_.refs_6_.refs_7_, ...), custom_call_target="tpu_custom_call" | custom-call | tf_op jit(solution)/shard_map/unpack/pallas_call | solution.py:302
  157.8 1.3 copy-done
  159.2 0.7 copy-done.1
  159.8 1.3 collective-permute-start.10
  161.1 4.2 %collective-permute-start.9 = (bf16[16,2,64,128]{3,2,1,0:T(8,128)(2,1)}, bf16[16,2,64,128]{3,2,1,0:T(8,128)(2,1)S(1)}, u32[]{:S(2)}, u32[]{:S(2)}) collective-permute-start(bf16[16,2,64,128]{3,2,1,0:T(8,128)(2,1)} %get-tuple-element.60), channel_id=1, source_target_pairs={{0,1},{1,2},{2,3},{4,5},{5,6},{6,7},{8,9},{9,10},{10,11},{12,13},{... | collective-permute-start | bytes 1572872 | tf_op jit(solution)/shard_map/ppermute | solution.py:663
  165.4 9.6 %sweep.7 = (f32[16,2,256]{2,1,0:T(2,128)}, f32[2,32,256]{2,1,0:T(8,128)}) custom-call(s32[16]{0:T(128)} %fusion.21.slot_ref.refs_0_, bf16[16,1,256,128]{3,2,1,0:T(8,128)(2,1)} %get-tuple-element.56.refs_1_, bf16[16,2,256,128]{3,2,1,0:T(8,128)(2,1)} %copy-done, bf16[16,2,256,128]{3,2,1,0:T(8,128)(2,1)} %copy-done, ...), custom_call_target="tpu_custom_call" | custom-call | flops 3200000000 | bytes 6400000 | tf_op jit(solution)/shard_map/sweep/pallas_call | solution.py:559
  175.1 0.8 copy-done.13
  176.0 0.8 copy-done.14
  176.8 11.8 %sweep.6 = (f32[16,2,256]{2,1,0:T(2,128)}, f32[2,32,256]{2,1,0:T(8,128)}) custom-call(s32[16]{0:T(128)} %fusion.21.slot_ref.refs_0_, bf16[16,1,256,128]{3,2,1,0:T(8,128)(2,1)} %get-tuple-element.56.refs_1_, bf16[16,2,256,128]{3,2,1,0:T(8,128)(2,1)} %copy-done, bf16[16,2,256,128]{3,2,1,0:T(8,128)(2,1)} %copy-done, ...), custom_call_target="tpu_custom_call" | custom-call | flops 3200000000 | bytes 6400000 | tf_op jit(solution)/shard_map/sweep/pallas_call | solution.py:559
  188.6 0.8 copy-done.9
  189.4 2.5 %collect.1 = f32[4,128,256]{2,1,0:T(8,128)} custom-call(s32[4,128]{1,0:T(4,128)S(1)} %fusion.8.list_ref, s32[4]{0:T(128)S(1)} %bitcast.48, f32[2,32,256]{2,1,0:T(8,128)S(1)} %copy-done.6, f32[2,32,256]{2,1,0:T(8,128)S(1)} %copy-done.8, f32[2,32,256]{2,1,0:T(8,128)S(1)} %copy-done.7, f32[2,32,256]{2,1,0:T(8,128)S(1)} %copy-done.9), custom_call_target="tpu_custom_call" | custom-call | tf_op jit(solution)/shard_map/collect/pallas_call | solution.py:615
  192.0 3.6 %all-to-all-start.2 = ((f32[4,128,256]{2,1,0:T(8,128)}), f32[4,128,256]{2,1,0:T(8,128)S(1)}, u32[]{:S(2)}, u32[]{:S(2)}) async-start(f32[4,128,256]{2,1,0:T(8,128)} %collect.1), calls=%async_computation.2 | async-start | bytes 1048576 | tf_op jit(solution)/shard_map/all_to_all | solution.py:749
  195.6 0.1 slice_reduce_fusion.count_ref
  195.7 6.8 %all-to-all-done.2.got_ref = f32[4,128,256]{2,1,0:T(8,128)S(1)} async-done(((f32[4,128,256]{2,1,0:T(8,128)}), f32[4,128,256]{2,1,0:T(8,128)S(1)}, u32[]{:S(2)}, u32[]{:S(2)}) %all-to-all-start.2) | async-done | bytes 524320 | tf_op jit(solution)/shard_map/all_to_all | solution.py:749
  202.5 3.8 %place.1 = f32[512,256]{1,0:T(8,128)} custom-call(s32[4,128]{1,0:T(4,128)S(1)} %slice.36.slot_ref, s32[4]{0:T(128)S(1)} %slice_reduce_fusion.count_ref, f32[4,128,256]{2,1,0:T(8,128)S(1)} %all-to-all-done.2.got_ref), custom_call_target="tpu_custom_call" | custom-call | tf_op jit(solution)/shard_map/place/pallas_call | solution.py:647
  206.4 9.7 %all-to-all-start.3 = ((f32[32,16,256]{2,1,0:T(8,128)}), f32[32,16,256]{2,1,0:T(8,128)S(1)}, u32[]{:S(2)}, u32[]{:S(2)}) async-start(f32[32,16,256]{2,1,0:T(8,128)} %bitcast.19), calls=%async_computation.3 | async-start | bytes 1048576 | tf_op jit(solution)/shard_map/all_to_all | solution.py:683
  216.1 0.8 constant_dynamic-update-slice_fusion
  217.0 0.7 pad_maximum_fusion
  217.7 10.0 %all-to-all-done.3 = f32[32,16,256]{2,1,0:T(8,128)S(1)} async-done(((f32[32,16,256]{2,1,0:T(8,128)}), f32[32,16,256]{2,1,0:T(8,128)S(1)}, u32[]{:S(2)}, u32[]{:S(2)}) %all-to-all-start.3) | async-done | bytes 524320 | tf_op jit(solution)/shard_map/all_to_all | solution.py:683
  227.8 0.6 fusion.5
  (76 shorter events, 0.8 us)
Async XLA Ops:
  8.3 8.7 %copy-start.11 = (s32[1,1,4]{2,1,0:T(1,128)S(1)}, s32[1,1,4]{2,1,0:T(1,128)}, u32[]{:S(2)}) copy-start(s32[1,1,4]{2,1,0:T(1,128)} %param.41) | copy-start | bytes 52
  8.3 8.8 %copy-start.22 = (s32[1,1,4,128]{3,2,1,0:T(4,128)S(1)}, s32[1,1,4,128]{3,2,1,0:T(4,128)}, u32[]{:S(2)}) copy-start(s32[1,1,4,128]{3,2,1,0:T(4,128)} %param.40) | copy-start | bytes 6148
  8.3 86.6 %all-to-all-start.1 = ((bf16[32,3,256,128]{3,2,1,0:T(8,128)(2,1)}), bf16[32,3,256,128]{3,2,1,0:T(8,128)(2,1)}, u32[]{:S(2)}, u32[]{:S(2)}) async-start(bf16[32,3,256,128]{3,2,1,0:T(8,128)(2,1)} %bitcast.74), calls=%async_computation.1 | async-start | bytes 12582912 | tf_op jit(solution)/shard_map/all_to_all | solution.py:683
  17.2 38.4 %collective-permute-start.4 = (s32[1,256]{1,0:T(1,128)S(1)}, s32[1,256]{1,0:T(1,128)S(1)}, u32[]{:S(2)}, u32[]{:S(2)}) collective-permute-start(s32[1,256]{1,0:T(1,128)S(1)} %get-tuple-element.75), channel_id=1, source_target_pairs={{0,1},{1,2},{2,3},{3,0},{4,5},{5,6},{6,7},{7,4},{8,9},{9,10},{10,1... | collective-permute-start | bytes 3080 | tf_op jit(solution)/shard_map/ppermute | solution.py:713
  18.9 40.7 %collective-permute-start.5 = (s32[1,256]{1,0:T(1,128)S(1)}, s32[1,256]{1,0:T(1,128)S(1)}, u32[]{:S(2)}, u32[]{:S(2)}) collective-permute-start(s32[1,256]{1,0:T(1,128)S(1)} %get-tuple-element.76), channel_id=1, source_target_pairs={{0,2},{1,3},{2,0},{3,1},{4,6},{5,7},{6,4},{7,5},{8,10},{9,11},{10,... | collective-permute-start | bytes 3080 | tf_op jit(solution)/shard_map/ppermute | solution.py:713
  22.2 38.7 %collective-permute-start.6 = (s32[1,256]{1,0:T(1,128)S(1)}, s32[1,256]{1,0:T(1,128)S(1)}, u32[]{:S(2)}, u32[]{:S(2)}) collective-permute-start(s32[1,256]{1,0:T(1,128)S(1)} %get-tuple-element.77), channel_id=1, source_target_pairs={{0,3},{1,0},{2,1},{3,2},{4,7},{5,4},{6,5},{7,6},{8,11},{9,8},{10,9... | collective-permute-start | bytes 3080 | tf_op jit(solution)/shard_map/ppermute | solution.py:713
  30.2 14.0 %copy-start.16 = (s32[16,4,512]{2,1,0:T(4,128)S(1)}, s32[16,4,512]{2,1,0:T(4,128)}, u32[]{:S(2)}) copy-start(s32[16,4,512]{2,1,0:T(4,128)} %index_ref.1) | copy-start | bytes 393220
  30.2 14.1 %copy-start.21 = (f32[64]{0:T(128)S(1)}, f32[64]{0:T(128)}, u32[]{:S(2)}) copy-start(f32[64]{0:T(128)} %param.34) | copy-start | bytes 772
  36.5 8.9 %copy-start.25 = (bf16[1,128]{1,0:T(2,128)(2,1)S(1)}, bf16[1,128]{1,0:T(2,128)(2,1)}, u32[]{:S(2)}) copy-start(bf16[1,128]{1,0:T(2,128)(2,1)} %constant.271) | copy-start | bytes 772
  36.5 8.9 %copy-start.26 = (bf16[1,128]{1,0:T(2,128)(2,1)S(1)}, bf16[1,128]{1,0:T(2,128)(2,1)}, u32[]{:S(2)}) copy-start(bf16[1,128]{1,0:T(2,128)(2,1)} %constant.272) | copy-start | bytes 772
  36.5 9.5 %copy-start.15 = (f32[16,4,512]{2,1,0:T(4,128)S(1)}, f32[16,4,512]{2,1,0:T(4,128)}, u32[]{:S(2)}) copy-start(f32[16,4,512]{2,1,0:T(4,128)} %param.36) | copy-start | bytes 393220
  36.5 9.5 %copy-start.24 = (f32[16]{0:T(128)S(1)}, f32[16]{0:T(128)}, u32[]{:S(2)}) copy-start(f32[16]{0:T(128)} %param.35) | copy-start | bytes 196
  37.9 32.1 %collective-permute-start = (bf16[16,4,64,128]{3,2,1,0:T(8,128)(2,1)S(1)}, bf16[16,4,64,128]{3,2,1,0:T(8,128)(2,1)}, u32[]{:S(2)}, u32[]{:S(2)}) collective-permute-start(bf16[16,4,64,128]{3,2,1,0:T(8,128)(2,1)S(1)} %slice.30), channel_id=1, source_target_pairs={{0,1},{1,2},{2,3},{4,5},{5,6},{6,7},{8,9},{9,10},{10,11},{12,13},{... | collective-permute-start | bytes 3145736 | tf_op jit(solution)/shard_map/ppermute | solution.py:663
  42.9 27.2 %collective-permute-start.2 = (bf16[16,4,64,128]{3,2,1,0:T(8,128)(2,1)S(1)}, bf16[16,4,64,128]{3,2,1,0:T(8,128)(2,1)}, u32[]{:S(2)}, u32[]{:S(2)}) collective-permute-start(bf16[16,4,64,128]{3,2,1,0:T(8,128)(2,1)S(1)} %slice.32), channel_id=1, source_target_pairs={{1,0},{2,1},{3,2},{5,4},{6,5},{7,6},{9,8},{10,9},{11,10},{13,12},{... | collective-permute-start | bytes 3145736 | tf_op jit(solution)/shard_map/ppermute | solution.py:664
  55.6 6.6 %collective-permute-start.1 = (bf16[16,128]{1,0:T(8,128)(2,1)S(1)}, bf16[16,128]{1,0:T(8,128)(2,1)S(1)}, u32[]{:S(2)}, u32[]{:S(2)}) collective-permute-start(bf16[16,128]{1,0:T(8,128)(2,1)S(1)} %reshape.88), channel_id=1, source_target_pairs={{0,1},{1,2},{2,3},{4,5},{5,6},{6,7},{8,9},{9,10},{10,11},{12,13},{... | collective-permute-start | bytes 12296 | tf_op jit(solution)/shard_map/ppermute | solution.py:663
  59.6 8.6 %collective-permute-start.3 = (bf16[16,128]{1,0:T(8,128)(2,1)S(1)}, bf16[16,128]{1,0:T(8,128)(2,1)S(1)}, u32[]{:S(2)}, u32[]{:S(2)}) collective-permute-start(bf16[16,128]{1,0:T(8,128)(2,1)S(1)} %reshape.90), channel_id=1, source_target_pairs={{1,0},{2,1},{3,2},{5,4},{6,5},{7,6},{9,8},{10,9},{11,10},{13,12},{... | collective-permute-start | bytes 12296 | tf_op jit(solution)/shard_map/ppermute | solution.py:664
  95.0 57.5 %all-to-all-start = ((bf16[32,392,128]{2,1,0:T(8,128)(2,1)}), bf16[32,392,128]{2,1,0:T(8,128)(2,1)S(1)}, u32[]{:S(2)}, u32[]{:S(2)}) async-start(bf16[32,392,128]{2,1,0:T(8,128)(2,1)} %pack.1), calls=%async_computation | async-start | bytes 6422528 | tf_op jit(solution)/shard_map/all_to_all | solution.py:683
  115.1 20.6 %collective-permute-start.7 = (bf16[16,3,64,128]{3,2,1,0:T(8,128)(2,1)}, bf16[16,3,64,128]{3,2,1,0:T(8,128)(2,1)}, u32[]{:S(2)}, u32[]{:S(2)}) collective-permute-start(bf16[16,3,64,128]{3,2,1,0:T(8,128)(2,1)} %get-tuple-element.48), channel_id=1, source_target_pairs={{0,1},{1,2},{2,3},{4,5},{5,6},{6,7},{8,9},{9,10},{10,11},{12,13},{... | collective-permute-start | bytes 2359304 | tf_op jit(solution)/shard_map/ppermute | solution.py:663
  119.6 20.8 %collective-permute-start.8 = (bf16[16,3,64,128]{3,2,1,0:T(8,128)(2,1)}, bf16[16,3,64,128]{3,2,1,0:T(8,128)(2,1)}, u32[]{:S(2)}, u32[]{:S(2)}) collective-permute-start(bf16[16,3,64,128]{3,2,1,0:T(8,128)(2,1)} %get-tuple-element.49), channel_id=1, source_target_pairs={{1,0},{2,1},{3,2},{5,4},{6,5},{7,6},{9,8},{10,9},{11,10},{13,12},{... | collective-permute-start | bytes 2359304 | tf_op jit(solution)/shard_map/ppermute | solution.py:664
  140.4 12.1 %copy-start.2 = (bf16[128,256]{1,0:T(8,128)(2,1)S(1)}, bf16[128,256]{1,0:T(8,128)(2,1)}, u32[]{:S(2)}) copy-start(bf16[128,256]{1,0:T(8,128)(2,1)} %constant.160.clone.refs_8_.refs_11_) | copy-start | bytes 196612
  140.4 12.1 %copy-start.3 = (bf16[128,256]{1,0:T(8,128)(2,1)S(1)}, bf16[128,256]{1,0:T(8,128)(2,1)}, u32[]{:S(2)}) copy-start(bf16[128,256]{1,0:T(8,128)(2,1)} %constant.163.clone.refs_16_.refs_8_) | copy-start | bytes 196612
  140.4 12.1 %copy-start.4 = (bf16[256,256]{1,0:T(8,128)(2,1)S(1)}, bf16[256,256]{1,0:T(8,128)(2,1)}, u32[]{:S(2)}) copy-start(bf16[256,256]{1,0:T(8,128)(2,1)} %constant.169.clone.refs_10_) | copy-start | bytes 393220
  140.4 12.2 %copy-start.5 = (bf16[256,128]{1,0:T(8,128)(2,1)S(1)}, bf16[256,128]{1,0:T(8,128)(2,1)}, u32[]{:S(2)}) copy-start(bf16[256,128]{1,0:T(8,128)(2,1)} %constant.168.clone.refs_9_) | copy-start | bytes 196612
  140.4 12.2 %copy-start.10 = (s32[16]{0:T(128)S(1)}, s32[16]{0:T(128)}, u32[]{:S(2)}) copy-start(s32[16]{0:T(128)} %fusion.21.slot_ref.refs_0_) | copy-start | bytes 196
  152.6 12.8 %copy-start.23 = (s32[1,1,4,128]{3,2,1,0:T(4,128)S(1)}, s32[1,1,4,128]{3,2,1,0:T(4,128)}, u32[]{:S(2)}) copy-start(s32[1,1,4,128]{3,2,1,0:T(4,128)} %param.39) | copy-start | bytes 6148
  157.8 1.4 copy-start
  159.2 0.7 copy-start.1
  159.8 15.3 %collective-permute-start.10 = (bf16[16,2,64,128]{3,2,1,0:T(8,128)(2,1)}, bf16[16,2,64,128]{3,2,1,0:T(8,128)(2,1)S(1)}, u32[]{:S(2)}, u32[]{:S(2)}) collective-permute-start(bf16[16,2,64,128]{3,2,1,0:T(8,128)(2,1)} %get-tuple-element.61), channel_id=1, source_target_pairs={{1,0},{2,1},{3,2},{5,4},{6,5},{7,6},{9,8},{10,9},{11,10},{13,12},{... | collective-permute-start | bytes 1572872 | tf_op jit(solution)/shard_map/ppermute | solution.py:664
  161.1 14.0 %collective-permute-start.9 = (bf16[16,2,64,128]{3,2,1,0:T(8,128)(2,1)}, bf16[16,2,64,128]{3,2,1,0:T(8,128)(2,1)S(1)}, u32[]{:S(2)}, u32[]{:S(2)}) collective-permute-start(bf16[16,2,64,128]{3,2,1,0:T(8,128)(2,1)} %get-tuple-element.60), channel_id=1, source_target_pairs={{0,1},{1,2},{2,3},{4,5},{5,6},{6,7},{8,9},{9,10},{10,11},{12,13},{... | collective-permute-start | bytes 1572872 | tf_op jit(solution)/shard_map/ppermute | solution.py:663
  175.0 13.5 %copy-start.6 = (f32[2,32,256]{2,1,0:T(8,128)S(1)}, f32[2,32,256]{2,1,0:T(8,128)}, u32[]{:S(2)}) copy-start(f32[2,32,256]{2,1,0:T(8,128)} %get-tuple-element.66.a_ref) | copy-start | bytes 196612
  175.0 13.5 %copy-start.7 = (f32[2,32,256]{2,1,0:T(8,128)S(1)}, f32[2,32,256]{2,1,0:T(8,128)}, u32[]{:S(2)}) copy-start(f32[2,32,256]{2,1,0:T(8,128)} %get-tuple-element.68.c_ref) | copy-start | bytes 196612
  175.0 13.5 %copy-start.8 = (f32[2,32,256]{2,1,0:T(8,128)S(1)}, f32[2,32,256]{2,1,0:T(8,128)}, u32[]{:S(2)}) copy-start(f32[2,32,256]{2,1,0:T(8,128)} %get-tuple-element.67.b_ref) | copy-start | bytes 196612
  175.1 13.5 %copy-start.12 = (s32[1,1,4]{2,1,0:T(1,128)S(1)}, s32[1,1,4]{2,1,0:T(1,128)}, u32[]{:S(2)}) copy-start(s32[1,1,4]{2,1,0:T(1,128)} %param.41) | copy-start | bytes 52
  175.1 20.5 %copy-start.20 = (s32[4,256]{1,0:T(4,128)S(1)}, s32[4,256]{1,0:T(4,128)}, u32[]{:S(2)}) copy-start(s32[4,256]{1,0:T(4,128)} %broadcast_select_fusion) | copy-start | bytes 12292
  175.1 41.0 %copy-start.17 = (f32[16,2,256]{2,1,0:T(2,128)S(1)}, f32[16,2,256]{2,1,0:T(2,128)}, u32[]{:S(2)}) copy-start(f32[16,2,256]{2,1,0:T(2,128)} %get-tuple-element.55) | copy-start | bytes 98308
  175.1 41.9 %copy-start.18 = (f32[16,2,256]{2,1,0:T(2,128)S(1)}, f32[16,2,256]{2,1,0:T(2,128)}, u32[]{:S(2)}) copy-start(f32[16,2,256]{2,1,0:T(2,128)} %get-tuple-element.63) | copy-start | bytes 98308
  175.1 41.9 %copy-start.19 = (f32[16,2,256]{2,1,0:T(2,128)S(1)}, f32[16,2,256]{2,1,0:T(2,128)}, u32[]{:S(2)}) copy-start(f32[16,2,256]{2,1,0:T(2,128)} %get-tuple-element.64) | copy-start | bytes 98308
  175.1 0.8 copy-start.13
  176.0 0.8 copy-start.14
  188.6 0.8 copy-start.9
  192.0 10.6 %all-to-all-start.2 = ((f32[4,128,256]{2,1,0:T(8,128)}), f32[4,128,256]{2,1,0:T(8,128)S(1)}, u32[]{:S(2)}, u32[]{:S(2)}) async-start(f32[4,128,256]{2,1,0:T(8,128)} %collect.1), calls=%async_computation.2 | async-start | bytes 1048576 | tf_op jit(solution)/shard_map/all_to_all | solution.py:749
  206.4 21.3 %all-to-all-start.3 = ((f32[32,16,256]{2,1,0:T(8,128)}), f32[32,16,256]{2,1,0:T(8,128)S(1)}, u32[]{:S(2)}, u32[]{:S(2)}) async-start(f32[32,16,256]{2,1,0:T(8,128)} %bitcast.19), calls=%async_computation.3 | async-start | bytes 1048576 | tf_op jit(solution)/shard_map/all_to_all | solution.py:683

commit v6 on v5

--- a/solution.py
+++ b/solution.py
@@ -43,9 +43,12 @@
 
 
 def row_masks():
-    y = np.arange(16)[:, None]
-    k = np.arange(256)[None, :] % 4
-    return jnp.asarray((np.abs(k - y) <= 1) & (y < 4), BF)
+    masks = np.zeros((16, 256), np.float32)
+    for y in range(4):
+        masks[y] = np.abs(np.arange(256) % 4 - y) <= 1
+    masks[8, 0:64] = 1.0
+    masks[11, 64:128] = 1.0
+    return jnp.asarray(masks, BF)
 
 
 def flips():
@@ -428,20 +431,19 @@
         if halo:
             up = joined(up_refs, g)
             down = joined(down_refs, g)
-            above = dot(edge_ref[g, 0][:, 0:64], up)
-            below = dot(edge_ref[g, 0][:, 64:128], down)
+            rhs = jnp.concatenate([rhs, up, down], axis=0)
+            sides = edge_ref[g, 0]
         else:
             up = down = None
         mean_b, inv_b = boxed_stats(stats, up, down)
         own = own_ref[g, 0]
         masked = jnp.concatenate([own * mask_ref[y : y + 1, :] for y in ys], axis=0)
+        if halo:
+            sides = jnp.concatenate([sides * mask_ref[8 + y : 9 + y, 0:128] for y in ys], axis=0)
+            masked = jnp.concatenate([masked, sides], axis=1)
         product = dot(masked, rhs)
         for i, y in enumerate(ys):
             p = product[WIN * i : WIN * i + WIN]
-            if y == 0:
-                p = p + above
-            if y == 3:
-                p = p + below
             z = jnp.where(
                 wrapped, p[16:80, 128:], jnp.where(first, p[80:144, :128], p[16:80, :128])
             )
@@ -481,21 +483,31 @@
     turned = pltpu.roll(both, 64, 1)
     left = lax.broadcasted_iota(jnp.int32, (1, 128), 1) < 64
     cell_iota = lax.broadcasted_iota(jnp.int32, (128, 128), 0)
+    blank = jnp.zeros((4, 128), F32)
     for g in range(group):
-        for i, y in enumerate(ys):
-            at = (count * g + i) // 2 * 4
-            lo, hi = (both, turned) if i % 2 == 0 else (turned, both)
-            mean_ref[g, i : i + 1, :] = jnp.where(left, lo[at : at + 1], hi[at + 1 : at + 2])
-            c = jnp.where(left, lo[at + 2 : at + 3], hi[at + 3 : at + 4])
-            values = jnp.concatenate([c * elev_ref[g, y : y + 1, :], c], axis=0)
-            value_hi = values.astype(BF).astype(F32)
-            values = jnp.concatenate([value_hi, values - value_hi, jnp.zeros((4, 128), F32)], axis=0)
-            hot = jnp.where(cell_iota == cell_ref[g, y : y + 1, :], 1.0, 0.0).astype(BF)
-            binned = dot_nt(values.astype(BF), hot)
-            got = binned[0:2] + binned[2:4]
-            at = count * g + i
-            rows_ref[0, at : at + 1, 0:128] = got[0:1]
-            rows_ref[0, at : at + 1, 128:256] = got[1:2]
+        for i in range(0, count, 2):
+            lines = []
+            hots = []
+            for j, y in enumerate(ys[i : i + 2]):
+                at = (count * g + i) // 2 * 4
+                lo, hi = (both, turned) if j == 0 else (turned, both)
+                mean = jnp.where(left, lo[at : at + 1], hi[at + 1 : at + 2])
+                mean_ref[g, i + j : i + j + 1, :] = mean
+                c = jnp.where(left, lo[at + 2 : at + 3], hi[at + 3 : at + 4])
+                values = jnp.concatenate([c * elev_ref[g, y : y + 1, :], c], axis=0)
+                value_hi = values.astype(BF).astype(F32)
+                line = jnp.concatenate([value_hi, values - value_hi], axis=0)
+                lines.append(jnp.concatenate([line, blank] if j == 0 else [blank, line], axis=1))
+                hot = jnp.where(cell_iota == cell_ref[g, y : y + 1, :], 1.0, 0.0)
+                hots.append(hot.astype(BF))
+            binned = dot_nt(
+                jnp.concatenate(lines, axis=0).astype(BF), jnp.concatenate(hots, axis=1)
+            )
+            for j in range(2):
+                got = binned[4 * j : 4 * j + 2] + binned[4 * j + 2 : 4 * j + 4]
+                at = count * g + i + j
+                rows_ref[0, at : at + 1, 0:128] = got[0:1]
+                rows_ref[0, at : at + 1, 128:256] = got[1:2]
 
 
 def sweep_steps(

time: 230 us -> 229 us (level)
  Pallas kernels: 102 us -> 98.1 us
  transfers between devices with their start and end apart: 15 -> 15, of which waited for: 6 -> 7; matrix products, arithmetic and copies ran while one was open for 6% -> 6% of each run, Pallas kernels for 31% -> 31%
where the time goes in v6:
time: 229 us; the launch traced here: 227 us
  Pallas kernels  98.1 us (43%)
  starting transfers between devices  66.1 us (29%)
  waiting for transfers between devices  42 us (18%)
  local copies, waits for them, and re-layouts  14.9 us (7%)
  other arithmetic  5.15 us (2%)
    pallas_call x4, Pallas kernels, sweep_steps(): pl.pallas_call(functools.partial(sweep_kernel, group, ys, halo, late), gr...  41.2 us
    all_to_all x3, starting transfers between devices, exchange(): return lax.all_to_all(a, 'img', split_axis=0, concat_axis=0, tiled=True)  34.6 us
    all_to_all x3, waiting for transfers between devices, exchange(): return lax.all_to_all(a, 'img', split_axis=0, concat_axis=0, tiled=True)  19.4 us
    ppermute x4, starting transfers between devices, neighbour_rows(): above = lax.ppermute(tail, 'tile', [(i, i + 1) for i in range(count - 1)])  16.4 us
    pallas_call x1, Pallas kernels, prepare(): pl.pallas_call(prepare_kernel, grid=(images,), in_specs=[pl.BlockSpec((1,...  15.5 us
    pallas_call x2, Pallas kernels, pick(): pl.pallas_call(kernel, grid_spec=pltpu.PrefetchScalarGridSpec(num_scalar_...  12.5 us
    pallas_call x2, Pallas kernels, edges(): pl.pallas_call(edge_kernel, grid_spec=pltpu.PrefetchScalarGridSpec(num_sc...  11.3 us
    ppermute x4, waiting for transfers between devices, neighbour_rows(): below = lax.ppermute(head, 'tile', [(i + 1, i) for i in range(count - 1)])  10.4 us
  transfers between devices with their start and end apart: 15, of which 7 were waited for; matrix products, arithmetic and copies ran while one was open for 6% of the time, Pallas kernels for 31%

profile of v6, /device:TPU:1, one launch (start us, length us, event | category | flops | bytes accessed | tf_op | source)
XLA Modules:
  0.0 227.5 jit_solution(8701739224964926091)
XLA Ops:
  0.6 0.8 reshape.86
  1.4 0.7 add_select_fusion.1
  2.0 6.3 %pick.3 = bf16[32,3,64,4,128]{4,3,2,1,0:T(4,128)(2,1)} custom-call(s32[32]{0:T(128)} %get-tuple-element.73.idx_ref, bf16[16,64,4,768]{3,2,1,0:T(4,128)(2,1)} %features_ref.3), custom_call_target="tpu_custom_call" | custom-call | bytes 12582912 | tf_op jit(solution)/shard_map/pick/pallas_call | solution.py:128
  8.3 8.6 %all-to-all-start.1 = ((bf16[32,3,256,128]{3,2,1,0:T(8,128)(2,1)}), bf16[32,3,256,128]{3,2,1,0:T(8,128)(2,1)}, u32[]{:S(2)}, u32[]{:S(2)}) async-start(bf16[32,3,256,128]{3,2,1,0:T(8,128)(2,1)} %bitcast.74), calls=%async_computation.1 | async-start | bytes 12582912 | tf_op jit(solution)/shard_map/all_to_all | solution.py:695
  17.2 1.7 collective-permute-start.4
  18.9 3.3 %collective-permute-start.5 = (s32[1,256]{1,0:T(1,128)S(1)}, s32[1,256]{1,0:T(1,128)S(1)}, u32[]{:S(2)}, u32[]{:S(2)}) collective-permute-start(s32[1,256]{1,0:T(1,128)S(1)} %get-tuple-element.76), channel_id=1, source_target_pairs={{0,2},{1,3},{2,0},{3,1},{4,6},{5,7},{6,4},{7,5},{8,10},{9,11},{10,... | collective-permute-start | bytes 3080 | tf_op jit(solution)/shard_map/ppermute | solution.py:725
  22.2 0.7 collective-permute-start.6
  22.9 0.5 iota.15.idx_ref
  23.4 6.3 %pick.2 = bf16[16,5,64,4,128]{4,3,2,1,0:T(4,128)(2,1)} custom-call(s32[16]{0:T(128)} %iota.15.idx_ref, bf16[16,64,4,768]{3,2,1,0:T(4,128)(2,1)} %features_ref.3), custom_call_target="tpu_custom_call" | custom-call | bytes 10485760 | tf_op jit(solution)/shard_map/pick/pallas_call | solution.py:128
  29.7 0.5 iota.16.slot_ref
  30.2 6.3 %edges.2 = (bf16[16,5,64,128]{3,2,1,0:T(8,128)(2,1)}, bf16[16,5,64,128]{3,2,1,0:T(8,128)(2,1)}, f32[16,5,8,128]{3,2,1,0:T(8,128)}) custom-call(s32[16]{0:T(128)} %iota.16.slot_ref, bf16[16,5,256,128]{3,2,1,0:T(8,128)(2,1)} %bitcast.49, bf16[16,5,256,128]{3,2,1,0:T(8,128)(2,1)} %bitcast.50, bf16[16,5,256,128]{3,2,1,0:T(8,128)(2,1)} %bitcast.51, ...), custom_call_target="tpu_custom_call" | custom-call | flops 1600000000 | bytes 8000000 | tf_op jit(solution)/shard_map/edges/pallas_call | solution.py:277
  36.6 1.4 slice.30
  37.9 3.6 %collective-permute-start = (bf16[16,4,64,128]{3,2,1,0:T(8,128)(2,1)S(1)}, bf16[16,4,64,128]{3,2,1,0:T(8,128)(2,1)}, u32[]{:S(2)}, u32[]{:S(2)}) collective-permute-start(bf16[16,4,64,128]{3,2,1,0:T(8,128)(2,1)S(1)} %slice.30), channel_id=1, source_target_pairs={{0,1},{1,2},{2,3},{4,5},{5,6},{6,7},{8,9},{9,10},{10,11},{12,13},{... | collective-permute-start | bytes 3145736 | tf_op jit(solution)/shard_map/ppermute | solution.py:675
  41.5 1.3 slice.32
  42.9 1.3 collective-permute-start.2
  44.4 1.0 select_reduce_fusion
  45.4 0.6 pad_maximum_fusion.1.refs_37_.refs_8_
  46.0 0.8 fusion.refs_39_.refs_10_
  46.8 1.1 slice_bitcast_fusion
  47.9 0.2 copy.38
  48.1 0.1 reshape.88
  48.2 0.2 copy.40
  48.4 7.3 %pack.1 = bf16[32,392,128]{2,1,0:T(8,128)(2,1)} custom-call(s32[32]{0:T(128)} %get-tuple-element.73.idx_ref, bf16[16,5,256,128]{3,2,1,0:T(8,128)(2,1)} %bitcast.61, bf16[16,5,256,128]{3,2,1,0:T(8,128)(2,1)} %bitcast.58, bf16[16,5,256,128]{3,2,1,0:T(8,128)(2,1)} %bitcast.59, bf16[16,5,256,128]{3,2,1,0:T(8,128)(2,1)} %bitcast.60, ...), custom_call_target="tpu_custom_call" | custom-call | tf_op jit(solution)/shard_map/pack/pallas_call | solution.py:185
  55.7 4.0 %collective-permute-start.1 = (bf16[16,128]{1,0:T(8,128)(2,1)S(1)}, bf16[16,128]{1,0:T(8,128)(2,1)S(1)}, u32[]{:S(2)}, u32[]{:S(2)}) collective-permute-start(bf16[16,128]{1,0:T(8,128)(2,1)S(1)} %reshape.88), channel_id=1, source_target_pairs={{0,1},{1,2},{2,3},{4,5},{5,6},{6,7},{8,9},{9,10},{10,11},{12,13},{... | collective-permute-start | bytes 12296 | tf_op jit(solution)/shard_map/ppermute | solution.py:675
  59.7 1.3 collective-permute-start.3
  61.0 0.6 gather_fusion
  61.6 0.7 broadcast_select_fusion
  62.4 0.2 copy.39
  62.6 5.6 %collective-permute-done.3 = bf16[16,128]{1,0:T(8,128)(2,1)S(1)} collective-permute-done((bf16[16,128]{1,0:T(8,128)(2,1)S(1)}, bf16[16,128]{1,0:T(8,128)(2,1)S(1)}, u32[]{:S(2)}, u32[]{:S(2)}) %collective-permute-start.3) | collective-permute-done | bytes 4128 | tf_op jit(solution)/shard_map/ppermute | solution.py:676
  68.3 0.2 copy.41
  68.5 0.8 pad.13.up_last_ref
  69.3 0.8 pad.14.down_last_ref
  70.1 15.5 %prepare.1 = (bf16[16,4,144,256]{3,2,1,0:T(8,128)(2,1)}, bf16[16,4,144,128]{3,2,1,0:T(8,128)(2,1)}, bf16[16,4,64,128]{3,2,1,0:T(8,128)(2,1)}) custom-call(bf16[16,5,256,128]{3,2,1,0:T(8,128)(2,1)} %bitcast.73, bf16[16,4,64,128]{3,2,1,0:T(8,128)(2,1)} %collective-permute-done.up_ref, bf16[16,64,128]{2,1,0:T(8,128)(2,1)} %pad.13.up_last_ref, ...), custom_call_target="tpu_custom_call" | custom-call | flops 2560000000 | bytes 16000000 | tf_op jit(solution)/shard_map/prepare/pallas_call | solution.py:351
  85.5 9.4 %all-to-all-done.1.refs_0_.refs_1_.refs_2_.refs_3_.refs_4_.refs_5_.refs_6_.refs_7_.refs_8_.refs_9_.refs_10_.refs_11_.refs_12_.refs_13_.refs_14_.refs_15_.refs_16_.refs_17_.refs_18_.refs_19_.refs_20_.refs_21_.refs_22_.refs_23_.refs_24_.refs_25_.refs_26_.refs_27_.refs_28_.refs_29_.refs_30_.refs_31_.refs_32_ = bf16[32,3,256,128]{3,2,1,0:T(8,128)(2,1)} async-done(((bf16[32,3,256,128]{3,2,1,0:T(8,128)(2,1)}), ...) | async-done | bytes 6291488 | tf_op jit(solution)/shard_map/all_to_all | solution.py:695
  95.0 14.5 %all-to-all-start = ((bf16[32,392,128]{2,1,0:T(8,128)(2,1)}), bf16[32,392,128]{2,1,0:T(8,128)(2,1)S(1)}, u32[]{:S(2)}, u32[]{:S(2)}) async-start(bf16[32,392,128]{2,1,0:T(8,128)(2,1)} %pack.1), calls=%async_computation | async-start | bytes 6422528 | tf_op jit(solution)/shard_map/all_to_all | solution.py:695
  109.5 0.6 fusion.21.slot_ref.refs_0_
  110.1 5.0 %edges.3 = (bf16[16,3,64,128]{3,2,1,0:T(8,128)(2,1)}, bf16[16,3,64,128]{3,2,1,0:T(8,128)(2,1)}, f32[16,3,8,128]{3,2,1,0:T(8,128)}, bf16[16,1,256,128]{3,2,1,0:T(8,128)(2,1)}) custom-call(s32[16]{0:T(128)} %fusion.21.slot_ref.refs_0_, ...), custom_call_target="tpu_custom_call" | custom-call | flops 960000000 | bytes 4800000 | tf_op jit(solution)/shard_map/edges/pallas_call | solution.py:277
  115.1 4.5 %collective-permute-start.7 = (bf16[16,3,64,128]{3,2,1,0:T(8,128)(2,1)}, bf16[16,3,64,128]{3,2,1,0:T(8,128)(2,1)}, u32[]{:S(2)}, u32[]{:S(2)}) collective-permute-start(bf16[16,3,64,128]{3,2,1,0:T(8,128)(2,1)} %get-tuple-element.48), channel_id=1, source_target_pairs={{0,1},{1,2},{2,3},{4,5},{5,6},{6,7},{8,9},{9,10},{10,11},{12,13},{... | collective-permute-start | bytes 2359304 | tf_op jit(solution)/shard_map/ppermute | solution.py:675
  119.6 1.5 collective-permute-start.8
  121.1 9.5 %sweep.4 = (f32[16,2,256]{2,1,0:T(2,128)}, f32[2,32,256]{2,1,0:T(8,128)}) custom-call(s32[16]{0:T(128)} %fusion.21.slot_ref.refs_0_, ...), custom_call_target="tpu_custom_call" | custom-call | flops 3200000000 | bytes 6400000 | tf_op jit(solution)/shard_map/sweep/pallas_call | solution.py:571
  130.6 5.1 %collective-permute-done.7.refs_43_.refs_44_.refs_15_ = bf16[16,3,64,128]{3,2,1,0:T(8,128)(2,1)} collective-permute-done((bf16[16,3,64,128]{3,2,1,0:T(8,128)(2,1)}, bf16[16,3,64,128]{3,2,1,0:T(8,128)(2,1)}, u32[]{:S(2)}, u32[]{:S(2)}) %collective-permute-start.7) | collective-permute-done | bytes 786464 | tf_op jit(solution)/shard_map/ppermute | solution.py:675
  135.6 4.7 %collective-permute-done.8.refs_45_.refs_46_.refs_18_ = bf16[16,3,64,128]{3,2,1,0:T(8,128)(2,1)} collective-permute-done((bf16[16,3,64,128]{3,2,1,0:T(8,128)(2,1)}, bf16[16,3,64,128]{3,2,1,0:T(8,128)(2,1)}, u32[]{:S(2)}, u32[]{:S(2)}) %collective-permute-start.8) | collective-permute-done | bytes 786464 | tf_op jit(solution)/shard_map/ppermute | solution.py:676
  140.4 11.6 %sweep.5 = (f32[16,2,256]{2,1,0:T(2,128)}, f32[2,32,256]{2,1,0:T(8,128)}) custom-call(s32[16]{0:T(128)} %fusion.21.slot_ref.refs_0_, ...), custom_call_target="tpu_custom_call" | custom-call | flops 3200000000 | bytes 6400000 | tf_op jit(solution)/shard_map/sweep/pallas_call | solution.py:571
  152.1 5.2 %unpack.1 = (bf16[16,2,64,128]{3,2,1,0:T(8,128)(2,1)}, bf16[16,2,64,128]{3,2,1,0:T(8,128)(2,1)}, f32[16,2,8,128]{3,2,1,0:T(8,128)S(1)}, bf16[16,2,256,128]{3,2,1,0:T(8,128)(2,1)S(1)}) custom-call(s32[16]{0:T(128)S(1)} %copy-done.10, bf16[32,392,128]{2,1,0:T(8,128)(2,1)S(1)} %all-to-all-done.refs_0_.refs_1_.refs_2_.refs_3_.refs_4_.refs_5_.refs_6_.refs_7_, ...), custom_call_target="tpu_custom_call" | custom-call | tf_op jit(solution)/shard_map/unpack/pallas_call | solution.py:305
  157.3 1.3 copy-done
  158.7 0.7 copy-done.1
  159.3 1.3 collective-permute-start.10
  160.6 4.2 %collective-permute-start.9 = (bf16[16,2,64,128]{3,2,1,0:T(8,128)(2,1)}, bf16[16,2,64,128]{3,2,1,0:T(8,128)(2,1)S(1)}, u32[]{:S(2)}, u32[]{:S(2)}) collective-permute-start(bf16[16,2,64,128]{3,2,1,0:T(8,128)(2,1)} %get-tuple-element.60), channel_id=1, source_target_pairs={{0,1},{1,2},{2,3},{4,5},{5,6},{6,7},{8,9},{9,10},{10,11},{12,13},{... | collective-permute-start | bytes 1572872 | tf_op jit(solution)/shard_map/ppermute | solution.py:675
  164.9 9.2 %sweep.7 = (f32[16,2,256]{2,1,0:T(2,128)}, f32[2,32,256]{2,1,0:T(8,128)}) custom-call(s32[16]{0:T(128)} %fusion.21.slot_ref.refs_0_, bf16[16,1,256,128]{3,2,1,0:T(8,128)(2,1)} %get-tuple-element.56.refs_1_, bf16[16,2,256,128]{3,2,1,0:T(8,128)(2,1)} %copy-done, bf16[16,2,256,128]{3,2,1,0:T(8,128)(2,1)} %copy-done, ...), custom_call_target="tpu_custom_call" | custom-call | flops 3200000000 | bytes 6400000 | tf_op jit(solution)/shard_map/sweep/pallas_call | solution.py:571
  174.2 0.3 collective-permute-done.9.refs_16_.refs_17_
  174.5 0.5 copy-done.13
  175.0 0.8 copy-done.14
  175.8 11.0 %sweep.6 = (f32[16,2,256]{2,1,0:T(2,128)}, f32[2,32,256]{2,1,0:T(8,128)}) custom-call(s32[16]{0:T(128)} %fusion.21.slot_ref.refs_0_, bf16[16,1,256,128]{3,2,1,0:T(8,128)(2,1)} %get-tuple-element.56.refs_1_, bf16[16,2,256,128]{3,2,1,0:T(8,128)(2,1)} %copy-done, bf16[16,2,256,128]{3,2,1,0:T(8,128)(2,1)} %copy-done, ...), custom_call_target="tpu_custom_call" | custom-call | flops 3200000000 | bytes 6400000 | tf_op jit(solution)/shard_map/sweep/pallas_call | solution.py:571
  186.8 0.8 copy-done.9
  187.7 2.6 %collect.1 = f32[4,128,256]{2,1,0:T(8,128)} custom-call(s32[4,128]{1,0:T(4,128)S(1)} %fusion.8.list_ref, s32[4]{0:T(128)S(1)} %bitcast.48, f32[2,32,256]{2,1,0:T(8,128)S(1)} %copy-done.6, f32[2,32,256]{2,1,0:T(8,128)S(1)} %copy-done.8, f32[2,32,256]{2,1,0:T(8,128)S(1)} %copy-done.7, f32[2,32,256]{2,1,0:T(8,128)S(1)} %copy-done.9), custom_call_target="tpu_custom_call" | custom-call | tf_op jit(solution)/shard_map/collect/pallas_call | solution.py:627
  190.3 4.1 %all-to-all-start.2 = ((f32[4,128,256]{2,1,0:T(8,128)}), f32[4,128,256]{2,1,0:T(8,128)S(1)}, u32[]{:S(2)}, u32[]{:S(2)}) async-start(f32[4,128,256]{2,1,0:T(8,128)} %collect.1), calls=%async_computation.2 | async-start | bytes 1048576 | tf_op jit(solution)/shard_map/all_to_all | solution.py:761
  194.4 0.1 slice_reduce_fusion.count_ref
  194.5 6.8 %all-to-all-done.2.got_ref = f32[4,128,256]{2,1,0:T(8,128)S(1)} async-done(((f32[4,128,256]{2,1,0:T(8,128)}), f32[4,128,256]{2,1,0:T(8,128)S(1)}, u32[]{:S(2)}, u32[]{:S(2)}) %all-to-all-start.2) | async-done | bytes 524320 | tf_op jit(solution)/shard_map/all_to_all | solution.py:761
  201.3 2.4 %place.1 = f32[512,256]{1,0:T(8,128)} custom-call(s32[4,128]{1,0:T(4,128)S(1)} %slice.36.slot_ref, s32[4]{0:T(128)S(1)} %slice_reduce_fusion.count_ref, f32[4,128,256]{2,1,0:T(8,128)S(1)} %all-to-all-done.2.got_ref), custom_call_target="tpu_custom_call" | custom-call | tf_op jit(solution)/shard_map/place/pallas_call | solution.py:659
  203.7 11.4 %all-to-all-start.3 = ((f32[32,16,256]{2,1,0:T(8,128)}), f32[32,16,256]{2,1,0:T(8,128)S(1)}, u32[]{:S(2)}, u32[]{:S(2)}) async-start(f32[32,16,256]{2,1,0:T(8,128)} %bitcast.19), calls=%async_computation.3 | async-start | bytes 1048576 | tf_op jit(solution)/shard_map/all_to_all | solution.py:695
  215.2 0.8 constant_dynamic-update-slice_fusion
  216.1 0.7 pad_maximum_fusion
  216.8 10.0 %all-to-all-done.3 = f32[32,16,256]{2,1,0:T(8,128)S(1)} async-done(((f32[32,16,256]{2,1,0:T(8,128)}), f32[32,16,256]{2,1,0:T(8,128)S(1)}, u32[]{:S(2)}, u32[]{:S(2)}) %all-to-all-start.3) | async-done | bytes 524320 | tf_op jit(solution)/shard_map/all_to_all | solution.py:695
  226.9 0.6 fusion.5
  (76 shorter events, 0.9 us)
Async XLA Ops:
  8.3 8.7 %copy-start.11 = (s32[1,1,4]{2,1,0:T(1,128)S(1)}, s32[1,1,4]{2,1,0:T(1,128)}, u32[]{:S(2)}) copy-start(s32[1,1,4]{2,1,0:T(1,128)} %param.41) | copy-start | bytes 52
  8.3 8.8 %copy-start.22 = (s32[1,1,4,128]{3,2,1,0:T(4,128)S(1)}, s32[1,1,4,128]{3,2,1,0:T(4,128)}, u32[]{:S(2)}) copy-start(s32[1,1,4,128]{3,2,1,0:T(4,128)} %param.40) | copy-start | bytes 6148
  8.3 86.6 %all-to-all-start.1 = ((bf16[32,3,256,128]{3,2,1,0:T(8,128)(2,1)}), bf16[32,3,256,128]{3,2,1,0:T(8,128)(2,1)}, u32[]{:S(2)}, u32[]{:S(2)}) async-start(bf16[32,3,256,128]{3,2,1,0:T(8,128)(2,1)} %bitcast.74), calls=%async_computation.1 | async-start | bytes 12582912 | tf_op jit(solution)/shard_map/all_to_all | solution.py:695
  17.2 38.6 %collective-permute-start.4 = (s32[1,256]{1,0:T(1,128)S(1)}, s32[1,256]{1,0:T(1,128)S(1)}, u32[]{:S(2)}, u32[]{:S(2)}) collective-permute-start(s32[1,256]{1,0:T(1,128)S(1)} %get-tuple-element.75), channel_id=1, source_target_pairs={{0,1},{1,2},{2,3},{3,0},{4,5},{5,6},{6,7},{7,4},{8,9},{9,10},{10,1... | collective-permute-start | bytes 3080 | tf_op jit(solution)/shard_map/ppermute | solution.py:725
  18.9 40.8 %collective-permute-start.5 = (s32[1,256]{1,0:T(1,128)S(1)}, s32[1,256]{1,0:T(1,128)S(1)}, u32[]{:S(2)}, u32[]{:S(2)}) collective-permute-start(s32[1,256]{1,0:T(1,128)S(1)} %get-tuple-element.76), channel_id=1, source_target_pairs={{0,2},{1,3},{2,0},{3,1},{4,6},{5,7},{6,4},{7,5},{8,10},{9,11},{10,... | collective-permute-start | bytes 3080 | tf_op jit(solution)/shard_map/ppermute | solution.py:725
  22.2 38.9 %collective-permute-start.6 = (s32[1,256]{1,0:T(1,128)S(1)}, s32[1,256]{1,0:T(1,128)S(1)}, u32[]{:S(2)}, u32[]{:S(2)}) collective-permute-start(s32[1,256]{1,0:T(1,128)S(1)} %get-tuple-element.77), channel_id=1, source_target_pairs={{0,3},{1,0},{2,1},{3,2},{4,7},{5,4},{6,5},{7,6},{8,11},{9,8},{10,9... | collective-permute-start | bytes 3080 | tf_op jit(solution)/shard_map/ppermute | solution.py:725
  30.2 14.0 %copy-start.16 = (s32[16,4,512]{2,1,0:T(4,128)S(1)}, s32[16,4,512]{2,1,0:T(4,128)}, u32[]{:S(2)}) copy-start(s32[16,4,512]{2,1,0:T(4,128)} %index_ref.1) | copy-start | bytes 393220
  30.2 14.1 %copy-start.21 = (f32[64]{0:T(128)S(1)}, f32[64]{0:T(128)}, u32[]{:S(2)}) copy-start(f32[64]{0:T(128)} %param.34) | copy-start | bytes 772
  36.5 8.9 %copy-start.25 = (bf16[1,128]{1,0:T(2,128)(2,1)S(1)}, bf16[1,128]{1,0:T(2,128)(2,1)}, u32[]{:S(2)}) copy-start(bf16[1,128]{1,0:T(2,128)(2,1)} %constant.271) | copy-start | bytes 772
  36.5 8.9 %copy-start.26 = (bf16[1,128]{1,0:T(2,128)(2,1)S(1)}, bf16[1,128]{1,0:T(2,128)(2,1)}, u32[]{:S(2)}) copy-start(bf16[1,128]{1,0:T(2,128)(2,1)} %constant.272) | copy-start | bytes 772
  36.5 9.5 %copy-start.15 = (f32[16,4,512]{2,1,0:T(4,128)S(1)}, f32[16,4,512]{2,1,0:T(4,128)}, u32[]{:S(2)}) copy-start(f32[16,4,512]{2,1,0:T(4,128)} %param.36) | copy-start | bytes 393220
  36.5 9.5 %copy-start.24 = (f32[16]{0:T(128)S(1)}, f32[16]{0:T(128)}, u32[]{:S(2)}) copy-start(f32[16]{0:T(128)} %param.35) | copy-start | bytes 196
  37.9 32.1 %collective-permute-start = (bf16[16,4,64,128]{3,2,1,0:T(8,128)(2,1)S(1)}, bf16[16,4,64,128]{3,2,1,0:T(8,128)(2,1)}, u32[]{:S(2)}, u32[]{:S(2)}) collective-permute-start(bf16[16,4,64,128]{3,2,1,0:T(8,128)(2,1)S(1)} %slice.30), channel_id=1, source_target_pairs={{0,1},{1,2},{2,3},{4,5},{5,6},{6,7},{8,9},{9,10},{10,11},{12,13},{... | collective-permute-start | bytes 3145736 | tf_op jit(solution)/shard_map/ppermute | solution.py:675
  42.9 27.2 %collective-permute-start.2 = (bf16[16,4,64,128]{3,2,1,0:T(8,128)(2,1)S(1)}, bf16[16,4,64,128]{3,2,1,0:T(8,128)(2,1)}, u32[]{:S(2)}, u32[]{:S(2)}) collective-permute-start(bf16[16,4,64,128]{3,2,1,0:T(8,128)(2,1)S(1)} %slice.32), channel_id=1, source_target_pairs={{1,0},{2,1},{3,2},{5,4},{6,5},{7,6},{9,8},{10,9},{11,10},{13,12},{... | collective-permute-start | bytes 3145736 | tf_op jit(solution)/shard_map/ppermute | solution.py:676
  55.7 6.6 %collective-permute-start.1 = (bf16[16,128]{1,0:T(8,128)(2,1)S(1)}, bf16[16,128]{1,0:T(8,128)(2,1)S(1)}, u32[]{:S(2)}, u32[]{:S(2)}) collective-permute-start(bf16[16,128]{1,0:T(8,128)(2,1)S(1)} %reshape.88), channel_id=1, source_target_pairs={{0,1},{1,2},{2,3},{4,5},{5,6},{6,7},{8,9},{9,10},{10,11},{12,13},{... | collective-permute-start | bytes 12296 | tf_op jit(solution)/shard_map/ppermute | solution.py:675
  59.7 8.5 %collective-permute-start.3 = (bf16[16,128]{1,0:T(8,128)(2,1)S(1)}, bf16[16,128]{1,0:T(8,128)(2,1)S(1)}, u32[]{:S(2)}, u32[]{:S(2)}) collective-permute-start(bf16[16,128]{1,0:T(8,128)(2,1)S(1)} %reshape.90), channel_id=1, source_target_pairs={{1,0},{2,1},{3,2},{5,4},{6,5},{7,6},{9,8},{10,9},{11,10},{13,12},{... | collective-permute-start | bytes 12296 | tf_op jit(solution)/shard_map/ppermute | solution.py:676
  95.0 57.1 %all-to-all-start = ((bf16[32,392,128]{2,1,0:T(8,128)(2,1)}), bf16[32,392,128]{2,1,0:T(8,128)(2,1)S(1)}, u32[]{:S(2)}, u32[]{:S(2)}) async-start(bf16[32,392,128]{2,1,0:T(8,128)(2,1)} %pack.1), calls=%async_computation | async-start | bytes 6422528 | tf_op jit(solution)/shard_map/all_to_all | solution.py:695
  115.1 20.6 %collective-permute-start.7 = (bf16[16,3,64,128]{3,2,1,0:T(8,128)(2,1)}, bf16[16,3,64,128]{3,2,1,0:T(8,128)(2,1)}, u32[]{:S(2)}, u32[]{:S(2)}) collective-permute-start(bf16[16,3,64,128]{3,2,1,0:T(8,128)(2,1)} %get-tuple-element.48), channel_id=1, source_target_pairs={{0,1},{1,2},{2,3},{4,5},{5,6},{6,7},{8,9},{9,10},{10,11},{12,13},{... | collective-permute-start | bytes 2359304 | tf_op jit(solution)/shard_map/ppermute | solution.py:675
  119.6 20.8 %collective-permute-start.8 = (bf16[16,3,64,128]{3,2,1,0:T(8,128)(2,1)}, bf16[16,3,64,128]{3,2,1,0:T(8,128)(2,1)}, u32[]{:S(2)}, u32[]{:S(2)}) collective-permute-start(bf16[16,3,64,128]{3,2,1,0:T(8,128)(2,1)} %get-tuple-element.49), channel_id=1, source_target_pairs={{1,0},{2,1},{3,2},{5,4},{6,5},{7,6},{9,8},{10,9},{11,10},{13,12},{... | collective-permute-start | bytes 2359304 | tf_op jit(solution)/shard_map/ppermute | solution.py:676
  140.4 11.7 %copy-start.2 = (bf16[128,256]{1,0:T(8,128)(2,1)S(1)}, bf16[128,256]{1,0:T(8,128)(2,1)}, u32[]{:S(2)}) copy-start(bf16[128,256]{1,0:T(8,128)(2,1)} %constant.160.clone.refs_8_.refs_11_) | copy-start | bytes 196612
  140.4 11.7 %copy-start.3 = (bf16[128,256]{1,0:T(8,128)(2,1)S(1)}, bf16[128,256]{1,0:T(8,128)(2,1)}, u32[]{:S(2)}) copy-start(bf16[128,256]{1,0:T(8,128)(2,1)} %constant.163.clone.refs_16_.refs_8_) | copy-start | bytes 196612
  140.4 11.7 %copy-start.4 = (bf16[256,256]{1,0:T(8,128)(2,1)S(1)}, bf16[256,256]{1,0:T(8,128)(2,1)}, u32[]{:S(2)}) copy-start(bf16[256,256]{1,0:T(8,128)(2,1)} %constant.169.clone.refs_10_) | copy-start | bytes 393220
  140.4 11.7 %copy-start.5 = (bf16[256,128]{1,0:T(8,128)(2,1)S(1)}, bf16[256,128]{1,0:T(8,128)(2,1)}, u32[]{:S(2)}) copy-start(bf16[256,128]{1,0:T(8,128)(2,1)} %constant.168.clone.refs_9_) | copy-start | bytes 196612
  140.4 11.7 %copy-start.10 = (s32[16]{0:T(128)S(1)}, s32[16]{0:T(128)}, u32[]{:S(2)}) copy-start(s32[16]{0:T(128)} %fusion.21.slot_ref.refs_0_) | copy-start | bytes 196
  152.1 12.8 %copy-start.23 = (s32[1,1,4,128]{3,2,1,0:T(4,128)S(1)}, s32[1,1,4,128]{3,2,1,0:T(4,128)}, u32[]{:S(2)}) copy-start(s32[1,1,4,128]{3,2,1,0:T(4,128)} %param.39) | copy-start | bytes 6148
  157.3 1.4 copy-start
  158.7 0.7 copy-start.1
  159.3 14.8 %collective-permute-start.10 = (bf16[16,2,64,128]{3,2,1,0:T(8,128)(2,1)}, bf16[16,2,64,128]{3,2,1,0:T(8,128)(2,1)S(1)}, u32[]{:S(2)}, u32[]{:S(2)}) collective-permute-start(bf16[16,2,64,128]{3,2,1,0:T(8,128)(2,1)} %get-tuple-element.61), channel_id=1, source_target_pairs={{1,0},{2,1},{3,2},{5,4},{6,5},{7,6},{9,8},{10,9},{11,10},{13,12},{... | collective-permute-start | bytes 1572872 | tf_op jit(solution)/shard_map/ppermute | solution.py:676
  160.6 13.9 %collective-permute-start.9 = (bf16[16,2,64,128]{3,2,1,0:T(8,128)(2,1)}, bf16[16,2,64,128]{3,2,1,0:T(8,128)(2,1)S(1)}, u32[]{:S(2)}, u32[]{:S(2)}) collective-permute-start(bf16[16,2,64,128]{3,2,1,0:T(8,128)(2,1)} %get-tuple-element.60), channel_id=1, source_target_pairs={{0,1},{1,2},{2,3},{4,5},{5,6},{6,7},{8,9},{9,10},{10,11},{12,13},{... | collective-permute-start | bytes 1572872 | tf_op jit(solution)/shard_map/ppermute | solution.py:675
  174.1 12.7 %copy-start.6 = (f32[2,32,256]{2,1,0:T(8,128)S(1)}, f32[2,32,256]{2,1,0:T(8,128)}, u32[]{:S(2)}) copy-start(f32[2,32,256]{2,1,0:T(8,128)} %get-tuple-element.66.a_ref) | copy-start | bytes 196612
  174.1 12.7 %copy-start.7 = (f32[2,32,256]{2,1,0:T(8,128)S(1)}, f32[2,32,256]{2,1,0:T(8,128)}, u32[]{:S(2)}) copy-start(f32[2,32,256]{2,1,0:T(8,128)} %get-tuple-element.68.c_ref) | copy-start | bytes 196612
  174.1 12.7 %copy-start.8 = (f32[2,32,256]{2,1,0:T(8,128)S(1)}, f32[2,32,256]{2,1,0:T(8,128)}, u32[]{:S(2)}) copy-start(f32[2,32,256]{2,1,0:T(8,128)} %get-tuple-element.67.b_ref) | copy-start | bytes 196612
  174.1 12.7 %copy-start.12 = (s32[1,1,4]{2,1,0:T(1,128)S(1)}, s32[1,1,4]{2,1,0:T(1,128)}, u32[]{:S(2)}) copy-start(s32[1,1,4]{2,1,0:T(1,128)} %param.41) | copy-start | bytes 52
  174.1 20.3 %copy-start.20 = (s32[4,256]{1,0:T(4,128)S(1)}, s32[4,256]{1,0:T(4,128)}, u32[]{:S(2)}) copy-start(s32[4,256]{1,0:T(4,128)} %broadcast_select_fusion) | copy-start | bytes 12292
  174.1 41.1 %copy-start.17 = (f32[16,2,256]{2,1,0:T(2,128)S(1)}, f32[16,2,256]{2,1,0:T(2,128)}, u32[]{:S(2)}) copy-start(f32[16,2,256]{2,1,0:T(2,128)} %get-tuple-element.55) | copy-start | bytes 98308
  174.1 41.9 %copy-start.18 = (f32[16,2,256]{2,1,0:T(2,128)S(1)}, f32[16,2,256]{2,1,0:T(2,128)}, u32[]{:S(2)}) copy-start(f32[16,2,256]{2,1,0:T(2,128)} %get-tuple-element.63) | copy-start | bytes 98308
  174.2 41.9 %copy-start.19 = (f32[16,2,256]{2,1,0:T(2,128)S(1)}, f32[16,2,256]{2,1,0:T(2,128)}, u32[]{:S(2)}) copy-start(f32[16,2,256]{2,1,0:T(2,128)} %get-tuple-element.64) | copy-start | bytes 98308
  174.2 0.8 copy-start.13
  175.0 0.8 copy-start.14
  186.8 0.8 copy-start.9
  190.3 11.0 %all-to-all-start.2 = ((f32[4,128,256]{2,1,0:T(8,128)}), f32[4,128,256]{2,1,0:T(8,128)S(1)}, u32[]{:S(2)}, u32[]{:S(2)}) async-start(f32[4,128,256]{2,1,0:T(8,128)} %collect.1), calls=%async_computation.2 | async-start | bytes 1048576 | tf_op jit(solution)/shard_map/all_to_all | solution.py:761
  203.7 23.1 %all-to-all-start.3 = ((f32[32,16,256]{2,1,0:T(8,128)}), f32[32,16,256]{2,1,0:T(8,128)S(1)}, u32[]{:S(2)}, u32[]{:S(2)}) async-start(f32[32,16,256]{2,1,0:T(8,128)} %bitcast.19), calls=%async_computation.3 | async-start | bytes 1048576 | tf_op jit(solution)/shard_map/all_to_all | solution.py:695

commit v7 on v6

--- a/solution.py
+++ b/solution.py
@@ -19,6 +19,7 @@
 F32 = jnp.float32
 NT = (((1,), (1,)), ((), ()))
 PARAMS = pltpu.CompilerParams(vmem_limit_bytes=60 * 1024 * 1024)
+LATE = pltpu.CompilerParams(vmem_limit_bytes=40 * 1024 * 1024)
 SMALL = pltpu.CompilerParams(vmem_limit_bytes=24 * 1024 * 1024)
 
 
@@ -96,6 +97,7 @@
 
 PART = 8
 PACKED = 136
+PARTS = 4
 FIRST = 3
 
 
@@ -116,11 +118,17 @@
 
         for k in range(images):
             read(k).start()
-        for k in range(images):
-            read(k).wait()
-        for s in range(count):
-            for j in range(blocks):
-                write(s, j).start()
+        part = images // PARTS
+        for q in range(PARTS):
+            for k in range(q * part, (q + 1) * part):
+                read(k).wait()
+            for s in range(count):
+
+                @pl.when(idx_ref[s] // part == q)
+                def _():
+                    for j in range(blocks):
+                        write(s, j).start()
+
         for s in range(count):
             for j in range(blocks):
                 write(s, j).wait()
@@ -584,7 +592,7 @@
             jax.ShapeDtypeStruct((images, count, steps * 128), F32),
             jax.ShapeDtypeStruct((steps, images * count, 256), F32),
         ],
-        compiler_params=PARAMS,
+        compiler_params=LATE if late else PARAMS,
         cost_estimate=pl.CostEstimate(
             flops=work * 200_000_000, bytes_accessed=work * 400_000, transcendentals=0
         ),

time: 229 us -> 221 us (0.965)
  Pallas kernels: 98.1 us -> 91.1 us
  local copies, waits for them, and re-layouts: 14.9 us -> 12.3 us
    pallas_call x4, Pallas kernels: 41.2 us -> 36.2 us  [sweep_steps(): pl.pallas_call(functools.partial(sweep_kernel, group, ys, halo, late), gr...]
where the time goes in v7:
time: 221 us; the launch traced here: 219 us
  Pallas kernels  91.1 us (41%)
  starting transfers between devices  66.2 us (30%)
  waiting for transfers between devices  43.1 us (20%)
  local copies, waits for them, and re-layouts  12.3 us (6%)
  other arithmetic  5.19 us (2%)
    pallas_call x4, Pallas kernels, sweep_steps(): pl.pallas_call(functools.partial(sweep_kernel, group, ys, halo, late), gr...  36.2 us
    all_to_all x3, starting transfers between devices, exchange(): return lax.all_to_all(a, 'img', split_axis=0, concat_axis=0, tiled=True)  34.1 us
    all_to_all x3, waiting for transfers between devices, exchange(): return lax.all_to_all(a, 'img', split_axis=0, concat_axis=0, tiled=True)  20.7 us
    ppermute x4, starting transfers between devices, neighbour_rows(): above = lax.ppermute(tail, 'tile', [(i, i + 1) for i in range(count - 1)])  16.4 us
    pallas_call x1, Pallas kernels, prepare(): pl.pallas_call(prepare_kernel, grid=(images,), in_specs=[pl.BlockSpec((1,...  15.5 us
    pallas_call x2, Pallas kernels, edges(): pl.pallas_call(edge_kernel, grid_spec=pltpu.PrefetchScalarGridSpec(num_sc...  11.3 us
    pallas_call x2, Pallas kernels, pick(): pl.pallas_call(kernel, grid_spec=pltpu.PrefetchScalarGridSpec(num_scalar_...  11.2 us
    ppermute x4, waiting for transfers between devices, neighbour_rows(): below = lax.ppermute(head, 'tile', [(i + 1, i) for i in range(count - 1)])  10.3 us
  transfers between devices with their start and end apart: 15, of which 7 were waited for; matrix products, arithmetic and copies ran while one was open for 6% of the time, Pallas kernels for 31%

profile of v7, /device:TPU:1, one launch (start us, length us, event | category | flops | bytes accessed | tf_op | source)
XLA Modules:
  0.0 219.3 jit_solution(15883055604955213344)
XLA Ops:
  0.6 0.8 reshape.86
  1.4 0.7 add_select_fusion.1
  2.1 5.5 %pick.3 = bf16[32,3,64,4,128]{4,3,2,1,0:T(4,128)(2,1)} custom-call(s32[32]{0:T(128)} %get-tuple-element.73.idx_ref, bf16[16,64,4,768]{3,2,1,0:T(4,128)(2,1)} %features_ref.3), custom_call_target="tpu_custom_call" | custom-call | bytes 12582912 | tf_op jit(solution)/shard_map/pick/pallas_call | solution.py:136
  7.6 8.7 %all-to-all-start.1 = ((bf16[32,3,256,128]{3,2,1,0:T(8,128)(2,1)}), bf16[32,3,256,128]{3,2,1,0:T(8,128)(2,1)}, u32[]{:S(2)}, u32[]{:S(2)}) async-start(bf16[32,3,256,128]{3,2,1,0:T(8,128)(2,1)} %bitcast.74), calls=%async_computation.1 | async-start | bytes 12582912 | tf_op jit(solution)/shard_map/all_to_all | solution.py:703
  16.5 1.7 collective-permute-start.4
  18.2 3.3 %collective-permute-start.5 = (s32[1,256]{1,0:T(1,128)S(1)}, s32[1,256]{1,0:T(1,128)S(1)}, u32[]{:S(2)}, u32[]{:S(2)}) collective-permute-start(s32[1,256]{1,0:T(1,128)S(1)} %get-tuple-element.76), channel_id=1, source_target_pairs={{0,2},{1,3},{2,0},{3,1},{4,6},{5,7},{6,4},{7,5},{8,10},{9,11},{10,... | collective-permute-start | bytes 3080 | tf_op jit(solution)/shard_map/ppermute | solution.py:733
  21.5 0.7 collective-permute-start.6
  22.2 0.5 iota.15.idx_ref
  22.8 5.8 %pick.2 = bf16[16,5,64,4,128]{4,3,2,1,0:T(4,128)(2,1)} custom-call(s32[16]{0:T(128)} %iota.15.idx_ref, bf16[16,64,4,768]{3,2,1,0:T(4,128)(2,1)} %features_ref.3), custom_call_target="tpu_custom_call" | custom-call | bytes 10485760 | tf_op jit(solution)/shard_map/pick/pallas_call | solution.py:136
  28.5 0.5 iota.16.slot_ref
  29.0 6.3 %edges.2 = (bf16[16,5,64,128]{3,2,1,0:T(8,128)(2,1)}, bf16[16,5,64,128]{3,2,1,0:T(8,128)(2,1)}, f32[16,5,8,128]{3,2,1,0:T(8,128)}) custom-call(s32[16]{0:T(128)} %iota.16.slot_ref, bf16[16,5,256,128]{3,2,1,0:T(8,128)(2,1)} %bitcast.49, bf16[16,5,256,128]{3,2,1,0:T(8,128)(2,1)} %bitcast.50, bf16[16,5,256,128]{3,2,1,0:T(8,128)(2,1)} %bitcast.51, ...), custom_call_target="tpu_custom_call" | custom-call | flops 1600000000 | bytes 8000000 | tf_op jit(solution)/shard_map/edges/pallas_call | solution.py:285
  35.4 1.4 slice.30
  36.8 3.6 %collective-permute-start = (bf16[16,4,64,128]{3,2,1,0:T(8,128)(2,1)S(1)}, bf16[16,4,64,128]{3,2,1,0:T(8,128)(2,1)}, u32[]{:S(2)}, u32[]{:S(2)}) collective-permute-start(bf16[16,4,64,128]{3,2,1,0:T(8,128)(2,1)S(1)} %slice.30), channel_id=1, source_target_pairs={{0,1},{1,2},{2,3},{4,5},{5,6},{6,7},{8,9},{9,10},{10,11},{12,13},{... | collective-permute-start | bytes 3145736 | tf_op jit(solution)/shard_map/ppermute | solution.py:683
  40.4 1.3 slice.32
  41.7 1.3 collective-permute-start.2
  43.1 0.1 pad_bitcast_fusion
  43.2 1.0 select_reduce_fusion
  44.2 0.1 pad_bitcast_fusion.4
  44.3 0.6 pad_maximum_fusion.1.refs_37_.refs_8_
  44.9 0.8 fusion.refs_39_.refs_10_
  45.6 1.1 slice_bitcast_fusion
  46.7 0.2 copy.38
  46.9 0.1 reshape.88
  47.0 0.2 copy.40
  47.2 0.1 reshape.90
  47.3 7.3 %pack.1 = bf16[32,392,128]{2,1,0:T(8,128)(2,1)} custom-call(s32[32]{0:T(128)} %get-tuple-element.73.idx_ref, bf16[16,5,256,128]{3,2,1,0:T(8,128)(2,1)} %bitcast.61, bf16[16,5,256,128]{3,2,1,0:T(8,128)(2,1)} %bitcast.58, bf16[16,5,256,128]{3,2,1,0:T(8,128)(2,1)} %bitcast.59, bf16[16,5,256,128]{3,2,1,0:T(8,128)(2,1)} %bitcast.60, ...), custom_call_target="tpu_custom_call" | custom-call | tf_op jit(solution)/shard_map/pack/pallas_call | solution.py:193
  54.6 4.0 %collective-permute-start.1 = (bf16[16,128]{1,0:T(8,128)(2,1)S(1)}, bf16[16,128]{1,0:T(8,128)(2,1)S(1)}, u32[]{:S(2)}, u32[]{:S(2)}) collective-permute-start(bf16[16,128]{1,0:T(8,128)(2,1)S(1)} %reshape.88), channel_id=1, source_target_pairs={{0,1},{1,2},{2,3},{4,5},{5,6},{6,7},{8,9},{9,10},{10,11},{12,13},{... | collective-permute-start | bytes 12296 | tf_op jit(solution)/shard_map/ppermute | solution.py:683
  58.6 1.3 collective-permute-start.3
  60.0 0.6 gather_fusion
  60.5 0.7 broadcast_select_fusion
  61.2 0.1 reshape.89
  61.3 0.2 copy.39
  61.5 5.5 %collective-permute-done.3 = bf16[16,128]{1,0:T(8,128)(2,1)S(1)} collective-permute-done((bf16[16,128]{1,0:T(8,128)(2,1)S(1)}, bf16[16,128]{1,0:T(8,128)(2,1)S(1)}, u32[]{:S(2)}, u32[]{:S(2)}) %collective-permute-start.3) | collective-permute-done | bytes 4128 | tf_op jit(solution)/shard_map/ppermute | solution.py:684
  67.0 0.1 reshape.91
  67.1 0.2 copy.41
  67.3 0.8 pad.13.up_last_ref
  68.1 0.8 pad.14.down_last_ref
  68.9 15.5 %prepare.1 = (bf16[16,4,144,256]{3,2,1,0:T(8,128)(2,1)}, bf16[16,4,144,128]{3,2,1,0:T(8,128)(2,1)}, bf16[16,4,64,128]{3,2,1,0:T(8,128)(2,1)}) custom-call(bf16[16,5,256,128]{3,2,1,0:T(8,128)(2,1)} %bitcast.73, bf16[16,4,64,128]{3,2,1,0:T(8,128)(2,1)} %collective-permute-done.up_ref, bf16[16,64,128]{2,1,0:T(8,128)(2,1)} %pad.13.up_last_ref, ...), custom_call_target="tpu_custom_call" | custom-call | flops 2560000000 | bytes 16000000 | tf_op jit(solution)/shard_map/prepare/pallas_call | solution.py:359
  84.4 9.9 %all-to-all-done.1.refs_0_.refs_1_.refs_2_.refs_3_.refs_4_.refs_5_.refs_6_.refs_7_.refs_8_.refs_9_.refs_10_.refs_11_.refs_12_.refs_13_.refs_14_.refs_15_.refs_16_.refs_17_.refs_18_.refs_19_.refs_20_.refs_21_.refs_22_.refs_23_.refs_24_.refs_25_.refs_26_.refs_27_.refs_28_.refs_29_.refs_30_.refs_31_.refs_32_ = bf16[32,3,256,128]{3,2,1,0:T(8,128)(2,1)} async-done(((bf16[32,3,256,128]{3,2,1,0:T(8,128)(2,1)}), ...) | async-done | bytes 6291488 | tf_op jit(solution)/shard_map/all_to_all | solution.py:703
  94.3 14.5 %all-to-all-start = ((bf16[32,392,128]{2,1,0:T(8,128)(2,1)}), bf16[32,392,128]{2,1,0:T(8,128)(2,1)S(1)}, u32[]{:S(2)}, u32[]{:S(2)}) async-start(bf16[32,392,128]{2,1,0:T(8,128)(2,1)} %pack.1), calls=%async_computation | async-start | bytes 6422528 | tf_op jit(solution)/shard_map/all_to_all | solution.py:703
  108.9 0.6 fusion.21.slot_ref.refs_0_
  109.4 5.0 %edges.3 = (bf16[16,3,64,128]{3,2,1,0:T(8,128)(2,1)}, bf16[16,3,64,128]{3,2,1,0:T(8,128)(2,1)}, f32[16,3,8,128]{3,2,1,0:T(8,128)}, bf16[16,1,256,128]{3,2,1,0:T(8,128)(2,1)}) custom-call(s32[16]{0:T(128)} %fusion.21.slot_ref.refs_0_, ...), custom_call_target="tpu_custom_call" | custom-call | flops 960000000 | bytes 4800000 | tf_op jit(solution)/shard_map/edges/pallas_call | solution.py:285
  114.4 4.5 %collective-permute-start.7 = (bf16[16,3,64,128]{3,2,1,0:T(8,128)(2,1)}, bf16[16,3,64,128]{3,2,1,0:T(8,128)(2,1)}, u32[]{:S(2)}, u32[]{:S(2)}) collective-permute-start(bf16[16,3,64,128]{3,2,1,0:T(8,128)(2,1)} %get-tuple-element.48), channel_id=1, source_target_pairs={{0,1},{1,2},{2,3},{4,5},{5,6},{6,7},{8,9},{9,10},{10,11},{12,13},{... | collective-permute-start | bytes 2359304 | tf_op jit(solution)/shard_map/ppermute | solution.py:683
  118.9 1.5 collective-permute-start.8
  120.4 9.5 %sweep.4 = (f32[16,2,256]{2,1,0:T(2,128)}, f32[2,32,256]{2,1,0:T(8,128)}) custom-call(s32[16]{0:T(128)} %fusion.21.slot_ref.refs_0_, ...), custom_call_target="tpu_custom_call" | custom-call | flops 3200000000 | bytes 6400000 | tf_op jit(solution)/shard_map/sweep/pallas_call | solution.py:579
  129.9 5.1 %collective-permute-done.7.refs_43_.refs_44_.refs_15_ = bf16[16,3,64,128]{3,2,1,0:T(8,128)(2,1)} collective-permute-done((bf16[16,3,64,128]{3,2,1,0:T(8,128)(2,1)}, bf16[16,3,64,128]{3,2,1,0:T(8,128)(2,1)}, u32[]{:S(2)}, u32[]{:S(2)}) %collective-permute-start.7) | collective-permute-done | bytes 786464 | tf_op jit(solution)/shard_map/ppermute | solution.py:683
  135.0 4.7 %collective-permute-done.8.refs_45_.refs_46_.refs_18_ = bf16[16,3,64,128]{3,2,1,0:T(8,128)(2,1)} collective-permute-done((bf16[16,3,64,128]{3,2,1,0:T(8,128)(2,1)}, bf16[16,3,64,128]{3,2,1,0:T(8,128)(2,1)}, u32[]{:S(2)}, u32[]{:S(2)}) %collective-permute-start.8) | collective-permute-done | bytes 786464 | tf_op jit(solution)/shard_map/ppermute | solution.py:684
  139.7 11.6 %sweep.5 = (f32[16,2,256]{2,1,0:T(2,128)}, f32[2,32,256]{2,1,0:T(8,128)}) custom-call(s32[16]{0:T(128)} %fusion.21.slot_ref.refs_0_, ...), custom_call_target="tpu_custom_call" | custom-call | flops 3200000000 | bytes 6400000 | tf_op jit(solution)/shard_map/sweep/pallas_call | solution.py:579
  151.5 4.4 %unpack.1 = (bf16[16,2,64,128]{3,2,1,0:T(8,128)(2,1)S(1)}, bf16[16,2,64,128]{3,2,1,0:T(8,128)(2,1)S(1)}, f32[16,2,8,128]{3,2,1,0:T(8,128)S(1)}, bf16[16,2,256,128]{3,2,1,0:T(8,128)(2,1)S(1)}) custom-call(s32[16]{0:T(128)S(1)} %copy-done.18, bf16[32,392,128]{2,1,0:T(8,128)(2,1)S(1)} %all-to-all-done.refs_0_.refs_1_.refs_2_.refs_3_.refs_4_.refs_5_.refs_6_.refs_7_, ...), custom_call_target="tpu_custom_call" | custom-call | tf_op jit(solution)/shard_map/unpack/pallas_call | solution.py:313
  155.9 1.3 collective-permute-start.10
  157.2 4.2 %collective-permute-start.9 = (bf16[16,2,64,128]{3,2,1,0:T(8,128)(2,1)S(1)}, bf16[16,2,64,128]{3,2,1,0:T(8,128)(2,1)S(1)}, u32[]{:S(2)}, u32[]{:S(2)}) collective-permute-start(bf16[16,2,64,128]{3,2,1,0:T(8,128)(2,1)S(1)} %get-tuple-element.60), channel_id=1, source_target_pairs={{0,1},{1,2},{2,3},{4,5},{5,6},{6,7},{8,9},{9,10},{10,11},{12,13},{... | collective-permute-start | bytes 1572872 | tf_op jit(solution)/shard_map/ppermute | solution.py:683
  161.6 2.3 %copy-done = bf16[16,4,144,256]{3,2,1,0:T(8,128)(2,1)S(1)} copy-done((bf16[16,4,144,256]{3,2,1,0:T(8,128)(2,1)S(1)}, bf16[16,4,144,256]{3,2,1,0:T(8,128)(2,1)}, u32[]{:S(2)}) %copy-start) | copy-done | bytes 4718616
  164.0 6.5 %sweep.7 = (f32[16,2,256]{2,1,0:T(2,128)S(1)}, f32[2,32,256]{2,1,0:T(8,128)S(1)}) custom-call(s32[16]{0:T(128)S(1)} %copy-done.18, bf16[16,1,256,128]{3,2,1,0:T(8,128)(2,1)S(1)} %copy-done.4, bf16[16,2,256,128]{3,2,1,0:T(8,128)(2,1)S(1)} %get-tuple-element.58.refs_2_.refs_3_, bf16[16,2,256,128]{3,2,1,0:T(8,128)(2,1)S(1)} %get-tuple-element.58.refs_2_.refs_3_, ...), custom_call_target="tpu_custom_call" | custom-call | flops 3200000000 | bytes 6400000 | tf_op jit(solution)/shard_map/sweep/pallas_call | solution.py:579
  170.5 0.3 collective-permute-done.9.refs_16_.refs_17_
  170.8 8.6 %sweep.6 = (f32[16,2,256]{2,1,0:T(2,128)S(1)}, f32[2,32,256]{2,1,0:T(8,128)S(1)}) custom-call(s32[16]{0:T(128)S(1)} %copy-done.18, bf16[16,1,256,128]{3,2,1,0:T(8,128)(2,1)S(1)} %copy-done.4, bf16[16,2,256,128]{3,2,1,0:T(8,128)(2,1)S(1)} %get-tuple-element.58.refs_2_.refs_3_, bf16[16,2,256,128]{3,2,1,0:T(8,128)(2,1)S(1)} %get-tuple-element.58.refs_2_.refs_3_, ...), custom_call_target="tpu_custom_call" | custom-call | flops 3200000000 | bytes 6400000 | tf_op jit(solution)/shard_map/sweep/pallas_call | solution.py:579
  179.4 2.6 %collect.1 = f32[4,128,256]{2,1,0:T(8,128)} custom-call(s32[4,128]{1,0:T(4,128)S(1)} %fusion.8.list_ref, s32[4]{0:T(128)S(1)} %bitcast.48, f32[2,32,256]{2,1,0:T(8,128)S(1)} %copy-done.16, f32[2,32,256]{2,1,0:T(8,128)S(1)} %get-tuple-element.67.b_ref, f32[2,32,256]{2,1,0:T(8,128)S(1)} %copy-done.17, f32[2,32,256]{2,1,0:T(8,128)S(1)} %get-tuple-element.69.d_ref), custom_call_target="tpu_custom_call" | custom-call | tf_op jit(solution)/shard_map/collect/pallas_call | solution.py:635
  182.1 4.7 %all-to-all-start.2 = ((f32[4,128,256]{2,1,0:T(8,128)}), f32[4,128,256]{2,1,0:T(8,128)S(1)}, u32[]{:S(2)}, u32[]{:S(2)}) async-start(f32[4,128,256]{2,1,0:T(8,128)} %collect.1), calls=%async_computation.2 | async-start | bytes 1048576 | tf_op jit(solution)/shard_map/all_to_all | solution.py:769
  186.8 0.1 slice_reduce_fusion.count_ref
  186.9 6.8 %all-to-all-done.2.got_ref = f32[4,128,256]{2,1,0:T(8,128)S(1)} async-done(((f32[4,128,256]{2,1,0:T(8,128)}), f32[4,128,256]{2,1,0:T(8,128)S(1)}, u32[]{:S(2)}, u32[]{:S(2)}) %all-to-all-start.2) | async-done | bytes 524320 | tf_op jit(solution)/shard_map/all_to_all | solution.py:769
  193.7 2.5 %place.1 = f32[512,256]{1,0:T(8,128)} custom-call(s32[4,128]{1,0:T(4,128)S(1)} %slice.36.slot_ref, s32[4]{0:T(128)S(1)} %slice_reduce_fusion.count_ref, f32[4,128,256]{2,1,0:T(8,128)S(1)} %all-to-all-done.2.got_ref), custom_call_target="tpu_custom_call" | custom-call | tf_op jit(solution)/shard_map/place/pallas_call | solution.py:667
  196.2 10.8 %all-to-all-start.3 = ((f32[32,16,256]{2,1,0:T(8,128)}), f32[32,16,256]{2,1,0:T(8,128)S(1)}, u32[]{:S(2)}, u32[]{:S(2)}) async-start(f32[32,16,256]{2,1,0:T(8,128)} %bitcast.19), calls=%async_computation.3 | async-start | bytes 1048576 | tf_op jit(solution)/shard_map/all_to_all | solution.py:703
  207.2 0.7 pad_maximum_fusion
  207.9 10.8 %all-to-all-done.3 = f32[32,16,256]{2,1,0:T(8,128)S(1)} async-done(((f32[32,16,256]{2,1,0:T(8,128)}), f32[32,16,256]{2,1,0:T(8,128)S(1)}, u32[]{:S(2)}, u32[]{:S(2)}) %all-to-all-start.3) | async-done | bytes 524320 | tf_op jit(solution)/shard_map/all_to_all | solution.py:703
  218.7 0.6 fusion.5
  (86 shorter events, 0.5 us)
Async XLA Ops:
  7.6 8.8 %copy-start.19 = (s32[1,1,4]{2,1,0:T(1,128)S(1)}, s32[1,1,4]{2,1,0:T(1,128)}, u32[]{:S(2)}) copy-start(s32[1,1,4]{2,1,0:T(1,128)} %param.41) | copy-start | bytes 52
  7.6 8.9 %copy-start.27 = (s32[1,1,4,128]{3,2,1,0:T(4,128)S(1)}, s32[1,1,4,128]{3,2,1,0:T(4,128)}, u32[]{:S(2)}) copy-start(s32[1,1,4,128]{3,2,1,0:T(4,128)} %param.40) | copy-start | bytes 6148
  7.6 86.7 %all-to-all-start.1 = ((bf16[32,3,256,128]{3,2,1,0:T(8,128)(2,1)}), bf16[32,3,256,128]{3,2,1,0:T(8,128)(2,1)}, u32[]{:S(2)}, u32[]{:S(2)}) async-start(bf16[32,3,256,128]{3,2,1,0:T(8,128)(2,1)} %bitcast.74), calls=%async_computation.1 | async-start | bytes 12582912 | tf_op jit(solution)/shard_map/all_to_all | solution.py:703
  16.5 38.1 %collective-permute-start.4 = (s32[1,256]{1,0:T(1,128)S(1)}, s32[1,256]{1,0:T(1,128)S(1)}, u32[]{:S(2)}, u32[]{:S(2)}) collective-permute-start(s32[1,256]{1,0:T(1,128)S(1)} %get-tuple-element.75), channel_id=1, source_target_pairs={{0,1},{1,2},{2,3},{3,0},{4,5},{5,6},{6,7},{7,4},{8,9},{9,10},{10,1... | collective-permute-start | bytes 3080 | tf_op jit(solution)/shard_map/ppermute | solution.py:733
  18.2 40.4 %collective-permute-start.5 = (s32[1,256]{1,0:T(1,128)S(1)}, s32[1,256]{1,0:T(1,128)S(1)}, u32[]{:S(2)}, u32[]{:S(2)}) collective-permute-start(s32[1,256]{1,0:T(1,128)S(1)} %get-tuple-element.76), channel_id=1, source_target_pairs={{0,2},{1,3},{2,0},{3,1},{4,6},{5,7},{6,4},{7,5},{8,10},{9,11},{10,... | collective-permute-start | bytes 3080 | tf_op jit(solution)/shard_map/ppermute | solution.py:733
  21.5 38.4 %collective-permute-start.6 = (s32[1,256]{1,0:T(1,128)S(1)}, s32[1,256]{1,0:T(1,128)S(1)}, u32[]{:S(2)}, u32[]{:S(2)}) collective-permute-start(s32[1,256]{1,0:T(1,128)S(1)} %get-tuple-element.77), channel_id=1, source_target_pairs={{0,3},{1,0},{2,1},{3,2},{4,7},{5,4},{6,5},{7,6},{8,11},{9,8},{10,9... | collective-permute-start | bytes 3080 | tf_op jit(solution)/shard_map/ppermute | solution.py:733
  29.0 14.0 %copy-start.22 = (s32[16,4,512]{2,1,0:T(4,128)S(1)}, s32[16,4,512]{2,1,0:T(4,128)}, u32[]{:S(2)}) copy-start(s32[16,4,512]{2,1,0:T(4,128)} %index_ref.1) | copy-start | bytes 393220
  29.0 14.1 %copy-start.26 = (f32[64]{0:T(128)S(1)}, f32[64]{0:T(128)}, u32[]{:S(2)}) copy-start(f32[64]{0:T(128)} %param.34) | copy-start | bytes 772
  35.3 8.9 %copy-start.30 = (bf16[1,128]{1,0:T(2,128)(2,1)S(1)}, bf16[1,128]{1,0:T(2,128)(2,1)}, u32[]{:S(2)}) copy-start(bf16[1,128]{1,0:T(2,128)(2,1)} %constant.271) | copy-start | bytes 772
  35.3 8.9 %copy-start.31 = (bf16[1,128]{1,0:T(2,128)(2,1)S(1)}, bf16[1,128]{1,0:T(2,128)(2,1)}, u32[]{:S(2)}) copy-start(bf16[1,128]{1,0:T(2,128)(2,1)} %constant.272) | copy-start | bytes 772
  35.4 9.5 %copy-start.21 = (f32[16,4,512]{2,1,0:T(4,128)S(1)}, f32[16,4,512]{2,1,0:T(4,128)}, u32[]{:S(2)}) copy-start(f32[16,4,512]{2,1,0:T(4,128)} %param.36) | copy-start | bytes 393220
  35.4 9.5 %copy-start.29 = (f32[16]{0:T(128)S(1)}, f32[16]{0:T(128)}, u32[]{:S(2)}) copy-start(f32[16]{0:T(128)} %param.35) | copy-start | bytes 196
  36.8 32.1 %collective-permute-start = (bf16[16,4,64,128]{3,2,1,0:T(8,128)(2,1)S(1)}, bf16[16,4,64,128]{3,2,1,0:T(8,128)(2,1)}, u32[]{:S(2)}, u32[]{:S(2)}) collective-permute-start(bf16[16,4,64,128]{3,2,1,0:T(8,128)(2,1)S(1)} %slice.30), channel_id=1, source_target_pairs={{0,1},{1,2},{2,3},{4,5},{5,6},{6,7},{8,9},{9,10},{10,11},{12,13},{... | collective-permute-start | bytes 3145736 | tf_op jit(solution)/shard_map/ppermute | solution.py:683
  41.7 27.2 %collective-permute-start.2 = (bf16[16,4,64,128]{3,2,1,0:T(8,128)(2,1)S(1)}, bf16[16,4,64,128]{3,2,1,0:T(8,128)(2,1)}, u32[]{:S(2)}, u32[]{:S(2)}) collective-permute-start(bf16[16,4,64,128]{3,2,1,0:T(8,128)(2,1)S(1)} %slice.32), channel_id=1, source_target_pairs={{1,0},{2,1},{3,2},{5,4},{6,5},{7,6},{9,8},{10,9},{11,10},{13,12},{... | collective-permute-start | bytes 3145736 | tf_op jit(solution)/shard_map/ppermute | solution.py:684
  54.6 6.6 %collective-permute-start.1 = (bf16[16,128]{1,0:T(8,128)(2,1)S(1)}, bf16[16,128]{1,0:T(8,128)(2,1)S(1)}, u32[]{:S(2)}, u32[]{:S(2)}) collective-permute-start(bf16[16,128]{1,0:T(8,128)(2,1)S(1)} %reshape.88), channel_id=1, source_target_pairs={{0,1},{1,2},{2,3},{4,5},{5,6},{6,7},{8,9},{9,10},{10,11},{12,13},{... | collective-permute-start | bytes 12296 | tf_op jit(solution)/shard_map/ppermute | solution.py:683
  58.6 8.4 %collective-permute-start.3 = (bf16[16,128]{1,0:T(8,128)(2,1)S(1)}, bf16[16,128]{1,0:T(8,128)(2,1)S(1)}, u32[]{:S(2)}, u32[]{:S(2)}) collective-permute-start(bf16[16,128]{1,0:T(8,128)(2,1)S(1)} %reshape.90), channel_id=1, source_target_pairs={{1,0},{2,1},{3,2},{5,4},{6,5},{7,6},{9,8},{10,9},{11,10},{13,12},{... | collective-permute-start | bytes 12296 | tf_op jit(solution)/shard_map/ppermute | solution.py:684
  94.3 57.0 %all-to-all-start = ((bf16[32,392,128]{2,1,0:T(8,128)(2,1)}), bf16[32,392,128]{2,1,0:T(8,128)(2,1)S(1)}, u32[]{:S(2)}, u32[]{:S(2)}) async-start(bf16[32,392,128]{2,1,0:T(8,128)(2,1)} %pack.1), calls=%async_computation | async-start | bytes 6422528 | tf_op jit(solution)/shard_map/all_to_all | solution.py:703
  114.4 20.6 %collective-permute-start.7 = (bf16[16,3,64,128]{3,2,1,0:T(8,128)(2,1)}, bf16[16,3,64,128]{3,2,1,0:T(8,128)(2,1)}, u32[]{:S(2)}, u32[]{:S(2)}) collective-permute-start(bf16[16,3,64,128]{3,2,1,0:T(8,128)(2,1)} %get-tuple-element.48), channel_id=1, source_target_pairs={{0,1},{1,2},{2,3},{4,5},{5,6},{6,7},{8,9},{9,10},{10,11},{12,13},{... | collective-permute-start | bytes 2359304 | tf_op jit(solution)/shard_map/ppermute | solution.py:683
  118.9 20.8 %collective-permute-start.8 = (bf16[16,3,64,128]{3,2,1,0:T(8,128)(2,1)}, bf16[16,3,64,128]{3,2,1,0:T(8,128)(2,1)}, u32[]{:S(2)}, u32[]{:S(2)}) collective-permute-start(bf16[16,3,64,128]{3,2,1,0:T(8,128)(2,1)} %get-tuple-element.49), channel_id=1, source_target_pairs={{1,0},{2,1},{3,2},{5,4},{6,5},{7,6},{9,8},{10,9},{11,10},{13,12},{... | collective-permute-start | bytes 2359304 | tf_op jit(solution)/shard_map/ppermute | solution.py:684
  139.7 11.7 %copy-start.9 = (bf16[128,256]{1,0:T(8,128)(2,1)S(1)}, bf16[128,256]{1,0:T(8,128)(2,1)}, u32[]{:S(2)}) copy-start(bf16[128,256]{1,0:T(8,128)(2,1)} %constant.160.clone.refs_8_.refs_11_) | copy-start | bytes 196612
  139.7 11.7 %copy-start.11 = (bf16[128,256]{1,0:T(8,128)(2,1)S(1)}, bf16[128,256]{1,0:T(8,128)(2,1)}, u32[]{:S(2)}) copy-start(bf16[128,256]{1,0:T(8,128)(2,1)} %constant.163.clone.refs_16_.refs_8_) | copy-start | bytes 196612
  139.7 11.7 %copy-start.12 = (bf16[256,256]{1,0:T(8,128)(2,1)S(1)}, bf16[256,256]{1,0:T(8,128)(2,1)}, u32[]{:S(2)}) copy-start(bf16[256,256]{1,0:T(8,128)(2,1)} %constant.169.clone.refs_10_) | copy-start | bytes 393220
  139.7 11.7 %copy-start.15 = (bf16[256,128]{1,0:T(8,128)(2,1)S(1)}, bf16[256,128]{1,0:T(8,128)(2,1)}, u32[]{:S(2)}) copy-start(bf16[256,128]{1,0:T(8,128)(2,1)} %constant.168.clone.refs_9_) | copy-start | bytes 196612
  139.7 11.7 %copy-start.18 = (s32[16]{0:T(128)S(1)}, s32[16]{0:T(128)}, u32[]{:S(2)}) copy-start(s32[16]{0:T(128)} %fusion.21.slot_ref.refs_0_) | copy-start | bytes 196
  151.4 10.1 %copy-start.28 = (s32[1,1,4,128]{3,2,1,0:T(4,128)S(1)}, s32[1,1,4,128]{3,2,1,0:T(4,128)}, u32[]{:S(2)}) copy-start(s32[1,1,4,128]{3,2,1,0:T(4,128)} %param.39) | copy-start | bytes 6148
  151.4 10.1 %copy-start.1 = (bf16[16,4,64,128]{3,2,1,0:T(8,128)(2,1)S(1)}, bf16[16,4,64,128]{3,2,1,0:T(8,128)(2,1)}, u32[]{:S(2)}) copy-start(bf16[16,4,64,128]{3,2,1,0:T(8,128)(2,1)} %get-tuple-element.44.refs_34_.refs_5_) | copy-start | bytes 3145732
  151.4 10.1 %copy-start.3 = (f32[16,3,8,128]{3,2,1,0:T(8,128)S(1)}, f32[16,3,8,128]{3,2,1,0:T(8,128)}, u32[]{:S(2)}) copy-start(f32[16,3,8,128]{3,2,1,0:T(8,128)} %get-tuple-element.47.refs_41_.refs_42_.refs_12_) | copy-start | bytes 589828
  151.4 10.1 %copy-start.4 = (bf16[16,1,256,128]{3,2,1,0:T(8,128)(2,1)S(1)}, bf16[16,1,256,128]{3,2,1,0:T(8,128)(2,1)}, u32[]{:S(2)}) copy-start(bf16[16,1,256,128]{3,2,1,0:T(8,128)(2,1)} %get-tuple-element.56.refs_1_) | copy-start | bytes 3145732
  151.5 10.1 %copy-start.5 = (f32[16,4,512]{2,1,0:T(4,128)S(1)}, f32[16,4,512]{2,1,0:T(4,128)}, u32[]{:S(2)}) copy-start(f32[16,4,512]{2,1,0:T(4,128)} %fusion.refs_39_.refs_10_) | copy-start | bytes 393220
  151.5 10.1 %copy-start.6 = (s32[16,4,512]{2,1,0:T(4,128)S(1)}, s32[16,4,512]{2,1,0:T(4,128)}, u32[]{:S(2)}) copy-start(s32[16,4,512]{2,1,0:T(4,128)} %refs_11_.4) | copy-start | bytes 393220
  151.5 10.1 %copy-start.8 = (bf16[128,768]{1,0:T(8,128)(2,1)S(1)}, bf16[128,768]{1,0:T(8,128)(2,1)}, u32[]{:S(2)}) copy-start(bf16[128,768]{1,0:T(8,128)(2,1)} %constant.165.clone.refs_35_.refs_6_) | copy-start | bytes 589828
  151.5 10.1 %copy-start.10 = (bf16[128,128]{1,0:T(8,128)(2,1)S(1)}, bf16[128,128]{1,0:T(8,128)(2,1)}, u32[]{:S(2)}) copy-start(bf16[128,128]{1,0:T(8,128)(2,1)} %constant.162.clone.flip_ref.refs_38_.refs_9_) | copy-start | bytes 98308
  151.5 10.1 %copy-start.13 = (bf16[16,256]{1,0:T(8,128)(2,1)S(1)}, bf16[16,256]{1,0:T(8,128)(2,1)}, u32[]{:S(2)}) copy-start(bf16[16,256]{1,0:T(8,128)(2,1)} %constant.166.clone.refs_36_.refs_7_) | copy-start | bytes 24580
  151.5 10.1 %copy-start.14 = (bf16[8,256]{1,0:T(8,128)(2,1)S(1)}, bf16[8,256]{1,0:T(8,128)(2,1)}, u32[]{:S(2)}) copy-start(bf16[8,256]{1,0:T(8,128)(2,1)} %pad_maximum_fusion.1.refs_37_.refs_8_) | copy-start | bytes 12292
  155.9 14.6 %collective-permute-start.10 = (bf16[16,2,64,128]{3,2,1,0:T(8,128)(2,1)S(1)}, bf16[16,2,64,128]{3,2,1,0:T(8,128)(2,1)S(1)}, u32[]{:S(2)}, u32[]{:S(2)}) collective-permute-start(bf16[16,2,64,128]{3,2,1,0:T(8,128)(2,1)S(1)} %get-tuple-element.61), channel_id=1, source_target_pairs={{1,0},{2,1},{3,2},{5,4},{6,5},{7,6},{9,8},{10,9},{11,10},{13,12},{... | collective-permute-start | bytes 1572872 | tf_op jit(solution)/shard_map/ppermute | solution.py:684
  157.2 13.5 %collective-permute-start.9 = (bf16[16,2,64,128]{3,2,1,0:T(8,128)(2,1)S(1)}, bf16[16,2,64,128]{3,2,1,0:T(8,128)(2,1)S(1)}, u32[]{:S(2)}, u32[]{:S(2)}) collective-permute-start(bf16[16,2,64,128]{3,2,1,0:T(8,128)(2,1)S(1)} %get-tuple-element.60), channel_id=1, source_target_pairs={{0,1},{1,2},{2,3},{4,5},{5,6},{6,7},{8,9},{9,10},{10,11},{12,13},{... | collective-permute-start | bytes 1572872 | tf_op jit(solution)/shard_map/ppermute | solution.py:683
  161.6 2.3 %copy-start = (bf16[16,4,144,256]{3,2,1,0:T(8,128)(2,1)S(1)}, bf16[16,4,144,256]{3,2,1,0:T(8,128)(2,1)}, u32[]{:S(2)}) copy-start(bf16[16,4,144,256]{3,2,1,0:T(8,128)(2,1)} %get-tuple-element.43.refs_33_.refs_4_) | copy-start | bytes 14155780
  164.0 6.8 %copy-start.2 = (bf16[16,4,144,128]{3,2,1,0:T(8,128)(2,1)S(1)}, bf16[16,4,144,128]{3,2,1,0:T(8,128)(2,1)}, u32[]{:S(2)}) copy-start(bf16[16,4,144,128]{3,2,1,0:T(8,128)(2,1)} %get-tuple-element.53.refs_47_.refs_21_) | copy-start | bytes 7077892
  164.0 6.8 %copy-start.7 = (bf16[128,768]{1,0:T(8,128)(2,1)S(1)}, bf16[128,768]{1,0:T(8,128)(2,1)}, u32[]{:S(2)}) copy-start(bf16[128,768]{1,0:T(8,128)(2,1)} %constant.167.clone.refs_35_.refs_6_) | copy-start | bytes 589828
  170.4 9.0 %copy-start.16 = (f32[2,32,256]{2,1,0:T(8,128)S(1)}, f32[2,32,256]{2,1,0:T(8,128)}, u32[]{:S(2)}) copy-start(f32[2,32,256]{2,1,0:T(8,128)} %get-tuple-element.66.a_ref) | copy-start | bytes 196612
  170.4 9.0 %copy-start.17 = (f32[2,32,256]{2,1,0:T(8,128)S(1)}, f32[2,32,256]{2,1,0:T(8,128)}, u32[]{:S(2)}) copy-start(f32[2,32,256]{2,1,0:T(8,128)} %get-tuple-element.68.c_ref) | copy-start | bytes 196612
  170.5 9.0 %copy-start.20 = (s32[1,1,4]{2,1,0:T(1,128)S(1)}, s32[1,1,4]{2,1,0:T(1,128)}, u32[]{:S(2)}) copy-start(s32[1,1,4]{2,1,0:T(1,128)} %param.41) | copy-start | bytes 52
  170.5 16.3 %copy-start.25 = (s32[4,256]{1,0:T(4,128)S(1)}, s32[4,256]{1,0:T(4,128)}, u32[]{:S(2)}) copy-start(s32[4,256]{1,0:T(4,128)} %broadcast_select_fusion) | copy-start | bytes 12292
  170.5 36.6 %copy-start.23 = (f32[16,2,256]{2,1,0:T(2,128)S(1)}, f32[16,2,256]{2,1,0:T(2,128)}, u32[]{:S(2)}) copy-start(f32[16,2,256]{2,1,0:T(2,128)} %get-tuple-element.55) | copy-start | bytes 98308
  170.5 36.7 %copy-start.24 = (f32[16,2,256]{2,1,0:T(2,128)S(1)}, f32[16,2,256]{2,1,0:T(2,128)}, u32[]{:S(2)}) copy-start(f32[16,2,256]{2,1,0:T(2,128)} %get-tuple-element.63) | copy-start | bytes 98308
  182.1 11.6 %all-to-all-start.2 = ((f32[4,128,256]{2,1,0:T(8,128)}), f32[4,128,256]{2,1,0:T(8,128)S(1)}, u32[]{:S(2)}, u32[]{:S(2)}) async-start(f32[4,128,256]{2,1,0:T(8,128)} %collect.1), calls=%async_computation.2 | async-start | bytes 1048576 | tf_op jit(solution)/shard_map/all_to_all | solution.py:769
  196.2 22.5 %all-to-all-start.3 = ((f32[32,16,256]{2,1,0:T(8,128)}), f32[32,16,256]{2,1,0:T(8,128)S(1)}, u32[]{:S(2)}, u32[]{:S(2)}) async-start(f32[32,16,256]{2,1,0:T(8,128)} %bitcast.19), calls=%async_computation.3 | async-start | bytes 1048576 | tf_op jit(solution)/shard_map/all_to_all | solution.py:703

commit v8 on v7

--- a/solution.py
+++ b/solution.py
@@ -592,7 +592,7 @@
             jax.ShapeDtypeStruct((images, count, steps * 128), F32),
             jax.ShapeDtypeStruct((steps, images * count, 256), F32),
         ],
-        compiler_params=LATE if late else PARAMS,
+        compiler_params=LATE,
         cost_estimate=pl.CostEstimate(
             flops=work * 200_000_000, bytes_accessed=work * 400_000, transcendentals=0
         ),

time: 221 us -> 225 us (1.018)
  local copies, waits for them, and re-layouts: 12.3 us -> 23.7 us
  Pallas kernels: 91.1 us -> 88 us
  waiting for transfers between devices: 43.1 us -> 40.6 us
    unnamed x66 -> x94, local copies, waits for them, and re-layouts: 2.54 us -> 13.9 us
    pallas_call x4, Pallas kernels: 36.2 us -> 33.5 us  [sweep_steps(): pl.pallas_call(functools.partial(sweep_kernel, group, ys, halo, late), gr...]
  transfers between devices with their start and end apart: 15 -> 15, of which waited for: 7 -> 8; matrix products, arithmetic and copies ran while one was open for 6% -> 5% of each run, Pallas kernels for 31% -> 29%
where the time goes in v8:
time: 225 us; the launch traced here: 223 us
  Pallas kernels  88 us (39%)
  starting transfers between devices  65.8 us (29%)
  waiting for transfers between devices  40.6 us (18%)
  local copies, waits for them, and re-layouts  23.7 us (11%)
  other arithmetic  3.88 us (2%)
    all_to_all x3, starting transfers between devices, exchange(): return lax.all_to_all(a, 'img', split_axis=0, concat_axis=0, tiled=True)  34.1 us
    pallas_call x4, Pallas kernels, sweep_steps(): pl.pallas_call(functools.partial(sweep_kernel, group, ys, halo, late), gr...  33.5 us
    all_to_all x3, waiting for transfers between devices, exchange(): return lax.all_to_all(a, 'img', split_axis=0, concat_axis=0, tiled=True)  20.6 us
    pallas_call x1, Pallas kernels, prepare(): pl.pallas_call(prepare_kernel, grid=(images,), in_specs=[pl.BlockSpec((1,...  15.5 us
    ppermute x4, starting transfers between devices, neighbour_rows(): above = lax.ppermute(tail, 'tile', [(i, i + 1) for i in range(count - 1)])  15.4 us
    unnamed x94, local copies, waits for them, and re-layouts  13.9 us
    pallas_call x2, Pallas kernels, edges(): pl.pallas_call(edge_kernel, grid_spec=pltpu.PrefetchScalarGridSpec(num_sc...  11.5 us
    pallas_call x2, Pallas kernels, pick(): pl.pallas_call(kernel, grid_spec=pltpu.PrefetchScalarGridSpec(num_scalar_...  11.3 us
  transfers between devices with their start and end apart: 15, of which 8 were waited for; matrix products, arithmetic and copies ran while one was open for 5% of the time, Pallas kernels for 29%

profile of v8, /device:TPU:1, one launch (start us, length us, event | category | flops | bytes accessed | tf_op | source)
XLA Modules:
  0.0 223.3 jit_solution(9695541459867189257)
XLA Ops:
  0.6 0.8 reshape.86
  1.4 0.6 add_select_fusion.1
  2.0 5.5 %pick.3 = bf16[32,3,64,4,128]{4,3,2,1,0:T(4,128)(2,1)} custom-call(s32[32]{0:T(128)} %get-tuple-element.73.idx_ref, bf16[16,64,4,768]{3,2,1,0:T(4,128)(2,1)} %features_ref.3), custom_call_target="tpu_custom_call" | custom-call | bytes 12582912 | tf_op jit(solution)/shard_map/pick/pallas_call | solution.py:136
  7.6 8.6 %all-to-all-start.1 = ((bf16[32,3,256,128]{3,2,1,0:T(8,128)(2,1)}), bf16[32,3,256,128]{3,2,1,0:T(8,128)(2,1)}, u32[]{:S(2)}, u32[]{:S(2)}) async-start(bf16[32,3,256,128]{3,2,1,0:T(8,128)(2,1)} %bitcast.74), calls=%async_computation.1 | async-start | bytes 12582912 | tf_op jit(solution)/shard_map/all_to_all | solution.py:703
  16.4 1.7 collective-permute-start.4
  18.1 3.3 %collective-permute-start.5 = (s32[1,256]{1,0:T(1,128)S(1)}, s32[1,256]{1,0:T(1,128)S(1)}, u32[]{:S(2)}, u32[]{:S(2)}) collective-permute-start(s32[1,256]{1,0:T(1,128)S(1)} %get-tuple-element.76), channel_id=1, source_target_pairs={{0,2},{1,3},{2,0},{3,1},{4,6},{5,7},{6,4},{7,5},{8,10},{9,11},{10,... | collective-permute-start | bytes 3080 | tf_op jit(solution)/shard_map/ppermute | solution.py:733
  21.4 0.7 collective-permute-start.6
  22.1 0.5 iota.15.idx_ref
  22.7 5.8 %pick.2 = bf16[16,5,64,4,128]{4,3,2,1,0:T(4,128)(2,1)} custom-call(s32[16]{0:T(128)} %iota.15.idx_ref, bf16[16,64,4,768]{3,2,1,0:T(4,128)(2,1)} %features_ref.3), custom_call_target="tpu_custom_call" | custom-call | bytes 10485760 | tf_op jit(solution)/shard_map/pick/pallas_call | solution.py:136
  28.4 0.5 iota.16.slot_ref
  29.0 6.3 %edges.2 = (bf16[16,5,64,128]{3,2,1,0:T(8,128)(2,1)}, bf16[16,5,64,128]{3,2,1,0:T(8,128)(2,1)}, f32[16,5,8,128]{3,2,1,0:T(8,128)}) custom-call(s32[16]{0:T(128)} %iota.16.slot_ref, bf16[16,5,256,128]{3,2,1,0:T(8,128)(2,1)} %bitcast.49, bf16[16,5,256,128]{3,2,1,0:T(8,128)(2,1)} %bitcast.50, bf16[16,5,256,128]{3,2,1,0:T(8,128)(2,1)} %bitcast.51, ...), custom_call_target="tpu_custom_call" | custom-call | flops 1600000000 | bytes 8000000 | tf_op jit(solution)/shard_map/edges/pallas_call | solution.py:285
  35.3 1.4 slice.30
  36.7 3.6 %collective-permute-start = (bf16[16,4,64,128]{3,2,1,0:T(8,128)(2,1)S(1)}, bf16[16,4,64,128]{3,2,1,0:T(8,128)(2,1)}, u32[]{:S(2)}, u32[]{:S(2)}) collective-permute-start(bf16[16,4,64,128]{3,2,1,0:T(8,128)(2,1)S(1)} %slice.30), channel_id=1, source_target_pairs={{0,1},{1,2},{2,3},{4,5},{5,6},{6,7},{8,9},{9,10},{10,11},{12,13},{... | collective-permute-start | bytes 3145736 | tf_op jit(solution)/shard_map/ppermute | solution.py:683
  40.3 1.3 slice.32
  41.6 1.3 collective-permute-start.2
  43.1 1.0 select_reduce_fusion
  44.3 1.1 slice_bitcast_fusion
  46.0 6.6 %pack.1 = bf16[32,392,128]{2,1,0:T(8,128)(2,1)} custom-call(s32[32]{0:T(128)} %get-tuple-element.73.idx_ref, bf16[16,5,256,128]{3,2,1,0:T(8,128)(2,1)} %bitcast.61, bf16[16,5,256,128]{3,2,1,0:T(8,128)(2,1)} %bitcast.58, bf16[16,5,256,128]{3,2,1,0:T(8,128)(2,1)} %bitcast.59, bf16[16,5,256,128]{3,2,1,0:T(8,128)(2,1)} %bitcast.60, ...), custom_call_target="tpu_custom_call" | custom-call | tf_op jit(solution)/shard_map/pack/pallas_call | solution.py:193
  52.6 4.0 %collective-permute-start.1 = (bf16[16,128]{1,0:T(8,128)(2,1)S(1)}, bf16[16,128]{1,0:T(8,128)(2,1)S(1)}, u32[]{:S(2)}, u32[]{:S(2)}) collective-permute-start(bf16[16,128]{1,0:T(8,128)(2,1)S(1)} %reshape.88), channel_id=1, source_target_pairs={{0,1},{1,2},{2,3},{4,5},{5,6},{6,7},{8,9},{9,10},{10,11},{12,13},{... | collective-permute-start | bytes 12296 | tf_op jit(solution)/shard_map/ppermute | solution.py:683
  56.6 1.3 collective-permute-start.3
  57.9 0.6 gather_fusion
  58.5 0.7 broadcast_select_fusion
  59.2 1.5 collective-permute-done.1
  61.0 5.9 %collective-permute-done.3 = bf16[16,128]{1,0:T(8,128)(2,1)S(1)} collective-permute-done((bf16[16,128]{1,0:T(8,128)(2,1)S(1)}, bf16[16,128]{1,0:T(8,128)(2,1)S(1)}, u32[]{:S(2)}, u32[]{:S(2)}) %collective-permute-start.3) | collective-permute-done | bytes 4128 | tf_op jit(solution)/shard_map/ppermute | solution.py:684
  67.3 0.8 pad.13.up_last_ref
  68.0 0.8 pad.14.down_last_ref
  68.8 15.5 %prepare.1 = (bf16[16,4,144,256]{3,2,1,0:T(8,128)(2,1)}, bf16[16,4,144,128]{3,2,1,0:T(8,128)(2,1)}, bf16[16,4,64,128]{3,2,1,0:T(8,128)(2,1)}) custom-call(bf16[16,5,256,128]{3,2,1,0:T(8,128)(2,1)} %bitcast.73, bf16[16,4,64,128]{3,2,1,0:T(8,128)(2,1)} %collective-permute-done.up_ref, bf16[16,64,128]{2,1,0:T(8,128)(2,1)} %pad.13.up_last_ref, ...), custom_call_target="tpu_custom_call" | custom-call | flops 2560000000 | bytes 16000000 | tf_op jit(solution)/shard_map/prepare/pallas_call | solution.py:359
  84.3 9.9 %all-to-all-done.1.refs_0_.refs_1_.refs_2_.refs_3_.refs_4_.refs_5_.refs_6_.refs_7_.refs_8_.refs_9_.refs_10_.refs_11_.refs_12_.refs_13_.refs_14_.refs_15_.refs_16_.refs_17_.refs_18_.refs_19_.refs_20_.refs_21_.refs_22_.refs_23_.refs_24_.refs_25_.refs_26_.refs_27_.refs_28_.refs_29_.refs_30_.refs_31_.refs_32_ = bf16[32,3,256,128]{3,2,1,0:T(8,128)(2,1)} async-done(((bf16[32,3,256,128]{3,2,1,0:T(8,128)(2,1)}), ...) | async-done | bytes 6291488 | tf_op jit(solution)/shard_map/all_to_all | solution.py:703
  94.2 14.5 %all-to-all-start = ((bf16[32,392,128]{2,1,0:T(8,128)(2,1)}), bf16[32,392,128]{2,1,0:T(8,128)(2,1)S(1)}, u32[]{:S(2)}, u32[]{:S(2)}) async-start(bf16[32,392,128]{2,1,0:T(8,128)(2,1)} %pack.1), calls=%async_computation | async-start | bytes 6422528 | tf_op jit(solution)/shard_map/all_to_all | solution.py:703
  108.8 0.5 fusion.21.slot_ref.refs_0_
  109.3 5.2 %edges.3 = (bf16[16,3,64,128]{3,2,1,0:T(8,128)(2,1)}, bf16[16,3,64,128]{3,2,1,0:T(8,128)(2,1)}, f32[16,3,8,128]{3,2,1,0:T(8,128)}, bf16[16,1,256,128]{3,2,1,0:T(8,128)(2,1)}) custom-call(s32[16]{0:T(128)} %fusion.21.slot_ref.refs_0_, ...), custom_call_target="tpu_custom_call" | custom-call | flops 960000000 | bytes 4800000 | tf_op jit(solution)/shard_map/edges/pallas_call | solution.py:285
  114.5 3.6 %collective-permute-start.7 = (bf16[16,3,64,128]{3,2,1,0:T(8,128)(2,1)}, bf16[16,3,64,128]{3,2,1,0:T(8,128)(2,1)S(1)}, u32[]{:S(2)}, u32[]{:S(2)}) collective-permute-start(bf16[16,3,64,128]{3,2,1,0:T(8,128)(2,1)} %get-tuple-element.48), channel_id=1, source_target_pairs={{0,1},{1,2},{2,3},{4,5},{5,6},{6,7},{8,9},{9,10},{10,11},{12,13},{... | collective-permute-start | bytes 2359304 | tf_op jit(solution)/shard_map/ppermute | solution.py:683
  118.1 1.5 collective-permute-start.8
  119.7 2.3 %copy-done = bf16[16,4,144,256]{3,2,1,0:T(8,128)(2,1)S(1)} copy-done((bf16[16,4,144,256]{3,2,1,0:T(8,128)(2,1)S(1)}, bf16[16,4,144,256]{3,2,1,0:T(8,128)(2,1)}, u32[]{:S(2)}) %copy-start) | copy-done | bytes 4718616
  122.0 1.2 copy-done.2
  123.2 0.9 copy-done.11
  124.1 8.6 %sweep.4 = (f32[16,2,256]{2,1,0:T(2,128)S(1)}, f32[2,32,256]{2,1,0:T(8,128)S(1)}) custom-call(s32[16]{0:T(128)S(1)} %copy-done.34, ...), custom_call_target="tpu_custom_call" | custom-call | flops 3200000000 | bytes 6400000 | tf_op jit(solution)/shard_map/sweep/pallas_call | solution.py:579
  132.7 0.6 copy-done.26
  133.4 0.6 copy-done.32
  134.0 1.1 collective-permute-done.7.refs_43_.refs_44_.refs_15_
  135.1 4.0 %collective-permute-done.8.refs_45_.refs_46_.refs_18_ = bf16[16,3,64,128]{3,2,1,0:T(8,128)(2,1)S(1)} collective-permute-done((bf16[16,3,64,128]{3,2,1,0:T(8,128)(2,1)}, bf16[16,3,64,128]{3,2,1,0:T(8,128)(2,1)S(1)}, u32[]{:S(2)}, u32[]{:S(2)}) %collective-permute-start.8) | collective-permute-done | bytes 786464 | tf_op jit(solution)/shard_map/ppermute | solution.py:684
  139.1 10.1 %sweep.5 = (f32[16,2,256]{2,1,0:T(2,128)S(1)}, f32[2,32,256]{2,1,0:T(8,128)S(1)}) custom-call(s32[16]{0:T(128)S(1)} %copy-done.34, ...), custom_call_target="tpu_custom_call" | custom-call | flops 3200000000 | bytes 6400000 | tf_op jit(solution)/shard_map/sweep/pallas_call | solution.py:579
  149.2 0.9 copy-done.7
  150.1 0.9 copy-done.9
  151.0 0.6 copy-done.28
  151.6 0.6 copy-done.30
  152.2 0.8 copy-done.22
  153.1 0.9 copy-done.23
  154.0 0.8 copy-done.25
  154.9 4.4 %unpack.1 = (bf16[16,2,64,128]{3,2,1,0:T(8,128)(2,1)S(1)}, bf16[16,2,64,128]{3,2,1,0:T(8,128)(2,1)S(1)}, f32[16,2,8,128]{3,2,1,0:T(8,128)S(1)}, bf16[16,2,256,128]{3,2,1,0:T(8,128)(2,1)S(1)}) custom-call(s32[16]{0:T(128)S(1)} %copy-done.34, bf16[32,392,128]{2,1,0:T(8,128)(2,1)S(1)} %all-to-all-done.refs_0_.refs_1_.refs_2_.refs_3_.refs_4_.refs_5_.refs_6_.refs_7_, ...), custom_call_target="tpu_custom_call" | custom-call | tf_op jit(solution)/shard_map/unpack/pallas_call | solution.py:313
  159.3 1.3 collective-permute-start.10
  160.6 4.2 %collective-permute-start.9 = (bf16[16,2,64,128]{3,2,1,0:T(8,128)(2,1)S(1)}, bf16[16,2,64,128]{3,2,1,0:T(8,128)(2,1)S(1)}, u32[]{:S(2)}, u32[]{:S(2)}) collective-permute-start(bf16[16,2,64,128]{3,2,1,0:T(8,128)(2,1)S(1)} %get-tuple-element.60), channel_id=1, source_target_pairs={{0,1},{1,2},{2,3},{4,5},{5,6},{6,7},{8,9},{9,10},{10,11},{12,13},{... | collective-permute-start | bytes 1572872 | tf_op jit(solution)/shard_map/ppermute | solution.py:683
  164.9 2.3 %copy-done.1 = bf16[16,4,144,256]{3,2,1,0:T(8,128)(2,1)S(1)} copy-done((bf16[16,4,144,256]{3,2,1,0:T(8,128)(2,1)S(1)}, bf16[16,4,144,256]{3,2,1,0:T(8,128)(2,1)}, u32[]{:S(2)}) %copy-start.1) | copy-done | bytes 4718616
  167.3 6.5 %sweep.7 = (f32[16,2,256]{2,1,0:T(2,128)S(1)}, f32[2,32,256]{2,1,0:T(8,128)S(1)}) custom-call(s32[16]{0:T(128)S(1)} %copy-done.34, bf16[16,1,256,128]{3,2,1,0:T(8,128)(2,1)S(1)} %copy-done.13, bf16[16,2,256,128]{3,2,1,0:T(8,128)(2,1)S(1)} %get-tuple-element.58.refs_2_.refs_3_, bf16[16,2,256,128]{3,2,1,0:T(8,128)(2,1)S(1)} %get-tuple-element.58.refs_2_.refs_3_, ...), custom_call_target="tpu_custom_call" | custom-call | flops 3200000000 | bytes 6400000 | tf_op jit(solution)/shard_map/sweep/pallas_call | solution.py:579
  173.8 0.5 collective-permute-done.9.refs_16_.refs_17_
  174.3 8.4 %sweep.6 = (f32[16,2,256]{2,1,0:T(2,128)S(1)}, f32[2,32,256]{2,1,0:T(8,128)S(1)}) custom-call(s32[16]{0:T(128)S(1)} %copy-done.34, bf16[16,1,256,128]{3,2,1,0:T(8,128)(2,1)S(1)} %copy-done.13, bf16[16,2,256,128]{3,2,1,0:T(8,128)(2,1)S(1)} %get-tuple-element.58.refs_2_.refs_3_, bf16[16,2,256,128]{3,2,1,0:T(8,128)(2,1)S(1)} %get-tuple-element.58.refs_2_.refs_3_, ...), custom_call_target="tpu_custom_call" | custom-call | flops 3200000000 | bytes 6400000 | tf_op jit(solution)/shard_map/sweep/pallas_call | solution.py:579
  182.8 2.6 %collect.1 = f32[4,128,256]{2,1,0:T(8,128)} custom-call(s32[4,128]{1,0:T(4,128)S(1)} %fusion.8.list_ref, s32[4]{0:T(128)S(1)} %bitcast.48, f32[2,32,256]{2,1,0:T(8,128)S(1)} %copy-done.27, f32[2,32,256]{2,1,0:T(8,128)S(1)} %get-tuple-element.67.b_ref, f32[2,32,256]{2,1,0:T(8,128)S(1)} %copy-done.29, f32[2,32,256]{2,1,0:T(8,128)S(1)} %get-tuple-element.69.d_ref), custom_call_target="tpu_custom_call" | custom-call | tf_op jit(solution)/shard_map/collect/pallas_call | solution.py:635
  185.5 5.2 %all-to-all-start.2 = ((f32[4,128,256]{2,1,0:T(8,128)}), f32[4,128,256]{2,1,0:T(8,128)S(1)}, u32[]{:S(2)}, u32[]{:S(2)}) async-start(f32[4,128,256]{2,1,0:T(8,128)} %collect.1), calls=%async_computation.2 | async-start | bytes 1048576 | tf_op jit(solution)/shard_map/all_to_all | solution.py:769
  190.7 6.8 %all-to-all-done.2.got_ref = f32[4,128,256]{2,1,0:T(8,128)S(1)} async-done(((f32[4,128,256]{2,1,0:T(8,128)}), f32[4,128,256]{2,1,0:T(8,128)S(1)}, u32[]{:S(2)}, u32[]{:S(2)}) %all-to-all-start.2) | async-done | bytes 524320 | tf_op jit(solution)/shard_map/all_to_all | solution.py:769
  197.6 2.5 %place.1 = f32[512,256]{1,0:T(8,128)} custom-call(s32[4,128]{1,0:T(4,128)S(1)} %slice.36.slot_ref, s32[4]{0:T(128)S(1)} %slice_reduce_fusion.count_ref, f32[4,128,256]{2,1,0:T(8,128)S(1)} %all-to-all-done.2.got_ref), custom_call_target="tpu_custom_call" | custom-call | tf_op jit(solution)/shard_map/place/pallas_call | solution.py:667
  200.0 11.0 %all-to-all-start.3 = ((f32[32,16,256]{2,1,0:T(8,128)}), f32[32,16,256]{2,1,0:T(8,128)S(1)}, u32[]{:S(2)}, u32[]{:S(2)}) async-start(f32[32,16,256]{2,1,0:T(8,128)} %bitcast.19), calls=%async_computation.3 | async-start | bytes 1048576 | tf_op jit(solution)/shard_map/all_to_all | solution.py:703
  211.1 0.7 pad_maximum_fusion
  211.9 10.8 %all-to-all-done.3 = f32[32,16,256]{2,1,0:T(8,128)S(1)} async-done(((f32[32,16,256]{2,1,0:T(8,128)}), f32[32,16,256]{2,1,0:T(8,128)S(1)}, u32[]{:S(2)}, u32[]{:S(2)}) %all-to-all-start.3) | async-done | bytes 524320 | tf_op jit(solution)/shard_map/all_to_all | solution.py:703
  222.7 0.6 fusion.5
  (114 shorter events, 2.1 us)
Async XLA Ops:
  7.6 8.7 %copy-start.35 = (s32[1,1,4]{2,1,0:T(1,128)S(1)}, s32[1,1,4]{2,1,0:T(1,128)}, u32[]{:S(2)}) copy-start(s32[1,1,4]{2,1,0:T(1,128)} %param.41) | copy-start | bytes 52
  7.6 8.8 %copy-start.41 = (s32[1,1,4,128]{3,2,1,0:T(4,128)S(1)}, s32[1,1,4,128]{3,2,1,0:T(4,128)}, u32[]{:S(2)}) copy-start(s32[1,1,4,128]{3,2,1,0:T(4,128)} %param.40) | copy-start | bytes 6148
  7.6 86.6 %all-to-all-start.1 = ((bf16[32,3,256,128]{3,2,1,0:T(8,128)(2,1)}), bf16[32,3,256,128]{3,2,1,0:T(8,128)(2,1)}, u32[]{:S(2)}, u32[]{:S(2)}) async-start(bf16[32,3,256,128]{3,2,1,0:T(8,128)(2,1)} %bitcast.74), calls=%async_computation.1 | async-start | bytes 12582912 | tf_op jit(solution)/shard_map/all_to_all | solution.py:703
  16.4 36.2 %collective-permute-start.4 = (s32[1,256]{1,0:T(1,128)S(1)}, s32[1,256]{1,0:T(1,128)S(1)}, u32[]{:S(2)}, u32[]{:S(2)}) collective-permute-start(s32[1,256]{1,0:T(1,128)S(1)} %get-tuple-element.75), channel_id=1, source_target_pairs={{0,1},{1,2},{2,3},{3,0},{4,5},{5,6},{6,7},{7,4},{8,9},{9,10},{10,1... | collective-permute-start | bytes 3080 | tf_op jit(solution)/shard_map/ppermute | solution.py:733
  18.1 38.5 %collective-permute-start.5 = (s32[1,256]{1,0:T(1,128)S(1)}, s32[1,256]{1,0:T(1,128)S(1)}, u32[]{:S(2)}, u32[]{:S(2)}) collective-permute-start(s32[1,256]{1,0:T(1,128)S(1)} %get-tuple-element.76), channel_id=1, source_target_pairs={{0,2},{1,3},{2,0},{3,1},{4,6},{5,7},{6,4},{7,5},{8,10},{9,11},{10,... | collective-permute-start | bytes 3080 | tf_op jit(solution)/shard_map/ppermute | solution.py:733
  21.4 36.5 %collective-permute-start.6 = (s32[1,256]{1,0:T(1,128)S(1)}, s32[1,256]{1,0:T(1,128)S(1)}, u32[]{:S(2)}, u32[]{:S(2)}) collective-permute-start(s32[1,256]{1,0:T(1,128)S(1)} %get-tuple-element.77), channel_id=1, source_target_pairs={{0,3},{1,0},{2,1},{3,2},{4,7},{5,4},{6,5},{7,6},{8,11},{9,8},{10,9... | collective-permute-start | bytes 3080 | tf_op jit(solution)/shard_map/ppermute | solution.py:733
  29.0 14.0 %copy-start.38 = (s32[16,4,512]{2,1,0:T(4,128)S(1)}, s32[16,4,512]{2,1,0:T(4,128)}, u32[]{:S(2)}) copy-start(s32[16,4,512]{2,1,0:T(4,128)} %index_ref.1) | copy-start | bytes 393220
  29.0 14.1 %copy-start.40 = (f32[64]{0:T(128)S(1)}, f32[64]{0:T(128)}, u32[]{:S(2)}) copy-start(f32[64]{0:T(128)} %param.34) | copy-start | bytes 772
  35.3 8.9 %copy-start.44 = (bf16[1,128]{1,0:T(2,128)(2,1)S(1)}, bf16[1,128]{1,0:T(2,128)(2,1)}, u32[]{:S(2)}) copy-start(bf16[1,128]{1,0:T(2,128)(2,1)} %constant.271) | copy-start | bytes 772
  35.3 8.9 %copy-start.45 = (bf16[1,128]{1,0:T(2,128)(2,1)S(1)}, bf16[1,128]{1,0:T(2,128)(2,1)}, u32[]{:S(2)}) copy-start(bf16[1,128]{1,0:T(2,128)(2,1)} %constant.272) | copy-start | bytes 772
  35.3 8.9 %copy-start.37 = (f32[16,4,512]{2,1,0:T(4,128)S(1)}, f32[16,4,512]{2,1,0:T(4,128)}, u32[]{:S(2)}) copy-start(f32[16,4,512]{2,1,0:T(4,128)} %param.36) | copy-start | bytes 393220
  35.3 8.9 %copy-start.43 = (f32[16]{0:T(128)S(1)}, f32[16]{0:T(128)}, u32[]{:S(2)}) copy-start(f32[16]{0:T(128)} %param.35) | copy-start | bytes 196
  36.7 32.2 %collective-permute-start = (bf16[16,4,64,128]{3,2,1,0:T(8,128)(2,1)S(1)}, bf16[16,4,64,128]{3,2,1,0:T(8,128)(2,1)}, u32[]{:S(2)}, u32[]{:S(2)}) collective-permute-start(bf16[16,4,64,128]{3,2,1,0:T(8,128)(2,1)S(1)} %slice.30), channel_id=1, source_target_pairs={{0,1},{1,2},{2,3},{4,5},{5,6},{6,7},{8,9},{9,10},{10,11},{12,13},{... | collective-permute-start | bytes 3145736 | tf_op jit(solution)/shard_map/ppermute | solution.py:683
  41.6 27.2 %collective-permute-start.2 = (bf16[16,4,64,128]{3,2,1,0:T(8,128)(2,1)S(1)}, bf16[16,4,64,128]{3,2,1,0:T(8,128)(2,1)}, u32[]{:S(2)}, u32[]{:S(2)}) collective-permute-start(bf16[16,4,64,128]{3,2,1,0:T(8,128)(2,1)S(1)} %slice.32), channel_id=1, source_target_pairs={{1,0},{2,1},{3,2},{5,4},{6,5},{7,6},{9,8},{10,9},{11,10},{13,12},{... | collective-permute-start | bytes 3145736 | tf_op jit(solution)/shard_map/ppermute | solution.py:684
  52.6 8.1 %collective-permute-start.1 = (bf16[16,128]{1,0:T(8,128)(2,1)S(1)}, bf16[16,128]{1,0:T(8,128)(2,1)S(1)}, u32[]{:S(2)}, u32[]{:S(2)}) collective-permute-start(bf16[16,128]{1,0:T(8,128)(2,1)S(1)} %reshape.88), channel_id=1, source_target_pairs={{0,1},{1,2},{2,3},{4,5},{5,6},{6,7},{8,9},{9,10},{10,11},{12,13},{... | collective-permute-start | bytes 12296 | tf_op jit(solution)/shard_map/ppermute | solution.py:683
  56.6 10.3 %collective-permute-start.3 = (bf16[16,128]{1,0:T(8,128)(2,1)S(1)}, bf16[16,128]{1,0:T(8,128)(2,1)S(1)}, u32[]{:S(2)}, u32[]{:S(2)}) collective-permute-start(bf16[16,128]{1,0:T(8,128)(2,1)S(1)} %reshape.90), channel_id=1, source_target_pairs={{1,0},{2,1},{3,2},{5,4},{6,5},{7,6},{9,8},{10,9},{11,10},{13,12},{... | collective-permute-start | bytes 12296 | tf_op jit(solution)/shard_map/ppermute | solution.py:684
  94.2 58.0 %all-to-all-start = ((bf16[32,392,128]{2,1,0:T(8,128)(2,1)}), bf16[32,392,128]{2,1,0:T(8,128)(2,1)S(1)}, u32[]{:S(2)}, u32[]{:S(2)}) async-start(bf16[32,392,128]{2,1,0:T(8,128)(2,1)} %pack.1), calls=%async_computation | async-start | bytes 6422528 | tf_op jit(solution)/shard_map/all_to_all | solution.py:703
  109.3 10.3 %copy-start.14 = (s32[16,4,512]{2,1,0:T(4,128)S(1)}, s32[16,4,512]{2,1,0:T(4,128)}, u32[]{:S(2)}) copy-start(s32[16,4,512]{2,1,0:T(4,128)} %refs_11_.4) | copy-start | bytes 393220
  109.3 10.3 %copy-start.17 = (bf16[128,768]{1,0:T(8,128)(2,1)S(1)}, bf16[128,768]{1,0:T(8,128)(2,1)}, u32[]{:S(2)}) copy-start(bf16[128,768]{1,0:T(8,128)(2,1)} %constant.165.clone.refs_35_.refs_6_) | copy-start | bytes 589828
  109.3 10.3 %copy-start.20 = (bf16[128,128]{1,0:T(8,128)(2,1)S(1)}, bf16[128,128]{1,0:T(8,128)(2,1)}, u32[]{:S(2)}) copy-start(bf16[128,128]{1,0:T(8,128)(2,1)} %constant.162.clone.flip_ref.refs_38_.refs_9_) | copy-start | bytes 98308
  109.3 10.3 %copy-start.24 = (bf16[16,256]{1,0:T(8,128)(2,1)S(1)}, bf16[16,256]{1,0:T(8,128)(2,1)}, u32[]{:S(2)}) copy-start(bf16[16,256]{1,0:T(8,128)(2,1)} %constant.166.clone.refs_36_.refs_7_) | copy-start | bytes 24580
  109.3 10.3 %copy-start.34 = (s32[16]{0:T(128)S(1)}, s32[16]{0:T(128)}, u32[]{:S(2)}) copy-start(s32[16]{0:T(128)} %fusion.21.slot_ref.refs_0_) | copy-start | bytes 196
  114.5 20.5 %collective-permute-start.7 = (bf16[16,3,64,128]{3,2,1,0:T(8,128)(2,1)}, bf16[16,3,64,128]{3,2,1,0:T(8,128)(2,1)S(1)}, u32[]{:S(2)}, u32[]{:S(2)}) collective-permute-start(bf16[16,3,64,128]{3,2,1,0:T(8,128)(2,1)} %get-tuple-element.48), channel_id=1, source_target_pairs={{0,1},{1,2},{2,3},{4,5},{5,6},{6,7},{8,9},{9,10},{10,11},{12,13},{... | collective-permute-start | bytes 2359304 | tf_op jit(solution)/shard_map/ppermute | solution.py:683
  118.1 21.0 %collective-permute-start.8 = (bf16[16,3,64,128]{3,2,1,0:T(8,128)(2,1)}, bf16[16,3,64,128]{3,2,1,0:T(8,128)(2,1)S(1)}, u32[]{:S(2)}, u32[]{:S(2)}) collective-permute-start(bf16[16,3,64,128]{3,2,1,0:T(8,128)(2,1)} %get-tuple-element.49), channel_id=1, source_target_pairs={{1,0},{2,1},{3,2},{5,4},{6,5},{7,6},{9,8},{10,9},{11,10},{13,12},{... | collective-permute-start | bytes 2359304 | tf_op jit(solution)/shard_map/ppermute | solution.py:684
  119.7 2.3 %copy-start = (bf16[16,4,144,256]{3,2,1,0:T(8,128)(2,1)S(1)}, bf16[16,4,144,256]{3,2,1,0:T(8,128)(2,1)}, u32[]{:S(2)}) copy-start(bf16[16,4,144,256]{3,2,1,0:T(8,128)(2,1)} %get-tuple-element.43.refs_33_.refs_4_) | copy-start | bytes 14155780
  122.0 1.2 copy-start.2
  123.2 0.9 copy-start.11
  124.1 15.0 %copy-start.3 = (bf16[16,4,64,128]{3,2,1,0:T(8,128)(2,1)S(1)}, bf16[16,4,64,128]{3,2,1,0:T(8,128)(2,1)}, u32[]{:S(2)}) copy-start(bf16[16,4,64,128]{3,2,1,0:T(8,128)(2,1)} %get-tuple-element.44.refs_34_.refs_5_) | copy-start | bytes 3145732
  124.1 15.0 %copy-start.5 = (bf16[16,4,144,128]{3,2,1,0:T(8,128)(2,1)S(1)}, bf16[16,4,144,128]{3,2,1,0:T(8,128)(2,1)}, u32[]{:S(2)}) copy-start(bf16[16,4,144,128]{3,2,1,0:T(8,128)(2,1)} %get-tuple-element.53.refs_47_.refs_21_) | copy-start | bytes 7077892
  124.1 15.0 %copy-start.15 = (bf16[128,768]{1,0:T(8,128)(2,1)S(1)}, bf16[128,768]{1,0:T(8,128)(2,1)}, u32[]{:S(2)}) copy-start(bf16[128,768]{1,0:T(8,128)(2,1)} %constant.167.clone.refs_35_.refs_6_) | copy-start | bytes 589828
  132.7 0.6 copy-start.26
  133.4 0.6 copy-start.32
  139.1 13.1 %copy-start.19 = (bf16[128,256]{1,0:T(8,128)(2,1)S(1)}, bf16[128,256]{1,0:T(8,128)(2,1)}, u32[]{:S(2)}) copy-start(bf16[128,256]{1,0:T(8,128)(2,1)} %constant.160.clone.refs_8_.refs_11_) | copy-start | bytes 196612
  149.2 0.9 copy-start.7
  150.1 0.9 copy-start.9
  151.0 0.6 copy-start.28
  151.6 0.6 copy-start.30
  152.2 0.8 copy-start.22
  153.1 0.9 copy-start.23
  154.0 0.8 copy-start.25
  154.8 10.0 %copy-start.42 = (s32[1,1,4,128]{3,2,1,0:T(4,128)S(1)}, s32[1,1,4,128]{3,2,1,0:T(4,128)}, u32[]{:S(2)}) copy-start(s32[1,1,4,128]{3,2,1,0:T(4,128)} %param.39) | copy-start | bytes 6148
  154.8 10.0 %copy-start.4 = (bf16[16,4,64,128]{3,2,1,0:T(8,128)(2,1)S(1)}, bf16[16,4,64,128]{3,2,1,0:T(8,128)(2,1)}, u32[]{:S(2)}) copy-start(bf16[16,4,64,128]{3,2,1,0:T(8,128)(2,1)} %get-tuple-element.44.refs_34_.refs_5_) | copy-start | bytes 3145732
  154.8 10.0 %copy-start.12 = (f32[16,3,8,128]{3,2,1,0:T(8,128)S(1)}, f32[16,3,8,128]{3,2,1,0:T(8,128)}, u32[]{:S(2)}) copy-start(f32[16,3,8,128]{3,2,1,0:T(8,128)} %get-tuple-element.47.refs_41_.refs_42_.refs_12_) | copy-start | bytes 589828
  154.8 10.1 %copy-start.13 = (bf16[16,1,256,128]{3,2,1,0:T(8,128)(2,1)S(1)}, bf16[16,1,256,128]{3,2,1,0:T(8,128)(2,1)}, u32[]{:S(2)}) copy-start(bf16[16,1,256,128]{3,2,1,0:T(8,128)(2,1)} %get-tuple-element.56.refs_1_) | copy-start | bytes 3145732
  154.8 10.1 %copy-start.18 = (bf16[128,768]{1,0:T(8,128)(2,1)S(1)}, bf16[128,768]{1,0:T(8,128)(2,1)}, u32[]{:S(2)}) copy-start(bf16[128,768]{1,0:T(8,128)(2,1)} %constant.165.clone.refs_35_.refs_6_) | copy-start | bytes 589828
  154.9 10.1 %copy-start.21 = (bf16[128,128]{1,0:T(8,128)(2,1)S(1)}, bf16[128,128]{1,0:T(8,128)(2,1)}, u32[]{:S(2)}) copy-start(bf16[128,128]{1,0:T(8,128)(2,1)} %constant.162.clone.flip_ref.refs_38_.refs_9_) | copy-start | bytes 98308
  159.3 14.5 %collective-permute-start.10 = (bf16[16,2,64,128]{3,2,1,0:T(8,128)(2,1)S(1)}, bf16[16,2,64,128]{3,2,1,0:T(8,128)(2,1)S(1)}, u32[]{:S(2)}, u32[]{:S(2)}) collective-permute-start(bf16[16,2,64,128]{3,2,1,0:T(8,128)(2,1)S(1)} %get-tuple-element.61), channel_id=1, source_target_pairs={{1,0},{2,1},{3,2},{5,4},{6,5},{7,6},{9,8},{10,9},{11,10},{13,12},{... | collective-permute-start | bytes 1572872 | tf_op jit(solution)/shard_map/ppermute | solution.py:684
  160.6 13.7 %collective-permute-start.9 = (bf16[16,2,64,128]{3,2,1,0:T(8,128)(2,1)S(1)}, bf16[16,2,64,128]{3,2,1,0:T(8,128)(2,1)S(1)}, u32[]{:S(2)}, u32[]{:S(2)}) collective-permute-start(bf16[16,2,64,128]{3,2,1,0:T(8,128)(2,1)S(1)} %get-tuple-element.60), channel_id=1, source_target_pairs={{0,1},{1,2},{2,3},{4,5},{5,6},{6,7},{8,9},{9,10},{10,11},{12,13},{... | collective-permute-start | bytes 1572872 | tf_op jit(solution)/shard_map/ppermute | solution.py:683
  164.9 2.3 %copy-start.1 = (bf16[16,4,144,256]{3,2,1,0:T(8,128)(2,1)S(1)}, bf16[16,4,144,256]{3,2,1,0:T(8,128)(2,1)}, u32[]{:S(2)}) copy-start(bf16[16,4,144,256]{3,2,1,0:T(8,128)(2,1)} %get-tuple-element.43.refs_33_.refs_4_) | copy-start | bytes 14155780
  167.3 7.1 %copy-start.6 = (bf16[16,4,144,128]{3,2,1,0:T(8,128)(2,1)S(1)}, bf16[16,4,144,128]{3,2,1,0:T(8,128)(2,1)}, u32[]{:S(2)}) copy-start(bf16[16,4,144,128]{3,2,1,0:T(8,128)(2,1)} %get-tuple-element.53.refs_47_.refs_21_) | copy-start | bytes 7077892
  167.3 7.1 %copy-start.8 = (bf16[16,3,64,128]{3,2,1,0:T(8,128)(2,1)S(1)}, bf16[16,3,64,128]{3,2,1,0:T(8,128)(2,1)}, u32[]{:S(2)}) copy-start(bf16[16,3,64,128]{3,2,1,0:T(8,128)(2,1)} %copy-done.7) | copy-start | bytes 2359300
  167.3 7.1 %copy-start.10 = (bf16[16,3,64,128]{3,2,1,0:T(8,128)(2,1)S(1)}, bf16[16,3,64,128]{3,2,1,0:T(8,128)(2,1)}, u32[]{:S(2)}) copy-start(bf16[16,3,64,128]{3,2,1,0:T(8,128)(2,1)} %copy-done.9) | copy-start | bytes 2359300
  167.3 7.1 %copy-start.16 = (bf16[128,768]{1,0:T(8,128)(2,1)S(1)}, bf16[128,768]{1,0:T(8,128)(2,1)}, u32[]{:S(2)}) copy-start(bf16[128,768]{1,0:T(8,128)(2,1)} %constant.167.clone.refs_35_.refs_6_) | copy-start | bytes 589828
  173.8 9.0 %copy-start.27 = (f32[2,32,256]{2,1,0:T(8,128)S(1)}, f32[2,32,256]{2,1,0:T(8,128)}, u32[]{:S(2)}) copy-start(f32[2,32,256]{2,1,0:T(8,128)} %copy-done.26) | copy-start | bytes 196612
  173.8 9.0 %copy-start.29 = (f32[2,32,256]{2,1,0:T(8,128)S(1)}, f32[2,32,256]{2,1,0:T(8,128)}, u32[]{:S(2)}) copy-start(f32[2,32,256]{2,1,0:T(8,128)} %copy-done.28) | copy-start | bytes 196612
  173.8 9.0 %copy-start.36 = (s32[1,1,4]{2,1,0:T(1,128)S(1)}, s32[1,1,4]{2,1,0:T(1,128)}, u32[]{:S(2)}) copy-start(s32[1,1,4]{2,1,0:T(1,128)} %param.41) | copy-start | bytes 52
  173.8 16.8 %copy-start.39 = (s32[4,256]{1,0:T(4,128)S(1)}, s32[4,256]{1,0:T(4,128)}, u32[]{:S(2)}) copy-start(s32[4,256]{1,0:T(4,128)} %broadcast_select_fusion) | copy-start | bytes 12292
  173.8 37.2 %copy-start.31 = (f32[16,2,256]{2,1,0:T(2,128)S(1)}, f32[16,2,256]{2,1,0:T(2,128)}, u32[]{:S(2)}) copy-start(f32[16,2,256]{2,1,0:T(2,128)} %copy-done.30) | copy-start | bytes 98308
  173.8 37.3 %copy-start.33 = (f32[16,2,256]{2,1,0:T(2,128)S(1)}, f32[16,2,256]{2,1,0:T(2,128)}, u32[]{:S(2)}) copy-start(f32[16,2,256]{2,1,0:T(2,128)} %copy-done.32) | copy-start | bytes 98308
  185.5 12.1 %all-to-all-start.2 = ((f32[4,128,256]{2,1,0:T(8,128)}), f32[4,128,256]{2,1,0:T(8,128)S(1)}, u32[]{:S(2)}, u32[]{:S(2)}) async-start(f32[4,128,256]{2,1,0:T(8,128)} %collect.1), calls=%async_computation.2 | async-start | bytes 1048576 | tf_op jit(solution)/shard_map/all_to_all | solution.py:769
  200.0 22.6 %all-to-all-start.3 = ((f32[32,16,256]{2,1,0:T(8,128)}), f32[32,16,256]{2,1,0:T(8,128)S(1)}, u32[]{:S(2)}, u32[]{:S(2)}) async-start(f32[32,16,256]{2,1,0:T(8,128)} %bitcast.19), calls=%async_computation.3 | async-start | bytes 1048576 | tf_op jit(solution)/shard_map/all_to_all | solution.py:703

commit v9 on v8

--- a/solution.py
+++ b/solution.py
@@ -592,7 +592,7 @@
             jax.ShapeDtypeStruct((images, count, steps * 128), F32),
             jax.ShapeDtypeStruct((steps, images * count, 256), F32),
         ],
-        compiler_params=LATE,
+        compiler_params=LATE if late or halo else PARAMS,
         cost_estimate=pl.CostEstimate(
             flops=work * 200_000_000, bytes_accessed=work * 400_000, transcendentals=0
         ),

time: 225 us -> 230 us (1.022)
  waiting for transfers between devices: 40.6 us -> 43.7 us
    ppermute x4, waiting for transfers between devices: 3.12 us -> 5.57 us  [neighbour_rows(): above = lax.ppermute(tail, 'tile', [(i, i + 1) for i in range(count - 1)])]
    unnamed x94 -> x82, local copies, waits for them, and re-layouts: 13.9 us -> 12.4 us
  transfers between devices with their start and end apart: 15 -> 15, of which waited for: 8 -> 8; matrix products, arithmetic and copies ran while one was open for 5% -> 6% of each run, Pallas kernels for 29% -> 29%
where the time goes in v9:
time: 230 us; the launch traced here: 228 us
  Pallas kernels  89.6 us (39%)
  starting transfers between devices  66.4 us (29%)
  waiting for transfers between devices  43.7 us (19%)
  local copies, waits for them, and re-layouts  22.2 us (10%)
  other arithmetic  5.19 us (2%)
    pallas_call x4, Pallas kernels, sweep_steps(): pl.pallas_call(functools.partial(sweep_kernel, group, ys, halo, late), gr...  34.9 us
    all_to_all x3, starting transfers between devices, exchange(): return lax.all_to_all(a, 'img', split_axis=0, concat_axis=0, tiled=True)  34.4 us
    all_to_all x3, waiting for transfers between devices, exchange(): return lax.all_to_all(a, 'img', split_axis=0, concat_axis=0, tiled=True)  20.7 us
    ppermute x4, starting transfers between devices, neighbour_rows(): above = lax.ppermute(tail, 'tile', [(i, i + 1) for i in range(count - 1)])  16.3 us
    pallas_call x1, Pallas kernels, prepare(): pl.pallas_call(prepare_kernel, grid=(images,), in_specs=[pl.BlockSpec((1,...  15.5 us
    unnamed x82, local copies, waits for them, and re-layouts  12.4 us
    pallas_call x2, Pallas kernels, pick(): pl.pallas_call(kernel, grid_spec=pltpu.PrefetchScalarGridSpec(num_scalar_...  11.4 us
    pallas_call x2, Pallas kernels, edges(): pl.pallas_call(edge_kernel, grid_spec=pltpu.PrefetchScalarGridSpec(num_sc...  11.3 us
  transfers between devices with their start and end apart: 15, of which 8 were waited for; matrix products, arithmetic and copies ran while one was open for 6% of the time, Pallas kernels for 29%

profile of v9, /device:TPU:1, one launch (start us, length us, event | category | flops | bytes accessed | tf_op | source)
XLA Modules:
  0.0 228.5 jit_solution(14804073579490166231)
XLA Ops:
  0.6 0.8 reshape.86
  1.4 0.7 add_select_fusion.1
  2.1 5.6 %pick.3 = bf16[32,3,64,4,128]{4,3,2,1,0:T(4,128)(2,1)} custom-call(s32[32]{0:T(128)} %get-tuple-element.73.idx_ref, bf16[16,64,4,768]{3,2,1,0:T(4,128)(2,1)} %features_ref.3), custom_call_target="tpu_custom_call" | custom-call | bytes 12582912 | tf_op jit(solution)/shard_map/pick/pallas_call | solution.py:136
  7.8 8.6 %all-to-all-start.1 = ((bf16[32,3,256,128]{3,2,1,0:T(8,128)(2,1)}), bf16[32,3,256,128]{3,2,1,0:T(8,128)(2,1)}, u32[]{:S(2)}, u32[]{:S(2)}) async-start(bf16[32,3,256,128]{3,2,1,0:T(8,128)(2,1)} %bitcast.74), calls=%async_computation.1 | async-start | bytes 12582912 | tf_op jit(solution)/shard_map/all_to_all | solution.py:703
  16.5 1.7 collective-permute-start.4
  18.2 3.3 %collective-permute-start.5 = (s32[1,256]{1,0:T(1,128)S(1)}, s32[1,256]{1,0:T(1,128)S(1)}, u32[]{:S(2)}, u32[]{:S(2)}) collective-permute-start(s32[1,256]{1,0:T(1,128)S(1)} %get-tuple-element.76), channel_id=1, source_target_pairs={{0,2},{1,3},{2,0},{3,1},{4,6},{5,7},{6,4},{7,5},{8,10},{9,11},{10,... | collective-permute-start | bytes 3080 | tf_op jit(solution)/shard_map/ppermute | solution.py:733
  21.5 0.7 collective-permute-start.6
  22.2 0.5 iota.15.idx_ref
  22.8 5.8 %pick.2 = bf16[16,5,64,4,128]{4,3,2,1,0:T(4,128)(2,1)} custom-call(s32[16]{0:T(128)} %iota.15.idx_ref, bf16[16,64,4,768]{3,2,1,0:T(4,128)(2,1)} %features_ref.3), custom_call_target="tpu_custom_call" | custom-call | bytes 10485760 | tf_op jit(solution)/shard_map/pick/pallas_call | solution.py:136
  28.6 0.5 iota.16.slot_ref
  29.1 6.3 %edges.2 = (bf16[16,5,64,128]{3,2,1,0:T(8,128)(2,1)}, bf16[16,5,64,128]{3,2,1,0:T(8,128)(2,1)}, f32[16,5,8,128]{3,2,1,0:T(8,128)}) custom-call(s32[16]{0:T(128)} %iota.16.slot_ref, bf16[16,5,256,128]{3,2,1,0:T(8,128)(2,1)} %bitcast.49, bf16[16,5,256,128]{3,2,1,0:T(8,128)(2,1)} %bitcast.50, bf16[16,5,256,128]{3,2,1,0:T(8,128)(2,1)} %bitcast.51, ...), custom_call_target="tpu_custom_call" | custom-call | flops 1600000000 | bytes 8000000 | tf_op jit(solution)/shard_map/edges/pallas_call | solution.py:285
  35.4 1.4 slice.30
  36.8 3.6 %collective-permute-start = (bf16[16,4,64,128]{3,2,1,0:T(8,128)(2,1)S(1)}, bf16[16,4,64,128]{3,2,1,0:T(8,128)(2,1)}, u32[]{:S(2)}, u32[]{:S(2)}) collective-permute-start(bf16[16,4,64,128]{3,2,1,0:T(8,128)(2,1)S(1)} %slice.30), channel_id=1, source_target_pairs={{0,1},{1,2},{2,3},{4,5},{5,6},{6,7},{8,9},{9,10},{10,11},{12,13},{... | collective-permute-start | bytes 3145736 | tf_op jit(solution)/shard_map/ppermute | solution.py:683
  40.4 1.3 slice.32
  41.7 1.3 collective-permute-start.2
  43.2 1.0 select_reduce_fusion
  44.3 0.6 pad_maximum_fusion.1.refs_37_.refs_8_
  44.9 0.8 fusion.refs_39_.refs_10_
  45.7 1.1 slice_bitcast_fusion
  47.3 6.5 %pack.1 = bf16[32,392,128]{2,1,0:T(8,128)(2,1)} custom-call(s32[32]{0:T(128)} %get-tuple-element.73.idx_ref, bf16[16,5,256,128]{3,2,1,0:T(8,128)(2,1)} %bitcast.61, bf16[16,5,256,128]{3,2,1,0:T(8,128)(2,1)} %bitcast.58, bf16[16,5,256,128]{3,2,1,0:T(8,128)(2,1)} %bitcast.59, bf16[16,5,256,128]{3,2,1,0:T(8,128)(2,1)} %bitcast.60, ...), custom_call_target="tpu_custom_call" | custom-call | tf_op jit(solution)/shard_map/pack/pallas_call | solution.py:193
  53.8 4.0 %collective-permute-start.1 = (bf16[16,128]{1,0:T(8,128)(2,1)S(1)}, bf16[16,128]{1,0:T(8,128)(2,1)S(1)}, u32[]{:S(2)}, u32[]{:S(2)}) collective-permute-start(bf16[16,128]{1,0:T(8,128)(2,1)S(1)} %reshape.88), channel_id=1, source_target_pairs={{0,1},{1,2},{2,3},{4,5},{5,6},{6,7},{8,9},{9,10},{10,11},{12,13},{... | collective-permute-start | bytes 12296 | tf_op jit(solution)/shard_map/ppermute | solution.py:683
  57.9 1.3 collective-permute-start.3
  59.2 0.6 gather_fusion
  59.8 0.7 broadcast_select_fusion
  60.4 0.4 collective-permute-done.1
  60.9 0.2 copy.39
  61.1 5.9 %collective-permute-done.3 = bf16[16,128]{1,0:T(8,128)(2,1)S(1)} collective-permute-done((bf16[16,128]{1,0:T(8,128)(2,1)S(1)}, bf16[16,128]{1,0:T(8,128)(2,1)S(1)}, u32[]{:S(2)}, u32[]{:S(2)}) %collective-permute-start.3) | collective-permute-done | bytes 4128 | tf_op jit(solution)/shard_map/ppermute | solution.py:684
  67.4 0.8 pad.13.up_last_ref
  68.1 0.8 pad.14.down_last_ref
  68.9 15.5 %prepare.1 = (bf16[16,4,144,256]{3,2,1,0:T(8,128)(2,1)}, bf16[16,4,144,128]{3,2,1,0:T(8,128)(2,1)}, bf16[16,4,64,128]{3,2,1,0:T(8,128)(2,1)}) custom-call(bf16[16,5,256,128]{3,2,1,0:T(8,128)(2,1)} %bitcast.73, bf16[16,4,64,128]{3,2,1,0:T(8,128)(2,1)} %collective-permute-done.up_ref, bf16[16,64,128]{2,1,0:T(8,128)(2,1)} %pad.13.up_last_ref, ...), custom_call_target="tpu_custom_call" | custom-call | flops 2560000000 | bytes 16000000 | tf_op jit(solution)/shard_map/prepare/pallas_call | solution.py:359
  84.4 9.9 %all-to-all-done.1.refs_0_.refs_1_.refs_2_.refs_3_.refs_4_.refs_5_.refs_6_.refs_7_.refs_8_.refs_9_.refs_10_.refs_11_.refs_12_.refs_13_.refs_14_.refs_15_.refs_16_.refs_17_.refs_18_.refs_19_.refs_20_.refs_21_.refs_22_.refs_23_.refs_24_.refs_25_.refs_26_.refs_27_.refs_28_.refs_29_.refs_30_.refs_31_.refs_32_ = bf16[32,3,256,128]{3,2,1,0:T(8,128)(2,1)} async-done(((bf16[32,3,256,128]{3,2,1,0:T(8,128)(2,1)}), ...) | async-done | bytes 6291488 | tf_op jit(solution)/shard_map/all_to_all | solution.py:703
  94.3 14.5 %all-to-all-start = ((bf16[32,392,128]{2,1,0:T(8,128)(2,1)}), bf16[32,392,128]{2,1,0:T(8,128)(2,1)S(1)}, u32[]{:S(2)}, u32[]{:S(2)}) async-start(bf16[32,392,128]{2,1,0:T(8,128)(2,1)} %pack.1), calls=%async_computation | async-start | bytes 6422528 | tf_op jit(solution)/shard_map/all_to_all | solution.py:703
  108.9 0.6 fusion.21.slot_ref.refs_0_
  109.4 5.0 %edges.3 = (bf16[16,3,64,128]{3,2,1,0:T(8,128)(2,1)}, bf16[16,3,64,128]{3,2,1,0:T(8,128)(2,1)}, f32[16,3,8,128]{3,2,1,0:T(8,128)}, bf16[16,1,256,128]{3,2,1,0:T(8,128)(2,1)}) custom-call(s32[16]{0:T(128)} %fusion.21.slot_ref.refs_0_, ...), custom_call_target="tpu_custom_call" | custom-call | flops 960000000 | bytes 4800000 | tf_op jit(solution)/shard_map/edges/pallas_call | solution.py:285
  114.4 4.5 %collective-permute-start.7 = (bf16[16,3,64,128]{3,2,1,0:T(8,128)(2,1)}, bf16[16,3,64,128]{3,2,1,0:T(8,128)(2,1)}, u32[]{:S(2)}, u32[]{:S(2)}) collective-permute-start(bf16[16,3,64,128]{3,2,1,0:T(8,128)(2,1)} %get-tuple-element.48), channel_id=1, source_target_pairs={{0,1},{1,2},{2,3},{4,5},{5,6},{6,7},{8,9},{9,10},{10,11},{12,13},{... | collective-permute-start | bytes 2359304 | tf_op jit(solution)/shard_map/ppermute | solution.py:683
  118.9 1.5 collective-permute-start.8
  120.5 9.6 %sweep.4 = (f32[16,2,256]{2,1,0:T(2,128)}, f32[2,32,256]{2,1,0:T(8,128)}) custom-call(s32[16]{0:T(128)} %fusion.21.slot_ref.refs_0_, ...), custom_call_target="tpu_custom_call" | custom-call | flops 3200000000 | bytes 6400000 | tf_op jit(solution)/shard_map/sweep/pallas_call | solution.py:579
  130.1 4.9 %collective-permute-done.7.refs_43_.refs_44_.refs_15_ = bf16[16,3,64,128]{3,2,1,0:T(8,128)(2,1)} collective-permute-done((bf16[16,3,64,128]{3,2,1,0:T(8,128)(2,1)}, bf16[16,3,64,128]{3,2,1,0:T(8,128)(2,1)}, u32[]{:S(2)}, u32[]{:S(2)}) %collective-permute-start.7) | collective-permute-done | bytes 786464 | tf_op jit(solution)/shard_map/ppermute | solution.py:683
  135.0 4.7 %collective-permute-done.8.refs_45_.refs_46_.refs_18_ = bf16[16,3,64,128]{3,2,1,0:T(8,128)(2,1)} collective-permute-done((bf16[16,3,64,128]{3,2,1,0:T(8,128)(2,1)}, bf16[16,3,64,128]{3,2,1,0:T(8,128)(2,1)}, u32[]{:S(2)}, u32[]{:S(2)}) %collective-permute-start.8) | collective-permute-done | bytes 786464 | tf_op jit(solution)/shard_map/ppermute | solution.py:684
  139.8 2.3 %copy-done = bf16[16,4,144,256]{3,2,1,0:T(8,128)(2,1)S(1)} copy-done((bf16[16,4,144,256]{3,2,1,0:T(8,128)(2,1)S(1)}, bf16[16,4,144,256]{3,2,1,0:T(8,128)(2,1)}, u32[]{:S(2)}) %copy-start) | copy-done | bytes 4718616
  142.1 1.2 copy-done.2
  143.3 1.7 copy-done.4
  145.0 10.2 %sweep.5 = (f32[16,2,256]{2,1,0:T(2,128)S(1)}, f32[2,32,256]{2,1,0:T(8,128)S(1)}) custom-call(s32[16]{0:T(128)S(1)} %copy-done.27, ...), custom_call_target="tpu_custom_call" | custom-call | flops 3200000000 | bytes 6400000 | tf_op jit(solution)/shard_map/sweep/pallas_call | solution.py:579
  155.2 0.6 copy-done.23
  155.8 0.6 copy-done.25
  156.4 0.8 copy-done.14
  157.2 0.8 copy-done.17
  158.1 0.9 copy-done.18
  159.0 0.8 copy-done.21
  159.9 4.4 %unpack.1 = (bf16[16,2,64,128]{3,2,1,0:T(8,128)(2,1)S(1)}, bf16[16,2,64,128]{3,2,1,0:T(8,128)(2,1)S(1)}, f32[16,2,8,128]{3,2,1,0:T(8,128)S(1)}, bf16[16,2,256,128]{3,2,1,0:T(8,128)(2,1)S(1)}) custom-call(s32[16]{0:T(128)S(1)} %copy-done.27, bf16[32,392,128]{2,1,0:T(8,128)(2,1)S(1)} %all-to-all-done.refs_0_.refs_1_.refs_2_.refs_3_.refs_4_.refs_5_.refs_6_.refs_7_, ...), custom_call_target="tpu_custom_call" | custom-call | tf_op jit(solution)/shard_map/unpack/pallas_call | solution.py:313
  164.3 1.3 collective-permute-start.10
  165.6 4.2 %collective-permute-start.9 = (bf16[16,2,64,128]{3,2,1,0:T(8,128)(2,1)S(1)}, bf16[16,2,64,128]{3,2,1,0:T(8,128)(2,1)S(1)}, u32[]{:S(2)}, u32[]{:S(2)}) collective-permute-start(bf16[16,2,64,128]{3,2,1,0:T(8,128)(2,1)S(1)} %get-tuple-element.60), channel_id=1, source_target_pairs={{0,1},{1,2},{2,3},{4,5},{5,6},{6,7},{8,9},{9,10},{10,11},{12,13},{... | collective-permute-start | bytes 1572872 | tf_op jit(solution)/shard_map/ppermute | solution.py:683
  169.9 2.3 %copy-done.1 = bf16[16,4,144,256]{3,2,1,0:T(8,128)(2,1)S(1)} copy-done((bf16[16,4,144,256]{3,2,1,0:T(8,128)(2,1)S(1)}, bf16[16,4,144,256]{3,2,1,0:T(8,128)(2,1)}, u32[]{:S(2)}) %copy-start.1) | copy-done | bytes 4718616
  172.2 6.5 %sweep.7 = (f32[16,2,256]{2,1,0:T(2,128)S(1)}, f32[2,32,256]{2,1,0:T(8,128)S(1)}) custom-call(s32[16]{0:T(128)S(1)} %copy-done.27, bf16[16,1,256,128]{3,2,1,0:T(8,128)(2,1)S(1)} %copy-done.7, bf16[16,2,256,128]{3,2,1,0:T(8,128)(2,1)S(1)} %get-tuple-element.58.refs_2_.refs_3_, bf16[16,2,256,128]{3,2,1,0:T(8,128)(2,1)S(1)} %get-tuple-element.58.refs_2_.refs_3_, ...), custom_call_target="tpu_custom_call" | custom-call | flops 3200000000 | bytes 6400000 | tf_op jit(solution)/shard_map/sweep/pallas_call | solution.py:579
  178.8 0.3 collective-permute-done.9.refs_16_.refs_17_
  179.1 8.6 %sweep.6 = (f32[16,2,256]{2,1,0:T(2,128)S(1)}, f32[2,32,256]{2,1,0:T(8,128)S(1)}) custom-call(s32[16]{0:T(128)S(1)} %copy-done.27, bf16[16,1,256,128]{3,2,1,0:T(8,128)(2,1)S(1)} %copy-done.7, bf16[16,2,256,128]{3,2,1,0:T(8,128)(2,1)S(1)} %get-tuple-element.58.refs_2_.refs_3_, bf16[16,2,256,128]{3,2,1,0:T(8,128)(2,1)S(1)} %get-tuple-element.58.refs_2_.refs_3_, ...), custom_call_target="tpu_custom_call" | custom-call | flops 3200000000 | bytes 6400000 | tf_op jit(solution)/shard_map/sweep/pallas_call | solution.py:579
  187.7 2.6 %collect.1 = f32[4,128,256]{2,1,0:T(8,128)} custom-call(s32[4,128]{1,0:T(4,128)S(1)} %fusion.8.list_ref, s32[4]{0:T(128)S(1)} %bitcast.48, f32[2,32,256]{2,1,0:T(8,128)S(1)} %copy-done.22, f32[2,32,256]{2,1,0:T(8,128)S(1)} %get-tuple-element.67.b_ref, f32[2,32,256]{2,1,0:T(8,128)S(1)} %copy-done.24, f32[2,32,256]{2,1,0:T(8,128)S(1)} %get-tuple-element.69.d_ref), custom_call_target="tpu_custom_call" | custom-call | tf_op jit(solution)/shard_map/collect/pallas_call | solution.py:635
  190.4 4.6 %all-to-all-start.2 = ((f32[4,128,256]{2,1,0:T(8,128)}), f32[4,128,256]{2,1,0:T(8,128)S(1)}, u32[]{:S(2)}, u32[]{:S(2)}) async-start(f32[4,128,256]{2,1,0:T(8,128)} %collect.1), calls=%async_computation.2 | async-start | bytes 1048576 | tf_op jit(solution)/shard_map/all_to_all | solution.py:769
  195.1 6.8 %all-to-all-done.2.got_ref = f32[4,128,256]{2,1,0:T(8,128)S(1)} async-done(((f32[4,128,256]{2,1,0:T(8,128)}), f32[4,128,256]{2,1,0:T(8,128)S(1)}, u32[]{:S(2)}, u32[]{:S(2)}) %all-to-all-start.2) | async-done | bytes 524320 | tf_op jit(solution)/shard_map/all_to_all | solution.py:769
  201.9 3.0 %place.1 = f32[512,256]{1,0:T(8,128)} custom-call(s32[4,128]{1,0:T(4,128)S(1)} %slice.36.slot_ref, s32[4]{0:T(128)S(1)} %slice_reduce_fusion.count_ref, f32[4,128,256]{2,1,0:T(8,128)S(1)} %all-to-all-done.2.got_ref), custom_call_target="tpu_custom_call" | custom-call | tf_op jit(solution)/shard_map/place/pallas_call | solution.py:667
  204.9 11.3 %all-to-all-start.3 = ((f32[32,16,256]{2,1,0:T(8,128)}), f32[32,16,256]{2,1,0:T(8,128)S(1)}, u32[]{:S(2)}, u32[]{:S(2)}) async-start(f32[32,16,256]{2,1,0:T(8,128)} %bitcast.19), calls=%async_computation.3 | async-start | bytes 1048576 | tf_op jit(solution)/shard_map/all_to_all | solution.py:703
  216.3 0.7 pad_maximum_fusion
  217.1 10.8 %all-to-all-done.3 = f32[32,16,256]{2,1,0:T(8,128)S(1)} async-done(((f32[32,16,256]{2,1,0:T(8,128)}), f32[32,16,256]{2,1,0:T(8,128)S(1)}, u32[]{:S(2)}, u32[]{:S(2)}) %all-to-all-start.3) | async-done | bytes 524320 | tf_op jit(solution)/shard_map/all_to_all | solution.py:703
  227.9 0.6 fusion.5
  (102 shorter events, 1.8 us)
Async XLA Ops:
  7.7 8.7 %copy-start.28 = (s32[1,1,4]{2,1,0:T(1,128)S(1)}, s32[1,1,4]{2,1,0:T(1,128)}, u32[]{:S(2)}) copy-start(s32[1,1,4]{2,1,0:T(1,128)} %param.41) | copy-start | bytes 52
  7.7 8.7 %copy-start.35 = (s32[1,1,4,128]{3,2,1,0:T(4,128)S(1)}, s32[1,1,4,128]{3,2,1,0:T(4,128)}, u32[]{:S(2)}) copy-start(s32[1,1,4,128]{3,2,1,0:T(4,128)} %param.40) | copy-start | bytes 6148
  7.8 86.6 %all-to-all-start.1 = ((bf16[32,3,256,128]{3,2,1,0:T(8,128)(2,1)}), bf16[32,3,256,128]{3,2,1,0:T(8,128)(2,1)}, u32[]{:S(2)}, u32[]{:S(2)}) async-start(bf16[32,3,256,128]{3,2,1,0:T(8,128)(2,1)} %bitcast.74), calls=%async_computation.1 | async-start | bytes 12582912 | tf_op jit(solution)/shard_map/all_to_all | solution.py:703
  16.5 37.3 %collective-permute-start.4 = (s32[1,256]{1,0:T(1,128)S(1)}, s32[1,256]{1,0:T(1,128)S(1)}, u32[]{:S(2)}, u32[]{:S(2)}) collective-permute-start(s32[1,256]{1,0:T(1,128)S(1)} %get-tuple-element.75), channel_id=1, source_target_pairs={{0,1},{1,2},{2,3},{3,0},{4,5},{5,6},{6,7},{7,4},{8,9},{9,10},{10,1... | collective-permute-start | bytes 3080 | tf_op jit(solution)/shard_map/ppermute | solution.py:733
  18.2 39.6 %collective-permute-start.5 = (s32[1,256]{1,0:T(1,128)S(1)}, s32[1,256]{1,0:T(1,128)S(1)}, u32[]{:S(2)}, u32[]{:S(2)}) collective-permute-start(s32[1,256]{1,0:T(1,128)S(1)} %get-tuple-element.76), channel_id=1, source_target_pairs={{0,2},{1,3},{2,0},{3,1},{4,6},{5,7},{6,4},{7,5},{8,10},{9,11},{10,... | collective-permute-start | bytes 3080 | tf_op jit(solution)/shard_map/ppermute | solution.py:733
  21.5 37.7 %collective-permute-start.6 = (s32[1,256]{1,0:T(1,128)S(1)}, s32[1,256]{1,0:T(1,128)S(1)}, u32[]{:S(2)}, u32[]{:S(2)}) collective-permute-start(s32[1,256]{1,0:T(1,128)S(1)} %get-tuple-element.77), channel_id=1, source_target_pairs={{0,3},{1,0},{2,1},{3,2},{4,7},{5,4},{6,5},{7,6},{8,11},{9,8},{10,9... | collective-permute-start | bytes 3080 | tf_op jit(solution)/shard_map/ppermute | solution.py:733
  29.1 14.0 %copy-start.31 = (s32[16,4,512]{2,1,0:T(4,128)S(1)}, s32[16,4,512]{2,1,0:T(4,128)}, u32[]{:S(2)}) copy-start(s32[16,4,512]{2,1,0:T(4,128)} %index_ref.1) | copy-start | bytes 393220
  29.1 14.0 %copy-start.34 = (f32[64]{0:T(128)S(1)}, f32[64]{0:T(128)}, u32[]{:S(2)}) copy-start(f32[64]{0:T(128)} %param.34) | copy-start | bytes 772
  35.4 8.9 %copy-start.38 = (bf16[1,128]{1,0:T(2,128)(2,1)S(1)}, bf16[1,128]{1,0:T(2,128)(2,1)}, u32[]{:S(2)}) copy-start(bf16[1,128]{1,0:T(2,128)(2,1)} %constant.271) | copy-start | bytes 772
  35.4 8.9 %copy-start.39 = (bf16[1,128]{1,0:T(2,128)(2,1)S(1)}, bf16[1,128]{1,0:T(2,128)(2,1)}, u32[]{:S(2)}) copy-start(bf16[1,128]{1,0:T(2,128)(2,1)} %constant.272) | copy-start | bytes 772
  35.4 9.5 %copy-start.30 = (f32[16,4,512]{2,1,0:T(4,128)S(1)}, f32[16,4,512]{2,1,0:T(4,128)}, u32[]{:S(2)}) copy-start(f32[16,4,512]{2,1,0:T(4,128)} %param.36) | copy-start | bytes 393220
  35.4 9.5 %copy-start.37 = (f32[16]{0:T(128)S(1)}, f32[16]{0:T(128)}, u32[]{:S(2)}) copy-start(f32[16]{0:T(128)} %param.35) | copy-start | bytes 196
  36.8 32.1 %collective-permute-start = (bf16[16,4,64,128]{3,2,1,0:T(8,128)(2,1)S(1)}, bf16[16,4,64,128]{3,2,1,0:T(8,128)(2,1)}, u32[]{:S(2)}, u32[]{:S(2)}) collective-permute-start(bf16[16,4,64,128]{3,2,1,0:T(8,128)(2,1)S(1)} %slice.30), channel_id=1, source_target_pairs={{0,1},{1,2},{2,3},{4,5},{5,6},{6,7},{8,9},{9,10},{10,11},{12,13},{... | collective-permute-start | bytes 3145736 | tf_op jit(solution)/shard_map/ppermute | solution.py:683
  41.7 27.2 %collective-permute-start.2 = (bf16[16,4,64,128]{3,2,1,0:T(8,128)(2,1)S(1)}, bf16[16,4,64,128]{3,2,1,0:T(8,128)(2,1)}, u32[]{:S(2)}, u32[]{:S(2)}) collective-permute-start(bf16[16,4,64,128]{3,2,1,0:T(8,128)(2,1)S(1)} %slice.32), channel_id=1, source_target_pairs={{1,0},{2,1},{3,2},{5,4},{6,5},{7,6},{9,8},{10,9},{11,10},{13,12},{... | collective-permute-start | bytes 3145736 | tf_op jit(solution)/shard_map/ppermute | solution.py:684
  53.8 7.0 %collective-permute-start.1 = (bf16[16,128]{1,0:T(8,128)(2,1)S(1)}, bf16[16,128]{1,0:T(8,128)(2,1)S(1)}, u32[]{:S(2)}, u32[]{:S(2)}) collective-permute-start(bf16[16,128]{1,0:T(8,128)(2,1)S(1)} %reshape.88), channel_id=1, source_target_pairs={{0,1},{1,2},{2,3},{4,5},{5,6},{6,7},{8,9},{9,10},{10,11},{12,13},{... | collective-permute-start | bytes 12296 | tf_op jit(solution)/shard_map/ppermute | solution.py:683
  57.9 9.2 %collective-permute-start.3 = (bf16[16,128]{1,0:T(8,128)(2,1)S(1)}, bf16[16,128]{1,0:T(8,128)(2,1)S(1)}, u32[]{:S(2)}, u32[]{:S(2)}) collective-permute-start(bf16[16,128]{1,0:T(8,128)(2,1)S(1)} %reshape.90), channel_id=1, source_target_pairs={{1,0},{2,1},{3,2},{5,4},{6,5},{7,6},{9,8},{10,9},{11,10},{13,12},{... | collective-permute-start | bytes 12296 | tf_op jit(solution)/shard_map/ppermute | solution.py:684
  94.3 62.1 %all-to-all-start = ((bf16[32,392,128]{2,1,0:T(8,128)(2,1)}), bf16[32,392,128]{2,1,0:T(8,128)(2,1)S(1)}, u32[]{:S(2)}, u32[]{:S(2)}) async-start(bf16[32,392,128]{2,1,0:T(8,128)(2,1)} %pack.1), calls=%async_computation | async-start | bytes 6422528 | tf_op jit(solution)/shard_map/all_to_all | solution.py:703
  114.4 20.6 %collective-permute-start.7 = (bf16[16,3,64,128]{3,2,1,0:T(8,128)(2,1)}, bf16[16,3,64,128]{3,2,1,0:T(8,128)(2,1)}, u32[]{:S(2)}, u32[]{:S(2)}) collective-permute-start(bf16[16,3,64,128]{3,2,1,0:T(8,128)(2,1)} %get-tuple-element.48), channel_id=1, source_target_pairs={{0,1},{1,2},{2,3},{4,5},{5,6},{6,7},{8,9},{9,10},{10,11},{12,13},{... | collective-permute-start | bytes 2359304 | tf_op jit(solution)/shard_map/ppermute | solution.py:683
  118.9 20.8 %collective-permute-start.8 = (bf16[16,3,64,128]{3,2,1,0:T(8,128)(2,1)}, bf16[16,3,64,128]{3,2,1,0:T(8,128)(2,1)}, u32[]{:S(2)}, u32[]{:S(2)}) collective-permute-start(bf16[16,3,64,128]{3,2,1,0:T(8,128)(2,1)} %get-tuple-element.49), channel_id=1, source_target_pairs={{1,0},{2,1},{3,2},{5,4},{6,5},{7,6},{9,8},{10,9},{11,10},{13,12},{... | collective-permute-start | bytes 2359304 | tf_op jit(solution)/shard_map/ppermute | solution.py:684
  120.4 19.3 %copy-start.6 = (f32[16,3,8,128]{3,2,1,0:T(8,128)S(1)}, f32[16,3,8,128]{3,2,1,0:T(8,128)}, u32[]{:S(2)}) copy-start(f32[16,3,8,128]{3,2,1,0:T(8,128)} %get-tuple-element.47.refs_41_.refs_42_.refs_12_) | copy-start | bytes 589828
  120.4 19.3 %copy-start.8 = (f32[16,4,512]{2,1,0:T(4,128)S(1)}, f32[16,4,512]{2,1,0:T(4,128)}, u32[]{:S(2)}) copy-start(f32[16,4,512]{2,1,0:T(4,128)} %fusion.refs_39_.refs_10_) | copy-start | bytes 393220
  120.4 19.3 %copy-start.9 = (s32[16,4,512]{2,1,0:T(4,128)S(1)}, s32[16,4,512]{2,1,0:T(4,128)}, u32[]{:S(2)}) copy-start(s32[16,4,512]{2,1,0:T(4,128)} %refs_11_.4) | copy-start | bytes 393220
  120.4 19.3 %copy-start.11 = (bf16[128,768]{1,0:T(8,128)(2,1)S(1)}, bf16[128,768]{1,0:T(8,128)(2,1)}, u32[]{:S(2)}) copy-start(bf16[128,768]{1,0:T(8,128)(2,1)} %constant.167.clone.refs_35_.refs_6_) | copy-start | bytes 589828
  120.4 19.3 %copy-start.15 = (bf16[128,128]{1,0:T(8,128)(2,1)S(1)}, bf16[128,128]{1,0:T(8,128)(2,1)}, u32[]{:S(2)}) copy-start(bf16[128,128]{1,0:T(8,128)(2,1)} %constant.162.clone.flip_ref.refs_38_.refs_9_) | copy-start | bytes 98308
  120.4 19.3 %copy-start.19 = (bf16[16,256]{1,0:T(8,128)(2,1)S(1)}, bf16[16,256]{1,0:T(8,128)(2,1)}, u32[]{:S(2)}) copy-start(bf16[16,256]{1,0:T(8,128)(2,1)} %constant.166.clone.refs_36_.refs_7_) | copy-start | bytes 24580
  120.5 19.3 %copy-start.20 = (bf16[8,256]{1,0:T(8,128)(2,1)S(1)}, bf16[8,256]{1,0:T(8,128)(2,1)}, u32[]{:S(2)}) copy-start(bf16[8,256]{1,0:T(8,128)(2,1)} %pad_maximum_fusion.1.refs_37_.refs_8_) | copy-start | bytes 12292
  120.5 19.3 %copy-start.27 = (s32[16]{0:T(128)S(1)}, s32[16]{0:T(128)}, u32[]{:S(2)}) copy-start(s32[16]{0:T(128)} %fusion.21.slot_ref.refs_0_) | copy-start | bytes 196
  139.8 2.3 %copy-start = (bf16[16,4,144,256]{3,2,1,0:T(8,128)(2,1)S(1)}, bf16[16,4,144,256]{3,2,1,0:T(8,128)(2,1)}, u32[]{:S(2)}) copy-start(bf16[16,4,144,256]{3,2,1,0:T(8,128)(2,1)} %get-tuple-element.43.refs_33_.refs_4_) | copy-start | bytes 14155780
  142.1 1.2 copy-start.2
  143.3 1.7 copy-start.4
  155.2 0.6 copy-start.23
  155.8 0.6 copy-start.25
  156.4 0.8 copy-start.14
  157.2 0.8 copy-start.17
  158.1 0.9 copy-start.18
  159.0 0.8 copy-start.21
  159.8 10.0 %copy-start.36 = (s32[1,1,4,128]{3,2,1,0:T(4,128)S(1)}, s32[1,1,4,128]{3,2,1,0:T(4,128)}, u32[]{:S(2)}) copy-start(s32[1,1,4,128]{3,2,1,0:T(4,128)} %param.39) | copy-start | bytes 6148
  159.8 10.0 %copy-start.3 = (bf16[16,4,64,128]{3,2,1,0:T(8,128)(2,1)S(1)}, bf16[16,4,64,128]{3,2,1,0:T(8,128)(2,1)}, u32[]{:S(2)}) copy-start(bf16[16,4,64,128]{3,2,1,0:T(8,128)(2,1)} %get-tuple-element.44.refs_34_.refs_5_) | copy-start | bytes 3145732
  159.8 10.0 %copy-start.7 = (bf16[16,1,256,128]{3,2,1,0:T(8,128)(2,1)S(1)}, bf16[16,1,256,128]{3,2,1,0:T(8,128)(2,1)}, u32[]{:S(2)}) copy-start(bf16[16,1,256,128]{3,2,1,0:T(8,128)(2,1)} %get-tuple-element.56.refs_1_) | copy-start | bytes 3145732
  159.8 10.1 %copy-start.10 = (s32[16,4,512]{2,1,0:T(4,128)S(1)}, s32[16,4,512]{2,1,0:T(4,128)}, u32[]{:S(2)}) copy-start(s32[16,4,512]{2,1,0:T(4,128)} %refs_11_.4) | copy-start | bytes 393220
  159.8 10.1 %copy-start.13 = (bf16[128,768]{1,0:T(8,128)(2,1)S(1)}, bf16[128,768]{1,0:T(8,128)(2,1)}, u32[]{:S(2)}) copy-start(bf16[128,768]{1,0:T(8,128)(2,1)} %constant.165.clone.refs_35_.refs_6_) | copy-start | bytes 589828
  159.8 10.1 %copy-start.16 = (bf16[128,128]{1,0:T(8,128)(2,1)S(1)}, bf16[128,128]{1,0:T(8,128)(2,1)}, u32[]{:S(2)}) copy-start(bf16[128,128]{1,0:T(8,128)(2,1)} %constant.162.clone.flip_ref.refs_38_.refs_9_) | copy-start | bytes 98308
  164.3 14.5 %collective-permute-start.10 = (bf16[16,2,64,128]{3,2,1,0:T(8,128)(2,1)S(1)}, bf16[16,2,64,128]{3,2,1,0:T(8,128)(2,1)S(1)}, u32[]{:S(2)}, u32[]{:S(2)}) collective-permute-start(bf16[16,2,64,128]{3,2,1,0:T(8,128)(2,1)S(1)} %get-tuple-element.61), channel_id=1, source_target_pairs={{1,0},{2,1},{3,2},{5,4},{6,5},{7,6},{9,8},{10,9},{11,10},{13,12},{... | collective-permute-start | bytes 1572872 | tf_op jit(solution)/shard_map/ppermute | solution.py:684
  165.6 13.5 %collective-permute-start.9 = (bf16[16,2,64,128]{3,2,1,0:T(8,128)(2,1)S(1)}, bf16[16,2,64,128]{3,2,1,0:T(8,128)(2,1)S(1)}, u32[]{:S(2)}, u32[]{:S(2)}) collective-permute-start(bf16[16,2,64,128]{3,2,1,0:T(8,128)(2,1)S(1)} %get-tuple-element.60), channel_id=1, source_target_pairs={{0,1},{1,2},{2,3},{4,5},{5,6},{6,7},{8,9},{9,10},{10,11},{12,13},{... | collective-permute-start | bytes 1572872 | tf_op jit(solution)/shard_map/ppermute | solution.py:683
  169.9 2.3 %copy-start.1 = (bf16[16,4,144,256]{3,2,1,0:T(8,128)(2,1)S(1)}, bf16[16,4,144,256]{3,2,1,0:T(8,128)(2,1)}, u32[]{:S(2)}) copy-start(bf16[16,4,144,256]{3,2,1,0:T(8,128)(2,1)} %get-tuple-element.43.refs_33_.refs_4_) | copy-start | bytes 14155780
  172.2 6.9 %copy-start.5 = (bf16[16,4,144,128]{3,2,1,0:T(8,128)(2,1)S(1)}, bf16[16,4,144,128]{3,2,1,0:T(8,128)(2,1)}, u32[]{:S(2)}) copy-start(bf16[16,4,144,128]{3,2,1,0:T(8,128)(2,1)} %get-tuple-element.53.refs_47_.refs_21_) | copy-start | bytes 7077892
  172.2 6.9 %copy-start.12 = (bf16[128,768]{1,0:T(8,128)(2,1)S(1)}, bf16[128,768]{1,0:T(8,128)(2,1)}, u32[]{:S(2)}) copy-start(bf16[128,768]{1,0:T(8,128)(2,1)} %constant.167.clone.refs_35_.refs_6_) | copy-start | bytes 589828
  178.7 9.0 %copy-start.22 = (f32[2,32,256]{2,1,0:T(8,128)S(1)}, f32[2,32,256]{2,1,0:T(8,128)}, u32[]{:S(2)}) copy-start(f32[2,32,256]{2,1,0:T(8,128)} %get-tuple-element.66.a_ref) | copy-start | bytes 196612
  178.7 9.0 %copy-start.24 = (f32[2,32,256]{2,1,0:T(8,128)S(1)}, f32[2,32,256]{2,1,0:T(8,128)}, u32[]{:S(2)}) copy-start(f32[2,32,256]{2,1,0:T(8,128)} %copy-done.23) | copy-start | bytes 196612
  178.7 9.0 %copy-start.29 = (s32[1,1,4]{2,1,0:T(1,128)S(1)}, s32[1,1,4]{2,1,0:T(1,128)}, u32[]{:S(2)}) copy-start(s32[1,1,4]{2,1,0:T(1,128)} %param.41) | copy-start | bytes 52
  178.8 16.3 %copy-start.33 = (s32[4,256]{1,0:T(4,128)S(1)}, s32[4,256]{1,0:T(4,128)}, u32[]{:S(2)}) copy-start(s32[4,256]{1,0:T(4,128)} %broadcast_select_fusion) | copy-start | bytes 12292
  178.8 37.5 %copy-start.26 = (f32[16,2,256]{2,1,0:T(2,128)S(1)}, f32[16,2,256]{2,1,0:T(2,128)}, u32[]{:S(2)}) copy-start(f32[16,2,256]{2,1,0:T(2,128)} %copy-done.25) | copy-start | bytes 98308
  178.8 37.5 %copy-start.32 = (f32[16,2,256]{2,1,0:T(2,128)S(1)}, f32[16,2,256]{2,1,0:T(2,128)}, u32[]{:S(2)}) copy-start(f32[16,2,256]{2,1,0:T(2,128)} %get-tuple-element.63) | copy-start | bytes 98308
  190.4 11.6 %all-to-all-start.2 = ((f32[4,128,256]{2,1,0:T(8,128)}), f32[4,128,256]{2,1,0:T(8,128)S(1)}, u32[]{:S(2)}, u32[]{:S(2)}) async-start(f32[4,128,256]{2,1,0:T(8,128)} %collect.1), calls=%async_computation.2 | async-start | bytes 1048576 | tf_op jit(solution)/shard_map/all_to_all | solution.py:769
  204.9 22.9 %all-to-all-start.3 = ((f32[32,16,256]{2,1,0:T(8,128)}), f32[32,16,256]{2,1,0:T(8,128)S(1)}, u32[]{:S(2)}, u32[]{:S(2)}) async-start(f32[32,16,256]{2,1,0:T(8,128)} %bitcast.19), calls=%async_computation.3 | async-start | bytes 1048576 | tf_op jit(solution)/shard_map/all_to_all | solution.py:703
